TPU v7x, 32 devices: a whole 2x2x4 slice. The times are simulated.
32 devices in a mesh: dp: 4 (over x, core), ctx: 8 (over z, y).
Axes of the slice: x: 2, y: 2, z: 4, core: 2. Of those that a mesh axis runs over, the one named last changes fastest.
Arguments:
- inputs: bfloat16 [4, 1024, 2048], P('dp', 'ctx'), may hold values from -6 to 6
- b_proj: bfloat16 [4, 1024, 64], P('dp', 'ctx'), may hold values from -0.75 to 0.75
- c_proj: bfloat16 [4, 1024, 64], P('dp', 'ctx'), may hold values from -6 to 6
- step_sizes: float32 [4, 32, 1024], P('dp', None, 'ctx'), may hold values from 0.0001 to 0.37
- a_log: float32 [32], replicated, may hold values from -8 to -1.7
- skip_gain: float32 [32], replicated, may hold values from 0.5 to 1.5
- doc_lengths: int32 [4, 16], P('dp'), may hold values from 1 to 256, 1024 in all within a row
- grad_out: bfloat16 [4, 1024, 2048], P('dp', 'ctx'), may hold values from -6 to 6
Outputs:
- input_grads: bfloat16 [4, 1024, 2048], P('dp', 'ctx')
- b_gradient: bfloat16 [4, 1024, 64], P('dp', 'ctx')
- c_gradient: bfloat16 [4, 1024, 64], P('dp', 'ctx')
- step_grads: float32 [4, 32, 1024], P('dp', None, 'ctx')
- alog_grads: float32 [32], replicated
- skip_grads: float32 [32], replicated
Inputs may be any that keep to these rules, and one draw needn't show every extreme that they name: `doc_lengths`: each row holds the 16 document lengths of one packed sequence, in order, summing to 1024; the longest is exactly 256.
All inputs are finite; a program needn't handle non-finite values.
Results may differ from a plain program's by a relative error of at most 0.0012.
Values sent between devices are 32-bit elements; how exact they have to be, the bound alone decides.
No kernel may reach another device: no remote copies, remote signals or barrier semaphores. Data moves between devices by JAX's collectives and lax.ppermute only.
A program may use at most 256 MiB of HBM per device.

v0:
```python
import jax
import jax.numpy as jnp
from jax import lax
from jax.sharding import PartitionSpec as P

GROUP = 128


very_negative = -1e30
highest = lax.Precision.HIGHEST


def prefix_2(x, axis, combine, identity, reverse):
    count, index = (lax.axis_size(axis), lax.axis_index(axis))
    everything = jax.tree.map(lambda part: lax.all_gather(part, axis), x)
    start = jax.tree.map(
        lambda part, zero: jnp.broadcast_to(jnp.asarray(zero, part.dtype), part.shape), x, identity
    )

    def step(k, before):
        at = count - 1 - k if reverse else k
        reached = at > index if reverse else at < index
        new = combine(before, jax.tree.map(lambda part: part[at], everything))
        return jax.tree.map(lambda a, b: jnp.where(reached, a, b), new, before)

    return lax.fori_loop(0, count, step, start)


def segment_ids(lengths, offset, row_count):
    starts = jnp.cumsum(lengths) - lengths
    places = offset + jnp.arange(row_count, dtype=jnp.int32)
    return jnp.sum((starts[None, :] <= places[:, None]).astype(jnp.int32), axis=1) - 1


def decay_logs(deltas, rate_log):
    return deltas * (-jnp.exp(rate_log))[:, None]


def intra_group(values, bvectors, cvectors, deltas, rate_log, segment):
    cumulated = jnp.cumsum(decay_logs(deltas, rate_log), axis=1)
    spread = cumulated[:, :, None] - cumulated[:, None, :]
    places = jnp.arange(segment.shape[0])
    allowed = (places[:, None] >= places[None, :]) & (segment[:, None] == segment[None, :])
    kernel = jnp.exp(jnp.where(allowed[None], spread, very_negative))
    scores = jnp.dot(cvectors, bvectors.T, precision=highest)
    weights = kernel * scores[None] * deltas[:, None, :]
    return jnp.einsum("hts,shp->thp", weights, values, precision=highest)


def group_cross(values, bvectors, cvectors, deltas, rate_log, segment, before, incoming):
    cumulated = jnp.cumsum(decay_logs(deltas, rate_log), axis=1)
    living = (segment == before).astype(cumulated.dtype)
    carried = jnp.exp(cumulated) * living[None, :]
    readout = (
        jnp.einsum("tn,hpn->thp", cvectors, incoming, precision=highest)
        * jnp.transpose(carried)[:, :, None]
    )
    ending = (segment == segment[-1]).astype(cumulated.dtype)
    keeping = jnp.exp(cumulated[:, -1:] - cumulated) * deltas * ending[None, :]
    weighted = values * jnp.transpose(keeping)[:, :, None]
    fresh_part = jnp.einsum("shp,sn->hpn", weighted, bvectors, precision=highest)
    return (readout, carried[:, -1][:, None, None] * incoming + fresh_part)


def intra_run(values, bvectors, cvectors, deltas, rate_log, segment):
    row_count = values.shape[0]
    group_count = row_count // GROUP
    pieces = (
        values.reshape(group_count, GROUP, values.shape[1], values.shape[2]),
        bvectors.reshape(group_count, GROUP, bvectors.shape[1]),
        cvectors.reshape(group_count, GROUP, cvectors.shape[1]),
        jnp.transpose(deltas.reshape(deltas.shape[0], group_count, GROUP), (1, 0, 2)),
        segment.reshape(group_count, GROUP),
    )

    def within(pieces_now):
        return intra_group(
            pieces_now[0], pieces_now[1], pieces_now[2], pieces_now[3], rate_log, pieces_now[4]
        )

    outcome = lax.map(jax.checkpoint(within), pieces)
    return outcome.reshape(row_count, values.shape[1], values.shape[2])


def cross_run(values, bvectors, cvectors, deltas, rate_log, segment, before, incoming):
    row_count = values.shape[0]
    group_count = row_count // GROUP
    befores = jnp.concatenate([jnp.reshape(before, (1,)), segment[GROUP - 1 :: GROUP][:-1]])
    pieces = (
        values.reshape(group_count, GROUP, values.shape[1], values.shape[2]),
        bvectors.reshape(group_count, GROUP, bvectors.shape[1]),
        cvectors.reshape(group_count, GROUP, cvectors.shape[1]),
        jnp.transpose(deltas.reshape(deltas.shape[0], group_count, GROUP), (1, 0, 2)),
        segment.reshape(group_count, GROUP),
        befores,
    )

    def advance(carried_state, pieces_now):
        readout, next_state = group_cross(
            pieces_now[0],
            pieces_now[1],
            pieces_now[2],
            pieces_now[3],
            rate_log,
            pieces_now[4],
            pieces_now[5],
            carried_state,
        )
        return (next_state, readout)

    ending_state, readout = lax.scan(jax.checkpoint(advance), incoming, pieces)
    return (readout.reshape(row_count, values.shape[1], values.shape[2]), ending_state)


def combine_pairs(earlier, later):
    return (earlier[0] * later[0], later[0][:, None, None] * earlier[1] + later[1])


def per_device(inputs, b_proj, c_proj, step_sizes, a_log, skip_gain, doc_lengths, grad_out):
    row_count = inputs.shape[1]
    head_count = a_log.shape[0]
    head_width = inputs.shape[2] // head_count
    values = inputs[0].astype(jnp.float32).reshape(row_count, head_count, head_width)
    bvectors = b_proj[0].astype(jnp.float32)
    cvectors = c_proj[0].astype(jnp.float32)
    deltas = step_sizes[0]
    lengths = doc_lengths[0]
    upstream = grad_out[0].astype(jnp.float32).reshape(row_count, head_count, head_width)
    state_width = bvectors.shape[1]
    offset = lax.axis_index("ctx") * row_count
    segment = segment_ids(lengths, offset, row_count)
    before = segment_ids(lengths, offset - 1, 1)[0]

    def local_part(value_in, bvec_in, cvec_in, delta_in, rate_in, skip_in):
        return (
            intra_run(value_in, bvec_in, cvec_in, delta_in, rate_in, segment)
            + skip_in[None, :, None] * value_in
        )

    outcome, pull_local = jax.vjp(local_part, values, bvectors, cvectors, deltas, a_log, skip_gain)
    local_grads = pull_local(upstream)
    nothing = jnp.zeros((head_count, head_width, state_width), jnp.float32)
    readout, own_states = cross_run(
        values, bvectors, cvectors, deltas, a_log, segment, before, nothing
    )
    log_decay = decay_logs(deltas, a_log)
    through = jnp.exp(jnp.sum(log_decay, axis=1)) * (segment[-1] == before).astype(jnp.float32)
    carried = (
        jnp.exp(jnp.cumsum(log_decay, axis=1)) * (segment == before).astype(jnp.float32)[None, :]
    )
    pulled = jnp.einsum(
        "thp,tn->hpn", upstream * jnp.transpose(carried)[:, :, None], cvectors, precision=highest
    )
    identity_pair = (jnp.ones((head_count,), jnp.float32), nothing)
    prefix = prefix_2((through, own_states), "ctx", combine_pairs, identity_pair, False)
    suffix = prefix_2((through, pulled), "ctx", combine_pairs, identity_pair, True)
    incoming = prefix[1]

    def cross_part(value_in, bvec_in, cvec_in, delta_in, rate_in):
        return cross_run(value_in, bvec_in, cvec_in, delta_in, rate_in, segment, before, incoming)

    outflow, pull_cross = jax.vjp(cross_part, values, bvectors, cvectors, deltas, a_log)
    cross_grads = pull_cross((upstream, suffix[1]))
    rate_grad = local_grads[4] + cross_grads[4]
    totals = lax.psum((rate_grad, local_grads[5]), ("dp", "ctx"))
    value_grads = (local_grads[0] + cross_grads[0]).reshape(row_count, head_count * head_width)
    return (
        value_grads.astype(jnp.bfloat16)[None],
        (local_grads[1] + cross_grads[1]).astype(jnp.bfloat16)[None],
        (local_grads[2] + cross_grads[2]).astype(jnp.bfloat16)[None],
        (local_grads[3] + cross_grads[3])[None],
        totals[0],
        totals[1],
    )


def solution(mesh):
    in_specs = (
        P("dp", "ctx", None),
        P("dp", "ctx", None),
        P("dp", "ctx", None),
        P("dp", None, "ctx"),
        P(),
        P(),
        P("dp", None),
        P("dp", "ctx", None),
    )
    out_specs = (
        P("dp", "ctx", None),
        P("dp", "ctx", None),
        P("dp", "ctx", None),
        P("dp", None, "ctx"),
        P(),
        P(),
    )
    return jax.shard_map(
        per_device, mesh=mesh, in_specs=in_specs, out_specs=out_specs, check_vma=False
    )
```

profile of v0, /device:TPU:0, one launch (start us, length us, event | category | flops | bytes accessed | tf_op | source)
XLA Modules:
  0.0 357.8 jit_solution(2004591855677435305)
XLA Ops:
  14.1 1.5 copy.41
  17.0 1.6 convolution_add_fusion
  18.7 1.6 fusion.42
  22.4 23.7 %all-reduce.2 = f32[256]{0:T(256)S(1)} all-reduce(f32[256]{0:T(256)S(1)} %multiply_dynamic-update-slice_fusion), channel_id=2, replica_groups=mesh['dp'=4,'ctx'=8] {'ctx'}, use_global_device_ids=true, to_apply=%add.2 | all-reduce | flops 256 | bytes 2048
  49.1 97.5 %all-gather.6.cloned.1.call-done = f32[256,64,64]{2,1,0:T(8,128)} async-done(((f32[32,64,64]{2,1,0:T(8,128)}), f32[256,64,64]{2,1,0:T(8,128)}) %all-gather.6.cloned.1.call-update) | async-done | bytes 4194320 | tf_op jit(solution)/shard_map/all_gather | solution.py:15
  146.6 12.2 %while.20 = (s32[]{:T(128)}, f32[32,64,64]{2,1,0:T(8,128)S(1)}, s32[]{:T(128)}, f32[8,32]{1,0:T(8,128)S(1)}, f32[8,32,64,64]{3,2,1,0:T(8,128)}, /*index=5*/s32[]{:T(128)}, s32[]{:T(128)}) while((s32[]{:T(128)}, f32[32,64,64]{2,1,0:T(8,128)S(1)}, s32[]{:T(128)}, f32[8,32]{1,0:T(8,128)S(1)}, f32[8,32,64,64]{3,2,1,0:T(8,128)}, ...), condition=%wide.region_7.8_spmd.clone, body=%wide.region_6.7_spmd.clone.sunk | while | flops 524292 | bytes 1573353 | solution.py:26
  152.6 1.5 fusion.67
  154.1 1.6 fusion.67
  155.8 1.5 fusion.67
  158.8 113.1 %all-gather.8.cloned.1.call-done = f32[256,64,64]{2,1,0:T(8,128)} async-done(((f32[32,64,64]{2,1,0:T(8,128)}), f32[256,64,64]{2,1,0:T(8,128)}) %all-gather.8.cloned.1.call-update) | async-done | bytes 4194320 | tf_op jit(solution)/shard_map/all_gather | solution.py:15
  271.9 12.3 %while.21 = (s32[]{:T(128)}, f32[32,64,64]{2,1,0:T(8,128)S(1)}, s32[]{:T(128)}, f32[8,32]{1,0:T(8,128)S(1)}, f32[8,32,64,64]{3,2,1,0:T(8,128)}, /*index=5*/s32[]{:T(128)}, s32[]{:T(128)}, s32[]{:T(128)}, s32[]{:T(128)}) while((s32[]{:T(128)}, f32[32,64,64]{2,1,0:T(8,128)S(1)}, s32[]{:T(128)}, f32[8,32]{1,0:T(8,128)S(1)}, ...), condition=%wide.region_9.10_spmd.clone, body=%wide.region_8.9_spmd.clone.sunk | while | flops 524296 | bytes 1573415 | solution.py:26
  273.4 1.5 fusion.68
  274.9 1.5 fusion.68
  276.5 1.5 fusion.68
  279.5 1.5 fusion.68
  282.5 1.5 fusion.68
  284.6 6.1 %fusion.8 = (f32[32,128]{1,0:T(8,128)S(1)}, f32[32,128]{1,0:T(8,128)S(1)}, f32[32,128]{1,0:T(8,128)S(1)}, f32[128,128]{1,0:T(8,128)S(1)}) fusion(f32[32,128]{1,0:T(8,128)S(1)} %bitcast.150, f32[128,128]{1,0:T(8,128)S(1)} %fusion.49, f32[32,128]{1,0:T(8,128)S(1)} %reduce_window_sum.58, pred[128,128]{1,0:T(8,128)(4,1)S(1)} %fusion.30, ...), kind=kOutput, calls=%fused_computation.17 | convolution fusion | flops 409440256 | bytes 2326528 | tf_op jit(solution)/shard_map/transpose(jvp())/while/body/eval_jaxpr/checkpoint/hts,shp->thp/dot_general | solution.py:47
  291.1 3.4 fusion.2
  297.6 2.0 multiply_reduce_fusion.4
  300.3 2.2 fusion.6
  304.1 2.5 fusion.14
  307.4 1.7 fusion.16
  310.1 38.3 %all-reduce.3 = (f32[32]{0:T(128)}, f32[32]{0:T(128)}) all-reduce(f32[32]{0:T(128)S(1)} %multiply_add_fusion, f32[32]{0:T(128)S(1)} %reduce_sum.207), channel_id=1, replica_groups=mesh['dp'=4,'ctx'=8] {'dp','ctx'}, use_global_device_ids=true, to_apply=%region_23.24 | all-reduce | flops 64 | bytes 512 | tf_op jit(solution)/shard_map/psum | solution.py:165
  348.4 2.5 fusion.13
  (105 shorter events, 31.1 us)
Async XLA Ops:
  7.2 9.1 %copy-start.6 = (f32[1,32,128]{2,1,0:T(8,128)S(1)}, f32[1,32,128]{2,1,0:T(8,128)}, u32[]{:S(2)}) copy-start(f32[1,32,128]{2,1,0:T(8,128)} %param.15) | copy-start | bytes 49156
  7.2 139.5 %all-gather.6.cloned.1.call-start = ((), (), s32[]{:S(2)}) async-start(), calls=%async_computation | async-start | bytes 9437184 | tf_op jit(solution)/shard_map/all_gather | solution.py:15
  14.1 32.0 %copy-start.2 = (bf16[1,128,2048]{1,2,0:T(8,128)(2,1)}, bf16[1,128,2048]{1,2,0:T(8,128)(2,1)S(1)}, u32[]{:S(2)}) copy-start(bf16[1,128,2048]{1,2,0:T(8,128)(2,1)S(1)} %copy.40) | copy-start | bytes 1572868
  14.1 2.9 copy-start.8
  15.6 3.0 copy-start.4
  16.9 1.7 copy-start.7
  18.6 2.4 copy-start.11
  18.6 253.3 %all-gather.8.cloned.1.call-start = ((), (), s32[]{:S(2)}) async-start(), calls=%async_computation.1 | async-start | bytes 9437184 | tf_op jit(solution)/shard_map/all_gather | solution.py:15
  20.3 28.3 %copy-start.9 = (f32[32]{0:T(128)S(1)}, f32[32]{0:T(128)}, u32[]{:S(2)}) copy-start(f32[32]{0:T(128)} %param.17) | copy-start | bytes 388
  271.9 12.3 %copy-start.10 = (f32[32]{0:T(128)S(1)}, f32[32]{0:T(128)}, u32[]{:S(2)}) copy-start(f32[32]{0:T(128)} %param.16) | copy-start | bytes 388
  284.6 6.5 %copy-start = (f32[128,32,64]{0,2,1:T(8,128)S(1)}, f32[128,32,64]{0,2,1:T(8,128)}, u32[]{:S(2)}) copy-start(f32[128,32,64]{0,2,1:T(8,128)} %convert.3) | copy-start | bytes 3145732
  304.1 3.3 copy-start.3
  304.1 3.3 copy-start.5
  307.4 41.0 %copy-start.1 = (f32[128,32,64]{0,2,1:T(8,128)S(1)}, f32[128,32,64]{0,2,1:T(8,128)}, u32[]{:S(2)}) copy-start(f32[128,32,64]{0,2,1:T(8,128)} %convert.3) | copy-start | bytes 3145732
Sparse Core Ops, SparseCore 0:
  18.7 127.8 all-gather.5
  148.8 123.1 all-gather.7
where the time goes:
time: 359 us; the launch traced here: 358 us
  waiting for transfers between devices  211 us (59%)
  blocking collectives  62 us (17%)
  other arithmetic  38.8 us (11%)
  matrix products  22.6 us (6%)
  between operations  16.3 us (5%)
  local copies, waits for them, and re-layouts  6.59 us (2%)
    all_gather x2, waiting for transfers between devices, prefix_2(): everything = jax.tree.map(lambda part: lax.all_gather(part, axis), x)  211 us
    psum x1, blocking collectives, per_device(): totals = lax.psum((rate_grad, local_grads[5]), ('dp', 'ctx'))  38.3 us
    unnamed x1, blocking collectives  23.7 us
    select_n x16, other arithmetic, step(): return jax.tree.map(lambda a, b: jnp.where(reached, a, b), new, before)  23.6 us
    dot_general x2, matrix products, intra_group(): return jnp.einsum('hts,shp->thp', weights, values, precision=highest)  9.49 us
  transfers between devices with their start and end apart: 2, of which 2 were waited for; matrix products, arithmetic and copies ran while one was open for 5% of the time, Pallas kernels for 0%

commit v1 on v0

v1 whole, which is shorter than its diff:
```python
import functools

import jax
import jax.numpy as jnp
from jax import lax
from jax.experimental import pallas as pl
from jax.experimental.pallas import tpu as pltpu
from jax.sharding import PartitionSpec as P

F32 = jnp.float32
BF16 = jnp.bfloat16
HIGHEST = lax.Precision.HIGHEST
LANES = 128
WIDE = 256
PARTS = WIDE // LANES
FAR = 2**30
VMEM_LIMIT = 48 * 1024 * 1024


def dot(a, b, ca, cb, precision=None):
    return lax.dot_general(
        a, b, (((ca,), (cb,)), ((), ())), precision=precision, preferred_element_type=F32
    )


def iota(shape, dim):
    return lax.broadcasted_iota(jnp.int32, shape, dim)


def split2(a):
    high = a.astype(BF16)
    return high, (a - high.astype(F32)).astype(BF16)


def split3(a):
    high = a.astype(BF16)
    rest = a - high.astype(F32)
    middle = rest.astype(BF16)
    return high, middle, (rest - middle.astype(F32)).astype(BF16)


def dot_pairs(a, b, ca, cb):
    return dot(a[0], b[0], ca, cb) + (dot(a[0], b[1], ca, cb) + dot(a[1], b[0], ca, cb))


def document_places(lens_ref, rows):
    offset = lax.axis_index("ctx") * rows
    starts = [jnp.int32(0)]
    for d in range(lens_ref.shape[1] - 1):
        starts.append(starts[-1] + lens_ref[0, d])
    first = jnp.int32(FAR)
    last = jnp.int32(0)
    for start in starts:
        first = jnp.minimum(first, jnp.where(start >= offset, start, FAR))
        last = jnp.maximum(last, jnp.where(start < offset + rows, start, 0))
    return starts, offset, first, last


def rate_column(alog_ref):
    heads = alog_ref.shape[1]
    square = jnp.broadcast_to(alog_ref[...], (heads, heads))
    picked = jnp.where(iota((heads, heads), 0) == iota((heads, heads), 1), square, 0.0)
    return -jnp.exp(jnp.sum(picked, axis=1, keepdims=True))


def head_block(heads, head_width, block, copies):
    shape = (copies * heads, WIDE)
    row = lax.rem(iota(shape, 0), heads)
    column = lax.div(iota(shape, 1) + block * WIDE, head_width)
    return jnp.where(row == column, 1.0, 0.0).astype(BF16)


def head_sums(ones, a):
    total = None
    for part in split3(a):
        term = dot(ones, part, 1, 1)
        total = term if total is None else total + term
    return total


def message_block(ref, block, width):
    at = block * PARTS
    return jnp.concatenate(
        [ref[(at + i) * width : (at + i + 1) * width, :] for i in range(PARTS)], axis=1
    )


def message_tail(ref, block, width):
    tail = ref.shape[0] // (width + 1) * width + block * PARTS
    return jnp.concatenate([ref[tail + i : tail + i + 1, :] for i in range(PARTS)], axis=1)


def received(refs, block, width):
    total = message_block(refs[-1], block, width)
    for ref in refs[-2::-1]:
        total = message_block(ref, block, width) + message_tail(ref, block, width) * total
    return total


def masked_rows(a, mask):
    return jnp.where(mask, a.astype(F32), 0.0).astype(BF16)


def states_kernel(
    lens_ref, alog_ref, dt_ref, x_ref, b_ref, dy_ref, c_ref, fwd_ref, bwd_ref, u_ref, v_ref, l_ref
):
    rows, columns = x_ref.shape[1:]
    heads, width = dt_ref.shape[1], b_ref.shape[2]
    _, offset, first, last = document_places(lens_ref, rows)
    through = jnp.where(first >= offset + rows, 1.0, 0.0)
    dt = dt_ref[0]
    decay = dt * rate_column(alog_ref)
    square = (rows, rows)
    lower = jnp.where(iota(square, 0) >= iota(square, 1), 1.0, 0.0)
    eye = jnp.where(iota(square, 0) == iota(square, 1), 1.0, 0.0)
    logs = dot(lower, decay, 1, 1, HIGHEST)
    steps = dot(eye, dt, 1, 1, HIGHEST)
    u = jnp.concatenate(split3(jnp.exp(logs)), axis=1)
    v = jnp.concatenate(split3(jnp.exp(-logs) * steps), axis=1)
    u_ref[...] = u
    v_ref[...] = v
    l_ref[...] = jnp.concatenate(split3(logs), axis=1)
    place = iota((rows, width), 0) + offset
    b_end = masked_rows(b_ref[0], place >= last)
    c_live = masked_rows(c_ref[0], place < first)
    for block in range(columns // WIDE):
        at = slice(block * WIDE, (block + 1) * WIDE)
        spread = head_block(heads, columns // heads, block, 3)
        u_wide = dot(u, spread, 1, 0)
        v_wide = dot(v, spread, 1, 0)
        x_high, x_low = split2(x_ref[0, :, at].astype(F32) * v_wide)
        y_high, y_low = split2(dy_ref[0, :, at].astype(F32) * u_wide)
        ending = u_wide[rows - 1 : rows, :]
        state = (dot(b_end, x_high, 0, 0) + dot(b_end, x_low, 0, 0)) * ending
        pulled = dot(c_live, y_high, 0, 0) + dot(c_live, y_low, 0, 0)
        kept = ending * through
        for i in range(PARTS):
            one = block * PARTS + i
            part = slice(i * LANES, (i + 1) * LANES)
            tail = columns // LANES * width + one
            fwd_ref[one * width : (one + 1) * width, :] = state[:, part]
            bwd_ref[one * width : (one + 1) * width, :] = pulled[:, part]
            fwd_ref[tail : tail + 1, :] = kept[:, part]
            bwd_ref[tail : tail + 1, :] = kept[:, part]


def inside_kernel(
    lens_ref,
    alog_ref,
    skip_ref,
    dt_ref,
    x_ref,
    b_ref,
    dy_ref,
    c_ref,
    u_ref,
    v_ref,
    l_ref,
    xh_ref,
    xl_ref,
    yh_ref,
    yl_ref,
    v_wide_ref,
    dx_ref,
    db_ref,
    dc_ref,
    dl_ref,
    sums_ref,
    fwd_ref,
    bwd_ref,
    small_ref,
):
    rows, columns = x_ref.shape[1:]
    heads, width = dt_ref.shape[1], b_ref.shape[2]
    starts, offset, first, last = document_places(lens_ref, rows)
    square = (rows, rows)
    place0, place1 = iota(square, 0) + offset, iota(square, 1) + offset
    segment0, segment1 = jnp.zeros(square, jnp.int32), jnp.zeros(square, jnp.int32)
    for start in starts:
        segment0 += jnp.where(place0 >= start, 1, 0)
        segment1 += jnp.where(place1 >= start, 1, 0)
    same = segment0 == segment1
    down = same & (place0 >= place1)
    scores = jnp.where(down, dot(c_ref[0], b_ref[0], 1, 1), 0.0)
    flipped = jnp.where(same & (place1 >= place0), dot(b_ref[0], c_ref[0], 1, 1), 0.0)
    scores, flipped = split2(scores), split2(flipped)
    place = iota((rows, width), 0) + offset
    b_end = masked_rows(b_ref[0], place >= last)
    c_live = masked_rows(c_ref[0], place < first)
    skips = jnp.concatenate(split3(jnp.broadcast_to(skip_ref[...], (16, heads))), axis=1)
    d_scores = jnp.zeros(square, F32)
    dl = jnp.zeros((heads, rows), F32)
    sums = jnp.zeros((heads, rows), F32)
    small = jnp.zeros((heads, 8), F32)
    for block in range(columns // WIDE):
        at = slice(block * WIDE, (block + 1) * WIDE)
        spread = head_block(heads, columns // heads, block, 3)
        ones = spread[:heads]
        u_wide = dot(u_ref[...], spread, 1, 0)
        v_wide = dot(v_ref[...], spread, 1, 0)
        l_wide = dot(l_ref[...], spread, 1, 0)
        skip_wide = dot(skips, spread, 1, 0)[:1]
        x = x_ref[0, :, at].astype(F32)
        dy = dy_ref[0, :, at].astype(F32)
        xv = x * v_wide
        yu = dy * u_wide
        xs, ys = split2(xv), split2(yu)
        xh_ref[:, at], xl_ref[:, at] = xs
        yh_ref[:, at], yl_ref[:, at] = ys
        v_wide_ref[:, at] = v_wide
        out = dot_pairs(scores, xs, 1, 0)
        back = dot_pairs(flipped, ys, 1, 0)
        d_scores += dot_pairs(ys, xs, 1, 1)
        dx_ref[:, at] = v_wide * back + skip_wide * dy
        column_part = xv * back
        dl += head_sums(ones, yu * out - column_part)
        sums += head_sums(ones, column_part)
        small += head_sums(
            ones, jnp.broadcast_to(jnp.sum(x * dy, axis=0, keepdims=True), (8, WIDE))
        )
        ending = u_wide[rows - 1 : rows, :]
        end_log = l_wide[rows - 1 : rows, :]
        fwd_ref[:, at] = sum(dot(b_end, p, 0, 0) for p in split2(xv * (end_log - l_wide))) * ending
        bwd_ref[:, at] = sum(dot(c_live, p, 0, 0) for p in split2(yu * l_wide))
    d_scores = split2(jnp.where(down, d_scores, 0.0))
    dc_ref[...] = sum(dot(p, b_ref[0], 1, 0) for p in d_scores)
    db_ref[...] = sum(dot(p, c_ref[0], 0, 0) for p in d_scores)
    dl_ref[...] = dl
    sums_ref[...] = sums
    decay = dt_ref[0] * rate_column(alog_ref)
    lower = jnp.where(iota(square, 0) <= iota(square, 1), 1.0, 0.0)
    logs = dot(decay, lower, 1, 0, HIGHEST)
    rate_grad = jnp.sum(logs * dl, axis=1, keepdims=True)
    lane = iota((heads, LANES), 1)
    small_ref[...] = jnp.where(lane == 0, rate_grad, jnp.where(lane == 1, small[:, :1], 0.0))


def rates_kernel(reach, *refs):
    fwds, bwds = refs[:reach], refs[reach : 2 * reach]
    own_ref, u_ref, l_ref, fwd_ref, bwd_ref, small_ref, out_ref = refs[2 * reach :]
    width, columns = fwd_ref.shape
    heads = small_ref.shape[0]
    rows = u_ref.shape[0]
    total = jnp.zeros((heads, 8), F32)
    for block in range(columns // WIDE):
        at = slice(block * WIDE, (block + 1) * WIDE)
        spread = head_block(heads, columns // heads, block, 3)
        end_log = dot(l_ref[rows - 16 : rows, :], spread, 1, 0)[15:16]
        came = received(fwds, block, width)
        pull = received(bwds, block, width)
        kept = message_tail(own_ref, block, width) * end_log
        terms = came * bwd_ref[:, at] + pull * (fwd_ref[:, at] + kept * came)
        whole = jnp.sum(terms, axis=0, keepdims=True)
        total += head_sums(spread[:heads], jnp.broadcast_to(whole, (8, WIDE)))
    lane = iota((heads, LANES), 1)
    small = small_ref[...]
    small = small + jnp.where(lane == 0, total[:, :1], 0.0)
    shape = (heads, LANES)
    pick = iota(shape, 0) == lane
    shifted = iota(shape, 0) + heads == lane
    rate = jnp.sum(jnp.where(pick, small[:, 0:1], 0.0), axis=0, keepdims=True)
    skip = jnp.sum(jnp.where(shifted, small[:, 1:2], 0.0), axis=0, keepdims=True)
    out_ref[...] = rate + skip


def outputs_kernel(reach, *refs):
    fwds, bwds = refs[:reach], refs[reach : 2 * reach]
    (
        lens_ref,
        alog_ref,
        dt_ref,
        own_ref,
        b_ref,
        c_ref,
        u_ref,
        xh_ref,
        xl_ref,
        yh_ref,
        yl_ref,
        v_wide_ref,
        dx_ref,
        db_ref,
        dc_ref,
        dl_ref,
        sums_ref,
        dx_out,
        db_out,
        dc_out,
        dt_out,
    ) = refs[2 * reach :]
    rows, columns = dx_ref.shape
    heads, width = dt_ref.shape[1], b_ref.shape[2]
    _, offset, first, last = document_places(lens_ref, rows)
    place = iota((rows, width), 0) + offset
    ends, lives = place >= last, place < first
    b_end = masked_rows(b_ref[0], ends)
    c_live = masked_rows(c_ref[0], lives)
    dl = dl_ref[...]
    cross = jnp.zeros((heads, rows), F32)
    corner = jnp.zeros((heads, 8), F32)
    dc = jnp.zeros((rows, width), F32)
    db = jnp.zeros((rows, width), F32)
    for block in range(columns // WIDE):
        at = slice(block * WIDE, (block + 1) * WIDE)
        spread = head_block(heads, columns // heads, block, 3)
        ones = spread[:heads]
        ending = dot(u_ref[rows - 16 : rows, :], spread, 1, 0)[15:16]
        came = received(fwds, block, width)
        pull = received(bwds, block, width)
        kept = message_tail(own_ref, block, width)
        meet = jnp.sum(came * pull, axis=0, keepdims=True) * kept
        corner += head_sums(ones, jnp.broadcast_to(meet, (8, WIDE)))
        cames, pulls = split2(came), split2(pull * ending)
        xs = xh_ref[:, at], xl_ref[:, at]
        ys = yh_ref[:, at], yl_ref[:, at]
        out = sum(dot(c_live, p, 1, 0) for p in cames)
        back = sum(dot(b_end, p, 1, 0) for p in pulls)
        column_part = (xs[0].astype(F32) + xs[1].astype(F32)) * back
        row_part = (ys[0].astype(F32) + ys[1].astype(F32)) * out
        dl += head_sums(ones, row_part - column_part)
        cross += head_sums(ones, column_part)
        dc += dot_pairs(ys, cames, 1, 1)
        db += dot_pairs(xs, pulls, 1, 1)
        dx_out[0, :, at] = (dx_ref[:, at] + v_wide_ref[:, at] * back).astype(BF16)
    dc_out[0] = (dc_ref[...] + jnp.where(lives, dc, 0.0)).astype(BF16)
    db_out[0] = (db_ref[...] + jnp.where(ends, db, 0.0)).astype(BF16)
    square = (rows, rows)
    upper = jnp.where(iota(square, 0) >= iota(square, 1), 1.0, 0.0)
    at_end = jnp.sum(cross, axis=1, keepdims=True) + corner[:, :1]
    d_decay = dot(dl, upper, 1, 0, HIGHEST) + at_end
    dt_out[0] = (sums_ref[...] + cross) / dt_ref[0] + rate_column(alog_ref) * d_decay


def call(kernel, outs, kinds, flops, moved):
    specs = [
        pl.BlockSpec(memory_space=pltpu.SMEM if kind else pltpu.VMEM) for kind in kinds
    ]
    return pl.pallas_call(
        kernel,
        out_shape=[jax.ShapeDtypeStruct(*out) for out in outs],
        in_specs=specs,
        out_specs=[pl.BlockSpec(memory_space=pltpu.VMEM)] * len(outs),
        compiler_params=pltpu.CompilerParams(vmem_limit_bytes=VMEM_LIMIT),
        cost_estimate=pl.CostEstimate(flops=flops, bytes_accessed=moved, transcendentals=0),
    )


def shift(a, axis, by):
    count = lax.axis_size(axis)
    pairs = [(i, i + by) for i in range(count) if 0 <= i + by < count]
    return lax.ppermute(a, axis, pairs)


def sum_over(a, axis):
    count = lax.axis_size(axis)
    parts = [a] + [
        lax.ppermute(a, axis, [(i, i ^ other) for i in range(count)]) for other in range(1, count)
    ]
    while len(parts) > 1:
        parts = [parts[i] + parts[i + 1] for i in range(0, len(parts), 2)]
    return parts[0]


def per_device(inputs, b_proj, c_proj, step_sizes, a_log, skip_gain, doc_lengths, grad_out):
    rows, columns = inputs.shape[1:]
    heads, width = a_log.shape[0], b_proj.shape[2]
    reach = max(lax.axis_size("ctx") // 4, 1)
    alog, skip = a_log[None], skip_gain[None]
    message = ((columns // LANES * (width + 1), LANES), F32)
    table = ((rows, 3 * heads), BF16)
    state = ((width, columns), F32)
    wide16, wide32 = ((rows, columns), BF16), ((rows, columns), F32)
    narrow = ((rows, width), F32)
    per_head = ((heads, rows), F32)
    small = ((heads, LANES), F32)

    fwd, bwd, u, v, logs = call(
        states_kernel, [message, message, table, table, table], [1] + [0] * 6, 10**9, 4 * 2**20
    )(doc_lengths, alog, step_sizes, inputs, b_proj, grad_out, c_proj)
    fwds = [shift(fwd, "ctx", by) for by in range(1, reach + 1)]
    bwds = [shift(bwd, "ctx", -by) for by in range(1, reach + 1)]
    xh, xl, yh, yl, v_wide, dx, db, dc, dl, sums, fwd_logs, bwd_logs, parts = call(
        inside_kernel,
        [wide16] * 4 + [wide32] * 2 + [narrow] * 2 + [per_head] * 2 + [state] * 2 + [small],
        [1] + [0] * 10,
        4 * 10**9,
        12 * 2**20,
    )(doc_lengths, alog, skip, step_sizes, inputs, b_proj, grad_out, c_proj, u, v, logs)
    (partial,) = call(
        functools.partial(rates_kernel, reach),
        [((1, LANES), F32)],
        [0] * (2 * reach + 6),
        10**8,
        4 * 2**20,
    )(*fwds, *bwds, fwd, u, logs, fwd_logs, bwd_logs, parts)
    totals = sum_over(sum_over(partial[0], "dp"), "ctx")
    input_grads, b_gradient, c_gradient, step_grads = call(
        functools.partial(outputs_kernel, reach),
        [
            ((1, rows, columns), BF16),
            ((1, rows, width), BF16),
            ((1, rows, width), BF16),
            ((1, heads, rows), F32),
        ],
        [0] * (2 * reach) + [1] + [0] * 16,
        2 * 10**9,
        12 * 2**20,
    )(
        *fwds,
        *bwds,
        doc_lengths,
        alog,
        step_sizes,
        fwd,
        b_proj,
        c_proj,
        u,
        xh,
        xl,
        yh,
        yl,
        v_wide,
        dx,
        db,
        dc,
        dl,
        sums,
    )
    return (
        input_grads,
        b_gradient,
        c_gradient,
        step_grads,
        totals[:heads],
        totals[heads : 2 * heads],
    )


def solution(mesh):
    in_specs = (
        P("dp", "ctx", None),
        P("dp", "ctx", None),
        P("dp", "ctx", None),
        P("dp", None, "ctx"),
        P(),
        P(),
        P("dp", None),
        P("dp", "ctx", None),
    )
    out_specs = (
        P("dp", "ctx", None),
        P("dp", "ctx", None),
        P("dp", "ctx", None),
        P("dp", None, "ctx"),
        P(),
        P(),
    )
    return jax.shard_map(
        per_device, mesh=mesh, in_specs=in_specs, out_specs=out_specs, check_vma=False
    )
```

time: 359 us -> 68.6 us (0.19)
  waiting for transfers between devices: 211 us -> 17.3 us
  blocking collectives: 62 us -> 0 us
  other arithmetic: 38.8 us -> 0.02 us
  starting transfers between devices: 0.08 us -> 26.6 us
  matrix products: 22.6 us -> 0 us
  Pallas kernels: 0 us -> 17.1 us
  between operations: 16.3 us -> 0.78 us
    all_gather x2 -> x0, waiting for transfers between devices: 211 us -> none  [prefix_2(): everything = jax.tree.map(lambda part: lax.all_gather(part, axis), x)]
    psum x1 -> x0, blocking collectives: 38.3 us -> none  [per_device(): totals = lax.psum((rate_grad, local_grads[5]), ('dp', 'ctx'))]
    ppermute x0 -> x14, starting transfers between devices: none -> 26.6 us  [the longest x10 13.9 us: sum_over(): lax.ppermute(a, axis, [(i, i ^ other) for i in range(count)])]
    unnamed x1 -> x0, blocking collectives: 23.7 us -> none
    select_n x16 -> x0, other arithmetic: 23.6 us -> none  [step(): return jax.tree.map(lambda a, b: jnp.where(reached, a, b), new, before)]
    dot_general x11 -> x0, matrix products: 22.6 us -> none  [the longest x2 9.49 us: intra_group(): return jnp.einsum('hts,shp->thp', weights, values, precision=highest)]
    ppermute x0 -> x14, waiting for transfers between devices: none -> 17.3 us  [the longest x4 14.8 us: shift(): return lax.ppermute(a, axis, pairs)]
    pallas_call x0 -> x4, Pallas kernels: none -> 17.1 us  [the longest x1 6.69 us: per_device(): call(inside_kernel, [wide16] * 4 + [wide32] * 2 + [narrow] * 2 + [per_hea...]
  transfers between devices with their start and end apart: 2 -> 14, of which waited for: 2 -> 4; matrix products, arithmetic and copies ran while one was open for 5% -> 2% of each run, Pallas kernels for 0% -> 19%
where the time goes in v1:
time: 68.6 us; the launch traced here: 68.2 us
  starting transfers between devices  26.6 us (39%)
  waiting for transfers between devices  17.3 us (25%)
  Pallas kernels  17.1 us (25%)
  local copies, waits for them, and re-layouts  6.32 us (9%)
  between operations  0.78 us (1%)
    ppermute x4, waiting for transfers between devices, shift(): return lax.ppermute(a, axis, pairs)  14.8 us
    ppermute x10, starting transfers between devices, sum_over(): lax.ppermute(a, axis, [(i, i ^ other) for i in range(count)])  13.9 us
    ppermute x4, starting transfers between devices, shift(): return lax.ppermute(a, axis, pairs)  12.8 us
    pallas_call x1, Pallas kernels, per_device(): call(inside_kernel, [wide16] * 4 + [wide32] * 2 + [narrow] * 2 + [per_hea...  6.69 us
    pallas_call x1, Pallas kernels, per_device(): call(functools.partial(outputs_kernel, reach), [((1, rows, columns), BF16...  6.57 us
    unnamed x18, local copies, waits for them, and re-layouts  5.74 us
    pallas_call x1, Pallas kernels, per_device(): call(states_kernel, [message, message, table, table, table], [1] + [0] *...  2.74 us
    ppermute x10, waiting for transfers between devices, sum_over(): lax.ppermute(a, axis, [(i, i ^ other) for i in range(count)])  2.51 us
  transfers between devices with their start and end apart: 14, of which 4 were waited for; matrix products, arithmetic and copies ran while one was open for 2% of the time, Pallas kernels for 19%

profile of v1, /device:TPU:0, one launch (start us, length us, event | category | flops | bytes accessed | tf_op | source)
XLA Modules:
  0.0 68.2 jit_solution(8520964678236981963)
XLA Ops:
  0.6 0.8 %copy.14.b_ref.refs_8_ = bf16[1,128,64]{2,1,0:T(8,128)(2,1)S(1)} copy(bf16[1,128,64]{1,2,0:T(8,128)(2,1)} %param.9) | data formatting | bytes 32768 | tf_op args[1]
  1.6 0.6 copy-done.2
  2.3 1.0 %copy-done = bf16[1,128,2048]{2,1,0:T(8,128)(2,1)S(1)} copy-done((bf16[1,128,2048]{2,1,0:T(8,128)(2,1)S(1)}, bf16[1,128,2048]{2,1,0:T(8,128)(2,1)}, u32[]{:S(2)}) %copy-start) | copy-done | bytes 524312
  3.3 1.0 %copy-done.1 = bf16[1,128,2048]{2,1,0:T(8,128)(2,1)S(1)} copy-done((bf16[1,128,2048]{2,1,0:T(8,128)(2,1)S(1)}, bf16[1,128,2048]{2,1,0:T(8,128)(2,1)}, u32[]{:S(2)}) %copy-start.1) | copy-done | bytes 524312
  4.4 2.7 %shard_map.127 = (f32[1040,128]{1,0:T(8,128)S(1)}, f32[1040,128]{1,0:T(8,128)S(1)}, bf16[128,96]{1,0:T(8,128)(2,1)S(1)}, bf16[128,96]{1,0:T(8,128)(2,1)S(1)}, bf16[128,96]{1,0:T(8,128)(2,1)S(1)}) custom-call(s32[1,16]{1,0:T(1,128)S(1)} %copy-done.4, f32[1,32]{1,0:T(1,128)S(1)} %bitcast.8, f32[1,32,128]{2,1,0:T(8,128)S(1)} %copy-done.2, ...), custom_call_target="tpu_custom_call" | custom-call | flops 1000000000 | bytes 4194304 | tf_op jit(solution)/shard_map/pallas_call | solution.py:377
  7.1 1.3 %collective-permute-start.3 = (f32[1040,128]{1,0:T(8,128)S(1)}, f32[1040,128]{1,0:T(8,128)S(1)}, u32[]{:S(2)}, u32[]{:S(2)}) collective-permute-start(f32[1040,128]{1,0:T(8,128)S(1)} %get-tuple-element.29), channel_id=1, source_target_pairs={{2,0},{3,1},{4,2},{5,3},{6,4},{7,5},{10,8},{11,9},{12,10},{13,11},... | collective-permute-start | bytes 1597448 | tf_op jit(solution)/shard_map/ppermute | solution.py:351
  8.4 1.3 %collective-permute-start.2 = (f32[1040,128]{1,0:T(8,128)S(1)}, f32[1040,128]{1,0:T(8,128)S(1)}, u32[]{:S(2)}, u32[]{:S(2)}) collective-permute-start(f32[1040,128]{1,0:T(8,128)S(1)} %get-tuple-element.29), channel_id=1, source_target_pairs={{1,0},{2,1},{3,2},{4,3},{5,4},{6,5},{7,6},{9,8},{10,9},{11,10},{12... | collective-permute-start | bytes 1597448 | tf_op jit(solution)/shard_map/ppermute | solution.py:351
  9.7 7.0 %collective-permute-start.1 = (f32[1040,128]{1,0:T(8,128)S(1)}, f32[1040,128]{1,0:T(8,128)S(1)}, u32[]{:S(2)}, u32[]{:S(2)}) collective-permute-start(f32[1040,128]{1,0:T(8,128)S(1)} %get-tuple-element.28.refs_7_.refs_4_), channel_id=1, source_target_pairs={{0,2},{1,3},{2,4},{3,5},{4,6},{5,7},{8,10},{9,11},{10,12},{11,13},... | collective-permute-start | bytes 1597448 | tf_op jit(solution)/shard_map/ppermute | solution.py:351
  16.7 3.2 %collective-permute-start = (f32[1040,128]{1,0:T(8,128)S(1)}, f32[1040,128]{1,0:T(8,128)S(1)}, u32[]{:S(2)}, u32[]{:S(2)}) collective-permute-start(f32[1040,128]{1,0:T(8,128)S(1)} %get-tuple-element.28.refs_7_.refs_4_), channel_id=1, source_target_pairs={{0,1},{1,2},{2,3},{3,4},{4,5},{5,6},{6,7},{8,9},{9,10},{10,11},{11... | collective-permute-start | bytes 1597448 | tf_op jit(solution)/shard_map/ppermute | solution.py:351
  19.9 0.6 copy-done.3
  20.6 6.7 %shard_map.128 = (bf16[128,2048]{1,0:T(8,128)(2,1)S(1)}, bf16[128,2048]{1,0:T(8,128)(2,1)S(1)}, bf16[128,2048]{1,0:T(8,128)(2,1)S(1)}, bf16[128,2048]{1,0:T(8,12...) custom-call(s32[1,16]{1,0:T(1,128)S(1)} %copy-done.4, ...), custom_call_target="tpu_custom_call" | custom-call | flops 4000000000 | bytes 12582912 | tf_op jit(solution)/shard_map/pallas_call | solution.py:382
  27.7 14.3 %collective-permute-done.refs_0_ = f32[1040,128]{1,0:T(8,128)S(1)} collective-permute-done((f32[1040,128]{1,0:T(8,128)S(1)}, f32[1040,128]{1,0:T(8,128)S(1)}, u32[]{:S(2)}, u32[]{:S(2)}) %collective-permute-start) | collective-permute-done | bytes 532512 | tf_op jit(solution)/shard_map/ppermute | solution.py:351
  42.1 1.1 %shard_map.130 = f32[1,128]{1,0:T(1,128)S(1)} custom-call(f32[1040,128]{1,0:T(8,128)S(1)} %collective-permute-done.refs_0_, f32[1040,128]{1,0:T(8,128)S(1)} %collective-permute-done.1.refs_1_, f32[1040,128]{1,0:T(8,128)S(1)} %collective-permute-done.2.refs_2_, f32[1040,128]{1,0:T(8,128)S(1)} %collective-permute-done.3.refs_3_, ...), custom_call_target="tpu_custom_call" | custom-call | flops 100000000 | bytes 4194304 | tf_op jit(solution)/shard_map/pallas_call | solution.py:389
  43.2 1.7 %collective-permute-start.5 = (f32[128]{0:T(128)S(1)}, f32[128]{0:T(128)S(1)}, u32[]{:S(2)}, u32[]{:S(2)}) collective-permute-start(f32[128]{0:T(128)S(1)} %bitcast.4), channel_id=1, source_target_pairs={{0,16},{8,24},{16,0},{24,8},{1,17},{9,25},{17,1},{25,9},{2,18},{10... | collective-permute-start | bytes 1544 | tf_op jit(solution)/shard_map/ppermute | solution.py:357
  45.4 1.4 %collective-permute-done.5 = f32[128]{0:T(128)S(1)} collective-permute-done((f32[128]{0:T(128)S(1)}, f32[128]{0:T(128)S(1)}, u32[]{:S(2)}, u32[]{:S(2)}) %collective-permute-start.5) | collective-permute-done | bytes 544 | tf_op jit(solution)/shard_map/ppermute | solution.py:357
  46.8 1.1 %collective-permute-done.6 = f32[128]{0:T(128)S(1)} collective-permute-done((f32[128]{0:T(128)S(1)}, f32[128]{0:T(128)S(1)}, u32[]{:S(2)}, u32[]{:S(2)}) %collective-permute-start.6) | collective-permute-done | bytes 544 | tf_op jit(solution)/shard_map/ppermute | solution.py:357
  48.0 5.7 %collective-permute-start.12 = (f32[128]{0:T(128)S(1)}, f32[128]{0:T(128)S(1)}, u32[]{:S(2)}, u32[]{:S(2)}) collective-permute-start(f32[128]{0:T(128)S(1)} %add_add_fusion.1), channel_id=1, source_target_pairs={{0,6},{1,7},{2,4},{3,5},{4,2},{5,3},{6,0},{7,1},{8,14},{9,15},{10,... | collective-permute-start | bytes 1544 | tf_op jit(solution)/shard_map/ppermute | solution.py:357
  53.7 1.9 %collective-permute-start.10 = (f32[128]{0:T(128)S(1)}, f32[128]{0:T(128)S(1)}, u32[]{:S(2)}, u32[]{:S(2)}) collective-permute-start(f32[128]{0:T(128)S(1)} %add_add_fusion.1), channel_id=1, source_target_pairs={{0,4},{1,5},{2,6},{3,7},{4,0},{5,1},{6,2},{7,3},{8,12},{9,13},{10,... | collective-permute-start | bytes 1544 | tf_op jit(solution)/shard_map/ppermute | solution.py:357
  55.6 1.7 %collective-permute-start.9 = (f32[128]{0:T(128)S(1)}, f32[128]{0:T(128)S(1)}, u32[]{:S(2)}, u32[]{:S(2)}) collective-permute-start(f32[128]{0:T(128)S(1)} %add_add_fusion.1), channel_id=1, source_target_pairs={{0,3},{1,2},{2,1},{3,0},{4,7},{5,6},{6,5},{7,4},{8,11},{9,10},{10,... | collective-permute-start | bytes 1544 | tf_op jit(solution)/shard_map/ppermute | solution.py:357
  57.3 2.3 %collective-permute-start.8 = (f32[128]{0:T(128)S(1)}, f32[128]{0:T(128)S(1)}, u32[]{:S(2)}, u32[]{:S(2)}) collective-permute-start(f32[128]{0:T(128)S(1)} %add_add_fusion.1), channel_id=1, source_target_pairs={{0,2},{1,3},{2,0},{3,1},{4,6},{5,7},{6,4},{7,5},{8,10},{9,11},{10,... | collective-permute-start | bytes 1544 | tf_op jit(solution)/shard_map/ppermute | solution.py:357
  59.6 6.6 %shard_map.129 = (bf16[1,128,2048]{2,1,0:T(8,128)(2,1)}, bf16[1,128,64]{2,1,0:T(8,128)(2,1)S(1)}, bf16[1,128,64]{2,1,0:T(8,128)(2,1)S(1)}, f32[1,32,128]{2,1,0:T(8,128)}) custom-call(f32[1040,128]{1,0:T(8,128)S(1)} %collective-permute-done.refs_0_, f32[1040,128]{1,0:T(8,128)S(1)} %collective-permute-done.1.refs_1_, ...), custom_call_target="tpu_custom_call" | custom-call | flops 2000000000 | bytes 12582912 | tf_op jit(solution)/shard_map/pallas_call | solution.py:397
  66.1 0.7 %copy.20 = bf16[1,128,64]{1,2,0:T(8,128)(2,1)} copy(bf16[1,128,64]{2,1,0:T(8,128)(2,1)S(1)} %get-tuple-element.51) | data formatting | bytes 32768
  66.8 0.7 %copy.21 = bf16[1,128,64]{1,2,0:T(8,128)(2,1)} copy(bf16[1,128,64]{2,1,0:T(8,128)(2,1)S(1)} %get-tuple-element.52) | data formatting | bytes 32768
  67.6 0.6 fusion
  (29 shorter events, 1.3 us)
Async XLA Ops:
  0.6 0.8 %copy-start.6 = (bf16[1,128,64]{1,2,0:T(8,128)(2,1)S(1)}, bf16[1,128,64]{1,2,0:T(8,128)(2,1)}, u32[]{:S(2)}) copy-start(bf16[1,128,64]{1,2,0:T(8,128)(2,1)} %param.10) | copy-start | bytes 49156
  1.5 0.7 %copy-start.2 = (f32[1,32,128]{2,1,0:T(8,128)S(1)}, f32[1,32,128]{2,1,0:T(8,128)}, u32[]{:S(2)}) copy-start(f32[1,32,128]{2,1,0:T(8,128)} %refs_6_.1) | copy-start | bytes 49156
  1.6 0.7 copy-start.4
  1.6 0.7 copy-start.5
  2.3 1.0 %copy-start = (bf16[1,128,2048]{2,1,0:T(8,128)(2,1)S(1)}, bf16[1,128,2048]{2,1,0:T(8,128)(2,1)}, u32[]{:S(2)}) copy-start(bf16[1,128,2048]{2,1,0:T(8,128)(2,1)} %x_ref.3) | copy-start | bytes 1572868
  3.3 1.0 %copy-start.1 = (bf16[1,128,2048]{2,1,0:T(8,128)(2,1)S(1)}, bf16[1,128,2048]{2,1,0:T(8,128)(2,1)}, u32[]{:S(2)}) copy-start(bf16[1,128,2048]{2,1,0:T(8,128)(2,1)} %dy_ref.3) | copy-start | bytes 1572868
  7.1 20.1 %collective-permute-start.3 = (f32[1040,128]{1,0:T(8,128)S(1)}, f32[1040,128]{1,0:T(8,128)S(1)}, u32[]{:S(2)}, u32[]{:S(2)}) collective-permute-start(f32[1040,128]{1,0:T(8,128)S(1)} %get-tuple-element.29), channel_id=1, source_target_pairs={{2,0},{3,1},{4,2},{5,3},{6,4},{7,5},{10,8},{11,9},{12,10},{13,11},... | collective-permute-start | bytes 1597448 | tf_op jit(solution)/shard_map/ppermute | solution.py:351
  8.4 18.8 %collective-permute-start.2 = (f32[1040,128]{1,0:T(8,128)S(1)}, f32[1040,128]{1,0:T(8,128)S(1)}, u32[]{:S(2)}, u32[]{:S(2)}) collective-permute-start(f32[1040,128]{1,0:T(8,128)S(1)} %get-tuple-element.29), channel_id=1, source_target_pairs={{1,0},{2,1},{3,2},{4,3},{5,4},{6,5},{7,6},{9,8},{10,9},{11,10},{12... | collective-permute-start | bytes 1597448 | tf_op jit(solution)/shard_map/ppermute | solution.py:351
  9.7 18.0 %collective-permute-start.1 = (f32[1040,128]{1,0:T(8,128)S(1)}, f32[1040,128]{1,0:T(8,128)S(1)}, u32[]{:S(2)}, u32[]{:S(2)}) collective-permute-start(f32[1040,128]{1,0:T(8,128)S(1)} %get-tuple-element.28.refs_7_.refs_4_), channel_id=1, source_target_pairs={{0,2},{1,3},{2,4},{3,5},{4,6},{5,7},{8,10},{9,11},{10,12},{11,13},... | collective-permute-start | bytes 1597448 | tf_op jit(solution)/shard_map/ppermute | solution.py:351
  16.7 25.3 %collective-permute-start = (f32[1040,128]{1,0:T(8,128)S(1)}, f32[1040,128]{1,0:T(8,128)S(1)}, u32[]{:S(2)}, u32[]{:S(2)}) collective-permute-start(f32[1040,128]{1,0:T(8,128)S(1)} %get-tuple-element.28.refs_7_.refs_4_), channel_id=1, source_target_pairs={{0,1},{1,2},{2,3},{3,4},{4,5},{5,6},{6,7},{8,9},{9,10},{10,11},{11... | collective-permute-start | bytes 1597448 | tf_op jit(solution)/shard_map/ppermute | solution.py:351
  19.9 0.7 copy-start.3
  43.2 3.6 %collective-permute-start.5 = (f32[128]{0:T(128)S(1)}, f32[128]{0:T(128)S(1)}, u32[]{:S(2)}, u32[]{:S(2)}) collective-permute-start(f32[128]{0:T(128)S(1)} %bitcast.4), channel_id=1, source_target_pairs={{0,16},{8,24},{16,0},{24,8},{1,17},{9,25},{17,1},{25,9},{2,18},{10... | collective-permute-start | bytes 1544 | tf_op jit(solution)/shard_map/ppermute | solution.py:357
  44.9 3.0 %collective-permute-start.6 = (f32[128]{0:T(128)S(1)}, f32[128]{0:T(128)S(1)}, u32[]{:S(2)}, u32[]{:S(2)}) collective-permute-start(f32[128]{0:T(128)S(1)} %bitcast.5), channel_id=1, source_target_pairs={{0,24},{8,16},{16,8},{24,0},{1,25},{9,17},{17,9},{25,1},{2,26},{10... | collective-permute-start | bytes 1544 | tf_op jit(solution)/shard_map/ppermute | solution.py:357
  44.9 3.0 %collective-permute-start.4 = (f32[128]{0:T(128)S(1)}, f32[128]{0:T(128)S(1)}, u32[]{:S(2)}, u32[]{:S(2)}) collective-permute-start(f32[128]{0:T(128)S(1)} %bitcast.6), channel_id=1, source_target_pairs={{0,8},{8,0},{16,24},{24,16},{1,9},{9,1},{17,25},{25,17},{2,10},{10... | collective-permute-start | bytes 1544 | tf_op jit(solution)/shard_map/ppermute | solution.py:357
  47.9 9.4 %collective-permute-start.13 = (f32[128]{0:T(128)S(1)}, f32[128]{0:T(128)S(1)}, u32[]{:S(2)}, u32[]{:S(2)}) collective-permute-start(f32[128]{0:T(128)S(1)} %add_add_fusion.1), channel_id=1, source_target_pairs={{0,7},{1,6},{2,5},{3,4},{4,3},{5,2},{6,1},{7,0},{8,15},{9,14},{10,... | collective-permute-start | bytes 1544 | tf_op jit(solution)/shard_map/ppermute | solution.py:357
  48.0 11.6 %collective-permute-start.12 = (f32[128]{0:T(128)S(1)}, f32[128]{0:T(128)S(1)}, u32[]{:S(2)}, u32[]{:S(2)}) collective-permute-start(f32[128]{0:T(128)S(1)} %add_add_fusion.1), channel_id=1, source_target_pairs={{0,6},{1,7},{2,4},{3,5},{4,2},{5,3},{6,0},{7,1},{8,14},{9,15},{10,... | collective-permute-start | bytes 1544 | tf_op jit(solution)/shard_map/ppermute | solution.py:357
  53.7 13.8 %collective-permute-start.11 = (f32[128]{0:T(128)S(1)}, f32[128]{0:T(128)S(1)}, u32[]{:S(2)}, u32[]{:S(2)}) collective-permute-start(f32[128]{0:T(128)S(1)} %add_add_fusion.1), channel_id=1, source_target_pairs={{0,5},{1,4},{2,7},{3,6},{4,1},{5,0},{6,3},{7,2},{8,13},{9,12},{10,... | collective-permute-start | bytes 1544 | tf_op jit(solution)/shard_map/ppermute | solution.py:357
  53.7 13.8 %collective-permute-start.10 = (f32[128]{0:T(128)S(1)}, f32[128]{0:T(128)S(1)}, u32[]{:S(2)}, u32[]{:S(2)}) collective-permute-start(f32[128]{0:T(128)S(1)} %add_add_fusion.1), channel_id=1, source_target_pairs={{0,4},{1,5},{2,6},{3,7},{4,0},{5,1},{6,2},{7,3},{8,12},{9,13},{10,... | collective-permute-start | bytes 1544 | tf_op jit(solution)/shard_map/ppermute | solution.py:357
  55.6 11.9 %collective-permute-start.9 = (f32[128]{0:T(128)S(1)}, f32[128]{0:T(128)S(1)}, u32[]{:S(2)}, u32[]{:S(2)}) collective-permute-start(f32[128]{0:T(128)S(1)} %add_add_fusion.1), channel_id=1, source_target_pairs={{0,3},{1,2},{2,1},{3,0},{4,7},{5,6},{6,5},{7,4},{8,11},{9,10},{10,... | collective-permute-start | bytes 1544 | tf_op jit(solution)/shard_map/ppermute | solution.py:357
  57.3 10.3 %collective-permute-start.8 = (f32[128]{0:T(128)S(1)}, f32[128]{0:T(128)S(1)}, u32[]{:S(2)}, u32[]{:S(2)}) collective-permute-start(f32[128]{0:T(128)S(1)} %add_add_fusion.1), channel_id=1, source_target_pairs={{0,2},{1,3},{2,0},{3,1},{4,6},{5,7},{6,4},{7,5},{8,10},{9,11},{10,... | collective-permute-start | bytes 1544 | tf_op jit(solution)/shard_map/ppermute | solution.py:357
  59.6 8.0 %collective-permute-start.7 = (f32[128]{0:T(128)S(1)}, f32[128]{0:T(128)S(1)}, u32[]{:S(2)}, u32[]{:S(2)}) collective-permute-start(f32[128]{0:T(128)S(1)} %add_add_fusion.1), channel_id=1, source_target_pairs={{0,1},{1,0},{2,3},{3,2},{4,5},{5,4},{6,7},{7,6},{8,9},{9,8},{10,11... | collective-permute-start | bytes 1544 | tf_op jit(solution)/shard_map/ppermute | solution.py:357

commit v2 on v1

v2 whole, which is shorter than its diff:
```python
import functools

import jax
import jax.numpy as jnp
from jax import lax
from jax.experimental import pallas as pl
from jax.experimental.pallas import tpu as pltpu
from jax.sharding import PartitionSpec as P

F32 = jnp.float32
BF16 = jnp.bfloat16
LANES = 128
WIDE = 256
PARTS = WIDE // LANES
FAR = 2**30


def dot(a, b, ca, cb):
    return lax.dot_general(a, b, (((ca,), (cb,)), ((), ())), preferred_element_type=F32)


def iota(shape, dim):
    return lax.broadcasted_iota(jnp.int32, shape, dim)


def split2(a):
    high = a.astype(BF16)
    return high, (a - high.astype(F32)).astype(BF16)


def split3(a):
    high = a.astype(BF16)
    rest = a - high.astype(F32)
    middle = rest.astype(BF16)
    return high, middle, (rest - middle.astype(F32)).astype(BF16)


def dot_pairs(a, b, ca, cb):
    return dot(a[0], b[0], ca, cb) + (dot(a[0], b[1], ca, cb) + dot(a[1], b[0], ca, cb))


def stack(parts, axis):
    return jnp.concatenate(parts, axis=axis)


def document_places(lens_ref, rows):
    offset = lax.axis_index("ctx") * rows
    starts = [jnp.int32(0)]
    for d in range(lens_ref.shape[1] - 1):
        starts.append(starts[-1] + lens_ref[0, d])
    first = jnp.int32(FAR)
    last = jnp.int32(0)
    for start in starts:
        first = jnp.minimum(first, jnp.where(start >= offset, start, FAR))
        last = jnp.maximum(last, jnp.where(start < offset + rows, start, 0))
    return starts, offset, first, last


def rate_column(alog_ref):
    heads = alog_ref.shape[1]
    square = jnp.broadcast_to(alog_ref[...], (heads, heads))
    picked = jnp.where(iota((heads, heads), 0) == iota((heads, heads), 1), square, 0.0)
    return -jnp.exp(jnp.sum(picked, axis=1, keepdims=True))


def log2(size):
    assert size & (size - 1) == 0
    return size.bit_length() - 1


def head_distance(heads, head_width):
    shape = (3 * heads, WIDE)
    return (iota(shape, 0) & (heads - 1)) - lax.shift_right_logical(
        iota(shape, 1), log2(head_width)
    )


def head_rows(distance, head_width, block):
    return jnp.where(distance == block * (WIDE // head_width), 1.0, 0.0).astype(BF16)


def head_columns(heads, head_width, block):
    shape = (WIDE, heads)
    column = lax.shift_right_logical(iota(shape, 0), log2(head_width))
    return jnp.where(iota(shape, 1) - column == block * (WIDE // head_width), 1.0, 0.0).astype(BF16)


def is_odd(distance):
    return lax.rem(lax.div(lax.axis_index("ctx"), distance), 2)


def message_block(ref, block, width):
    at = block * PARTS
    return stack([ref[(at + i) * width : (at + i + 1) * width, :] for i in range(PARTS)], 1)


def message_tail(ref, block, width):
    tail = ref.shape[0] // (width + 1) * width + block * PARTS
    return stack([ref[tail + i : tail + i + 1, :] for i in range(PARTS)], 1)


def received(refs, block, width):
    came = pull = None
    for j in range(len(refs) // 2, 0, -1):
        one, two = refs[2 * j - 2], refs[2 * j - 1]
        a, b = message_block(one, block, width), message_block(two, block, width)
        odd = jnp.broadcast_to(is_odd(j), a.shape) == 1
        near_came, near_pull = jnp.where(odd, a, b), jnp.where(odd, b, a)
        if came is None:
            came, pull = near_came, near_pull
        else:
            a, b = message_tail(one, block, width), message_tail(two, block, width)
            odd = jnp.broadcast_to(is_odd(j), a.shape) == 1
            came = near_came + jnp.where(odd, a, b) * came
            pull = near_pull + jnp.where(odd, b, a) * pull
    return came, pull


def masked(a, mask):
    return jnp.where(mask, a.astype(F32), 0.0).astype(BF16)


def states_kernel(
    reach, lens_ref, alog_ref, dt_hbm, x_hbm, b_hbm, dy_hbm, c_hbm, u_ref, v_ref, l_ref, *refs
):
    dt_ref, x_ref, b_ref, dy_ref, c_ref = refs[:5]
    payloads = refs[5 : 5 + 2 * reach]
    small_sems, sems = refs[5 + 2 * reach :]
    rows, columns = x_ref.shape
    heads, width = dt_ref.shape[0], b_ref.shape[0]
    pieces = sems.shape[1]
    piece = columns // pieces
    small = [
        pltpu.make_async_copy(source.at[0], target, small_sems.at[i])
        for i, (source, target) in enumerate(((dt_hbm, dt_ref), (b_hbm, b_ref), (c_hbm, c_ref)))
    ]
    for copy in small:
        copy.start()
    large = []
    for i in range(pieces):
        at = slice(i * piece, (i + 1) * piece)
        for side, (source, target) in enumerate(((x_hbm, x_ref), (dy_hbm, dy_ref))):
            copy = pltpu.make_async_copy(
                source.at[0, :, at], target.at[:, at], sems.at[side, i]
            )
            copy.start()
            large.append(copy)
    _, offset, first, last = document_places(lens_ref, rows)
    through = jnp.where(first >= offset + rows, 1.0, 0.0)
    rate = rate_column(alog_ref)
    square = (rows, rows)
    lower = jnp.where(iota(square, 0) >= iota(square, 1), 1.0, 0.0).astype(BF16)
    eye = jnp.where(iota(square, 0) == iota(square, 1), 1.0, 0.0).astype(BF16)
    distance = head_distance(heads, columns // heads)
    place = iota((width, rows), 1) + offset
    for copy in small:
        copy.wait()
    dt = dt_ref[...]
    logs = sum(dot(lower, part, 1, 1) for part in split3(dt * rate))
    steps = sum(dot(eye, part, 1, 1) for part in split3(dt))
    u = stack(split3(jnp.exp(logs)), 1)
    v = stack(split3(jnp.exp(-logs) * steps), 1)
    u_ref[...] = u
    v_ref[...] = v
    l_ref[...] = stack(split3(logs), 1)
    both = stack([u, v], 0)
    b_end = masked(b_ref[...], place >= last)
    c_live = masked(c_ref[...], place < first)
    b_end, c_live = stack([b_end, b_end], 1), stack([c_live, c_live], 1)
    for block in range(columns // WIDE):
        if block * WIDE % piece == 0:
            large[block * WIDE // piece * 2].wait()
            large[block * WIDE // piece * 2 + 1].wait()
        at = slice(block * WIDE, (block + 1) * WIDE)
        wide = dot(both, head_rows(distance, columns // heads, block), 1, 0)
        u_wide, v_wide = wide[:rows], wide[rows:]
        ending = u_wide[rows - 1 : rows, :]
        state = dot(b_end, stack(split2(x_ref[:, at].astype(F32) * v_wide), 0), 1, 0) * ending
        pulled = dot(c_live, stack(split2(dy_ref[:, at].astype(F32) * u_wide), 0), 1, 0)
        kept = ending * through
        for j in range(1, reach + 1):
            odd = jnp.broadcast_to(is_odd(j), state.shape) == 1
            for ref, value in zip(
                payloads[2 * j - 2 : 2 * j],
                (jnp.where(odd, pulled, state), jnp.where(odd, state, pulled)),
            ):
                for i in range(PARTS):
                    one = block * PARTS + i
                    part = slice(i * LANES, (i + 1) * LANES)
                    tail = columns // LANES * width + one
                    ref[one * width : (one + 1) * width, :] = value[:, part]
                    ref[tail : tail + 1, :] = kept[:, part]


def inside_kernel(
    lens_ref,
    alog_ref,
    skip_ref,
    dt_ref,
    x_ref,
    b_ref,
    dy_ref,
    c_ref,
    u_ref,
    v_ref,
    l_ref,
    xs_ref,
    ys_ref,
    v_wide_ref,
    dx_ref,
    b_end_ref,
    c_live_ref,
    db_ref,
    dc_ref,
    sums_ref,
    fwd_ref,
    bwd_ref,
    ends_ref,
    small_ref,
):
    rows, columns = x_ref.shape
    heads, width = dt_ref.shape[0], b_ref.shape[0]
    head_width = columns // heads
    starts, offset, first, last = document_places(lens_ref, rows)
    through = jnp.where(first >= offset + rows, 1.0, 0.0)
    square = (rows, rows)
    place0, place1 = iota(square, 0) + offset, iota(square, 1) + offset
    segment0, segment1 = jnp.zeros(square, jnp.int32), jnp.zeros(square, jnp.int32)
    for start in starts:
        segment0 += jnp.where(place0 >= start, 1, 0)
        segment1 += jnp.where(place1 >= start, 1, 0)
    same = segment0 == segment1
    down = same & (place0 >= place1)
    bt, ct = b_ref[...], c_ref[...]
    scores = split2(jnp.where(down, dot(ct, bt, 0, 0), 0.0))
    flipped = split2(jnp.where(same & (place1 >= place0), dot(bt, ct, 0, 0), 0.0))
    place = iota((width, rows), 1) + offset
    bt_end = masked(bt, place >= last)
    ct_live = masked(ct, place < first)
    b_end = jnp.transpose(bt_end.astype(F32)).astype(BF16)
    c_live = jnp.transpose(ct_live.astype(F32)).astype(BF16)
    b_end_ref[...] = stack([b_end, b_end], 1)
    c_live_ref[...] = stack([c_live, c_live], 1)
    bt_end, ct_live = stack([bt_end, bt_end], 1), stack([ct_live, ct_live], 1)
    skips = stack(split3(jnp.broadcast_to(skip_ref[...], (16, heads))), 1)
    tables = stack([u_ref[...], v_ref[...], l_ref[...], skips], 0)
    distance = head_distance(heads, head_width)
    d_scores = jnp.zeros(square, F32)
    sums = jnp.zeros((2 * rows, heads), F32)
    products = jnp.zeros((8, heads), F32)
    for block in range(columns // WIDE):
        at = slice(block * WIDE, (block + 1) * WIDE)
        wide = dot(tables, head_rows(distance, head_width, block), 1, 0)
        ones = head_columns(heads, head_width, block)
        u_wide, v_wide, l_wide = wide[:rows], wide[rows : 2 * rows], wide[2 * rows : 3 * rows]
        skip_wide = wide[3 * rows : 3 * rows + 1]
        x = x_ref[:, at].astype(F32)
        dy = dy_ref[:, at].astype(F32)
        xv = x * v_wide
        yu = dy * u_wide
        xs, ys = split2(xv), split2(yu)
        xs_ref[:, at] = stack(xs, 0)
        ys_ref[:, at] = stack(ys, 0)
        v_wide_ref[:, at] = v_wide
        out = dot_pairs(scores, xs, 1, 0)
        back = dot_pairs(flipped, ys, 1, 0)
        d_scores += dot_pairs(ys, xs, 1, 1)
        dx_ref[:, at] = v_wide * back + skip_wide * dy
        column_part = xv * back
        for part in split3(stack([yu * out - column_part, column_part], 0)):
            sums += dot(part, ones, 1, 0)
        product = jnp.broadcast_to(jnp.sum(x * dy, axis=0, keepdims=True), (8, WIDE))
        for part in split3(product):
            products += dot(part, ones, 1, 0)
        ending = u_wide[rows - 1 : rows]
        end_log = l_wide[rows - 1 : rows]
        fwd_ref[:, at] = (
            dot(bt_end, stack(split2(xv * (end_log - l_wide)), 0), 1, 0) * ending
        )
        bwd_ref[:, at] = dot(ct_live, stack(split2(yu * l_wide), 0), 1, 0)
        ends_ref[0:1, at] = ending
        ends_ref[1:2, at] = ending * through
        ends_ref[2:3, at] = ending * through * end_log
    d_scores = split2(jnp.where(down, d_scores, 0.0))
    dc_ref[...] = sum(dot(bt, p, 1, 1) for p in d_scores)
    db_ref[...] = sum(dot(ct, p, 1, 0) for p in d_scores)
    sums_ref[...] = sums
    logs = l_ref[...].astype(F32)
    logs = (logs[:, :heads] + logs[:, heads : 2 * heads]) + logs[:, 2 * heads :]
    rate_grads = jnp.sum(logs * sums[:rows], axis=0, keepdims=True)
    empty = jnp.zeros((1, LANES - 2 * heads), F32)
    small_ref[...] = stack([rate_grads, products[:1], empty], 1)


def rates_kernel(reach, head_width, *refs):
    messages = refs[: 2 * reach]
    ends_ref, fwd_ref, bwd_ref, small_ref, out_ref = refs[2 * reach :]
    width, columns = fwd_ref.shape
    blocks = columns // WIDE
    whole = []
    for block in range(blocks):
        at = slice(block * WIDE, (block + 1) * WIDE)
        came, pull = received(messages, block, width)
        terms = came * bwd_ref[:, at] + pull * (fwd_ref[:, at] + ends_ref[2:3, at] * came)
        whole.append(jnp.sum(terms, axis=0, keepdims=True))
    whole = stack(whole, 0)
    own = WIDE // (head_width)
    shape = (WIDE, LANES)
    column = lax.shift_right_logical(iota(shape, 0), log2(head_width))
    ones = jnp.where(column == (iota(shape, 1) & (own - 1)), 1.0, 0.0).astype(BF16)
    sums = sum(dot(part, ones, 1, 0) for part in split3(whole))
    lane = iota(sums.shape, 1)
    mine = lax.shift_right_logical(lane, log2(own)) == iota(sums.shape, 0)
    total = small_ref[...] + jnp.sum(jnp.where(mine, sums, 0.0), axis=0, keepdims=True)
    out_ref[...] = jnp.broadcast_to(total, out_ref.shape)


def outputs_kernel(reach, *refs):
    messages = refs[: 2 * reach]
    (
        alog_ref,
        lens_ref,
        dt_ref,
        ends_ref,
        xs_ref,
        ys_ref,
        v_wide_ref,
        dx_ref,
        b_end_ref,
        c_live_ref,
        db_ref,
        dc_ref,
        sums_ref,
        dx_out,
        db_out,
        dc_out,
        dt_out,
    ) = refs[2 * reach :]
    rows, columns = dx_ref.shape
    heads, width = dt_ref.shape[0], db_ref.shape[0]
    head_width = columns // heads
    _, offset, first, last = document_places(lens_ref, rows)
    b_end, c_live = b_end_ref[...], c_live_ref[...]
    sums = sums_ref[...]
    own_sums = sums[rows:]
    dc = jnp.zeros((2 * width, 2 * rows), F32)
    db = jnp.zeros((2 * width, 2 * rows), F32)
    at_last = iota((rows, WIDE), 0) == rows - 1
    for block in range(columns // WIDE):
        at = slice(block * WIDE, (block + 1) * WIDE)
        ones = head_columns(heads, head_width, block)
        came, pull = received(messages, block, width)
        meet = jnp.sum(came * pull, axis=0, keepdims=True) * ends_ref[1:2, at]
        cames = stack(split2(came), 0)
        pulls = stack(split2(pull * ends_ref[0:1, at]), 0)
        xs, ys = xs_ref[:, at], ys_ref[:, at]
        out = dot(c_live, cames, 1, 0)
        back = dot(b_end, pulls, 1, 0)
        column_part = (xs[:rows].astype(F32) + xs[rows:].astype(F32)) * back
        row_part = (ys[:rows].astype(F32) + ys[rows:].astype(F32)) * out
        row_part = jnp.where(at_last, row_part + meet, row_part)
        for part in split2(stack([row_part - column_part, column_part], 0)):
            sums += dot(part, ones, 1, 0)
        dc += dot(cames, ys, 1, 1)
        db += dot(pulls, xs, 1, 1)
        dx_out[0, :, at] = (dx_ref[:, at] + v_wide_ref[:, at] * back).astype(BF16)
    place = iota((width, rows), 1) + offset
    dc = (dc[:width, :rows] + dc[:width, rows:]) + dc[width:, :rows]
    db = (db[:width, :rows] + db[:width, rows:]) + db[width:, :rows]
    dc_out[0] = (dc_ref[...] + jnp.where(place < first, dc, 0.0)).astype(BF16)
    db_out[0] = (db_ref[...] + jnp.where(place >= last, db, 0.0)).astype(BF16)
    square = (rows, rows)
    upper = jnp.where(iota(square, 0) >= iota(square, 1), 1.0, 0.0).astype(BF16)
    eye = jnp.where(iota(square, 0) == iota(square, 1), 1.0, 0.0).astype(BF16)
    at_end = jnp.sum(sums[rows:] - own_sums, axis=0, keepdims=True)
    dl = sums[:rows] + jnp.where(iota((rows, heads), 0) == rows - 1, at_end, 0.0)
    d_decay = sum(dot(part, upper, 0, 0) for part in split3(dl))
    total = sum(dot(part, eye, 0, 0) for part in split3(sums[rows:]))
    dt_out[0] = total / dt_ref[...] + rate_column(alog_ref) * d_decay


def call(kernel, reach, outs, kinds, flops, moved, scratch=()):
    spaces = {"s": pltpu.SMEM, "v": pltpu.VMEM, "h": pltpu.HBM}
    return pl.pallas_call(
        kernel,
        out_shape=[jax.ShapeDtypeStruct(*out) for out in outs],
        in_specs=[pl.BlockSpec(memory_space=spaces[kind]) for kind in kinds],
        out_specs=[pl.BlockSpec(memory_space=pltpu.VMEM)] * len(outs),
        scratch_shapes=scratch,
        compiler_params=pltpu.CompilerParams(
            vmem_limit_bytes=min(14 + 2 * reach, 56) * 2**20
        ),
        cost_estimate=pl.CostEstimate(flops=flops, bytes_accessed=moved, transcendentals=0),
    )


def swap(a, by, second):
    count = lax.axis_size("ctx")
    pairs = []
    for i in range(count - by):
        if i // by % 2 == second:
            pairs += [(i, i + by), (i + by, i)]
    return lax.ppermute(a, "ctx", pairs)


def per_device(inputs, b_proj, c_proj, step_sizes, a_log, skip_gain, doc_lengths, grad_out):
    rows, columns = inputs.shape[1:]
    heads, width = a_log.shape[0], b_proj.shape[2]
    reach = max(lax.axis_size("ctx") // 4, 1)
    devices = lax.axis_size("ctx") * lax.axis_size("dp")
    alog, skip = a_log[None], skip_gain[None]
    bt, ct = jnp.swapaxes(b_proj, 1, 2), jnp.swapaxes(c_proj, 1, 2)
    message = ((columns // LANES * (width + 1), LANES), F32)
    table = ((rows, 3 * heads), BF16)
    state = ((width, columns), F32)
    wide = ((rows, columns), F32)
    doubled = ((2 * rows, columns), BF16)
    half = ((rows, columns), BF16)
    transposed = ((width, rows), F32)
    pieces = 4

    u, v, logs, dt, x, b, dy, c, *payloads = call(
        functools.partial(states_kernel, reach),
        reach,
        [table] * 3
        + [((heads, rows), F32), half, ((width, rows), BF16), half, ((width, rows), BF16)]
        + [message] * (2 * reach),
        "svhhhhh",
        10**9,
        4 * 2**20,
        [pltpu.SemaphoreType.DMA((3,)), pltpu.SemaphoreType.DMA((2, pieces))],
    )(
        doc_lengths,
        alog,
        *(
            pltpu.with_memory_space_constraint(a, pltpu.HBM)
            for a in (step_sizes, inputs, bt, grad_out, ct)
        ),
    )
    messages = [None] * (2 * reach)
    for j in range(reach, 0, -1):
        for second in (1, 0):
            at = 2 * j - 2 + second
            messages[at] = swap(payloads[at], j, second)
    xs, ys, v_wide, dx, b_end, c_live, db, dc, sums, fwd_logs, bwd_logs, ends, small = call(
        inside_kernel,
        reach,
        [doubled, doubled, wide, wide]
        + [((rows, 2 * width), BF16)] * 2
        + [transposed] * 2
        + [((2 * rows, heads), F32), state, state, ((8, columns), F32), ((1, LANES), F32)],
        "s" + "v" * 10,
        4 * 10**9,
        12 * 2**20,
    )(doc_lengths, alog, skip, dt, x, b, dy, c, u, v, logs)
    (partial,) = call(
        functools.partial(rates_kernel, reach, columns // heads),
        reach,
        [((devices, LANES), F32)],
        "v" * (2 * reach + 4),
        10**8,
        4 * 2**20,
    )(*messages, ends, fwd_logs, bwd_logs, small)
    gathered = lax.all_to_all(partial, ("dp", "ctx"), 0, 0, tiled=True)
    totals = jnp.sum(gathered, axis=0)
    input_grads, b_gradient, c_gradient, step_grads = call(
        functools.partial(outputs_kernel, reach),
        reach,
        [
            ((1, rows, columns), BF16),
            ((1, width, rows), BF16),
            ((1, width, rows), BF16),
            ((1, heads, rows), F32),
        ],
        "v" * (2 * reach) + "vs" + "v" * 11,
        2 * 10**9,
        12 * 2**20,
    )(
        *messages,
        alog,
        doc_lengths,
        dt,
        ends,
        xs,
        ys,
        v_wide,
        dx,
        b_end,
        c_live,
        db,
        dc,
        sums,
    )
    return (
        input_grads,
        jnp.swapaxes(b_gradient, 1, 2),
        jnp.swapaxes(c_gradient, 1, 2),
        step_grads,
        totals[:heads],
        totals[heads : 2 * heads],
    )


def solution(mesh):
    in_specs = (
        P("dp", "ctx", None),
        P("dp", "ctx", None),
        P("dp", "ctx", None),
        P("dp", None, "ctx"),
        P(),
        P(),
        P("dp", None),
        P("dp", "ctx", None),
    )
    out_specs = (
        P("dp", "ctx", None),
        P("dp", "ctx", None),
        P("dp", "ctx", None),
        P("dp", None, "ctx"),
        P(),
        P(),
    )
    return jax.shard_map(
        per_device, mesh=mesh, in_specs=in_specs, out_specs=out_specs, check_vma=False
    )
```

time: 68.6 us -> 50.4 us (0.73)
  starting transfers between devices: 26.6 us -> 13.2 us
  Pallas kernels: 17.1 us -> 14.5 us
  waiting for transfers between devices: 17.3 us -> 15 us
    ppermute x14 -> x4, starting transfers between devices: 26.6 us -> 7.27 us  [swap(): return lax.ppermute(a, 'ctx', pairs)]
    all_to_all x0 -> x1, starting transfers between devices: none -> 5.95 us  [per_device(): gathered = lax.all_to_all(partial, ('dp', 'ctx'), 0, 0, tiled=True)]
    pallas_call x4, Pallas kernels: 17.1 us -> 14.5 us  [the longest x1 5.83 us: per_device(): call(inside_kernel, reach, [doubled, doubled, wide, wide] + [((rows, 2 *...]
    ppermute x14 -> x4, waiting for transfers between devices: 17.3 us -> 15 us  [swap(): return lax.ppermute(a, 'ctx', pairs)]
  transfers between devices with their start and end apart: 14 -> 5, of which waited for: 4 -> 2; matrix products, arithmetic and copies ran while one was open for 2% -> 0% of each run, Pallas kernels for 19% -> 19%
where the time goes in v2:
time: 50.4 us; the launch traced here: 50.1 us
  waiting for transfers between devices  15 us (30%)
  Pallas kernels  14.5 us (29%)
  starting transfers between devices  13.2 us (26%)
  local copies, waits for them, and re-layouts  6.54 us (13%)
  between operations  0.71 us (1%)
    ppermute x4, waiting for transfers between devices, swap(): return lax.ppermute(a, 'ctx', pairs)  15 us
    ppermute x4, starting transfers between devices, swap(): return lax.ppermute(a, 'ctx', pairs)  7.27 us
    unnamed x18, local copies, waits for them, and re-layouts  5.95 us
    all_to_all x1, starting transfers between devices, per_device(): gathered = lax.all_to_all(partial, ('dp', 'ctx'), 0, 0, tiled=True)  5.95 us
    pallas_call x1, Pallas kernels, per_device(): call(inside_kernel, reach, [doubled, doubled, wide, wide] + [((rows, 2 *...  5.83 us
    pallas_call x1, Pallas kernels, per_device(): call(functools.partial(states_kernel, reach), reach, [table] * 3 + [((hea...  3.98 us
    pallas_call x1, Pallas kernels, per_device(): call(functools.partial(outputs_kernel, reach), reach, [((1, rows, columns...  3.62 us
    pallas_call x1, Pallas kernels, per_device(): call(functools.partial(rates_kernel, reach, columns // heads), reach, [((...  1.1 us
  transfers between devices with their start and end apart: 5, of which 2 were waited for; matrix products, arithmetic and copies ran while one was open for 0% of the time, Pallas kernels for 19%

profile of v2, /device:TPU:0, one launch (start us, length us, event | category | flops | bytes accessed | tf_op | source)
XLA Modules:
  0.0 50.1 jit_solution(6418567367415192191)
XLA Ops:
  0.7 0.6 %copy-done.1 = s32[1,16]{1,0:T(1,128)S(1)} copy-done((s32[1,16]{1,0:T(1,128)S(1)}, s32[1,16]{1,0:T(1,128)}, u32[]{:S(2)}) %copy-start.1) | copy-done | bytes 88
  1.3 0.0 copy-done.2
  1.3 4.0 %shard_map.127 = (bf16[128,96]{1,0:T(8,128)(2,1)S(1)}, bf16[128,96]{1,0:T(8,128)(2,1)S(1)}, bf16[128,96]{1,0:T(8,128)(2,1)S(1)}, f32[32,128]{1,0:T(8,128)S(1)}, ...) custom-call(s32[1,16]{1,0:T(1,128)S(1)} %copy-done.1, ...), custom_call_target="tpu_custom_call" | custom-call | flops 1000000000 | bytes 4194304 | tf_op jit(solution)/shard_map/pallas_call | solution.py:422
  5.3 3.0 %collective-permute-start = (f32[1040,128]{1,0:T(8,128)S(1)}, f32[1040,128]{1,0:T(8,128)S(1)}, u32[]{:S(2)}, u32[]{:S(2)}) collective-permute-start(f32[1040,128]{1,0:T(8,128)S(1)} %get-tuple-element.35), channel_id=1, source_target_pairs={{0,1},{1,0},{2,3},{3,2},{4,5},{5,4},{6,7},{7,6},{8,9},{9,8},{10,11... | collective-permute-start | bytes 1597448 | tf_op jit(solution)/shard_map/ppermute | solution.py:403
  8.3 0.7 %collective-permute-start.1 = (f32[1040,128]{1,0:T(8,128)S(1)}, f32[1040,128]{1,0:T(8,128)S(1)}, u32[]{:S(2)}, u32[]{:S(2)}) collective-permute-start(f32[1040,128]{1,0:T(8,128)S(1)} %get-tuple-element.36), channel_id=1, source_target_pairs={{1,2},{2,1},{3,4},{4,3},{5,6},{6,5},{9,10},{10,9},{11,12},{12,11},... | collective-permute-start | bytes 1597448 | tf_op jit(solution)/shard_map/ppermute | solution.py:403
  9.0 2.9 %collective-permute-start.2 = (f32[1040,128]{1,0:T(8,128)S(1)}, f32[1040,128]{1,0:T(8,128)S(1)}, u32[]{:S(2)}, u32[]{:S(2)}) collective-permute-start(f32[1040,128]{1,0:T(8,128)S(1)} %get-tuple-element.37), channel_id=1, source_target_pairs={{0,2},{2,0},{1,3},{3,1},{4,6},{6,4},{5,7},{7,5},{8,10},{10,8},{9,1... | collective-permute-start | bytes 1597448 | tf_op jit(solution)/shard_map/ppermute | solution.py:403
  11.9 0.7 %collective-permute-start.3 = (f32[1040,128]{1,0:T(8,128)S(1)}, f32[1040,128]{1,0:T(8,128)S(1)}, u32[]{:S(2)}, u32[]{:S(2)}) collective-permute-start(f32[1040,128]{1,0:T(8,128)S(1)} %get-tuple-element.38), channel_id=1, source_target_pairs={{2,4},{4,2},{3,5},{5,3},{10,12},{12,10},{11,13},{13,11},{18,20},{2... | collective-permute-start | bytes 1597448 | tf_op jit(solution)/shard_map/ppermute | solution.py:403
  12.6 0.0 copy-start
  12.6 0.6 %copy-done = f32[32]{0:T(128)S(1)} copy-done((f32[32]{0:T(128)S(1)}, f32[32]{0:T(128)}, u32[]{:S(2)}) %copy-start) | copy-done | bytes 152
  13.2 5.8 %shard_map.128 = (bf16[256,2048]{1,0:T(8,128)(2,1)S(1)}, bf16[256,2048]{1,0:T(8,128)(2,1)S(1)}, f32[128,2048]{1,0:T(8,128)S(1)}, f32[128,2048]{1,0:T(8,128)S(1)}...) custom-call(s32[1,16]{1,0:T(1,128)S(1)} %copy-done.1, ...), custom_call_target="tpu_custom_call" | custom-call | flops 4000000000 | bytes 12582912 | tf_op jit(solution)/shard_map/pallas_call | solution.py:445
  19.1 1.0 %copy-done.5 = f32[128,2048]{1,0:T(8,128)} copy-done((f32[128,2048]{1,0:T(8,128)}, f32[128,2048]{1,0:T(8,128)S(1)}, u32[]{:S(2)}) %copy-start.5) | copy-done | bytes 1048600
  20.0 11.0 %collective-permute-done.refs_0_ = f32[1040,128]{1,0:T(8,128)S(1)} collective-permute-done((f32[1040,128]{1,0:T(8,128)S(1)}, f32[1040,128]{1,0:T(8,128)S(1)}, u32[]{:S(2)}, u32[]{:S(2)}) %collective-permute-start) | collective-permute-done | bytes 532512 | tf_op jit(solution)/shard_map/ppermute | solution.py:403
  31.1 0.0 collective-permute-done.1.refs_1_
  31.1 4.0 %collective-permute-done.2.refs_2_ = f32[1040,128]{1,0:T(8,128)S(1)} collective-permute-done((f32[1040,128]{1,0:T(8,128)S(1)}, f32[1040,128]{1,0:T(8,128)S(1)}, u32[]{:S(2)}, u32[]{:S(2)}) %collective-permute-start.2) | collective-permute-done | bytes 532512 | tf_op jit(solution)/shard_map/ppermute | solution.py:403
  35.1 0.0 collective-permute-done.3.refs_3_
  35.1 1.1 %shard_map.130 = f32[32,128]{1,0:T(8,128)} custom-call(f32[1040,128]{1,0:T(8,128)S(1)} %collective-permute-done.refs_0_, f32[1040,128]{1,0:T(8,128)S(1)} %collective-permute-done.1.refs_1_, f32[1040,128]{1,0:T(8,128)S(1)} %collective-permute-done.2.refs_2_, f32[1040,128]{1,0:T(8,128)S(1)} %collective-permute-done.3.refs_3_, ...), custom_call_target="tpu_custom_call" | custom-call | flops 100000000 | bytes 4194304 | tf_op jit(solution)/shard_map/pallas_call | solution.py:456
  36.2 5.9 %all-to-all-start = ((f32[32,1,128]{2,1,0:T(1,128)}), f32[32,1,128]{2,1,0:T(1,128)S(1)}, u32[]{:S(2)}, u32[]{:S(2)}) async-start(f32[32,1,128]{2,1,0:T(1,128)} %bitcast.7), calls=%async_computation | async-start | bytes 32768 | tf_op jit(solution)/shard_map/all_to_all | solution.py:464
  42.1 1.2 %copy-done.4 = bf16[256,2048]{1,0:T(8,128)(2,1)S(1)} copy-done((bf16[256,2048]{1,0:T(8,128)(2,1)S(1)}, bf16[256,2048]{1,0:T(8,128)(2,1)}, u32[]{:S(2)}) %copy-start.4) | copy-done | bytes 1048600
  43.4 1.2 %copy-done.6 = f32[128,2048]{1,0:T(8,128)S(1)} copy-done((f32[128,2048]{1,0:T(8,128)S(1)}, f32[128,2048]{1,0:T(8,128)}, u32[]{:S(2)}) %copy-start.6) | copy-done | bytes 1048600
  44.6 1.2 %copy-done.8 = f32[128,2048]{1,0:T(8,128)S(1)} copy-done((f32[128,2048]{1,0:T(8,128)S(1)}, f32[128,2048]{1,0:T(8,128)}, u32[]{:S(2)}) %copy-start.8) | copy-done | bytes 1048600
  45.8 3.6 %shard_map.129 = (bf16[1,128,2048]{2,1,0:T(8,128)(2,1)}, bf16[1,64,128]{2,1,0:T(8,128)(2,1)}, bf16[1,64,128]{2,1,0:T(8,128)(2,1)}, f32[1,32,128]{2,1,0:T(8,128)}) custom-call(f32[1040,128]{1,0:T(8,128)S(1)} %collective-permute-done.refs_0_, f32[1040,128]{1,0:T(8,128)S(1)} %collective-permute-done.1.refs_1_, f32[1040,128]{1,0:T(8,128)S(1)} %collective-permute-done.2.refs_2_, ...), custom_call_target="tpu_custom_call" | custom-call | flops 2000000000 | bytes 12582912 | tf_op jit(solution)/shard_map/pallas_call | solution.py:466
  49.4 0.0 all-to-all-done
  49.4 0.1 reduce_sum.9
  49.5 0.6 %fusion = (f32[32]{0:T(128)}, f32[32]{0:T(128)}) fusion(f32[128]{0:T(128)S(1)} %reduce_sum.9), kind=kLoop, calls=%fused_computation | loop fusion | bytes 512 | tf_op jit(solution)/shard_map/slice | solution.py:500
  (10 shorter events, 0.0 us)
Async XLA Ops:
  0.6 0.7 %copy-start.1 = (s32[1,16]{1,0:T(1,128)S(1)}, s32[1,16]{1,0:T(1,128)}, u32[]{:S(2)}) copy-start(s32[1,16]{1,0:T(1,128)} %refs_5_.1) | copy-start | bytes 196
  0.6 0.7 %copy-start.2 = (f32[32]{0:T(128)S(1)}, f32[32]{0:T(128)}, u32[]{:S(2)}) copy-start(f32[32]{0:T(128)} %param.12) | copy-start | bytes 388
  5.3 25.8 %collective-permute-start = (f32[1040,128]{1,0:T(8,128)S(1)}, f32[1040,128]{1,0:T(8,128)S(1)}, u32[]{:S(2)}, u32[]{:S(2)}) collective-permute-start(f32[1040,128]{1,0:T(8,128)S(1)} %get-tuple-element.35), channel_id=1, source_target_pairs={{0,1},{1,0},{2,3},{3,2},{4,5},{5,4},{6,7},{7,6},{8,9},{9,8},{10,11... | collective-permute-start | bytes 1597448 | tf_op jit(solution)/shard_map/ppermute | solution.py:403
  8.3 22.8 %collective-permute-start.1 = (f32[1040,128]{1,0:T(8,128)S(1)}, f32[1040,128]{1,0:T(8,128)S(1)}, u32[]{:S(2)}, u32[]{:S(2)}) collective-permute-start(f32[1040,128]{1,0:T(8,128)S(1)} %get-tuple-element.36), channel_id=1, source_target_pairs={{1,2},{2,1},{3,4},{4,3},{5,6},{6,5},{9,10},{10,9},{11,12},{12,11},... | collective-permute-start | bytes 1597448 | tf_op jit(solution)/shard_map/ppermute | solution.py:403
  9.0 26.1 %collective-permute-start.2 = (f32[1040,128]{1,0:T(8,128)S(1)}, f32[1040,128]{1,0:T(8,128)S(1)}, u32[]{:S(2)}, u32[]{:S(2)}) collective-permute-start(f32[1040,128]{1,0:T(8,128)S(1)} %get-tuple-element.37), channel_id=1, source_target_pairs={{0,2},{2,0},{1,3},{3,1},{4,6},{6,4},{5,7},{7,5},{8,10},{10,8},{9,1... | collective-permute-start | bytes 1597448 | tf_op jit(solution)/shard_map/ppermute | solution.py:403
  11.9 23.2 %collective-permute-start.3 = (f32[1040,128]{1,0:T(8,128)S(1)}, f32[1040,128]{1,0:T(8,128)S(1)}, u32[]{:S(2)}, u32[]{:S(2)}) collective-permute-start(f32[1040,128]{1,0:T(8,128)S(1)} %get-tuple-element.38), channel_id=1, source_target_pairs={{2,4},{4,2},{3,5},{5,3},{10,12},{12,10},{11,13},{13,11},{18,20},{2... | collective-permute-start | bytes 1597448 | tf_op jit(solution)/shard_map/ppermute | solution.py:403
  12.6 0.7 %copy-start = (f32[32]{0:T(128)S(1)}, f32[32]{0:T(128)}, u32[]{:S(2)}) copy-start(f32[32]{0:T(128)} %param.13) | copy-start | bytes 388
  19.1 1.0 %copy-start.5 = (f32[128,2048]{1,0:T(8,128)}, f32[128,2048]{1,0:T(8,128)S(1)}, u32[]{:S(2)}) copy-start(f32[128,2048]{1,0:T(8,128)S(1)} %get-tuple-element.50.refs_10_) | copy-start | bytes 3145732
  20.0 16.1 %copy-start.3 = (bf16[256,2048]{1,0:T(8,128)(2,1)}, bf16[256,2048]{1,0:T(8,128)(2,1)S(1)}, u32[]{:S(2)}) copy-start(bf16[256,2048]{1,0:T(8,128)(2,1)S(1)} %get-tuple-element.49.refs_9_) | copy-start | bytes 3145732
  20.0 16.1 %copy-start.7 = (f32[128,2048]{1,0:T(8,128)}, f32[128,2048]{1,0:T(8,128)S(1)}, u32[]{:S(2)}) copy-start(f32[128,2048]{1,0:T(8,128)S(1)} %get-tuple-element.51.refs_11_) | copy-start | bytes 3145732
  36.2 13.3 %all-to-all-start = ((f32[32,1,128]{2,1,0:T(1,128)}), f32[32,1,128]{2,1,0:T(1,128)S(1)}, u32[]{:S(2)}, u32[]{:S(2)}) async-start(f32[32,1,128]{2,1,0:T(1,128)} %bitcast.7), calls=%async_computation | async-start | bytes 32768 | tf_op jit(solution)/shard_map/all_to_all | solution.py:464
  42.1 1.2 %copy-start.4 = (bf16[256,2048]{1,0:T(8,128)(2,1)S(1)}, bf16[256,2048]{1,0:T(8,128)(2,1)}, u32[]{:S(2)}) copy-start(bf16[256,2048]{1,0:T(8,128)(2,1)} %copy-done.3) | copy-start | bytes 3145732
  43.4 1.2 %copy-start.6 = (f32[128,2048]{1,0:T(8,128)S(1)}, f32[128,2048]{1,0:T(8,128)}, u32[]{:S(2)}) copy-start(f32[128,2048]{1,0:T(8,128)} %copy-done.5) | copy-start | bytes 3145732
  44.6 1.2 %copy-start.8 = (f32[128,2048]{1,0:T(8,128)S(1)}, f32[128,2048]{1,0:T(8,128)}, u32[]{:S(2)}) copy-start(f32[128,2048]{1,0:T(8,128)} %copy-done.7) | copy-start | bytes 3145732

commit v3 on v2

v3 whole, which is shorter than its diff:
```python
import functools

import jax
import jax.numpy as jnp
from jax import lax
from jax.experimental import pallas as pl
from jax.experimental.pallas import tpu as pltpu
from jax.sharding import PartitionSpec as P

F32 = jnp.float32
BF16 = jnp.bfloat16
LANES = 128
WIDE = 256
PARTS = WIDE // LANES
FAR = 2**30


def dot(a, b, ca, cb):
    return lax.dot_general(a, b, (((ca,), (cb,)), ((), ())), preferred_element_type=F32)


def iota(shape, dim):
    return lax.broadcasted_iota(jnp.int32, shape, dim)


def split2(a):
    high = a.astype(BF16)
    return high, (a - high.astype(F32)).astype(BF16)


def split3(a):
    high = a.astype(BF16)
    rest = a - high.astype(F32)
    middle = rest.astype(BF16)
    return high, middle, (rest - middle.astype(F32)).astype(BF16)


def dot_pairs(a, b, ca, cb):
    return dot(a[0], b[0], ca, cb) + (dot(a[0], b[1], ca, cb) + dot(a[1], b[0], ca, cb))


def stack(parts, axis):
    return jnp.concatenate(parts, axis=axis)


def document_places(lens_ref, rows):
    offset = lax.axis_index("ctx") * rows
    starts = [jnp.int32(0)]
    for d in range(lens_ref.shape[1] - 1):
        starts.append(starts[-1] + lens_ref[0, d])
    first = jnp.int32(FAR)
    last = jnp.int32(0)
    for start in starts:
        first = jnp.minimum(first, jnp.where(start >= offset, start, FAR))
        last = jnp.maximum(last, jnp.where(start < offset + rows, start, 0))
    return starts, offset, first, last


def rate_column(alog_ref):
    heads = alog_ref.shape[1]
    square = jnp.broadcast_to(alog_ref[...], (heads, heads))
    picked = jnp.where(iota((heads, heads), 0) == iota((heads, heads), 1), square, 0.0)
    return -jnp.exp(jnp.sum(picked, axis=1, keepdims=True))


def log2(size):
    assert size & (size - 1) == 0
    return size.bit_length() - 1


def head_distance(heads, head_width):
    shape = (3 * heads, WIDE)
    return (iota(shape, 0) & (heads - 1)) - lax.shift_right_logical(
        iota(shape, 1), log2(head_width)
    )


def head_rows(distance, head_width, block):
    return jnp.where(distance == block * (WIDE // head_width), 1.0, 0.0).astype(BF16)


def head_columns(heads, head_width, block):
    shape = (WIDE, heads)
    column = lax.shift_right_logical(iota(shape, 0), log2(head_width))
    return jnp.where(iota(shape, 1) - column == block * (WIDE // head_width), 1.0, 0.0).astype(BF16)


def is_odd(distance):
    return lax.rem(lax.div(lax.axis_index("ctx"), distance), 2)


def message_block(ref, block, width):
    at = block * PARTS
    return stack([ref[(at + i) * width : (at + i + 1) * width, :] for i in range(PARTS)], 1)


def message_tail(ref, block, width):
    tail = ref.shape[0] // (width + 1) * width + block * PARTS
    return stack([ref[tail + i : tail + i + 1, :] for i in range(PARTS)], 1)


def received(refs, block, width):
    came = pull = None
    for j in range(len(refs) // 2, 0, -1):
        one, two = refs[2 * j - 2], refs[2 * j - 1]
        a, b = message_block(one, block, width), message_block(two, block, width)
        odd = jnp.broadcast_to(is_odd(j), a.shape) == 1
        near_came, near_pull = jnp.where(odd, a, b), jnp.where(odd, b, a)
        if came is None:
            came, pull = near_came, near_pull
        else:
            a, b = message_tail(one, block, width), message_tail(two, block, width)
            odd = jnp.broadcast_to(is_odd(j), a.shape) == 1
            came = near_came + jnp.where(odd, a, b) * came
            pull = near_pull + jnp.where(odd, b, a) * pull
    return came, pull


def states_kernel(
    reach,
    sets,
    lens_hbm,
    alog_hbm,
    dt_hbm,
    x_hbm,
    b_hbm,
    dy_hbm,
    c_hbm,
    dt_ref,
    x_ref,
    b_ref,
    dy_ref,
    c_ref,
    *refs,
):
    payloads, (lens_ref, alog_ref, small_sems, sems) = refs[:-4], refs[-4:]
    rows, columns = x_ref.shape
    heads, width = dt_ref.shape[0], b_ref.shape[0]
    head_width = columns // heads
    pieces = sems.shape[1]
    piece = columns // pieces
    small = [
        pltpu.make_async_copy(source, target, small_sems.at[i])
        for i, (source, target) in enumerate(
            (
                (lens_hbm, lens_ref),
                (alog_hbm, alog_ref),
                (dt_hbm.at[0], dt_ref),
                (b_hbm.at[0], b_ref),
                (c_hbm.at[0], c_ref),
            )
        )
    ]
    for copy in small:
        copy.start()
    large = []
    for i in range(pieces):
        at = slice(i * piece, (i + 1) * piece)
        for side, (source, target) in enumerate(((x_hbm, x_ref), (dy_hbm, dy_ref))):
            copy = pltpu.make_async_copy(
                source.at[0, :, at], target.at[:, at], sems.at[side, i]
            )
            copy.start()
            large.append(copy)
    square = (rows, rows)
    upper = jnp.where(iota(square, 0) <= iota(square, 1), 1.0, 0.0).astype(BF16)
    odds = [
        jnp.broadcast_to(is_odd(j), (width, LANES)) == 1 for j in range(1, reach + 1)
    ]
    left = iota((1, LANES), 1) < head_width
    for copy in small:
        copy.wait()
    _, offset, first, last = document_places(lens_ref, rows)
    through = jnp.where(first >= offset + rows, 1.0, 0.0)
    dt = dt_ref[...]
    logs = sum(dot(part, upper, 1, 0) for part in split3(dt * rate_column(alog_ref)))
    end_log = logs[:, rows - 1 : rows]
    place = iota((heads, rows), 1) + offset
    keeping = jnp.where(place >= last, jnp.exp(end_log - logs) * dt, 0.0)
    carried = jnp.where(place < first, jnp.exp(logs), 0.0)
    kept = jnp.broadcast_to(jnp.exp(end_log) * through, (heads, LANES))
    b, c = b_ref[...].astype(F32), c_ref[...].astype(F32)
    own = LANES // head_width

    def pair_states(vectors, weights, values, pair):
        parts = []
        for h in range(own):
            row = weights[pair * own + h : pair * own + h + 1, :]
            parts += split2(vectors * row)
        out = dot(stack(parts, 0), values, 1, 0)
        sides = [
            out[2 * h * width : (2 * h + 1) * width]
            + out[(2 * h + 1) * width : (2 * h + 2) * width]
            for h in range(own)
        ]
        return jnp.where(left, sides[0], sides[1])

    done = 0
    for one, size in enumerate(sets):
        messages = payloads[2 * reach * one : 2 * reach * (one + 1)]
        for i in range(size * PARTS):
            pair = done * PARTS + i
            if pair * LANES % piece == 0:
                large[pair * LANES // piece * 2].wait()
                large[pair * LANES // piece * 2 + 1].wait()
            at = slice(pair * LANES, (pair + 1) * LANES)
            state = pair_states(b, keeping, x_ref[:, at], pair)
            pulled = pair_states(c, carried, dy_ref[:, at], pair)
            here = kept[pair * own : (pair + 1) * own]
            tail = jnp.where(left, here[:1], here[1:])
            for j in range(reach):
                values = jnp.where(odds[j], pulled, state), jnp.where(odds[j], state, pulled)
                for ref, value in zip(messages[2 * j : 2 * j + 2], values):
                    ref[i * width : (i + 1) * width, :] = value
                    ref[size * PARTS * width + i : size * PARTS * width + i + 1, :] = tail
        done += size


def inside_kernel(
    lens_ref,
    alog_ref,
    skip_ref,
    dt_ref,
    x_ref,
    b_ref,
    dy_ref,
    c_ref,
    xs_ref,
    ys_ref,
    v_wide_ref,
    dx_ref,
    b_end_ref,
    c_live_ref,
    masks_ref,
    db_ref,
    dc_ref,
    sums_ref,
    logs_ref,
    ends_ref,
    small_ref,
):
    rows, columns = x_ref.shape
    heads, width = dt_ref.shape[0], b_ref.shape[0]
    head_width = columns // heads
    starts, offset, first, last = document_places(lens_ref, rows)
    through = jnp.where(first >= offset + rows, 1.0, 0.0)
    square = (rows, rows)
    place0, place1 = iota(square, 0) + offset, iota(square, 1) + offset
    segment0, segment1 = jnp.zeros(square, jnp.int32), jnp.zeros(square, jnp.int32)
    for start in starts:
        segment0 += jnp.where(place0 >= start, 1, 0)
        segment1 += jnp.where(place1 >= start, 1, 0)
    same = segment0 == segment1
    down = same & (place0 >= place1)
    lower = jnp.where(place0 >= place1, 1.0, 0.0).astype(BF16)
    eye = jnp.where(place0 == place1, 1.0, 0.0).astype(BF16)
    dt = dt_ref[...]
    logs = sum(dot(lower, part, 1, 1) for part in split3(dt * rate_column(alog_ref)))
    steps = sum(dot(eye, part, 1, 1) for part in split3(dt))
    logs_ref[...] = logs
    bt, ct = b_ref[...], c_ref[...]
    scores = split2(jnp.where(down, dot(ct, bt, 0, 0), 0.0))
    flipped = split2(jnp.where(same & (place1 >= place0), dot(bt, ct, 0, 0), 0.0))
    place = iota((width, rows), 1) + offset
    b_end = jnp.transpose(jnp.where(place >= last, bt.astype(F32), 0.0)).astype(BF16)
    c_live = jnp.transpose(jnp.where(place < first, ct.astype(F32), 0.0)).astype(BF16)
    b_end_ref[...] = stack([b_end, b_end], 1)
    c_live_ref[...] = stack([c_live, c_live], 1)
    masks_ref[0:width] = jnp.where(place >= last, 1.0, 0.0)
    masks_ref[width : 2 * width] = jnp.where(place < first, 1.0, 0.0)
    tables = stack(
        [
            stack(split3(a), 1)
            for a in (
                jnp.exp(logs),
                jnp.exp(-logs) * steps,
                jnp.broadcast_to(skip_ref[...], (16, heads)),
            )
        ],
        0,
    )
    distance = head_distance(heads, head_width)
    d_scores = jnp.zeros(square, F32)
    sums = jnp.zeros((2 * rows, heads), F32)
    products = jnp.zeros((8, heads), F32)
    for block in range(columns // WIDE):
        at = slice(block * WIDE, (block + 1) * WIDE)
        wide = dot(tables, head_rows(distance, head_width, block), 1, 0)
        ones = head_columns(heads, head_width, block)
        u_wide, v_wide = wide[:rows], wide[rows : 2 * rows]
        skip_wide = wide[2 * rows : 2 * rows + 1]
        x = x_ref[:, at].astype(F32)
        dy = dy_ref[:, at].astype(F32)
        xv = x * v_wide
        yu = dy * u_wide
        xs, ys = split2(xv), split2(yu)
        xs_ref[:, at] = stack(xs, 0)
        ys_ref[:, at] = stack(ys, 0)
        v_wide_ref[:, at] = v_wide
        out = dot_pairs(scores, xs, 1, 0)
        back = dot_pairs(flipped, ys, 1, 0)
        d_scores += dot_pairs(ys, xs, 1, 1)
        dx_ref[:, at] = v_wide * back + skip_wide * dy
        column_part = xv * back
        for part in split3(stack([yu * out - column_part, column_part], 0)):
            sums += dot(part, ones, 1, 0)
        product = jnp.broadcast_to(jnp.sum(x * dy, axis=0, keepdims=True), (8, WIDE))
        for part in split3(product):
            products += dot(part, ones, 1, 0)
        ending = u_wide[rows - 1 : rows]
        ends_ref[0:1, at] = ending
        ends_ref[1:2, at] = ending * through
    d_scores = split2(jnp.where(down, d_scores, 0.0))
    dc_ref[...] = sum(dot(bt, p, 1, 1) for p in d_scores)
    db_ref[...] = sum(dot(ct, p, 1, 0) for p in d_scores)
    sums_ref[...] = sums
    small_ref[...] = products


def cross_kernel(start, size, final, *refs):
    (
        ends_ref,
        xs_ref,
        ys_ref,
        v_wide_ref,
        dx_ref,
        b_end_ref,
        c_live_ref,
        masks_ref,
        db_ref,
        dc_ref,
        sums_ref,
    ) = refs[:11]
    own_ref, logs_ref, alog_ref, dt_ref, small_ref = refs[11:16] if final else [None] * 5
    rest = refs[16:] if final else refs[11:]
    outs = 5 if final else 4
    rest, (stage_ref, sems) = rest[:-2], rest[-2:]
    messages = rest[(1 if start else 0) * final : len(rest) - outs]
    dx_out, db_out, dc_out, last_out, *partial_out = rest[len(rest) - outs :]
    rows, columns = dx_ref.shape
    heads, width = sums_ref.shape[1], db_ref.shape[0]
    head_width = columns // heads
    b_end, c_live = b_end_ref[...], c_live_ref[...]
    sums = sums_ref[...]
    dc = jnp.zeros((2 * width, 2 * rows), F32)
    db = jnp.zeros((2 * width, 2 * rows), F32)
    at_last = iota((rows, WIDE), 0) == rows - 1
    copies = []
    for i in range(size):
        block = start + i
        at = slice(block * WIDE, (block + 1) * WIDE)
        own = slice(i * WIDE, (i + 1) * WIDE)
        ones = head_columns(heads, head_width, block)
        came, pull = received(messages, i, width)
        meet = jnp.sum(came * pull, axis=0, keepdims=True) * ends_ref[1:2, at]
        cames = stack(split2(came), 0)
        pulls = stack(split2(pull * ends_ref[0:1, at]), 0)
        xs, ys = xs_ref[:, at], ys_ref[:, at]
        out = dot(c_live, cames, 1, 0)
        back = dot(b_end, pulls, 1, 0)
        stage_ref[:, own] = (dx_ref[:, at] + v_wide_ref[:, at] * back).astype(BF16)
        copy = pltpu.make_async_copy(stage_ref.at[:, own], dx_out.at[0, :, at], sems.at[i])
        copy.start()
        copies.append(copy)
        column_part = (xs[:rows].astype(F32) + xs[rows:].astype(F32)) * back
        row_part = (ys[:rows].astype(F32) + ys[rows:].astype(F32)) * out
        row_part = jnp.where(at_last, row_part + meet, row_part)
        for part in split3(stack([row_part - column_part, column_part], 0)):
            sums += dot(part, ones, 1, 0)
        dc += dot(cames, ys, 1, 1)
        db += dot(pulls, xs, 1, 1)
    dc = (dc[:width, :rows] + dc[:width, rows:]) + dc[width:, :rows]
    db = (db[:width, :rows] + db[:width, rows:]) + db[width:, :rows]
    db = db_ref[...] + masks_ref[0:width] * db
    dc = dc_ref[...] + masks_ref[width : 2 * width] * dc
    if final:
        db_out[0] = db.astype(BF16)
        dc_out[0] = dc.astype(BF16)
        square = (rows, rows)
        upper = jnp.where(iota(square, 0) >= iota(square, 1), 1.0, 0.0).astype(BF16)
        eye = jnp.where(iota(square, 0) == iota(square, 1), 1.0, 0.0).astype(BF16)
        at_end = jnp.sum(sums[rows:] - own_ref[rows:], axis=0, keepdims=True)
        dl = sums[:rows] + jnp.where(iota((rows, heads), 0) == rows - 1, at_end, 0.0)
        d_decay = sum(dot(part, upper, 0, 0) for part in split3(dl))
        total = sum(dot(part, eye, 0, 0) for part in split3(sums[rows:]))
        last_out[0] = total / dt_ref[...] + rate_column(alog_ref) * d_decay
        rate_grads = jnp.sum(logs_ref[...] * dl, axis=0, keepdims=True)
        empty = jnp.zeros((1, LANES - 2 * heads), F32)
        row = stack([rate_grads, small_ref[:1], empty], 1)
        partial_out[0][...] = jnp.broadcast_to(row, partial_out[0].shape)
    else:
        db_out[...] = db
        dc_out[...] = dc
        last_out[...] = sums
    for copy in copies:
        copy.wait()


def call(kernel, reach, outs, ins, flops, moved, scratch=(), aliases=None):
    spaces = {"s": pltpu.SMEM, "v": pltpu.VMEM, "h": pltpu.HBM}
    return pl.pallas_call(
        kernel,
        out_shape=[jax.ShapeDtypeStruct(*out) for _, out in outs],
        in_specs=[pl.BlockSpec(memory_space=spaces[place]) for place, _ in ins],
        out_specs=[pl.BlockSpec(memory_space=spaces[place]) for place, _ in outs],
        scratch_shapes=scratch,
        input_output_aliases=aliases or {},
        compiler_params=pltpu.CompilerParams(vmem_limit_bytes=min(16 + 2 * reach, 56) * 2**20),
        cost_estimate=pl.CostEstimate(flops=flops, bytes_accessed=moved, transcendentals=0),
    )(*(a for _, a in ins))


def swap(a, by, second):
    count = lax.axis_size("ctx")
    pairs = []
    for i in range(count - by):
        if i // by % 2 == second:
            pairs += [(i, i + by), (i + by, i)]
    return lax.ppermute(a, "ctx", pairs)


def in_hbm(a):
    return "h", pltpu.with_memory_space_constraint(a, pltpu.HBM)


def per_device(inputs, b_proj, c_proj, step_sizes, a_log, skip_gain, doc_lengths, grad_out):
    rows, columns = inputs.shape[1:]
    heads, width = a_log.shape[0], b_proj.shape[2]
    reach = max(lax.axis_size("ctx") // 4, 1)
    devices = lax.axis_size("ctx") * lax.axis_size("dp")
    alog, skip = a_log[None], skip_gain[None]
    bt, ct = jnp.swapaxes(b_proj, 1, 2), jnp.swapaxes(c_proj, 1, 2)
    blocks = columns // WIDE
    sets = (blocks,)
    pieces = 4

    def v(shape, kind=F32):
        return "v", (shape, kind)

    transposed = v((width, rows))
    per_token = v((2 * rows, heads))

    dt, x, b, dy, c, *payloads = call(
        functools.partial(states_kernel, reach, sets),
        reach,
        [
            v((heads, rows)),
            v((rows, columns), BF16),
            v((width, rows), BF16),
            v((rows, columns), BF16),
            v((width, rows), BF16),
        ]
        + [v((size * PARTS * (width + 1), LANES)) for size in sets for _ in range(2 * reach)],
        [in_hbm(a) for a in (doc_lengths, alog, step_sizes, inputs, bt, grad_out, ct)],
        10**9,
        4 * 2**20,
        [
            pltpu.SMEM(doc_lengths.shape, jnp.int32),
            pltpu.VMEM(alog.shape, F32),
            pltpu.SemaphoreType.DMA((5,)),
            pltpu.SemaphoreType.DMA((2, pieces)),
        ],
    )
    messages = [None] * len(payloads)
    for at in range(len(payloads) - 1, -1, -1):
        messages[at] = swap(payloads[at], at % (2 * reach) // 2 + 1, at % 2)
    xs, ys, v_wide, dx, b_end, c_live, masks, db, dc, own_sums, logs, ends, small = call(
        inside_kernel,
        reach,
        [v((2 * rows, columns), BF16)] * 2
        + [v((rows, columns))] * 2
        + [v((rows, 2 * width), BF16)] * 2
        + [v((2 * width, rows)), transposed, transposed, per_token]
        + [v((rows, heads)), v((8, columns)), v((8, heads))],
        [("s", doc_lengths)] + [("v", a) for a in (alog, skip, dt, x, b, dy, c)],
        4 * 10**9,
        12 * 2**20,
    )
    whole = "h", ((1, rows, columns), BF16)
    sums, input_grads = own_sums, None
    start = 0
    for one, size in enumerate(sets):
        final = one == len(sets) - 1
        outs = [whole, transposed, transposed, per_token]
        ins = [ends, xs, ys, v_wide, dx, b_end, c_live, masks, db, dc, sums]
        if final:
            ins += [own_sums, logs, alog, dt, small] + [input_grads] * (one > 0)
            narrow = v((1, width, rows), BF16)
            outs = [whole, narrow, narrow, v((1, heads, rows)), v((devices, LANES))]
        ins = [("h" if a is input_grads else "v", a) for a in ins]
        ins += [("v", a) for a in messages[2 * reach * one : 2 * reach * (one + 1)]]
        results = call(
            functools.partial(cross_kernel, start, size, final),
            reach,
            outs,
            ins,
            10**9,
            8 * 2**20,
            [pltpu.VMEM((rows, size * WIDE), BF16), pltpu.SemaphoreType.DMA((size,))],
            {16: 0} if final and one else None,
        )
        start += size
        if not final:
            input_grads, db, dc, sums = results
    input_grads, b_gradient, c_gradient, step_grads, partial = results
    gathered = lax.all_to_all(partial, ("dp", "ctx"), 0, 0, tiled=True)
    totals = jnp.sum(gathered, axis=0)
    return (
        input_grads,
        jnp.swapaxes(b_gradient, 1, 2),
        jnp.swapaxes(c_gradient, 1, 2),
        step_grads,
        totals[:heads],
        totals[heads : 2 * heads],
    )


def solution(mesh):
    in_specs = (
        P("dp", "ctx", None),
        P("dp", "ctx", None),
        P("dp", "ctx", None),
        P("dp", None, "ctx"),
        P(),
        P(),
        P("dp", None),
        P("dp", "ctx", None),
    )
    out_specs = (
        P("dp", "ctx", None),
        P("dp", "ctx", None),
        P("dp", "ctx", None),
        P("dp", None, "ctx"),
        P(),
        P(),
    )
    return jax.shard_map(
        per_device, mesh=mesh, in_specs=in_specs, out_specs=out_specs, check_vma=False
    )
```

time: 50.4 us -> 50.7 us (level)
  blocking collectives: 0 us -> 12.9 us
  starting transfers between devices: 13.2 us -> 7.27 us
  local copies, waits for them, and re-layouts: 6.54 us -> 1.25 us
  Pallas kernels: 14.5 us -> 11.7 us
  waiting for transfers between devices: 15 us -> 16.7 us
    all_to_all x0 -> x1, blocking collectives: none -> 12.9 us  [per_device(): gathered = lax.all_to_all(partial, ('dp', 'ctx'), 0, 0, tiled=True)]
    all_to_all x1 -> x0, starting transfers between devices: 5.95 us -> none  [per_device(): gathered = lax.all_to_all(partial, ('dp', 'ctx'), 0, 0, tiled=True)]
    unnamed x18 -> x6, local copies, waits for them, and re-layouts: 5.95 us -> 0.67 us
    pallas_call x4 -> x3, Pallas kernels: 14.5 us -> 11.7 us  [call(): pl.pallas_call(kernel, out_shape=[jax.ShapeDtypeStruct(*out) for _, out i...]
    ppermute x4, waiting for transfers between devices: 15 us -> 16.7 us  [swap(): return lax.ppermute(a, 'ctx', pairs)]
  transfers between devices with their start and end apart: 5 -> 4, of which waited for: 2 -> 2; matrix products, arithmetic and copies ran while one was open for 0% -> 0% of each run, Pallas kernels for 19% -> 10%
where the time goes in v3:
time: 50.7 us; the launch traced here: 50.5 us
  waiting for transfers between devices  16.7 us (33%)
  blocking collectives  12.9 us (25%)
  Pallas kernels  11.7 us (23%)
  starting transfers between devices  7.27 us (14%)
  local copies, waits for them, and re-layouts  1.25 us (2%)
  between operations  0.69 us (1%)
    ppermute x4, waiting for transfers between devices, swap(): return lax.ppermute(a, 'ctx', pairs)  16.7 us
    all_to_all x1, blocking collectives, per_device(): gathered = lax.all_to_all(partial, ('dp', 'ctx'), 0, 0, tiled=True)  12.9 us
    pallas_call x3, Pallas kernels, call(): pl.pallas_call(kernel, out_shape=[jax.ShapeDtypeStruct(*out) for _, out i...  11.7 us
    ppermute x4, starting transfers between devices, swap(): return lax.ppermute(a, 'ctx', pairs)  7.27 us
  transfers between devices with their start and end apart: 4, of which 2 were waited for; matrix products, arithmetic and copies ran while one was open for 0% of the time, Pallas kernels for 10%

profile of v3, /device:TPU:0, one launch (start us, length us, event | category | flops | bytes accessed | tf_op | source)
XLA Modules:
  0.0 50.5 jit_solution(7134809032036326456)
XLA Ops:
  0.6 2.8 %shard_map.127 = (f32[32,128]{1,0:T(8,128)S(1)}, bf16[128,2048]{1,0:T(8,128)(2,1)S(1)}, bf16[64,128]{1,0:T(8,128)(2,1)S(1)}, bf16[128,2048]{1,0:T(8,128)(2,1)S(1...) custom-call(s32[1,16]{1,0:T(1,128)} %lens_ref.1, ...), custom_call_target="tpu_custom_call" | custom-call | flops 1000000000 | bytes 4194304 | tf_op jit(solution)/shard_map/pallas_call | solution.py:401
  3.5 3.0 %collective-permute-start = (f32[1040,128]{1,0:T(8,128)S(1)}, f32[1040,128]{1,0:T(8,128)S(1)}, u32[]{:S(2)}, u32[]{:S(2)}) collective-permute-start(f32[1040,128]{1,0:T(8,128)S(1)} %get-tuple-element.51), channel_id=1, source_target_pairs={{0,1},{1,0},{2,3},{3,2},{4,5},{5,4},{6,7},{7,6},{8,9},{9,8},{10,11... | collective-permute-start | bytes 1597448 | tf_op jit(solution)/shard_map/ppermute | solution.py:419
  6.5 0.7 %collective-permute-start.1 = (f32[1040,128]{1,0:T(8,128)S(1)}, f32[1040,128]{1,0:T(8,128)S(1)}, u32[]{:S(2)}, u32[]{:S(2)}) collective-permute-start(f32[1040,128]{1,0:T(8,128)S(1)} %get-tuple-element.52), channel_id=1, source_target_pairs={{1,2},{2,1},{3,4},{4,3},{5,6},{6,5},{9,10},{10,9},{11,12},{12,11},... | collective-permute-start | bytes 1597448 | tf_op jit(solution)/shard_map/ppermute | solution.py:419
  7.2 2.9 %collective-permute-start.2 = (f32[1040,128]{1,0:T(8,128)S(1)}, f32[1040,128]{1,0:T(8,128)S(1)}, u32[]{:S(2)}, u32[]{:S(2)}) collective-permute-start(f32[1040,128]{1,0:T(8,128)S(1)} %get-tuple-element.53), channel_id=1, source_target_pairs={{0,2},{2,0},{1,3},{3,1},{4,6},{6,4},{5,7},{7,5},{8,10},{10,8},{9,1... | collective-permute-start | bytes 1597448 | tf_op jit(solution)/shard_map/ppermute | solution.py:419
  10.1 0.7 %collective-permute-start.3 = (f32[1040,128]{1,0:T(8,128)S(1)}, f32[1040,128]{1,0:T(8,128)S(1)}, u32[]{:S(2)}, u32[]{:S(2)}) collective-permute-start(f32[1040,128]{1,0:T(8,128)S(1)} %get-tuple-element.54), channel_id=1, source_target_pairs={{2,4},{4,2},{3,5},{5,3},{10,12},{12,10},{11,13},{13,11},{18,20},{2... | collective-permute-start | bytes 1597448 | tf_op jit(solution)/shard_map/ppermute | solution.py:419
  10.8 0.0 copy-start
  10.8 0.0 copy-start.1
  10.8 0.0 copy-start.2
  10.8 0.6 %copy-done = f32[32]{0:T(128)S(1)} copy-done((f32[32]{0:T(128)S(1)}, f32[32]{0:T(128)}, u32[]{:S(2)}) %copy-start) | copy-done | bytes 152
  11.4 0.0 copy-done.1
  11.4 0.0 copy-done.2
  11.4 5.1 %shard_map.128 = (bf16[256,2048]{1,0:T(8,128)(2,1)S(1)}, bf16[256,2048]{1,0:T(8,128)(2,1)S(1)}, f32[128,2048]{1,0:T(8,128)S(1)}, f32[128,2048]{1,0:T(8,128)S(1)}...) custom-call(s32[1,16]{1,0:T(1,128)S(1)} %copy-done.1, ...), custom_call_target="tpu_custom_call" | custom-call | flops 4000000000 | bytes 12582912 | tf_op jit(solution)/shard_map/pallas_call | solution.py:401
  16.6 12.7 %collective-permute-done.refs_16_ = f32[1040,128]{1,0:T(8,128)S(1)} collective-permute-done((f32[1040,128]{1,0:T(8,128)S(1)}, f32[1040,128]{1,0:T(8,128)S(1)}, u32[]{:S(2)}, u32[]{:S(2)}) %collective-permute-start) | collective-permute-done | bytes 532512 | tf_op jit(solution)/shard_map/ppermute | solution.py:419
  29.3 0.0 collective-permute-done.1.refs_17_
  29.3 4.0 %collective-permute-done.2.refs_18_ = f32[1040,128]{1,0:T(8,128)S(1)} collective-permute-done((f32[1040,128]{1,0:T(8,128)S(1)}, f32[1040,128]{1,0:T(8,128)S(1)}, u32[]{:S(2)}, u32[]{:S(2)}) %collective-permute-start.2) | collective-permute-done | bytes 532512 | tf_op jit(solution)/shard_map/ppermute | solution.py:419
  33.2 0.0 collective-permute-done.3.refs_19_
  33.2 3.8 %shard_map.129 = (bf16[1,128,2048]{2,1,0:T(8,128)(2,1)}, bf16[1,64,128]{2,1,0:T(8,128)(2,1)}, bf16[1,64,128]{2,1,0:T(8,128)(2,1)}, f32[1,32,128]{2,1,0:T(8,128)}, f32[32,128]{1,0:T(8,128)S(1)}) custom-call(f32[8,2048]{1,0:T(8,128)S(1)} %get-tuple-element.38.refs_0_, bf16[256,2048]{1,0:T(8,128)(2,1)S(1)} %get-tuple-element.39.refs_1_, ...), custom_call_target="tpu_custom_call" | custom-call | flops 1000000000 | bytes 8388608 | tf_op jit(solution)/shard_map/pallas_call | solution.py:401
  37.0 12.9 %all_to_all.9 = f32[32,1,128]{2,1,0:T(1,128)S(1)} all-to-all(f32[32,1,128]{2,1,0:T(1,128)S(1)} %bitcast.9), channel_id=1, replica_groups=mesh['dp'=4,'ctx'=8] {'dp','ctx'}, dimensions={0} | all-to-all | bytes 32768 | tf_op jit(solution)/shard_map/all_to_all | solution.py:506
  49.9 0.1 reduce_sum.9
  49.9 0.6 %fusion = (f32[32]{0:T(128)}, f32[32]{0:T(128)}) fusion(f32[128]{0:T(128)S(1)} %reduce_sum.9), kind=kLoop, calls=%fused_computation | loop fusion | bytes 512 | tf_op jit(solution)/shard_map/slice | solution.py:514
Async XLA Ops:
  3.5 25.8 %collective-permute-start = (f32[1040,128]{1,0:T(8,128)S(1)}, f32[1040,128]{1,0:T(8,128)S(1)}, u32[]{:S(2)}, u32[]{:S(2)}) collective-permute-start(f32[1040,128]{1,0:T(8,128)S(1)} %get-tuple-element.51), channel_id=1, source_target_pairs={{0,1},{1,0},{2,3},{3,2},{4,5},{5,4},{6,7},{7,6},{8,9},{9,8},{10,11... | collective-permute-start | bytes 1597448 | tf_op jit(solution)/shard_map/ppermute | solution.py:419
  6.5 22.8 %collective-permute-start.1 = (f32[1040,128]{1,0:T(8,128)S(1)}, f32[1040,128]{1,0:T(8,128)S(1)}, u32[]{:S(2)}, u32[]{:S(2)}) collective-permute-start(f32[1040,128]{1,0:T(8,128)S(1)} %get-tuple-element.52), channel_id=1, source_target_pairs={{1,2},{2,1},{3,4},{4,3},{5,6},{6,5},{9,10},{10,9},{11,12},{12,11},... | collective-permute-start | bytes 1597448 | tf_op jit(solution)/shard_map/ppermute | solution.py:419
  7.2 26.1 %collective-permute-start.2 = (f32[1040,128]{1,0:T(8,128)S(1)}, f32[1040,128]{1,0:T(8,128)S(1)}, u32[]{:S(2)}, u32[]{:S(2)}) collective-permute-start(f32[1040,128]{1,0:T(8,128)S(1)} %get-tuple-element.53), channel_id=1, source_target_pairs={{0,2},{2,0},{1,3},{3,1},{4,6},{6,4},{5,7},{7,5},{8,10},{10,8},{9,1... | collective-permute-start | bytes 1597448 | tf_op jit(solution)/shard_map/ppermute | solution.py:419
  10.1 23.2 %collective-permute-start.3 = (f32[1040,128]{1,0:T(8,128)S(1)}, f32[1040,128]{1,0:T(8,128)S(1)}, u32[]{:S(2)}, u32[]{:S(2)}) collective-permute-start(f32[1040,128]{1,0:T(8,128)S(1)} %get-tuple-element.54), channel_id=1, source_target_pairs={{2,4},{4,2},{3,5},{5,3},{10,12},{12,10},{11,13},{13,11},{18,20},{2... | collective-permute-start | bytes 1597448 | tf_op jit(solution)/shard_map/ppermute | solution.py:419
  10.8 0.7 %copy-start = (f32[32]{0:T(128)S(1)}, f32[32]{0:T(128)}, u32[]{:S(2)}) copy-start(f32[32]{0:T(128)} %param.12) | copy-start | bytes 388
  10.8 0.7 %copy-start.1 = (s32[1,16]{1,0:T(1,128)S(1)}, s32[1,16]{1,0:T(1,128)}, u32[]{:S(2)}) copy-start(s32[1,16]{1,0:T(1,128)} %lens_ref.1) | copy-start | bytes 196
  10.8 0.7 %copy-start.2 = (f32[32]{0:T(128)S(1)}, f32[32]{0:T(128)}, u32[]{:S(2)}) copy-start(f32[32]{0:T(128)} %param.13) | copy-start | bytes 388

commit v4 on v3

--- a/solution.py
+++ b/solution.py
@@ -118,7 +118,6 @@
 
 def states_kernel(
     reach,
-    sets,
     lens_hbm,
     alog_hbm,
     dt_hbm,
@@ -195,25 +194,20 @@
         ]
         return jnp.where(left, sides[0], sides[1])
 
-    done = 0
-    for one, size in enumerate(sets):
-        messages = payloads[2 * reach * one : 2 * reach * (one + 1)]
-        for i in range(size * PARTS):
-            pair = done * PARTS + i
-            if pair * LANES % piece == 0:
-                large[pair * LANES // piece * 2].wait()
-                large[pair * LANES // piece * 2 + 1].wait()
-            at = slice(pair * LANES, (pair + 1) * LANES)
-            state = pair_states(b, keeping, x_ref[:, at], pair)
-            pulled = pair_states(c, carried, dy_ref[:, at], pair)
-            here = kept[pair * own : (pair + 1) * own]
-            tail = jnp.where(left, here[:1], here[1:])
-            for j in range(reach):
-                values = jnp.where(odds[j], pulled, state), jnp.where(odds[j], state, pulled)
-                for ref, value in zip(messages[2 * j : 2 * j + 2], values):
-                    ref[i * width : (i + 1) * width, :] = value
-                    ref[size * PARTS * width + i : size * PARTS * width + i + 1, :] = tail
-        done += size
+    for pair in range(columns // LANES):
+        if pair * LANES % piece == 0:
+            large[pair * LANES // piece * 2].wait()
+            large[pair * LANES // piece * 2 + 1].wait()
+        at = slice(pair * LANES, (pair + 1) * LANES)
+        state = pair_states(b, keeping, x_ref[:, at], pair)
+        pulled = pair_states(c, carried, dy_ref[:, at], pair)
+        here = kept[pair * own : (pair + 1) * own]
+        tail = columns // LANES * width + pair
+        for j in range(reach):
+            values = jnp.where(odds[j], pulled, state), jnp.where(odds[j], state, pulled)
+            for ref, value in zip(payloads[2 * j : 2 * j + 2], values):
+                ref[pair * width : (pair + 1) * width, :] = value
+                ref[tail : tail + 1, :] = jnp.where(left, here[:1], here[1:])
 
 
 def inside_kernel(
@@ -227,17 +221,21 @@
     c_ref,
     xs_ref,
     ys_ref,
-    v_wide_ref,
-    dx_ref,
+    v_wide_hbm,
+    dx_hbm,
     b_end_ref,
     c_live_ref,
     masks_ref,
     db_ref,
     dc_ref,
     sums_ref,
-    logs_ref,
+    fwd_ref,
+    bwd_ref,
     ends_ref,
     small_ref,
+    v_stage,
+    dx_stage,
+    sems,
 ):
     rows, columns = x_ref.shape
     heads, width = dt_ref.shape[0], b_ref.shape[0]
@@ -257,23 +255,26 @@
     dt = dt_ref[...]
     logs = sum(dot(lower, part, 1, 1) for part in split3(dt * rate_column(alog_ref)))
     steps = sum(dot(eye, part, 1, 1) for part in split3(dt))
-    logs_ref[...] = logs
     bt, ct = b_ref[...], c_ref[...]
     scores = split2(jnp.where(down, dot(ct, bt, 0, 0), 0.0))
     flipped = split2(jnp.where(same & (place1 >= place0), dot(bt, ct, 0, 0), 0.0))
     place = iota((width, rows), 1) + offset
-    b_end = jnp.transpose(jnp.where(place >= last, bt.astype(F32), 0.0)).astype(BF16)
-    c_live = jnp.transpose(jnp.where(place < first, ct.astype(F32), 0.0)).astype(BF16)
+    bt_end = jnp.where(place >= last, bt.astype(F32), 0.0)
+    ct_live = jnp.where(place < first, ct.astype(F32), 0.0)
+    b_end, c_live = jnp.transpose(bt_end).astype(BF16), jnp.transpose(ct_live).astype(BF16)
+    bt_end, ct_live = bt_end.astype(BF16), ct_live.astype(BF16)
     b_end_ref[...] = stack([b_end, b_end], 1)
     c_live_ref[...] = stack([c_live, c_live], 1)
-    masks_ref[0:width] = jnp.where(place >= last, 1.0, 0.0)
-    masks_ref[width : 2 * width] = jnp.where(place < first, 1.0, 0.0)
+    bt_end, ct_live = stack([bt_end, bt_end], 1), stack([ct_live, ct_live], 1)
+    masks_ref[0:1] = jnp.where(place[:1] >= last, 1.0, 0.0)
+    masks_ref[1:2] = jnp.where(place[:1] < first, 1.0, 0.0)
     tables = stack(
         [
             stack(split3(a), 1)
             for a in (
                 jnp.exp(logs),
                 jnp.exp(-logs) * steps,
+                logs,
                 jnp.broadcast_to(skip_ref[...], (16, heads)),
             )
         ],
@@ -283,12 +284,13 @@
     d_scores = jnp.zeros(square, F32)
     sums = jnp.zeros((2 * rows, heads), F32)
     products = jnp.zeros((8, heads), F32)
+    copies = []
     for block in range(columns // WIDE):
         at = slice(block * WIDE, (block + 1) * WIDE)
         wide = dot(tables, head_rows(distance, head_width, block), 1, 0)
         ones = head_columns(heads, head_width, block)
-        u_wide, v_wide = wide[:rows], wide[rows : 2 * rows]
-        skip_wide = wide[2 * rows : 2 * rows + 1]
+        u_wide, v_wide, l_wide = wide[:rows], wide[rows : 2 * rows], wide[2 * rows : 3 * rows]
+        skip_wide = wide[3 * rows : 3 * rows + 1]
         x = x_ref[:, at].astype(F32)
         dy = dy_ref[:, at].astype(F32)
         xv = x * v_wide
@@ -296,11 +298,15 @@
         xs, ys = split2(xv), split2(yu)
         xs_ref[:, at] = stack(xs, 0)
         ys_ref[:, at] = stack(ys, 0)
-        v_wide_ref[:, at] = v_wide
+        v_stage[:, at] = v_wide
         out = dot_pairs(scores, xs, 1, 0)
         back = dot_pairs(flipped, ys, 1, 0)
         d_scores += dot_pairs(ys, xs, 1, 1)
-        dx_ref[:, at] = v_wide * back + skip_wide * dy
+        dx_stage[:, at] = v_wide * back + skip_wide * dy
+        for i, (stage, target) in enumerate(((v_stage, v_wide_hbm), (dx_stage, dx_hbm))):
+            copy = pltpu.make_async_copy(stage.at[:, at], target.at[:, at], sems.at[i, block])
+            copy.start()
+            copies.append(copy)
         column_part = xv * back
         for part in split3(stack([yu * out - column_part, column_part], 0)):
             sums += dot(part, ones, 1, 0)
@@ -308,103 +314,146 @@
         for part in split3(product):
             products += dot(part, ones, 1, 0)
         ending = u_wide[rows - 1 : rows]
+        end_log = l_wide[rows - 1 : rows]
+        gap = end_log - l_wide
+        fwd_ref[:, at] = dot(bt_end, stack(split2(xv * gap), 0), 1, 0) * ending
+        bwd_ref[:, at] = dot(ct_live, stack(split2(yu * l_wide), 0), 1, 0)
         ends_ref[0:1, at] = ending
         ends_ref[1:2, at] = ending * through
+        ends_ref[2:3, at] = ending * through * end_log
     d_scores = split2(jnp.where(down, d_scores, 0.0))
     dc_ref[...] = sum(dot(bt, p, 1, 1) for p in d_scores)
     db_ref[...] = sum(dot(ct, p, 1, 0) for p in d_scores)
     sums_ref[...] = sums
-    small_ref[...] = products
-
-
-def cross_kernel(start, size, final, *refs):
-    (
-        ends_ref,
-        xs_ref,
-        ys_ref,
-        v_wide_ref,
-        dx_ref,
-        b_end_ref,
-        c_live_ref,
-        masks_ref,
-        db_ref,
-        dc_ref,
-        sums_ref,
-    ) = refs[:11]
-    own_ref, logs_ref, alog_ref, dt_ref, small_ref = refs[11:16] if final else [None] * 5
-    rest = refs[16:] if final else refs[11:]
-    outs = 5 if final else 4
-    rest, (stage_ref, sems) = rest[:-2], rest[-2:]
-    messages = rest[(1 if start else 0) * final : len(rest) - outs]
-    dx_out, db_out, dc_out, last_out, *partial_out = rest[len(rest) - outs :]
-    rows, columns = dx_ref.shape
-    heads, width = sums_ref.shape[1], db_ref.shape[0]
-    head_width = columns // heads
+    rate_grads = jnp.sum(logs * sums[:rows], axis=0, keepdims=True)
+    empty = jnp.zeros((1, LANES - 2 * heads), F32)
+    small_ref[...] = stack([rate_grads, products[:1], empty], 1)
+    for copy in copies:
+        copy.wait()
+
+
+def swap_order(reach):
+    return [0, *range(2, 2 * reach), 1]
+
+
+def rates_kernel(reach, head_width, *refs):
+    messages = [ref for _, ref in sorted(zip(swap_order(reach), refs), key=lambda pair: pair[0])]
+    ends_ref, fwd_ref, bwd_ref, small_ref, out_ref, came_ref, pull_ref = refs[2 * reach :]
+    width, columns = fwd_ref.shape
+    blocks = columns // WIDE
+    whole = []
+    for block in range(blocks):
+        at = slice(block * WIDE, (block + 1) * WIDE)
+        came, pull = received(messages, block, width)
+        came_ref[:, at] = came
+        pull_ref[:, at] = pull
+        terms = came * bwd_ref[:, at] + pull * (fwd_ref[:, at] + ends_ref[2:3, at] * came)
+        whole.append(jnp.sum(terms, axis=0, keepdims=True))
+    own = WIDE // head_width
+    shape = (WIDE, LANES)
+    column = lax.shift_right_logical(iota(shape, 0), log2(head_width))
+    ones = jnp.where(column == (iota(shape, 1) & (own - 1)), 1.0, 0.0).astype(BF16)
+    sums = sum(dot(part, ones, 1, 0) for part in split3(stack(whole, 0)))
+    lane = iota(sums.shape, 1)
+    mine = lax.shift_right_logical(lane, log2(own)) == iota(sums.shape, 0)
+    total = small_ref[...] + jnp.sum(jnp.where(mine, sums, 0.0), axis=0, keepdims=True)
+    out_ref[...] = jnp.broadcast_to(total, out_ref.shape)
+
+
+def outputs_kernel(
+    came_ref,
+    pull_ref,
+    ends_ref,
+    xs_ref,
+    ys_ref,
+    v_wide_hbm,
+    dx_hbm,
+    b_end_ref,
+    c_live_ref,
+    masks_ref,
+    db_ref,
+    dc_ref,
+    sums_ref,
+    alog_ref,
+    dt_ref,
+    dx_out,
+    db_out,
+    dc_out,
+    dt_out,
+    v_stage,
+    dx_stage,
+    stage,
+    in_sems,
+    out_sems,
+):
+    rows, columns = dx_hbm.shape
+    heads, width = dt_ref.shape[0], db_ref.shape[0]
+    blocks = columns // WIDE
+    copies = []
+    for block in range(blocks):
+        at = slice(block * WIDE, (block + 1) * WIDE)
+        for i, (source, target) in enumerate(((v_wide_hbm, v_stage), (dx_hbm, dx_stage))):
+            copy = pltpu.make_async_copy(
+                source.at[:, at], target.at[:, at], in_sems.at[i, block]
+            )
+            copy.start()
+            copies.append(copy)
     b_end, c_live = b_end_ref[...], c_live_ref[...]
-    sums = sums_ref[...]
+    own_sums = sums_ref[...]
+    sums = own_sums
     dc = jnp.zeros((2 * width, 2 * rows), F32)
     db = jnp.zeros((2 * width, 2 * rows), F32)
     at_last = iota((rows, WIDE), 0) == rows - 1
-    copies = []
-    for i in range(size):
-        block = start + i
+    sent = []
+    for block in range(blocks):
         at = slice(block * WIDE, (block + 1) * WIDE)
-        own = slice(i * WIDE, (i + 1) * WIDE)
-        ones = head_columns(heads, head_width, block)
-        came, pull = received(messages, i, width)
+        ones = head_columns(heads, columns // heads, block)
+        came, pull = came_ref[:, at], pull_ref[:, at]
         meet = jnp.sum(came * pull, axis=0, keepdims=True) * ends_ref[1:2, at]
         cames = stack(split2(came), 0)
         pulls = stack(split2(pull * ends_ref[0:1, at]), 0)
         xs, ys = xs_ref[:, at], ys_ref[:, at]
         out = dot(c_live, cames, 1, 0)
         back = dot(b_end, pulls, 1, 0)
-        stage_ref[:, own] = (dx_ref[:, at] + v_wide_ref[:, at] * back).astype(BF16)
-        copy = pltpu.make_async_copy(stage_ref.at[:, own], dx_out.at[0, :, at], sems.at[i])
-        copy.start()
-        copies.append(copy)
         column_part = (xs[:rows].astype(F32) + xs[rows:].astype(F32)) * back
         row_part = (ys[:rows].astype(F32) + ys[rows:].astype(F32)) * out
         row_part = jnp.where(at_last, row_part + meet, row_part)
-        for part in split3(stack([row_part - column_part, column_part], 0)):
+        for part in split2(stack([row_part - column_part, column_part], 0)):
             sums += dot(part, ones, 1, 0)
         dc += dot(cames, ys, 1, 1)
         db += dot(pulls, xs, 1, 1)
+        copies[2 * block].wait()
+        copies[2 * block + 1].wait()
+        stage[:, at] = (dx_stage[:, at] + v_stage[:, at] * back).astype(BF16)
+        copy = pltpu.make_async_copy(stage.at[:, at], dx_out.at[0, :, at], out_sems.at[block])
+        copy.start()
+        sent.append(copy)
     dc = (dc[:width, :rows] + dc[:width, rows:]) + dc[width:, :rows]
     db = (db[:width, :rows] + db[:width, rows:]) + db[width:, :rows]
-    db = db_ref[...] + masks_ref[0:width] * db
-    dc = dc_ref[...] + masks_ref[width : 2 * width] * dc
-    if final:
-        db_out[0] = db.astype(BF16)
-        dc_out[0] = dc.astype(BF16)
-        square = (rows, rows)
-        upper = jnp.where(iota(square, 0) >= iota(square, 1), 1.0, 0.0).astype(BF16)
-        eye = jnp.where(iota(square, 0) == iota(square, 1), 1.0, 0.0).astype(BF16)
-        at_end = jnp.sum(sums[rows:] - own_ref[rows:], axis=0, keepdims=True)
-        dl = sums[:rows] + jnp.where(iota((rows, heads), 0) == rows - 1, at_end, 0.0)
-        d_decay = sum(dot(part, upper, 0, 0) for part in split3(dl))
-        total = sum(dot(part, eye, 0, 0) for part in split3(sums[rows:]))
-        last_out[0] = total / dt_ref[...] + rate_column(alog_ref) * d_decay
-        rate_grads = jnp.sum(logs_ref[...] * dl, axis=0, keepdims=True)
-        empty = jnp.zeros((1, LANES - 2 * heads), F32)
-        row = stack([rate_grads, small_ref[:1], empty], 1)
-        partial_out[0][...] = jnp.broadcast_to(row, partial_out[0].shape)
-    else:
-        db_out[...] = db
-        dc_out[...] = dc
-        last_out[...] = sums
-    for copy in copies:
+    db_out[0] = (db_ref[...] + masks_ref[0:1] * db).astype(BF16)
+    dc_out[0] = (dc_ref[...] + masks_ref[1:2] * dc).astype(BF16)
+    square = (rows, rows)
+    upper = jnp.where(iota(square, 0) >= iota(square, 1), 1.0, 0.0).astype(BF16)
+    eye = jnp.where(iota(square, 0) == iota(square, 1), 1.0, 0.0).astype(BF16)
+    at_end = jnp.sum(sums[rows:] - own_sums[rows:], axis=0, keepdims=True)
+    dl = sums[:rows] + jnp.where(iota((rows, heads), 0) == rows - 1, at_end, 0.0)
+    d_decay = sum(dot(part, upper, 0, 0) for part in split3(dl))
+    total = sum(dot(part, eye, 0, 0) for part in split3(sums[rows:]))
+    dt_out[0] = total / dt_ref[...] + rate_column(alog_ref) * d_decay
+    for copy in sent:
         copy.wait()
 
 
-def call(kernel, reach, outs, ins, flops, moved, scratch=(), aliases=None):
+def call(kernel, reach, outs, ins, flops, moved, scratch=()):
     spaces = {"s": pltpu.SMEM, "v": pltpu.VMEM, "h": pltpu.HBM}
     return pl.pallas_call(
         kernel,
-        out_shape=[jax.ShapeDtypeStruct(*out) for _, out in outs],
+        out_shape=[
+            pltpu.HBM(*out) if place == "h" else jax.ShapeDtypeStruct(*out) for place, out in outs
+        ],
         in_specs=[pl.BlockSpec(memory_space=spaces[place]) for place, _ in ins],
         out_specs=[pl.BlockSpec(memory_space=spaces[place]) for place, _ in outs],
         scratch_shapes=scratch,
-        input_output_aliases=aliases or {},
         compiler_params=pltpu.CompilerParams(vmem_limit_bytes=min(16 + 2 * reach, 56) * 2**20),
         cost_estimate=pl.CostEstimate(flops=flops, bytes_accessed=moved, transcendentals=0),
     )(*(a for _, a in ins))
@@ -431,17 +480,13 @@
     alog, skip = a_log[None], skip_gain[None]
     bt, ct = jnp.swapaxes(b_proj, 1, 2), jnp.swapaxes(c_proj, 1, 2)
     blocks = columns // WIDE
-    sets = (blocks,)
     pieces = 4
 
     def v(shape, kind=F32):
         return "v", (shape, kind)
 
-    transposed = v((width, rows))
-    per_token = v((2 * rows, heads))
-
     dt, x, b, dy, c, *payloads = call(
-        functools.partial(states_kernel, reach, sets),
+        functools.partial(states_kernel, reach),
         reach,
         [
             v((heads, rows)),
@@ -450,7 +495,7 @@
             v((rows, columns), BF16),
             v((width, rows), BF16),
         ]
-        + [v((size * PARTS * (width + 1), LANES)) for size in sets for _ in range(2 * reach)],
+        + [v((columns // LANES * (width + 1), LANES))] * (2 * reach),
         [in_hbm(a) for a in (doc_lengths, alog, step_sizes, inputs, bt, grad_out, ct)],
         10**9,
         4 * 2**20,
@@ -461,48 +506,51 @@
             pltpu.SemaphoreType.DMA((2, pieces)),
         ],
     )
-    messages = [None] * len(payloads)
-    for at in range(len(payloads) - 1, -1, -1):
-        messages[at] = swap(payloads[at], at % (2 * reach) // 2 + 1, at % 2)
-    xs, ys, v_wide, dx, b_end, c_live, masks, db, dc, own_sums, logs, ends, small = call(
+    messages = [swap(payloads[at], at // 2 + 1, at % 2) for at in swap_order(reach)]
+    whole = "h", ((rows, columns), F32)
+    state = v((width, columns))
+    stage = pltpu.VMEM((rows, columns), F32)
+    transposed = v((width, rows))
+    xs, ys, v_wide, dx, b_end, c_live, masks, db, dc, sums, fwd_logs, bwd_logs, ends, small = call(
         inside_kernel,
         reach,
         [v((2 * rows, columns), BF16)] * 2
-        + [v((rows, columns))] * 2
+        + [whole] * 2
         + [v((rows, 2 * width), BF16)] * 2
-        + [v((2 * width, rows)), transposed, transposed, per_token]
-        + [v((rows, heads)), v((8, columns)), v((8, heads))],
+        + [v((8, rows)), transposed, transposed, v((2 * rows, heads))]
+        + [state, state, v((8, columns)), v((1, LANES))],
         [("s", doc_lengths)] + [("v", a) for a in (alog, skip, dt, x, b, dy, c)],
         4 * 10**9,
         12 * 2**20,
-    )
-    whole = "h", ((1, rows, columns), BF16)
-    sums, input_grads = own_sums, None
-    start = 0
-    for one, size in enumerate(sets):
-        final = one == len(sets) - 1
-        outs = [whole, transposed, transposed, per_token]
-        ins = [ends, xs, ys, v_wide, dx, b_end, c_live, masks, db, dc, sums]
-        if final:
-            ins += [own_sums, logs, alog, dt, small] + [input_grads] * (one > 0)
-            narrow = v((1, width, rows), BF16)
-            outs = [whole, narrow, narrow, v((1, heads, rows)), v((devices, LANES))]
-        ins = [("h" if a is input_grads else "v", a) for a in ins]
-        ins += [("v", a) for a in messages[2 * reach * one : 2 * reach * (one + 1)]]
-        results = call(
-            functools.partial(cross_kernel, start, size, final),
-            reach,
-            outs,
-            ins,
-            10**9,
-            8 * 2**20,
-            [pltpu.VMEM((rows, size * WIDE), BF16), pltpu.SemaphoreType.DMA((size,))],
-            {16: 0} if final and one else None,
-        )
-        start += size
-        if not final:
-            input_grads, db, dc, sums = results
-    input_grads, b_gradient, c_gradient, step_grads, partial = results
+        [stage, stage, pltpu.SemaphoreType.DMA((2, blocks))],
+    )
+    partial, came, pull = call(
+        functools.partial(rates_kernel, reach, columns // heads),
+        reach,
+        [v((devices, LANES)), state, state],
+        [("v", a) for a in (*messages, ends, fwd_logs, bwd_logs, small)],
+        10**8,
+        4 * 2**20,
+    )
+    input_grads, b_gradient, c_gradient, step_grads = call(
+        outputs_kernel,
+        reach,
+        [("h", ((1, rows, columns), BF16))]
+        + [v((1, width, rows), BF16)] * 2
+        + [v((1, heads, rows))],
+        [("v", a) for a in (came, pull, ends, xs, ys)]
+        + [in_hbm(v_wide), in_hbm(dx)]
+        + [("v", a) for a in (b_end, c_live, masks, db, dc, sums, alog, dt)],
+        2 * 10**9,
+        12 * 2**20,
+        [
+            stage,
+            stage,
+            pltpu.VMEM((rows, columns), BF16),
+            pltpu.SemaphoreType.DMA((2, blocks)),
+            pltpu.SemaphoreType.DMA((blocks,)),
+        ],
+    )
     gathered = lax.all_to_all(partial, ("dp", "ctx"), 0, 0, tiled=True)
     totals = jnp.sum(gathered, axis=0)
     return (

time: 50.7 us -> 47.4 us (0.935)
  starting transfers between devices: 7.27 us -> 22.9 us
  blocking collectives: 12.9 us -> 0 us
  waiting for transfers between devices: 16.7 us -> 6.05 us
  Pallas kernels: 11.7 us -> 16.2 us
    all_to_all x0 -> x1, starting transfers between devices: none -> 16.9 us  [per_device(): gathered = lax.all_to_all(partial, ('dp', 'ctx'), 0, 0, tiled=True)]
    all_to_all x1 -> x0, blocking collectives: 12.9 us -> none  [per_device(): gathered = lax.all_to_all(partial, ('dp', 'ctx'), 0, 0, tiled=True)]
    ppermute x4, waiting for transfers between devices: 16.7 us -> 4.48 us  [swap(): return lax.ppermute(a, 'ctx', pairs)]
    pallas_call x3 -> x4, Pallas kernels: 11.7 us -> 16.2 us  [call(): pl.pallas_call(kernel, out_shape=[pltpu.HBM(*out) if place == 'h' else ja...]
    all_to_all x0 -> x1, waiting for transfers between devices: none -> 1.56 us  [per_device(): gathered = lax.all_to_all(partial, ('dp', 'ctx'), 0, 0, tiled=True)]
    ppermute x4, starting transfers between devices: 7.27 us -> 5.99 us  [swap(): return lax.ppermute(a, 'ctx', pairs)]
  transfers between devices with their start and end apart: 4 -> 5, of which waited for: 2 -> 3; matrix products, arithmetic and copies ran while one was open for 0% -> 0% of each run, Pallas kernels for 10% -> 26%
where the time goes in v4:
time: 47.4 us; the launch traced here: 47.2 us
  starting transfers between devices  22.9 us (48%)
  Pallas kernels  16.2 us (34%)
  waiting for transfers between devices  6.05 us (13%)
  local copies, waits for them, and re-layouts  1.25 us (3%)
  between operations  0.71 us (1%)
    all_to_all x1, starting transfers between devices, per_device(): gathered = lax.all_to_all(partial, ('dp', 'ctx'), 0, 0, tiled=True)  16.9 us
    pallas_call x4, Pallas kernels, call(): pl.pallas_call(kernel, out_shape=[pltpu.HBM(*out) if place == 'h' else ja...  16.2 us
    ppermute x4, starting transfers between devices, swap(): return lax.ppermute(a, 'ctx', pairs)  5.99 us
    ppermute x4, waiting for transfers between devices, swap(): return lax.ppermute(a, 'ctx', pairs)  4.48 us
    all_to_all x1, waiting for transfers between devices, per_device(): gathered = lax.all_to_all(partial, ('dp', 'ctx'), 0, 0, tiled=True)  1.56 us
  transfers between devices with their start and end apart: 5, of which 3 were waited for; matrix products, arithmetic and copies ran while one was open for 0% of the time, Pallas kernels for 26%

profile of v4, /device:TPU:0, one launch (start us, length us, event | category | flops | bytes accessed | tf_op | source)
XLA Modules:
  0.0 47.2 jit_solution(14079606618349634610)
XLA Ops:
  0.6 2.8 %shard_map.127 = (f32[32,128]{1,0:T(8,128)S(1)}, bf16[128,2048]{1,0:T(8,128)(2,1)S(1)}, bf16[64,128]{1,0:T(8,128)(2,1)S(1)}, bf16[128,2048]{1,0:T(8,128)(2,1)S(1...) custom-call(s32[1,16]{1,0:T(1,128)} %lens_ref.1, ...), custom_call_target="tpu_custom_call" | custom-call | flops 1000000000 | bytes 4194304 | tf_op jit(solution)/shard_map/pallas_call | solution.py:449
  3.5 3.0 %collective-permute-start = (f32[1040,128]{1,0:T(8,128)S(1)}, f32[1040,128]{1,0:T(8,128)S(1)}, u32[]{:S(2)}, u32[]{:S(2)}) collective-permute-start(f32[1040,128]{1,0:T(8,128)S(1)} %get-tuple-element.36), channel_id=1, source_target_pairs={{0,1},{1,0},{2,3},{3,2},{4,5},{5,4},{6,7},{7,6},{8,9},{9,8},{10,11... | collective-permute-start | bytes 1597448 | tf_op jit(solution)/shard_map/ppermute | solution.py:468
  6.5 1.6 %collective-permute-start.1 = (f32[1040,128]{1,0:T(8,128)S(1)}, f32[1040,128]{1,0:T(8,128)S(1)}, u32[]{:S(2)}, u32[]{:S(2)}) collective-permute-start(f32[1040,128]{1,0:T(8,128)S(1)} %get-tuple-element.37), channel_id=1, source_target_pairs={{0,2},{2,0},{1,3},{3,1},{4,6},{6,4},{5,7},{7,5},{8,10},{10,8},{9,1... | collective-permute-start | bytes 1597448 | tf_op jit(solution)/shard_map/ppermute | solution.py:468
  8.1 0.7 %collective-permute-start.2 = (f32[1040,128]{1,0:T(8,128)S(1)}, f32[1040,128]{1,0:T(8,128)S(1)}, u32[]{:S(2)}, u32[]{:S(2)}) collective-permute-start(f32[1040,128]{1,0:T(8,128)S(1)} %get-tuple-element.38), channel_id=1, source_target_pairs={{2,4},{4,2},{3,5},{5,3},{10,12},{12,10},{11,13},{13,11},{18,20},{2... | collective-permute-start | bytes 1597448 | tf_op jit(solution)/shard_map/ppermute | solution.py:468
  8.8 0.7 %collective-permute-start.3 = (f32[1040,128]{1,0:T(8,128)S(1)}, f32[1040,128]{1,0:T(8,128)S(1)}, u32[]{:S(2)}, u32[]{:S(2)}) collective-permute-start(f32[1040,128]{1,0:T(8,128)S(1)} %get-tuple-element.39), channel_id=1, source_target_pairs={{1,2},{2,1},{3,4},{4,3},{5,6},{6,5},{9,10},{10,9},{11,12},{12,11},... | collective-permute-start | bytes 1597448 | tf_op jit(solution)/shard_map/ppermute | solution.py:468
  9.5 0.0 copy-start
  9.5 0.0 copy-start.1
  9.5 0.0 copy-start.2
  9.5 0.6 %copy-done = s32[1,16]{1,0:T(1,128)S(1)} copy-done((s32[1,16]{1,0:T(1,128)S(1)}, s32[1,16]{1,0:T(1,128)}, u32[]{:S(2)}) %copy-start) | copy-done | bytes 88
  10.1 0.0 copy-done.1
  10.1 0.0 copy-done.2
  10.2 6.9 %shard_map.128 = (bf16[256,2048]{1,0:T(8,128)(2,1)S(1)}, bf16[256,2048]{1,0:T(8,128)(2,1)S(1)}, f32[128,2048]{1,0:T(8,128)}, f32[128,2048]{1,0:T(8,128)}, bf16[1...) custom-call(s32[1,16]{1,0:T(1,128)S(1)} %copy-done, ...), custom_call_target="tpu_custom_call" | custom-call | flops 4000000000 | bytes 12582912 | tf_op jit(solution)/shard_map/pallas_call | solution.py:449
  17.0 1.6 %collective-permute-done.refs_0_ = f32[1040,128]{1,0:T(8,128)S(1)} collective-permute-done((f32[1040,128]{1,0:T(8,128)S(1)}, f32[1040,128]{1,0:T(8,128)S(1)}, u32[]{:S(2)}, u32[]{:S(2)}) %collective-permute-start) | collective-permute-done | bytes 532512 | tf_op jit(solution)/shard_map/ppermute | solution.py:468
  18.6 2.9 %collective-permute-done.1.refs_1_ = f32[1040,128]{1,0:T(8,128)S(1)} collective-permute-done((f32[1040,128]{1,0:T(8,128)S(1)}, f32[1040,128]{1,0:T(8,128)S(1)}, u32[]{:S(2)}, u32[]{:S(2)}) %collective-permute-start.1) | collective-permute-done | bytes 532512 | tf_op jit(solution)/shard_map/ppermute | solution.py:468
  21.5 0.0 collective-permute-done.2.refs_2_
  21.5 0.0 collective-permute-done.3.refs_3_
  21.5 1.1 %shard_map.129 = (f32[32,128]{1,0:T(8,128)}, f32[64,2048]{1,0:T(8,128)S(1)}, f32[64,2048]{1,0:T(8,128)S(1)}) custom-call(f32[1040,128]{1,0:T(8,128)S(1)} %collective-permute-done.refs_0_, f32[1040,128]{1,0:T(8,128)S(1)} %collective-permute-done.1.refs_1_, f32[1040,128]{1,0:T(8,128)S(1)} %collective-permute-done.2.refs_2_, ...), custom_call_target="tpu_custom_call" | custom-call | flops 100000000 | bytes 4194304 | tf_op jit(solution)/shard_map/pallas_call | solution.py:449
  22.7 16.9 %all-to-all-start = ((f32[32,1,128]{2,1,0:T(1,128)}), f32[32,1,128]{2,1,0:T(1,128)S(1)}, u32[]{:S(2)}, u32[]{:S(2)}) async-start(f32[32,1,128]{2,1,0:T(1,128)} %bitcast.7), calls=%async_computation | async-start | bytes 32768 | tf_op jit(solution)/shard_map/all_to_all | solution.py:554
  39.6 5.4 %shard_map.130 = (bf16[1,128,2048]{2,1,0:T(8,128)(2,1)}, bf16[1,64,128]{2,1,0:T(8,128)(2,1)}, bf16[1,64,128]{2,1,0:T(8,128)(2,1)}, f32[1,32,128]{2,1,0:T(8,128)}) custom-call(f32[64,2048]{1,0:T(8,128)S(1)} %get-tuple-element.49.came_ref, f32[64,2048]{1,0:T(8,128)S(1)} %get-tuple-element.50.pull_ref, f32[8,2048]{1,0:T(8,128)S(1)} %get-tuple-element.45.refs_4_.ends_ref, ...), custom_call_target="tpu_custom_call" | custom-call | flops 2000000000 | bytes 12582912 | tf_op jit(solution)/shard_map/pallas_call | solution.py:449
  45.0 1.6 %all-to-all-done = f32[32,1,128]{2,1,0:T(1,128)S(1)} async-done(((f32[32,1,128]{2,1,0:T(1,128)}), f32[32,1,128]{2,1,0:T(1,128)S(1)}, u32[]{:S(2)}, u32[]{:S(2)}) %all-to-all-start) | async-done | bytes 16416 | tf_op jit(solution)/shard_map/all_to_all | solution.py:554
  46.6 0.1 reduce_sum.9
  46.6 0.6 %fusion = (f32[32]{0:T(128)}, f32[32]{0:T(128)}) fusion(f32[128]{0:T(128)S(1)} %reduce_sum.9), kind=kLoop, calls=%fused_computation | loop fusion | bytes 512 | tf_op jit(solution)/shard_map/slice | solution.py:562
Async XLA Ops:
  3.5 15.1 %collective-permute-start = (f32[1040,128]{1,0:T(8,128)S(1)}, f32[1040,128]{1,0:T(8,128)S(1)}, u32[]{:S(2)}, u32[]{:S(2)}) collective-permute-start(f32[1040,128]{1,0:T(8,128)S(1)} %get-tuple-element.36), channel_id=1, source_target_pairs={{0,1},{1,0},{2,3},{3,2},{4,5},{5,4},{6,7},{7,6},{8,9},{9,8},{10,11... | collective-permute-start | bytes 1597448 | tf_op jit(solution)/shard_map/ppermute | solution.py:468
  6.5 15.0 %collective-permute-start.1 = (f32[1040,128]{1,0:T(8,128)S(1)}, f32[1040,128]{1,0:T(8,128)S(1)}, u32[]{:S(2)}, u32[]{:S(2)}) collective-permute-start(f32[1040,128]{1,0:T(8,128)S(1)} %get-tuple-element.37), channel_id=1, source_target_pairs={{0,2},{2,0},{1,3},{3,1},{4,6},{6,4},{5,7},{7,5},{8,10},{10,8},{9,1... | collective-permute-start | bytes 1597448 | tf_op jit(solution)/shard_map/ppermute | solution.py:468
  8.1 13.5 %collective-permute-start.2 = (f32[1040,128]{1,0:T(8,128)S(1)}, f32[1040,128]{1,0:T(8,128)S(1)}, u32[]{:S(2)}, u32[]{:S(2)}) collective-permute-start(f32[1040,128]{1,0:T(8,128)S(1)} %get-tuple-element.38), channel_id=1, source_target_pairs={{2,4},{4,2},{3,5},{5,3},{10,12},{12,10},{11,13},{13,11},{18,20},{2... | collective-permute-start | bytes 1597448 | tf_op jit(solution)/shard_map/ppermute | solution.py:468
  8.8 12.8 %collective-permute-start.3 = (f32[1040,128]{1,0:T(8,128)S(1)}, f32[1040,128]{1,0:T(8,128)S(1)}, u32[]{:S(2)}, u32[]{:S(2)}) collective-permute-start(f32[1040,128]{1,0:T(8,128)S(1)} %get-tuple-element.39), channel_id=1, source_target_pairs={{1,2},{2,1},{3,4},{4,3},{5,6},{6,5},{9,10},{10,9},{11,12},{12,11},... | collective-permute-start | bytes 1597448 | tf_op jit(solution)/shard_map/ppermute | solution.py:468
  9.5 0.7 %copy-start = (s32[1,16]{1,0:T(1,128)S(1)}, s32[1,16]{1,0:T(1,128)}, u32[]{:S(2)}) copy-start(s32[1,16]{1,0:T(1,128)} %lens_ref.1) | copy-start | bytes 196
  9.5 0.7 %copy-start.1 = (f32[32]{0:T(128)S(1)}, f32[32]{0:T(128)}, u32[]{:S(2)}) copy-start(f32[32]{0:T(128)} %param.13) | copy-start | bytes 388
  9.5 0.7 %copy-start.2 = (f32[32]{0:T(128)S(1)}, f32[32]{0:T(128)}, u32[]{:S(2)}) copy-start(f32[32]{0:T(128)} %param.12) | copy-start | bytes 388
  22.7 23.9 %all-to-all-start = ((f32[32,1,128]{2,1,0:T(1,128)}), f32[32,1,128]{2,1,0:T(1,128)S(1)}, u32[]{:S(2)}, u32[]{:S(2)}) async-start(f32[32,1,128]{2,1,0:T(1,128)} %bitcast.7), calls=%async_computation | async-start | bytes 32768 | tf_op jit(solution)/shard_map/all_to_all | solution.py:554

commit v5 on v4

--- a/solution.py
+++ b/solution.py
@@ -13,6 +13,7 @@
 WIDE = 256
 PARTS = WIDE // LANES
 FAR = 2**30
+PIECES = 4
 
 
 def dot(a, b, ca, cb):
@@ -44,7 +45,7 @@
 
 
 def document_places(lens_ref, rows):
-    offset = lax.axis_index("ctx") * rows
+    offset = shard() * rows
     starts = [jnp.int32(0)]
     for d in range(lens_ref.shape[1] - 1):
         starts.append(starts[-1] + lens_ref[0, d])
@@ -85,8 +86,8 @@
     return jnp.where(iota(shape, 1) - column == block * (WIDE // head_width), 1.0, 0.0).astype(BF16)
 
 
-def is_odd(distance):
-    return lax.rem(lax.div(lax.axis_index("ctx"), distance), 2)
+def shard():
+    return lax.axis_index("ctx")
 
 
 def message_block(ref, block, width):
@@ -104,20 +105,19 @@
     for j in range(len(refs) // 2, 0, -1):
         one, two = refs[2 * j - 2], refs[2 * j - 1]
         a, b = message_block(one, block, width), message_block(two, block, width)
-        odd = jnp.broadcast_to(is_odd(j), a.shape) == 1
-        near_came, near_pull = jnp.where(odd, a, b), jnp.where(odd, b, a)
+        first = jnp.broadcast_to(lax.rem(shard() + j, 2), a.shape) == 0
+        near_came, near_pull = jnp.where(first, a, b), jnp.where(first, b, a)
         if came is None:
             came, pull = near_came, near_pull
         else:
             a, b = message_tail(one, block, width), message_tail(two, block, width)
-            odd = jnp.broadcast_to(is_odd(j), a.shape) == 1
-            came = near_came + jnp.where(odd, a, b) * came
-            pull = near_pull + jnp.where(odd, b, a) * pull
+            first = jnp.broadcast_to(lax.rem(shard() + j, 2), a.shape) == 0
+            came = near_came + jnp.where(first, a, b) * came
+            pull = near_pull + jnp.where(first, b, a) * pull
     return came, pull
 
 
 def states_kernel(
-    reach,
     lens_hbm,
     alog_hbm,
     dt_hbm,
@@ -130,14 +130,17 @@
     b_ref,
     dy_ref,
     c_ref,
-    *refs,
+    one_ref,
+    two_ref,
+    lens_ref,
+    alog_ref,
+    small_sems,
+    sems,
 ):
-    payloads, (lens_ref, alog_ref, small_sems, sems) = refs[:-4], refs[-4:]
     rows, columns = x_ref.shape
     heads, width = dt_ref.shape[0], b_ref.shape[0]
     head_width = columns // heads
-    pieces = sems.shape[1]
-    piece = columns // pieces
+    piece = columns // PIECES
     small = [
         pltpu.make_async_copy(source, target, small_sems.at[i])
         for i, (source, target) in enumerate(
@@ -153,7 +156,7 @@
     for copy in small:
         copy.start()
     large = []
-    for i in range(pieces):
+    for i in range(PIECES):
         at = slice(i * piece, (i + 1) * piece)
         for side, (source, target) in enumerate(((x_hbm, x_ref), (dy_hbm, dy_ref))):
             copy = pltpu.make_async_copy(
@@ -163,9 +166,7 @@
             large.append(copy)
     square = (rows, rows)
     upper = jnp.where(iota(square, 0) <= iota(square, 1), 1.0, 0.0).astype(BF16)
-    odds = [
-        jnp.broadcast_to(is_odd(j), (width, LANES)) == 1 for j in range(1, reach + 1)
-    ]
+    even = jnp.broadcast_to(lax.rem(shard(), 2), (width, LANES)) == 0
     left = iota((1, LANES), 1) < head_width
     for copy in small:
         copy.wait()
@@ -181,11 +182,10 @@
     b, c = b_ref[...].astype(F32), c_ref[...].astype(F32)
     own = LANES // head_width
 
-    def pair_states(vectors, weights, values, pair):
+    def pair_states(vectors, weights, values):
         parts = []
         for h in range(own):
-            row = weights[pair * own + h : pair * own + h + 1, :]
-            parts += split2(vectors * row)
+            parts += split2(vectors * weights[h : h + 1, :])
         out = dot(stack(parts, 0), values, 1, 0)
         sides = [
             out[2 * h * width : (2 * h + 1) * width]
@@ -199,15 +199,14 @@
             large[pair * LANES // piece * 2].wait()
             large[pair * LANES // piece * 2 + 1].wait()
         at = slice(pair * LANES, (pair + 1) * LANES)
-        state = pair_states(b, keeping, x_ref[:, at], pair)
-        pulled = pair_states(c, carried, dy_ref[:, at], pair)
-        here = kept[pair * own : (pair + 1) * own]
+        here = slice(pair * own, (pair + 1) * own)
+        state = pair_states(b, keeping[here], x_ref[:, at])
+        pulled = pair_states(c, carried[here], dy_ref[:, at])
         tail = columns // LANES * width + pair
-        for j in range(reach):
-            values = jnp.where(odds[j], pulled, state), jnp.where(odds[j], state, pulled)
-            for ref, value in zip(payloads[2 * j : 2 * j + 2], values):
-                ref[pair * width : (pair + 1) * width, :] = value
-                ref[tail : tail + 1, :] = jnp.where(left, here[:1], here[1:])
+        one_ref[pair * width : (pair + 1) * width, :] = jnp.where(even, state, pulled)
+        two_ref[pair * width : (pair + 1) * width, :] = jnp.where(even, pulled, state)
+        one_ref[tail : tail + 1, :] = jnp.where(left, kept[here][:1], kept[here][1:])
+        two_ref[tail : tail + 1, :] = jnp.where(left, kept[here][:1], kept[here][1:])
 
 
 def inside_kernel(
@@ -332,12 +331,12 @@
         copy.wait()
 
 
-def swap_order(reach):
-    return [0, *range(2, 2 * reach), 1]
+def send_order(reach):
+    return [*range(0, 2 * reach, 2), *range(1, 2 * reach, 2)]
 
 
 def rates_kernel(reach, head_width, *refs):
-    messages = [ref for _, ref in sorted(zip(swap_order(reach), refs), key=lambda pair: pair[0])]
+    messages = [ref for _, ref in sorted(zip(send_order(reach), refs), key=lambda pair: pair[0])]
     ends_ref, fwd_ref, bwd_ref, small_ref, out_ref, came_ref, pull_ref = refs[2 * reach :]
     width, columns = fwd_ref.shape
     blocks = columns // WIDE
@@ -459,13 +458,10 @@
     )(*(a for _, a in ins))
 
 
-def swap(a, by, second):
+def send(a, by, second):
     count = lax.axis_size("ctx")
-    pairs = []
-    for i in range(count - by):
-        if i // by % 2 == second:
-            pairs += [(i, i + by), (i + by, i)]
-    return lax.ppermute(a, "ctx", pairs)
+    pairs = [(i, i + by if (i + second) % 2 == 0 else i - by) for i in range(count)]
+    return lax.ppermute(a, "ctx", [(i, j) for i, j in pairs if 0 <= j < count])
 
 
 def in_hbm(a):
@@ -480,13 +476,12 @@
     alog, skip = a_log[None], skip_gain[None]
     bt, ct = jnp.swapaxes(b_proj, 1, 2), jnp.swapaxes(c_proj, 1, 2)
     blocks = columns // WIDE
-    pieces = 4
 
     def v(shape, kind=F32):
         return "v", (shape, kind)
 
     dt, x, b, dy, c, *payloads = call(
-        functools.partial(states_kernel, reach),
+        states_kernel,
         reach,
         [
             v((heads, rows)),
@@ -495,7 +490,7 @@
             v((rows, columns), BF16),
             v((width, rows), BF16),
         ]
-        + [v((columns // LANES * (width + 1), LANES))] * (2 * reach),
+        + [v((columns // LANES * (width + 1), LANES))] * 2,
         [in_hbm(a) for a in (doc_lengths, alog, step_sizes, inputs, bt, grad_out, ct)],
         10**9,
         4 * 2**20,
@@ -503,10 +498,10 @@
             pltpu.SMEM(doc_lengths.shape, jnp.int32),
             pltpu.VMEM(alog.shape, F32),
             pltpu.SemaphoreType.DMA((5,)),
-            pltpu.SemaphoreType.DMA((2, pieces)),
+            pltpu.SemaphoreType.DMA((2, PIECES)),
         ],
     )
-    messages = [swap(payloads[at], at // 2 + 1, at % 2) for at in swap_order(reach)]
+    messages = [send(payloads[at % 2], at // 2 + 1, at % 2) for at in send_order(reach)]
     whole = "h", ((rows, columns), F32)
     state = v((width, columns))
     stage = pltpu.VMEM((rows, columns), F32)

time: 47.4 us -> 50.4 us (1.063)
  waiting for transfers between devices: 6.05 us -> 18.4 us
  starting transfers between devices: 22.9 us -> 13.5 us
    ppermute x4, waiting for transfers between devices: 4.48 us -> 16.9 us  [send(): return lax.ppermute(a, 'ctx', [(i, j) for i, j in pairs if 0 <= j < count])]
    all_to_all x1, starting transfers between devices: 16.9 us -> 4.93 us  [per_device(): gathered = lax.all_to_all(partial, ('dp', 'ctx'), 0, 0, tiled=True)]
    ppermute x4, starting transfers between devices: 5.99 us -> 8.52 us  [send(): return lax.ppermute(a, 'ctx', [(i, j) for i, j in pairs if 0 <= j < count])]
  transfers between devices with their start and end apart: 5 -> 5, of which waited for: 3 -> 3; matrix products, arithmetic and copies ran while one was open for 0% -> 0% of each run, Pallas kernels for 26% -> 24%
where the time goes in v5:
time: 50.4 us; the launch traced here: 50.1 us
  waiting for transfers between devices  18.4 us (37%)
  Pallas kernels  16.2 us (32%)
  starting transfers between devices  13.5 us (27%)
  local copies, waits for them, and re-layouts  1.25 us (2%)
  between operations  0.72 us (1%)
    ppermute x4, waiting for transfers between devices, send(): return lax.ppermute(a, 'ctx', [(i, j) for i, j in pairs if 0 <= j < count])  16.9 us
    pallas_call x4, Pallas kernels, call(): pl.pallas_call(kernel, out_shape=[pltpu.HBM(*out) if place == 'h' else ja...  16.2 us
    ppermute x4, starting transfers between devices, send(): return lax.ppermute(a, 'ctx', [(i, j) for i, j in pairs if 0 <= j < count])  8.52 us
    all_to_all x1, starting transfers between devices, per_device(): gathered = lax.all_to_all(partial, ('dp', 'ctx'), 0, 0, tiled=True)  4.93 us
    all_to_all x1, waiting for transfers between devices, per_device(): gathered = lax.all_to_all(partial, ('dp', 'ctx'), 0, 0, tiled=True)  1.57 us
  transfers between devices with their start and end apart: 5, of which 3 were waited for; matrix products, arithmetic and copies ran while one was open for 0% of the time, Pallas kernels for 24%

profile of v5, /device:TPU:0, one launch (start us, length us, event | category | flops | bytes accessed | tf_op | source)
XLA Modules:
  0.0 50.1 jit_solution(4899333341495159691)
XLA Ops:
  0.6 2.8 %shard_map.127 = (f32[32,128]{1,0:T(8,128)S(1)}, bf16[128,2048]{1,0:T(8,128)(2,1)S(1)}, bf16[64,128]{1,0:T(8,128)(2,1)S(1)}, bf16[128,2048]{1,0:T(8,128)(2,1)S(1...) custom-call(s32[1,16]{1,0:T(1,128)} %lens_ref.1, f32[1,32]{1,0:T(1,128)} %bitcast.10, ...), custom_call_target="tpu_custom_call" | custom-call | flops 1000000000 | bytes 4194304 | tf_op jit(solution)/shard_map/pallas_call | solution.py:448
  3.5 3.0 %collective-permute-start = (f32[1040,128]{1,0:T(8,128)S(1)}, f32[1040,128]{1,0:T(8,128)S(1)}, u32[]{:S(2)}, u32[]{:S(2)}) collective-permute-start(f32[1040,128]{1,0:T(8,128)S(1)} %get-tuple-element.34), channel_id=1, source_target_pairs={{0,1},{1,0},{2,3},{3,2},{4,5},{5,4},{6,7},{7,6},{8,9},{9,8},{10,11... | collective-permute-start | bytes 1597448 | tf_op jit(solution)/shard_map/ppermute | solution.py:464
  6.5 3.5 %collective-permute-start.1 = (f32[1040,128]{1,0:T(8,128)S(1)}, f32[1040,128]{1,0:T(8,128)S(1)}, u32[]{:S(2)}, u32[]{:S(2)}) collective-permute-start(f32[1040,128]{1,0:T(8,128)S(1)} %get-tuple-element.34), channel_id=1, source_target_pairs={{0,2},{2,4},{3,1},{4,6},{5,3},{7,5},{8,10},{10,12},{11,9},{12,14},... | collective-permute-start | bytes 1597448 | tf_op jit(solution)/shard_map/ppermute | solution.py:464
  10.0 0.7 %collective-permute-start.2 = (f32[1040,128]{1,0:T(8,128)S(1)}, f32[1040,128]{1,0:T(8,128)S(1)}, u32[]{:S(2)}, u32[]{:S(2)}) collective-permute-start(f32[1040,128]{1,0:T(8,128)S(1)} %get-tuple-element.35), channel_id=1, source_target_pairs={{1,2},{2,1},{3,4},{4,3},{5,6},{6,5},{9,10},{10,9},{11,12},{12,11},... | collective-permute-start | bytes 1597448 | tf_op jit(solution)/shard_map/ppermute | solution.py:464
  10.7 1.3 %collective-permute-start.3 = (f32[1040,128]{1,0:T(8,128)S(1)}, f32[1040,128]{1,0:T(8,128)S(1)}, u32[]{:S(2)}, u32[]{:S(2)}) collective-permute-start(f32[1040,128]{1,0:T(8,128)S(1)} %get-tuple-element.35), channel_id=1, source_target_pairs={{1,3},{2,0},{3,5},{4,2},{5,7},{6,4},{9,11},{10,8},{11,13},{12,10},... | collective-permute-start | bytes 1597448 | tf_op jit(solution)/shard_map/ppermute | solution.py:464
  12.0 0.0 copy-start
  12.0 0.0 copy-start.1
  12.0 0.0 copy-start.2
  12.0 0.6 %copy-done = s32[1,16]{1,0:T(1,128)S(1)} copy-done((s32[1,16]{1,0:T(1,128)S(1)}, s32[1,16]{1,0:T(1,128)}, u32[]{:S(2)}) %copy-start) | copy-done | bytes 88
  12.7 0.0 copy-done.1
  12.7 0.0 copy-done.2
  12.7 6.9 %shard_map.128 = (bf16[256,2048]{1,0:T(8,128)(2,1)S(1)}, bf16[256,2048]{1,0:T(8,128)(2,1)S(1)}, f32[128,2048]{1,0:T(8,128)}, f32[128,2048]{1,0:T(8,128)}, bf16[1...) custom-call(s32[1,16]{1,0:T(1,128)S(1)} %copy-done, ...), custom_call_target="tpu_custom_call" | custom-call | flops 4000000000 | bytes 12582912 | tf_op jit(solution)/shard_map/pallas_call | solution.py:448
  19.6 9.7 %collective-permute-done.refs_0_ = f32[1040,128]{1,0:T(8,128)S(1)} collective-permute-done((f32[1040,128]{1,0:T(8,128)S(1)}, f32[1040,128]{1,0:T(8,128)S(1)}, u32[]{:S(2)}, u32[]{:S(2)}) %collective-permute-start) | collective-permute-done | bytes 532512 | tf_op jit(solution)/shard_map/ppermute | solution.py:464
  29.3 0.0 collective-permute-done.1.refs_1_
  29.3 0.0 collective-permute-done.2.refs_2_
  29.3 7.2 %collective-permute-done.3.refs_3_ = f32[1040,128]{1,0:T(8,128)S(1)} collective-permute-done((f32[1040,128]{1,0:T(8,128)S(1)}, f32[1040,128]{1,0:T(8,128)S(1)}, u32[]{:S(2)}, u32[]{:S(2)}) %collective-permute-start.3) | collective-permute-done | bytes 532512 | tf_op jit(solution)/shard_map/ppermute | solution.py:464
  36.4 1.1 %shard_map.129 = (f32[32,128]{1,0:T(8,128)}, f32[64,2048]{1,0:T(8,128)S(1)}, f32[64,2048]{1,0:T(8,128)S(1)}) custom-call(f32[1040,128]{1,0:T(8,128)S(1)} %collective-permute-done.refs_0_, f32[1040,128]{1,0:T(8,128)S(1)} %collective-permute-done.1.refs_1_, f32[1040,128]{1,0:T(8,128)S(1)} %collective-permute-done.2.refs_2_, ...), custom_call_target="tpu_custom_call" | custom-call | flops 100000000 | bytes 4194304 | tf_op jit(solution)/shard_map/pallas_call | solution.py:448
  37.6 4.9 %all-to-all-start = ((f32[32,1,128]{2,1,0:T(1,128)}), f32[32,1,128]{2,1,0:T(1,128)S(1)}, u32[]{:S(2)}, u32[]{:S(2)}) async-start(f32[32,1,128]{2,1,0:T(1,128)} %bitcast.7), calls=%async_computation | async-start | bytes 32768 | tf_op jit(solution)/shard_map/all_to_all | solution.py:549
  42.5 5.4 %shard_map.130 = (bf16[1,128,2048]{2,1,0:T(8,128)(2,1)}, bf16[1,64,128]{2,1,0:T(8,128)(2,1)}, bf16[1,64,128]{2,1,0:T(8,128)(2,1)}, f32[1,32,128]{2,1,0:T(8,128)}) custom-call(f32[64,2048]{1,0:T(8,128)S(1)} %get-tuple-element.45.came_ref, f32[64,2048]{1,0:T(8,128)S(1)} %get-tuple-element.46.pull_ref, f32[8,2048]{1,0:T(8,128)S(1)} %get-tuple-element.41.refs_4_.ends_ref, ...), custom_call_target="tpu_custom_call" | custom-call | flops 2000000000 | bytes 12582912 | tf_op jit(solution)/shard_map/pallas_call | solution.py:448
  47.9 1.6 %all-to-all-done = f32[32,1,128]{2,1,0:T(1,128)S(1)} async-done(((f32[32,1,128]{2,1,0:T(1,128)}), f32[32,1,128]{2,1,0:T(1,128)S(1)}, u32[]{:S(2)}, u32[]{:S(2)}) %all-to-all-start) | async-done | bytes 16416 | tf_op jit(solution)/shard_map/all_to_all | solution.py:549
  49.5 0.1 reduce_sum.9
  49.5 0.6 %fusion = (f32[32]{0:T(128)}, f32[32]{0:T(128)}) fusion(f32[128]{0:T(128)S(1)} %reduce_sum.9), kind=kLoop, calls=%fused_computation | loop fusion | bytes 512 | tf_op jit(solution)/shard_map/slice | solution.py:557
Async XLA Ops:
  3.5 25.8 %collective-permute-start = (f32[1040,128]{1,0:T(8,128)S(1)}, f32[1040,128]{1,0:T(8,128)S(1)}, u32[]{:S(2)}, u32[]{:S(2)}) collective-permute-start(f32[1040,128]{1,0:T(8,128)S(1)} %get-tuple-element.34), channel_id=1, source_target_pairs={{0,1},{1,0},{2,3},{3,2},{4,5},{5,4},{6,7},{7,6},{8,9},{9,8},{10,11... | collective-permute-start | bytes 1597448 | tf_op jit(solution)/shard_map/ppermute | solution.py:464
  6.5 22.8 %collective-permute-start.1 = (f32[1040,128]{1,0:T(8,128)S(1)}, f32[1040,128]{1,0:T(8,128)S(1)}, u32[]{:S(2)}, u32[]{:S(2)}) collective-permute-start(f32[1040,128]{1,0:T(8,128)S(1)} %get-tuple-element.34), channel_id=1, source_target_pairs={{0,2},{2,4},{3,1},{4,6},{5,3},{7,5},{8,10},{10,12},{11,9},{12,14},... | collective-permute-start | bytes 1597448 | tf_op jit(solution)/shard_map/ppermute | solution.py:464
  10.0 19.3 %collective-permute-start.2 = (f32[1040,128]{1,0:T(8,128)S(1)}, f32[1040,128]{1,0:T(8,128)S(1)}, u32[]{:S(2)}, u32[]{:S(2)}) collective-permute-start(f32[1040,128]{1,0:T(8,128)S(1)} %get-tuple-element.35), channel_id=1, source_target_pairs={{1,2},{2,1},{3,4},{4,3},{5,6},{6,5},{9,10},{10,9},{11,12},{12,11},... | collective-permute-start | bytes 1597448 | tf_op jit(solution)/shard_map/ppermute | solution.py:464
  10.7 25.7 %collective-permute-start.3 = (f32[1040,128]{1,0:T(8,128)S(1)}, f32[1040,128]{1,0:T(8,128)S(1)}, u32[]{:S(2)}, u32[]{:S(2)}) collective-permute-start(f32[1040,128]{1,0:T(8,128)S(1)} %get-tuple-element.35), channel_id=1, source_target_pairs={{1,3},{2,0},{3,5},{4,2},{5,7},{6,4},{9,11},{10,8},{11,13},{12,10},... | collective-permute-start | bytes 1597448 | tf_op jit(solution)/shard_map/ppermute | solution.py:464
  12.0 0.7 %copy-start = (s32[1,16]{1,0:T(1,128)S(1)}, s32[1,16]{1,0:T(1,128)}, u32[]{:S(2)}) copy-start(s32[1,16]{1,0:T(1,128)} %lens_ref.1) | copy-start | bytes 196
  12.0 0.7 %copy-start.1 = (f32[32]{0:T(128)S(1)}, f32[32]{0:T(128)}, u32[]{:S(2)}) copy-start(f32[32]{0:T(128)} %param.13) | copy-start | bytes 388
  12.0 0.7 %copy-start.2 = (f32[32]{0:T(128)S(1)}, f32[32]{0:T(128)}, u32[]{:S(2)}) copy-start(f32[32]{0:T(128)} %param.12) | copy-start | bytes 388
  37.6 11.9 %all-to-all-start = ((f32[32,1,128]{2,1,0:T(1,128)}), f32[32,1,128]{2,1,0:T(1,128)S(1)}, u32[]{:S(2)}, u32[]{:S(2)}) async-start(f32[32,1,128]{2,1,0:T(1,128)} %bitcast.7), calls=%async_computation | async-start | bytes 32768 | tf_op jit(solution)/shard_map/all_to_all | solution.py:549

commit v6 on v5

--- a/solution.py
+++ b/solution.py
@@ -332,7 +332,7 @@
 
 
 def send_order(reach):
-    return [*range(0, 2 * reach, 2), *range(1, 2 * reach, 2)]
+    return [at for j in range(reach) for at in (2 * j + 1, 2 * j)]
 
 
 def rates_kernel(reach, head_width, *refs):

time: 50.4 us -> 46.9 us (0.931)
  waiting for transfers between devices: 18.4 us -> 11.2 us
  starting transfers between devices: 13.5 us -> 17.1 us
    ppermute x4, waiting for transfers between devices: 16.9 us -> 9.67 us  [send(): return lax.ppermute(a, 'ctx', [(i, j) for i, j in pairs if 0 <= j < count])]
    ppermute x4, starting transfers between devices: 8.52 us -> 12.3 us  [send(): return lax.ppermute(a, 'ctx', [(i, j) for i, j in pairs if 0 <= j < count])]
  transfers between devices with their start and end apart: 5 -> 5, of which waited for: 3 -> 3; matrix products, arithmetic and copies ran while one was open for 0% -> 0% of each run, Pallas kernels for 24% -> 26%
where the time goes in v6:
time: 46.9 us; the launch traced here: 46.6 us
  starting transfers between devices  17.1 us (36%)
  Pallas kernels  16.2 us (35%)
  waiting for transfers between devices  11.2 us (24%)
  local copies, waits for them, and re-layouts  1.25 us (3%)
  between operations  0.73 us (2%)
    pallas_call x4, Pallas kernels, call(): pl.pallas_call(kernel, out_shape=[pltpu.HBM(*out) if place == 'h' else ja...  16.2 us
    ppermute x4, starting transfers between devices, send(): return lax.ppermute(a, 'ctx', [(i, j) for i, j in pairs if 0 <= j < count])  12.3 us
    ppermute x4, waiting for transfers between devices, send(): return lax.ppermute(a, 'ctx', [(i, j) for i, j in pairs if 0 <= j < count])  9.67 us
    all_to_all x1, starting transfers between devices, per_device(): gathered = lax.all_to_all(partial, ('dp', 'ctx'), 0, 0, tiled=True)  4.84 us
    all_to_all x1, waiting for transfers between devices, per_device(): gathered = lax.all_to_all(partial, ('dp', 'ctx'), 0, 0, tiled=True)  1.56 us
  transfers between devices with their start and end apart: 5, of which 3 were waited for; matrix products, arithmetic and copies ran while one was open for 0% of the time, Pallas kernels for 26%

profile of v6, /device:TPU:0, one launch (start us, length us, event | category | flops | bytes accessed | tf_op | source)
XLA Modules:
  0.0 46.6 jit_solution(11310541843366497298)
XLA Ops:
  0.6 2.8 %shard_map.127 = (f32[32,128]{1,0:T(8,128)S(1)}, bf16[128,2048]{1,0:T(8,128)(2,1)S(1)}, bf16[64,128]{1,0:T(8,128)(2,1)S(1)}, bf16[128,2048]{1,0:T(8,128)(2,1)S(1...) custom-call(s32[1,16]{1,0:T(1,128)} %lens_ref.1, f32[1,32]{1,0:T(1,128)} %bitcast.10, ...), custom_call_target="tpu_custom_call" | custom-call | flops 1000000000 | bytes 4194304 | tf_op jit(solution)/shard_map/pallas_call | solution.py:448
  3.5 0.7 %collective-permute-start = (f32[1040,128]{1,0:T(8,128)S(1)}, f32[1040,128]{1,0:T(8,128)S(1)}, u32[]{:S(2)}, u32[]{:S(2)}) collective-permute-start(f32[1040,128]{1,0:T(8,128)S(1)} %get-tuple-element.34), channel_id=1, source_target_pairs={{1,2},{2,1},{3,4},{4,3},{5,6},{6,5},{9,10},{10,9},{11,12},{12,11},... | collective-permute-start | bytes 1597448 | tf_op jit(solution)/shard_map/ppermute | solution.py:464
  4.2 5.8 %collective-permute-start.1 = (f32[1040,128]{1,0:T(8,128)S(1)}, f32[1040,128]{1,0:T(8,128)S(1)}, u32[]{:S(2)}, u32[]{:S(2)}) collective-permute-start(f32[1040,128]{1,0:T(8,128)S(1)} %get-tuple-element.35), channel_id=1, source_target_pairs={{0,1},{1,0},{2,3},{3,2},{4,5},{5,4},{6,7},{7,6},{8,9},{9,8},{10,11... | collective-permute-start | bytes 1597448 | tf_op jit(solution)/shard_map/ppermute | solution.py:464
  9.9 1.3 %collective-permute-start.2 = (f32[1040,128]{1,0:T(8,128)S(1)}, f32[1040,128]{1,0:T(8,128)S(1)}, u32[]{:S(2)}, u32[]{:S(2)}) collective-permute-start(f32[1040,128]{1,0:T(8,128)S(1)} %get-tuple-element.34), channel_id=1, source_target_pairs={{1,3},{2,0},{3,5},{4,2},{5,7},{6,4},{9,11},{10,8},{11,13},{12,10},... | collective-permute-start | bytes 1597448 | tf_op jit(solution)/shard_map/ppermute | solution.py:464
  11.2 4.6 %collective-permute-start.3 = (f32[1040,128]{1,0:T(8,128)S(1)}, f32[1040,128]{1,0:T(8,128)S(1)}, u32[]{:S(2)}, u32[]{:S(2)}) collective-permute-start(f32[1040,128]{1,0:T(8,128)S(1)} %get-tuple-element.35), channel_id=1, source_target_pairs={{0,2},{2,4},{3,1},{4,6},{5,3},{7,5},{8,10},{10,12},{11,9},{12,14},... | collective-permute-start | bytes 1597448 | tf_op jit(solution)/shard_map/ppermute | solution.py:464
  15.8 0.0 copy-start
  15.8 0.0 copy-start.1
  15.8 0.0 copy-start.2
  15.8 0.6 %copy-done = s32[1,16]{1,0:T(1,128)S(1)} copy-done((s32[1,16]{1,0:T(1,128)S(1)}, s32[1,16]{1,0:T(1,128)}, u32[]{:S(2)}) %copy-start) | copy-done | bytes 88
  16.5 0.0 copy-done.1
  16.5 0.0 copy-done.2
  16.5 6.9 %shard_map.128 = (bf16[256,2048]{1,0:T(8,128)(2,1)S(1)}, bf16[256,2048]{1,0:T(8,128)(2,1)S(1)}, f32[128,2048]{1,0:T(8,128)}, f32[128,2048]{1,0:T(8,128)}, bf16[1...) custom-call(s32[1,16]{1,0:T(1,128)S(1)} %copy-done, ...), custom_call_target="tpu_custom_call" | custom-call | flops 4000000000 | bytes 12582912 | tf_op jit(solution)/shard_map/pallas_call | solution.py:448
  23.4 0.0 collective-permute-done.refs_0_
  23.4 8.6 %collective-permute-done.1.refs_1_ = f32[1040,128]{1,0:T(8,128)S(1)} collective-permute-done((f32[1040,128]{1,0:T(8,128)S(1)}, f32[1040,128]{1,0:T(8,128)S(1)}, u32[]{:S(2)}, u32[]{:S(2)}) %collective-permute-start.1) | collective-permute-done | bytes 532512 | tf_op jit(solution)/shard_map/ppermute | solution.py:464
  32.0 1.1 %collective-permute-done.2.refs_2_ = f32[1040,128]{1,0:T(8,128)S(1)} collective-permute-done((f32[1040,128]{1,0:T(8,128)S(1)}, f32[1040,128]{1,0:T(8,128)S(1)}, u32[]{:S(2)}, u32[]{:S(2)}) %collective-permute-start.2) | collective-permute-done | bytes 532512 | tf_op jit(solution)/shard_map/ppermute | solution.py:464
  33.0 0.0 collective-permute-done.3.refs_3_
  33.1 1.1 %shard_map.129 = (f32[32,128]{1,0:T(8,128)}, f32[64,2048]{1,0:T(8,128)S(1)}, f32[64,2048]{1,0:T(8,128)S(1)}) custom-call(f32[1040,128]{1,0:T(8,128)S(1)} %collective-permute-done.refs_0_, f32[1040,128]{1,0:T(8,128)S(1)} %collective-permute-done.1.refs_1_, f32[1040,128]{1,0:T(8,128)S(1)} %collective-permute-done.2.refs_2_, ...), custom_call_target="tpu_custom_call" | custom-call | flops 100000000 | bytes 4194304 | tf_op jit(solution)/shard_map/pallas_call | solution.py:448
  34.2 4.8 %all-to-all-start = ((f32[32,1,128]{2,1,0:T(1,128)}), f32[32,1,128]{2,1,0:T(1,128)S(1)}, u32[]{:S(2)}, u32[]{:S(2)}) async-start(f32[32,1,128]{2,1,0:T(1,128)} %bitcast.7), calls=%async_computation | async-start | bytes 32768 | tf_op jit(solution)/shard_map/all_to_all | solution.py:549
  39.0 5.4 %shard_map.130 = (bf16[1,128,2048]{2,1,0:T(8,128)(2,1)}, bf16[1,64,128]{2,1,0:T(8,128)(2,1)}, bf16[1,64,128]{2,1,0:T(8,128)(2,1)}, f32[1,32,128]{2,1,0:T(8,128)}) custom-call(f32[64,2048]{1,0:T(8,128)S(1)} %get-tuple-element.45.came_ref, f32[64,2048]{1,0:T(8,128)S(1)} %get-tuple-element.46.pull_ref, f32[8,2048]{1,0:T(8,128)S(1)} %get-tuple-element.41.refs_4_.ends_ref, ...), custom_call_target="tpu_custom_call" | custom-call | flops 2000000000 | bytes 12582912 | tf_op jit(solution)/shard_map/pallas_call | solution.py:448
  44.4 1.6 %all-to-all-done = f32[32,1,128]{2,1,0:T(1,128)S(1)} async-done(((f32[32,1,128]{2,1,0:T(1,128)}), f32[32,1,128]{2,1,0:T(1,128)S(1)}, u32[]{:S(2)}, u32[]{:S(2)}) %all-to-all-start) | async-done | bytes 16416 | tf_op jit(solution)/shard_map/all_to_all | solution.py:549
  46.0 0.1 reduce_sum.9
  46.0 0.6 %fusion = (f32[32]{0:T(128)}, f32[32]{0:T(128)}) fusion(f32[128]{0:T(128)S(1)} %reduce_sum.9), kind=kLoop, calls=%fused_computation | loop fusion | bytes 512 | tf_op jit(solution)/shard_map/slice | solution.py:557
Async XLA Ops:
  3.5 19.9 %collective-permute-start = (f32[1040,128]{1,0:T(8,128)S(1)}, f32[1040,128]{1,0:T(8,128)S(1)}, u32[]{:S(2)}, u32[]{:S(2)}) collective-permute-start(f32[1040,128]{1,0:T(8,128)S(1)} %get-tuple-element.34), channel_id=1, source_target_pairs={{1,2},{2,1},{3,4},{4,3},{5,6},{6,5},{9,10},{10,9},{11,12},{12,11},... | collective-permute-start | bytes 1597448 | tf_op jit(solution)/shard_map/ppermute | solution.py:464
  4.2 27.8 %collective-permute-start.1 = (f32[1040,128]{1,0:T(8,128)S(1)}, f32[1040,128]{1,0:T(8,128)S(1)}, u32[]{:S(2)}, u32[]{:S(2)}) collective-permute-start(f32[1040,128]{1,0:T(8,128)S(1)} %get-tuple-element.35), channel_id=1, source_target_pairs={{0,1},{1,0},{2,3},{3,2},{4,5},{5,4},{6,7},{7,6},{8,9},{9,8},{10,11... | collective-permute-start | bytes 1597448 | tf_op jit(solution)/shard_map/ppermute | solution.py:464
  9.9 23.1 %collective-permute-start.2 = (f32[1040,128]{1,0:T(8,128)S(1)}, f32[1040,128]{1,0:T(8,128)S(1)}, u32[]{:S(2)}, u32[]{:S(2)}) collective-permute-start(f32[1040,128]{1,0:T(8,128)S(1)} %get-tuple-element.34), channel_id=1, source_target_pairs={{1,3},{2,0},{3,5},{4,2},{5,7},{6,4},{9,11},{10,8},{11,13},{12,10},... | collective-permute-start | bytes 1597448 | tf_op jit(solution)/shard_map/ppermute | solution.py:464
  11.2 21.8 %collective-permute-start.3 = (f32[1040,128]{1,0:T(8,128)S(1)}, f32[1040,128]{1,0:T(8,128)S(1)}, u32[]{:S(2)}, u32[]{:S(2)}) collective-permute-start(f32[1040,128]{1,0:T(8,128)S(1)} %get-tuple-element.35), channel_id=1, source_target_pairs={{0,2},{2,4},{3,1},{4,6},{5,3},{7,5},{8,10},{10,12},{11,9},{12,14},... | collective-permute-start | bytes 1597448 | tf_op jit(solution)/shard_map/ppermute | solution.py:464
  15.8 0.7 %copy-start = (s32[1,16]{1,0:T(1,128)S(1)}, s32[1,16]{1,0:T(1,128)}, u32[]{:S(2)}) copy-start(s32[1,16]{1,0:T(1,128)} %lens_ref.1) | copy-start | bytes 196
  15.8 0.7 %copy-start.1 = (f32[32]{0:T(128)S(1)}, f32[32]{0:T(128)}, u32[]{:S(2)}) copy-start(f32[32]{0:T(128)} %param.13) | copy-start | bytes 388
  15.8 0.7 %copy-start.2 = (f32[32]{0:T(128)S(1)}, f32[32]{0:T(128)}, u32[]{:S(2)}) copy-start(f32[32]{0:T(128)} %param.12) | copy-start | bytes 388
  34.2 11.8 %all-to-all-start = ((f32[32,1,128]{2,1,0:T(1,128)}), f32[32,1,128]{2,1,0:T(1,128)S(1)}, u32[]{:S(2)}, u32[]{:S(2)}) async-start(f32[32,1,128]{2,1,0:T(1,128)} %bitcast.7), calls=%async_computation | async-start | bytes 32768 | tf_op jit(solution)/shard_map/all_to_all | solution.py:549

commit v7 on v6

--- a/solution.py
+++ b/solution.py
@@ -359,54 +359,51 @@
     out_ref[...] = jnp.broadcast_to(total, out_ref.shape)
 
 
-def outputs_kernel(
-    came_ref,
-    pull_ref,
-    ends_ref,
-    xs_ref,
-    ys_ref,
-    v_wide_hbm,
-    dx_hbm,
-    b_end_ref,
-    c_live_ref,
-    masks_ref,
-    db_ref,
-    dc_ref,
-    sums_ref,
-    alog_ref,
-    dt_ref,
-    dx_out,
-    db_out,
-    dc_out,
-    dt_out,
-    v_stage,
-    dx_stage,
-    stage,
-    in_sems,
-    out_sems,
-):
+def outputs_kernel(start, size, final, *refs):
+    (
+        came_ref,
+        pull_ref,
+        ends_ref,
+        xs_ref,
+        ys_ref,
+        v_wide_hbm,
+        dx_hbm,
+        b_end_ref,
+        c_live_ref,
+        masks_ref,
+        db_ref,
+        dc_ref,
+        sums_ref,
+        own_ref,
+        alog_ref,
+        dt_ref,
+        *refs,
+    ) = refs
+    if start:
+        refs = refs[2:]
+    dx_out, db_out, dc_out, last_out = refs[:4]
+    v_stage, dx_stage, back_stage, stage, in_sems, out_sems = refs[4:]
     rows, columns = dx_hbm.shape
     heads, width = dt_ref.shape[0], db_ref.shape[0]
-    blocks = columns // WIDE
     copies = []
-    for block in range(blocks):
-        at = slice(block * WIDE, (block + 1) * WIDE)
-        for i, (source, target) in enumerate(((v_wide_hbm, v_stage), (dx_hbm, dx_stage))):
+    for i in range(size):
+        own = slice(i * WIDE, (i + 1) * WIDE)
+        at = slice((start + i) * WIDE, (start + i + 1) * WIDE)
+        for side, (source, target) in enumerate(((v_wide_hbm, v_stage), (dx_hbm, dx_stage))):
             copy = pltpu.make_async_copy(
-                source.at[:, at], target.at[:, at], in_sems.at[i, block]
+                source.at[:, at], target.at[:, own], in_sems.at[side, i]
             )
             copy.start()
             copies.append(copy)
     b_end, c_live = b_end_ref[...], c_live_ref[...]
-    own_sums = sums_ref[...]
-    sums = own_sums
+    sums = sums_ref[...]
     dc = jnp.zeros((2 * width, 2 * rows), F32)
     db = jnp.zeros((2 * width, 2 * rows), F32)
     at_last = iota((rows, WIDE), 0) == rows - 1
-    sent = []
-    for block in range(blocks):
-        at = slice(block * WIDE, (block + 1) * WIDE)
-        ones = head_columns(heads, columns // heads, block)
+    for i in range(size):
+        own = slice(i * WIDE, (i + 1) * WIDE)
+        at = slice((start + i) * WIDE, (start + i + 1) * WIDE)
+        ones = head_columns(heads, columns // heads, start + i)
         came, pull = came_ref[:, at], pull_ref[:, at]
         meet = jnp.sum(came * pull, axis=0, keepdims=True) * ends_ref[1:2, at]
         cames = stack(split2(came), 0)
@@ -414,6 +411,7 @@
         xs, ys = xs_ref[:, at], ys_ref[:, at]
         out = dot(c_live, cames, 1, 0)
         back = dot(b_end, pulls, 1, 0)
+        back_stage[:, own] = back
         column_part = (xs[:rows].astype(F32) + xs[rows:].astype(F32)) * back
         row_part = (ys[:rows].astype(F32) + ys[rows:].astype(F32)) * out
         row_part = jnp.where(at_last, row_part + meet, row_part)
@@ -421,29 +419,41 @@
             sums += dot(part, ones, 1, 0)
         dc += dot(cames, ys, 1, 1)
         db += dot(pulls, xs, 1, 1)
-        copies[2 * block].wait()
-        copies[2 * block + 1].wait()
-        stage[:, at] = (dx_stage[:, at] + v_stage[:, at] * back).astype(BF16)
-        copy = pltpu.make_async_copy(stage.at[:, at], dx_out.at[0, :, at], out_sems.at[block])
+    sent = []
+    for i in range(size):
+        own = slice(i * WIDE, (i + 1) * WIDE)
+        at = slice((start + i) * WIDE, (start + i + 1) * WIDE)
+        copies[2 * i].wait()
+        copies[2 * i + 1].wait()
+        total = dx_stage[:, own] + v_stage[:, own] * back_stage[:, own]
+        stage[:, own] = total.astype(BF16)
+        copy = pltpu.make_async_copy(stage.at[:, own], dx_out.at[0, :, at], out_sems.at[i])
         copy.start()
         sent.append(copy)
     dc = (dc[:width, :rows] + dc[:width, rows:]) + dc[width:, :rows]
     db = (db[:width, :rows] + db[:width, rows:]) + db[width:, :rows]
-    db_out[0] = (db_ref[...] + masks_ref[0:1] * db).astype(BF16)
-    dc_out[0] = (dc_ref[...] + masks_ref[1:2] * dc).astype(BF16)
-    square = (rows, rows)
-    upper = jnp.where(iota(square, 0) >= iota(square, 1), 1.0, 0.0).astype(BF16)
-    eye = jnp.where(iota(square, 0) == iota(square, 1), 1.0, 0.0).astype(BF16)
-    at_end = jnp.sum(sums[rows:] - own_sums[rows:], axis=0, keepdims=True)
-    dl = sums[:rows] + jnp.where(iota((rows, heads), 0) == rows - 1, at_end, 0.0)
-    d_decay = sum(dot(part, upper, 0, 0) for part in split3(dl))
-    total = sum(dot(part, eye, 0, 0) for part in split3(sums[rows:]))
-    dt_out[0] = total / dt_ref[...] + rate_column(alog_ref) * d_decay
+    db = db_ref[...] + masks_ref[0:1] * db
+    dc = dc_ref[...] + masks_ref[1:2] * dc
+    if final:
+        db_out[0] = db.astype(BF16)
+        dc_out[0] = dc.astype(BF16)
+        square = (rows, rows)
+        upper = jnp.where(iota(square, 0) >= iota(square, 1), 1.0, 0.0).astype(BF16)
+        eye = jnp.where(iota(square, 0) == iota(square, 1), 1.0, 0.0).astype(BF16)
+        at_end = jnp.sum(sums[rows:] - own_ref[rows:], axis=0, keepdims=True)
+        dl = sums[:rows] + jnp.where(iota((rows, heads), 0) == rows - 1, at_end, 0.0)
+        d_decay = sum(dot(part, upper, 0, 0) for part in split3(dl))
+        total = sum(dot(part, eye, 0, 0) for part in split3(sums[rows:]))
+        last_out[0] = total / dt_ref[...] + rate_column(alog_ref) * d_decay
+    else:
+        db_out[...] = db
+        dc_out[...] = dc
+        last_out[...] = sums
     for copy in sent:
         copy.wait()
 
 
-def call(kernel, reach, outs, ins, flops, moved, scratch=()):
+def call(kernel, reach, outs, ins, flops, moved, scratch=(), aliases=None):
     spaces = {"s": pltpu.SMEM, "v": pltpu.VMEM, "h": pltpu.HBM}
     return pl.pallas_call(
         kernel,
@@ -453,6 +463,7 @@
         in_specs=[pl.BlockSpec(memory_space=spaces[place]) for place, _ in ins],
         out_specs=[pl.BlockSpec(memory_space=spaces[place]) for place, _ in outs],
         scratch_shapes=scratch,
+        input_output_aliases=aliases or {},
         compiler_params=pltpu.CompilerParams(vmem_limit_bytes=min(16 + 2 * reach, 56) * 2**20),
         cost_estimate=pl.CostEstimate(flops=flops, bytes_accessed=moved, transcendentals=0),
     )(*(a for _, a in ins))
@@ -472,7 +483,6 @@
     rows, columns = inputs.shape[1:]
     heads, width = a_log.shape[0], b_proj.shape[2]
     reach = max(lax.axis_size("ctx") // 4, 1)
-    devices = lax.axis_size("ctx") * lax.axis_size("dp")
     alog, skip = a_log[None], skip_gain[None]
     bt, ct = jnp.swapaxes(b_proj, 1, 2), jnp.swapaxes(c_proj, 1, 2)
     blocks = columns // WIDE
@@ -506,7 +516,7 @@
     state = v((width, columns))
     stage = pltpu.VMEM((rows, columns), F32)
     transposed = v((width, rows))
-    xs, ys, v_wide, dx, b_end, c_live, masks, db, dc, sums, fwd_logs, bwd_logs, ends, small = call(
+    xs, ys, v_wide, dx, b_end, c_live, masks, db, dc, own_sums, *rest = call(
         inside_kernel,
         reach,
         [v((2 * rows, columns), BF16)] * 2
@@ -519,35 +529,52 @@
         12 * 2**20,
         [stage, stage, pltpu.SemaphoreType.DMA((2, blocks))],
     )
+    fwd_logs, bwd_logs, ends, small = rest
     partial, came, pull = call(
         functools.partial(rates_kernel, reach, columns // heads),
         reach,
-        [v((devices, LANES)), state, state],
+        [v((lax.axis_size("ctx"), LANES)), state, state],
         [("v", a) for a in (*messages, ends, fwd_logs, bwd_logs, small)],
         10**8,
         4 * 2**20,
     )
-    input_grads, b_gradient, c_gradient, step_grads = call(
-        outputs_kernel,
-        reach,
-        [("h", ((1, rows, columns), BF16))]
-        + [v((1, width, rows), BF16)] * 2
-        + [v((1, heads, rows))],
-        [("v", a) for a in (came, pull, ends, xs, ys)]
-        + [in_hbm(v_wide), in_hbm(dx)]
-        + [("v", a) for a in (b_end, c_live, masks, db, dc, sums, alog, dt)],
-        2 * 10**9,
-        12 * 2**20,
-        [
-            stage,
-            stage,
-            pltpu.VMEM((rows, columns), BF16),
-            pltpu.SemaphoreType.DMA((2, blocks)),
-            pltpu.SemaphoreType.DMA((blocks,)),
-        ],
-    )
-    gathered = lax.all_to_all(partial, ("dp", "ctx"), 0, 0, tiled=True)
-    totals = jnp.sum(gathered, axis=0)
+    half = blocks // 2
+    wide = (rows, half * WIDE)
+    sums, previous = own_sums, []
+    for start in (0, half):
+        final = start > 0
+        outs = [("h", ((1, rows, columns), BF16))]
+        if final:
+            outs += [v((1, width, rows), BF16)] * 2 + [v((1, heads, rows))]
+        else:
+            outs += [transposed, transposed, v((2 * rows, heads))]
+            gathered = lax.all_to_all(partial, "ctx", 0, 0, tiled=True)
+            own = jnp.broadcast_to(
+                jnp.sum(gathered, axis=0, keepdims=True), (lax.axis_size("dp"), LANES)
+            )
+        results = call(
+            functools.partial(outputs_kernel, start, half, final),
+            reach,
+            outs,
+            [("v", a) for a in (came, pull, ends, xs, ys)]
+            + [in_hbm(v_wide), in_hbm(dx)]
+            + [("v", a) for a in (b_end, c_live, masks, db, dc, sums, own_sums, alog, dt)]
+            + previous,
+            10**9,
+            6 * 2**20,
+            [pltpu.VMEM(wide, F32)] * 3
+            + [
+                pltpu.VMEM(wide, BF16),
+                pltpu.SemaphoreType.DMA((2, half)),
+                pltpu.SemaphoreType.DMA((half,)),
+            ],
+            {16: 0} if final else None,
+        )
+        if not final:
+            previous = [("h", results[0]), ("v", own)]
+            _, db, dc, sums = results
+    input_grads, b_gradient, c_gradient, step_grads = results
+    totals = jnp.sum(lax.all_to_all(own, "dp", 0, 0, tiled=True), axis=0)
     return (
         input_grads,
         jnp.swapaxes(b_gradient, 1, 2),

time: 46.9 us -> 60.4 us (1.29)
  local copies, waits for them, and re-layouts: 1.25 us -> 8.73 us
  starting transfers between devices: 17.1 us -> 20.9 us
  other arithmetic: 0.05 us -> 1.88 us
  waiting for transfers between devices: 11.2 us -> 9.65 us
  Pallas kernels: 16.2 us -> 17.7 us
    unnamed x6 -> x34, local copies, waits for them, and re-layouts: 0.67 us -> 6.9 us
    all_to_all x1 -> x2, starting transfers between devices: 4.84 us -> 8.57 us  [the longest x1 4.82 us: per_device(): gathered = lax.all_to_all(partial, 'ctx', 0, 0, tiled=True)]
    reduce_sum x1 -> x2, other arithmetic: 0.05 us -> 1.88 us  [the longest x1 1.2 us: per_device(): jnp.sum(gathered, axis=0, keepdims=True)]
    all_to_all x1 -> x2, waiting for transfers between devices: 1.56 us -> 0.01 us  [the longest x1 0.01 us: per_device(): gathered = lax.all_to_all(partial, 'ctx', 0, 0, tiled=True)]
    pallas_call x4 -> x5, Pallas kernels: 16.2 us -> 17.7 us  [call(): pl.pallas_call(kernel, out_shape=[pltpu.HBM(*out) if place == 'h' else ja...]
    broadcast_in_dim x0 -> x2, local copies, waits for them, and re-layouts: none -> 1.25 us  [per_device(): jnp.broadcast_to(jnp.sum(gathered, axis=0, keepdims=True), (lax.axis_size...]
  transfers between devices with their start and end apart: 5 -> 6, of which waited for: 3 -> 2; matrix products, arithmetic and copies ran while one was open for 0% -> 0% of each run, Pallas kernels for 26% -> 23%
where the time goes in v7:
time: 60.4 us; the launch traced here: 59.6 us
  starting transfers between devices  20.9 us (35%)
  Pallas kernels  17.7 us (29%)
  waiting for transfers between devices  9.65 us (16%)
  local copies, waits for them, and re-layouts  8.73 us (14%)
  other arithmetic  1.88 us (3%)
  between operations  0.81 us (1%)
    pallas_call x5, Pallas kernels, call(): pl.pallas_call(kernel, out_shape=[pltpu.HBM(*out) if place == 'h' else ja...  17.7 us
    ppermute x4, starting transfers between devices, send(): return lax.ppermute(a, 'ctx', [(i, j) for i, j in pairs if 0 <= j < count])  12.3 us
    ppermute x4, waiting for transfers between devices, send(): return lax.ppermute(a, 'ctx', [(i, j) for i, j in pairs if 0 <= j < count])  9.64 us
    unnamed x34, local copies, waits for them, and re-layouts  6.9 us
    all_to_all x1, starting transfers between devices, per_device(): gathered = lax.all_to_all(partial, 'ctx', 0, 0, tiled=True)  4.82 us
    all_to_all x1, starting transfers between devices, per_device(): totals = jnp.sum(lax.all_to_all(own, 'dp', 0, 0, tiled=True), axis=0)  3.75 us
    broadcast_in_dim x2, local copies, waits for them, and re-layouts, per_device(): jnp.broadcast_to(jnp.sum(gathered, axis=0, keepdims=True), (lax.axis_size...  1.25 us
  transfers between devices with their start and end apart: 6, of which 2 were waited for; matrix products, arithmetic and copies ran while one was open for 0% of the time, Pallas kernels for 23%

profile of v7, /device:TPU:0, one launch (start us, length us, event | category | flops | bytes accessed | tf_op | source)
XLA Modules:
  0.0 59.6 jit_solution(10753986254658929528)
XLA Ops:
  0.6 2.8 %shard_map.127 = (f32[32,128]{1,0:T(8,128)S(1)}, bf16[128,2048]{1,0:T(8,128)(2,1)S(1)}, bf16[64,128]{1,0:T(8,128)(2,1)S(1)}, bf16[128,2048]{1,0:T(8,128)(2,1)S(1...) custom-call(s32[1,16]{1,0:T(1,128)} %lens_ref.1, f32[1,32]{1,0:T(1,128)} %bitcast.10, ...), custom_call_target="tpu_custom_call" | custom-call | flops 1000000000 | bytes 4194304 | tf_op jit(solution)/shard_map/pallas_call | solution.py:458
  3.5 0.7 %collective-permute-start = (f32[1040,128]{1,0:T(8,128)S(1)}, f32[1040,128]{1,0:T(8,128)S(1)}, u32[]{:S(2)}, u32[]{:S(2)}) collective-permute-start(f32[1040,128]{1,0:T(8,128)S(1)} %get-tuple-element.38), channel_id=1, source_target_pairs={{1,2},{2,1},{3,4},{4,3},{5,6},{6,5},{9,10},{10,9},{11,12},{12,11},... | collective-permute-start | bytes 1597448 | tf_op jit(solution)/shard_map/ppermute | solution.py:475
  4.2 5.8 %collective-permute-start.1 = (f32[1040,128]{1,0:T(8,128)S(1)}, f32[1040,128]{1,0:T(8,128)S(1)}, u32[]{:S(2)}, u32[]{:S(2)}) collective-permute-start(f32[1040,128]{1,0:T(8,128)S(1)} %get-tuple-element.39), channel_id=1, source_target_pairs={{0,1},{1,0},{2,3},{3,2},{4,5},{5,4},{6,7},{7,6},{8,9},{9,8},{10,11... | collective-permute-start | bytes 1597448 | tf_op jit(solution)/shard_map/ppermute | solution.py:475
  9.9 1.3 %collective-permute-start.2 = (f32[1040,128]{1,0:T(8,128)S(1)}, f32[1040,128]{1,0:T(8,128)S(1)}, u32[]{:S(2)}, u32[]{:S(2)}) collective-permute-start(f32[1040,128]{1,0:T(8,128)S(1)} %get-tuple-element.38), channel_id=1, source_target_pairs={{1,3},{2,0},{3,5},{4,2},{5,7},{6,4},{9,11},{10,8},{11,13},{12,10},... | collective-permute-start | bytes 1597448 | tf_op jit(solution)/shard_map/ppermute | solution.py:475
  11.2 4.6 %collective-permute-start.3 = (f32[1040,128]{1,0:T(8,128)S(1)}, f32[1040,128]{1,0:T(8,128)S(1)}, u32[]{:S(2)}, u32[]{:S(2)}) collective-permute-start(f32[1040,128]{1,0:T(8,128)S(1)} %get-tuple-element.39), channel_id=1, source_target_pairs={{0,2},{2,4},{3,1},{4,6},{5,3},{7,5},{8,10},{10,12},{11,9},{12,14},... | collective-permute-start | bytes 1597448 | tf_op jit(solution)/shard_map/ppermute | solution.py:475
  15.8 0.6 %copy-done.11 = f32[32]{0:T(128)S(1)} copy-done((f32[32]{0:T(128)S(1)}, f32[32]{0:T(128)}, u32[]{:S(2)}) %copy-start.11) | copy-done | bytes 152
  16.5 6.9 %shard_map.128 = (bf16[256,2048]{1,0:T(8,128)(2,1)S(1)}, bf16[256,2048]{1,0:T(8,128)(2,1)S(1)}, f32[128,2048]{1,0:T(8,128)}, f32[128,2048]{1,0:T(8,128)}, bf16[1...) custom-call(s32[1,16]{1,0:T(1,128)S(1)} %copy-done.14, ...), custom_call_target="tpu_custom_call" | custom-call | flops 4000000000 | bytes 12582912 | tf_op jit(solution)/shard_map/pallas_call | solution.py:458
  23.4 8.6 %collective-permute-done.1.refs_1_ = f32[1040,128]{1,0:T(8,128)S(1)} collective-permute-done((f32[1040,128]{1,0:T(8,128)S(1)}, f32[1040,128]{1,0:T(8,128)S(1)}, u32[]{:S(2)}, u32[]{:S(2)}) %collective-permute-start.1) | collective-permute-done | bytes 532512 | tf_op jit(solution)/shard_map/ppermute | solution.py:475
  32.0 1.1 %collective-permute-done.2.refs_2_ = f32[1040,128]{1,0:T(8,128)S(1)} collective-permute-done((f32[1040,128]{1,0:T(8,128)S(1)}, f32[1040,128]{1,0:T(8,128)S(1)}, u32[]{:S(2)}, u32[]{:S(2)}) %collective-permute-start.2) | collective-permute-done | bytes 532512 | tf_op jit(solution)/shard_map/ppermute | solution.py:475
  33.1 1.1 %shard_map.129 = (f32[8,128]{1,0:T(8,128)}, f32[64,2048]{1,0:T(8,128)S(1)}, f32[64,2048]{1,0:T(8,128)S(1)}) custom-call(f32[1040,128]{1,0:T(8,128)S(1)} %collective-permute-done.refs_0_, f32[1040,128]{1,0:T(8,128)S(1)} %collective-permute-done.1.refs_1_, f32[1040,128]{1,0:T(8,128)S(1)} %collective-permute-done.2.refs_2_, ...), custom_call_target="tpu_custom_call" | custom-call | flops 100000000 | bytes 4194304 | tf_op jit(solution)/shard_map/pallas_call | solution.py:458
  34.2 4.8 %all-to-all-start = ((f32[8,1,128]{2,1,0:T(1,128)}), f32[8,1,128]{2,1,0:T(1,128)}, u32[]{:S(2)}, u32[]{:S(2)}) async-start(f32[8,1,128]{2,1,0:T(1,128)} %bitcast.5), calls=%async_computation | async-start | bytes 8192 | tf_op jit(solution)/shard_map/all_to_all | solution.py:551
  39.0 0.7 %copy-done.9 = f32[8,128]{1,0:T(8,128)S(1)} copy-done((f32[8,128]{1,0:T(8,128)S(1)}, f32[8,128]{1,0:T(8,128)}, u32[]{:S(2)}) %copy-start.9) | copy-done | bytes 4120
  39.7 0.8 %copy-done.1 = f32[64,128]{1,0:T(8,128)S(1)} copy-done((f32[64,128]{1,0:T(8,128)S(1)}, f32[64,128]{1,0:T(8,128)}, u32[]{:S(2)}) %copy-start.1) | copy-done | bytes 32792
  40.5 0.8 %copy-done.3 = f32[64,128]{1,0:T(8,128)S(1)} copy-done((f32[64,128]{1,0:T(8,128)S(1)}, f32[64,128]{1,0:T(8,128)}, u32[]{:S(2)}) %copy-start.3) | copy-done | bytes 32792
  41.2 3.1 %shard_map.130 = (bf16[1,128,2048]{2,1,0:T(8,128)(2,1)}, f32[64,128]{1,0:T(8,128)S(1)}, f32[64,128]{1,0:T(8,128)S(1)}, f32[256,32]{1,0:T(8,128)S(1)}) custom-call(f32[64,2048]{1,0:T(8,128)S(1)} %get-tuple-element.49.refs_0_, f32[64,2048]{1,0:T(8,128)S(1)} %get-tuple-element.50.refs_1_, f32[8,2048]{1,0:T(8,128)S(1)} %get-tuple-element.45.refs_4_.refs_2_, ...), custom_call_target="tpu_custom_call" | custom-call | flops 1000000000 | bytes 6291456 | tf_op jit(solution)/shard_map/pallas_call | solution.py:458
  45.5 1.2 %reduce_sum.18 = f32[128]{0:T(128)} reduce(f32[8,1,128]{2,1,0:T(1,128)} %all-to-all-done, f32[]{:T(128)} %constant.0.clone.1), dimensions={0,1}, to_apply=%region_0.0 | reduce | flops 896 | bytes 4612 | tf_op jit(solution)/shard_map/reduce_sum | solution.py:553
  46.7 1.2 %broadcast_in_dim.17 = f32[4,1,128]{2,1,0:T(1,128)} broadcast(f32[128]{0:T(128)} %reduce_sum.18), dimensions={2} | broadcast | bytes 2560 | tf_op jit(solution)/shard_map/broadcast_in_dim | solution.py:552
  48.0 3.8 %all-to-all-start.1 = ((f32[4,1,128]{2,1,0:T(1,128)}), f32[4,1,128]{2,1,0:T(1,128)}, u32[]{:S(2)}, u32[]{:S(2)}) async-start(f32[4,1,128]{2,1,0:T(1,128)} %broadcast_in_dim.17), calls=%async_computation.1 | async-start | bytes 4096 | tf_op jit(solution)/shard_map/all_to_all | solution.py:577
  51.8 0.7 %copy-done.16 = f32[128]{0:T(128)S(1)} copy-done((f32[128]{0:T(128)S(1)}, f32[128]{0:T(128)}, u32[]{:S(2)}) %copy-start.16) | copy-done | bytes 536
  52.4 0.6 %copy-done.13 = f32[32]{0:T(128)S(1)} copy-done((f32[32]{0:T(128)S(1)}, f32[32]{0:T(128)}, u32[]{:S(2)}) %copy-start.13) | copy-done | bytes 152
  53.1 0.8 %copy-done.5 = f32[64,128]{1,0:T(8,128)S(1)} copy-done((f32[64,128]{1,0:T(8,128)S(1)}, f32[64,128]{1,0:T(8,128)}, u32[]{:S(2)}) %copy-start.5) | copy-done | bytes 32792
  53.8 0.8 %copy-done.7 = f32[64,128]{1,0:T(8,128)S(1)} copy-done((f32[64,128]{1,0:T(8,128)S(1)}, f32[64,128]{1,0:T(8,128)}, u32[]{:S(2)}) %copy-start.7) | copy-done | bytes 32792
  54.6 3.8 %shard_map.131 = (bf16[1,128,2048]{2,1,0:T(8,128)(2,1)}, bf16[1,64,128]{2,1,0:T(8,128)(2,1)}, bf16[1,64,128]{2,1,0:T(8,128)(2,1)}, f32[1,32,128]{2,1,0:T(8,128)}) custom-call(f32[64,2048]{1,0:T(8,128)S(1)} %get-tuple-element.49.refs_0_, f32[64,2048]{1,0:T(8,128)S(1)} %get-tuple-element.50.refs_1_, ...), custom_call_target="tpu_custom_call", output_to_operand_aliasing={{0}: (16, {})} | custom-call | flops 1000000000 | bytes 6291456 | tf_op jit(solution)/shard_map/pallas_call | solution.py:458
  58.4 0.7 %reduce_sum.19 = f32[128]{0:T(128)S(1)} reduce(f32[4,1,128]{2,0,1:T(4,128)} %bitcast.8, f32[]{:T(128)} %constant.0.clone.1), dimensions={0,1}, to_apply=%region_1.0 | reduce | flops 384 | bytes 2564 | tf_op jit(solution)/shard_map/reduce_sum | solution.py:577
  (32 shorter events, 1.9 us)
Async XLA Ops:
  3.5 19.9 %collective-permute-start = (f32[1040,128]{1,0:T(8,128)S(1)}, f32[1040,128]{1,0:T(8,128)S(1)}, u32[]{:S(2)}, u32[]{:S(2)}) collective-permute-start(f32[1040,128]{1,0:T(8,128)S(1)} %get-tuple-element.38), channel_id=1, source_target_pairs={{1,2},{2,1},{3,4},{4,3},{5,6},{6,5},{9,10},{10,9},{11,12},{12,11},... | collective-permute-start | bytes 1597448 | tf_op jit(solution)/shard_map/ppermute | solution.py:475
  4.2 27.8 %collective-permute-start.1 = (f32[1040,128]{1,0:T(8,128)S(1)}, f32[1040,128]{1,0:T(8,128)S(1)}, u32[]{:S(2)}, u32[]{:S(2)}) collective-permute-start(f32[1040,128]{1,0:T(8,128)S(1)} %get-tuple-element.39), channel_id=1, source_target_pairs={{0,1},{1,0},{2,3},{3,2},{4,5},{5,4},{6,7},{7,6},{8,9},{9,8},{10,11... | collective-permute-start | bytes 1597448 | tf_op jit(solution)/shard_map/ppermute | solution.py:475
  9.9 23.1 %collective-permute-start.2 = (f32[1040,128]{1,0:T(8,128)S(1)}, f32[1040,128]{1,0:T(8,128)S(1)}, u32[]{:S(2)}, u32[]{:S(2)}) collective-permute-start(f32[1040,128]{1,0:T(8,128)S(1)} %get-tuple-element.38), channel_id=1, source_target_pairs={{1,3},{2,0},{3,5},{4,2},{5,7},{6,4},{9,11},{10,8},{11,13},{12,10},... | collective-permute-start | bytes 1597448 | tf_op jit(solution)/shard_map/ppermute | solution.py:475
  11.2 21.8 %collective-permute-start.3 = (f32[1040,128]{1,0:T(8,128)S(1)}, f32[1040,128]{1,0:T(8,128)S(1)}, u32[]{:S(2)}, u32[]{:S(2)}) collective-permute-start(f32[1040,128]{1,0:T(8,128)S(1)} %get-tuple-element.39), channel_id=1, source_target_pairs={{0,2},{2,4},{3,1},{4,6},{5,3},{7,5},{8,10},{10,12},{11,9},{12,14},... | collective-permute-start | bytes 1597448 | tf_op jit(solution)/shard_map/ppermute | solution.py:475
  15.8 0.7 %copy-start.11 = (f32[32]{0:T(128)S(1)}, f32[32]{0:T(128)}, u32[]{:S(2)}) copy-start(f32[32]{0:T(128)} %param.12) | copy-start | bytes 388
  15.8 0.7 %copy-start.14 = (s32[1,16]{1,0:T(1,128)S(1)}, s32[1,16]{1,0:T(1,128)}, u32[]{:S(2)}) copy-start(s32[1,16]{1,0:T(1,128)} %lens_ref.1) | copy-start | bytes 196
  15.8 0.7 %copy-start.15 = (f32[32]{0:T(128)S(1)}, f32[32]{0:T(128)}, u32[]{:S(2)}) copy-start(f32[32]{0:T(128)} %param.13) | copy-start | bytes 388
  23.4 10.8 %copy-start = (f32[64,128]{1,0:T(8,128)}, f32[64,128]{1,0:T(8,128)S(1)}, u32[]{:S(2)}) copy-start(f32[64,128]{1,0:T(8,128)S(1)} %get-tuple-element.58.refs_10_) | copy-start | bytes 98308
  23.4 10.8 %copy-start.2 = (f32[64,128]{1,0:T(8,128)}, f32[64,128]{1,0:T(8,128)S(1)}, u32[]{:S(2)}) copy-start(f32[64,128]{1,0:T(8,128)S(1)} %get-tuple-element.59.refs_11_) | copy-start | bytes 98308
  23.4 10.8 %copy-start.8 = (f32[8,128]{1,0:T(8,128)}, f32[8,128]{1,0:T(8,128)S(1)}, u32[]{:S(2)}) copy-start(f32[8,128]{1,0:T(8,128)S(1)} %get-tuple-element.57.refs_9_) | copy-start | bytes 12292
  34.2 11.3 %all-to-all-start = ((f32[8,1,128]{2,1,0:T(1,128)}), f32[8,1,128]{2,1,0:T(1,128)}, u32[]{:S(2)}, u32[]{:S(2)}) async-start(f32[8,1,128]{2,1,0:T(1,128)} %bitcast.5), calls=%async_computation | async-start | bytes 8192 | tf_op jit(solution)/shard_map/all_to_all | solution.py:551
  39.0 0.7 %copy-start.9 = (f32[8,128]{1,0:T(8,128)S(1)}, f32[8,128]{1,0:T(8,128)}, u32[]{:S(2)}) copy-start(f32[8,128]{1,0:T(8,128)} %copy-done.8) | copy-start | bytes 12292
  39.0 0.7 %copy-start.12 = (f32[32]{0:T(128)S(1)}, f32[32]{0:T(128)}, u32[]{:S(2)}) copy-start(f32[32]{0:T(128)} %param.12) | copy-start | bytes 388
  39.7 0.8 %copy-start.1 = (f32[64,128]{1,0:T(8,128)S(1)}, f32[64,128]{1,0:T(8,128)}, u32[]{:S(2)}) copy-start(f32[64,128]{1,0:T(8,128)} %copy-done) | copy-start | bytes 98308
  40.5 0.8 %copy-start.3 = (f32[64,128]{1,0:T(8,128)S(1)}, f32[64,128]{1,0:T(8,128)}, u32[]{:S(2)}) copy-start(f32[64,128]{1,0:T(8,128)} %copy-done.2) | copy-start | bytes 98308
  44.3 0.6 %copy-start.4 = (f32[64,128]{1,0:T(8,128)}, f32[64,128]{1,0:T(8,128)S(1)}, u32[]{:S(2)}) copy-start(f32[64,128]{1,0:T(8,128)S(1)} %get-tuple-element.61.refs_10_) | copy-start | bytes 98308
  44.9 0.6 %copy-start.6 = (f32[64,128]{1,0:T(8,128)}, f32[64,128]{1,0:T(8,128)S(1)}, u32[]{:S(2)}) copy-start(f32[64,128]{1,0:T(8,128)S(1)} %get-tuple-element.62.refs_11_) | copy-start | bytes 98308
  48.0 10.4 %all-to-all-start.1 = ((f32[4,1,128]{2,1,0:T(1,128)}), f32[4,1,128]{2,1,0:T(1,128)}, u32[]{:S(2)}, u32[]{:S(2)}) async-start(f32[4,1,128]{2,1,0:T(1,128)} %broadcast_in_dim.17), calls=%async_computation.1 | async-start | bytes 4096 | tf_op jit(solution)/shard_map/all_to_all | solution.py:577
  51.7 0.7 %copy-start.10 = (f32[8,128]{1,0:T(8,128)S(1)}, f32[8,128]{1,0:T(8,128)}, u32[]{:S(2)}) copy-start(f32[8,128]{1,0:T(8,128)} %copy-done.8) | copy-start | bytes 12292
  51.8 0.7 %copy-start.16 = (f32[128]{0:T(128)S(1)}, f32[128]{0:T(128)}, u32[]{:S(2)}) copy-start(f32[128]{0:T(128)} %reduce_sum.18) | copy-start | bytes 1540
  52.4 0.7 %copy-start.13 = (f32[32]{0:T(128)S(1)}, f32[32]{0:T(128)}, u32[]{:S(2)}) copy-start(f32[32]{0:T(128)} %param.12) | copy-start | bytes 388
  53.1 0.8 %copy-start.5 = (f32[64,128]{1,0:T(8,128)S(1)}, f32[64,128]{1,0:T(8,128)}, u32[]{:S(2)}) copy-start(f32[64,128]{1,0:T(8,128)} %copy-done.4) | copy-start | bytes 98308
  53.8 0.8 %copy-start.7 = (f32[64,128]{1,0:T(8,128)S(1)}, f32[64,128]{1,0:T(8,128)}, u32[]{:S(2)}) copy-start(f32[64,128]{1,0:T(8,128)} %copy-done.6) | copy-start | bytes 98308

commit v8 on v6

--- a/solution.py
+++ b/solution.py
@@ -100,17 +100,26 @@
     return stack([ref[tail + i : tail + i + 1, :] for i in range(PARTS)], 1)
 
 
-def received(refs, block, width):
+def message_plan(reach):
+    near = [(1, 0, 0)]
+    relayed = [(1, 1, 0), (1, 1, 1)]
+    far = [(2, 1, 0), (2, 1, 1), (2, 0, 0)] if reach > 1 else []
+    rest = [(j, *one) for j in range(3, reach + 1) for one in ((0, 0), (1, 0), (1, 1))]
+    return near + far + relayed + rest
+
+
+def received(messages, reach, block, blocks, width):
     came = pull = None
-    for j in range(len(refs) // 2, 0, -1):
-        one, two = refs[2 * j - 2], refs[2 * j - 1]
-        a, b = message_block(one, block, width), message_block(two, block, width)
+    half, inner = divmod(block, blocks // 2)
+    for j in range(reach, 0, -1):
+        one, two = messages[j, 0, 0], messages[j, 1, half]
+        a, b = message_block(one, block, width), message_block(two, inner, width)
         first = jnp.broadcast_to(lax.rem(shard() + j, 2), a.shape) == 0
         near_came, near_pull = jnp.where(first, a, b), jnp.where(first, b, a)
         if came is None:
             came, pull = near_came, near_pull
         else:
-            a, b = message_tail(one, block, width), message_tail(two, block, width)
+            a, b = message_tail(one, block, width), message_tail(two, inner, width)
             first = jnp.broadcast_to(lax.rem(shard() + j, 2), a.shape) == 0
             came = near_came + jnp.where(first, a, b) * came
             pull = near_pull + jnp.where(first, b, a) * pull
@@ -132,6 +141,7 @@
     c_ref,
     one_ref,
     two_ref,
+    three_ref,
     lens_ref,
     alog_ref,
     small_sems,
@@ -202,11 +212,16 @@
         here = slice(pair * own, (pair + 1) * own)
         state = pair_states(b, keeping[here], x_ref[:, at])
         pulled = pair_states(c, carried[here], dy_ref[:, at])
-        tail = columns // LANES * width + pair
-        one_ref[pair * width : (pair + 1) * width, :] = jnp.where(even, state, pulled)
-        two_ref[pair * width : (pair + 1) * width, :] = jnp.where(even, pulled, state)
-        one_ref[tail : tail + 1, :] = jnp.where(left, kept[here][:1], kept[here][1:])
-        two_ref[tail : tail + 1, :] = jnp.where(left, kept[here][:1], kept[here][1:])
+        kept_row = jnp.where(left, kept[here][:1], kept[here][1:])
+        first, second = jnp.where(even, state, pulled), jnp.where(even, pulled, state)
+        pairs = columns // LANES
+        half, inner = divmod(pair, pairs // 2)
+        for ref, at, whole, value in (
+            (one_ref, pair, pairs, first),
+            ((two_ref, three_ref)[half], inner, pairs // 2, second),
+        ):
+            ref[at * width : (at + 1) * width, :] = value
+            ref[whole * width + at : whole * width + at + 1, :] = kept_row
 
 
 def inside_kernel(
@@ -218,6 +233,7 @@
     b_ref,
     dy_ref,
     c_ref,
+    _,
     xs_ref,
     ys_ref,
     v_wide_hbm,
@@ -331,19 +347,16 @@
         copy.wait()
 
 
-def send_order(reach):
-    return [at for j in range(reach) for at in (2 * j + 1, 2 * j)]
-
-
 def rates_kernel(reach, head_width, *refs):
-    messages = [ref for _, ref in sorted(zip(send_order(reach), refs), key=lambda pair: pair[0])]
-    ends_ref, fwd_ref, bwd_ref, small_ref, out_ref, came_ref, pull_ref = refs[2 * reach :]
+    plan = message_plan(reach)
+    messages = dict(zip(plan, refs))
+    ends_ref, fwd_ref, bwd_ref, small_ref, out_ref, came_ref, pull_ref = refs[len(plan) :]
     width, columns = fwd_ref.shape
     blocks = columns // WIDE
     whole = []
     for block in range(blocks):
         at = slice(block * WIDE, (block + 1) * WIDE)
-        came, pull = received(messages, block, width)
+        came, pull = received(messages, reach, block, blocks, width)
         came_ref[:, at] = came
         pull_ref[:, at] = pull
         terms = came * bwd_ref[:, at] + pull * (fwd_ref[:, at] + ends_ref[2:3, at] * came)
@@ -444,7 +457,7 @@
 
 
 def call(kernel, reach, outs, ins, flops, moved, scratch=()):
-    spaces = {"s": pltpu.SMEM, "v": pltpu.VMEM, "h": pltpu.HBM}
+    spaces = {"s": pltpu.SMEM, "v": pltpu.VMEM, "h": pltpu.HBM, "any": pl.ANY}
     return pl.pallas_call(
         kernel,
         out_shape=[
@@ -464,6 +477,11 @@
     return lax.ppermute(a, "ctx", [(i, j) for i, j in pairs if 0 <= j < count])
 
 
+def hand_on(a):
+    count = lax.axis_size("ctx")
+    return lax.ppermute(a, "ctx", [(i, i ^ 1) for i in range(count)])
+
+
 def in_hbm(a):
     return "h", pltpu.with_memory_space_constraint(a, pltpu.HBM)
 
@@ -490,7 +508,7 @@
             v((rows, columns), BF16),
             v((width, rows), BF16),
         ]
-        + [v((columns // LANES * (width + 1), LANES))] * 2,
+        + [v((columns // LANES * (width + 1) // part, LANES)) for part in (1, 2, 2)],
         [in_hbm(a) for a in (doc_lengths, alog, step_sizes, inputs, bt, grad_out, ct)],
         10**9,
         4 * 2**20,
@@ -501,7 +519,16 @@
             pltpu.SemaphoreType.DMA((2, PIECES)),
         ],
     )
-    messages = [send(payloads[at % 2], at // 2 + 1, at % 2) for at in send_order(reach)]
+    messages = {}
+    for j, second, half in message_plan(reach):
+        if (j, second) == (1, 1) and reach > 1:
+            continue
+        payload = payloads[1 + half if second else 0]
+        messages[j, second, half] = send(payload, j, second)
+    if reach > 1:
+        for half in (0, 1):
+            messages[1, 1, half] = hand_on(messages[2, 1, half])
+    messages = [messages[one] for one in message_plan(reach)]
     whole = "h", ((rows, columns), F32)
     state = v((width, columns))
     stage = pltpu.VMEM((rows, columns), F32)
@@ -514,7 +541,8 @@
         + [v((rows, 2 * width), BF16)] * 2
         + [v((8, rows)), transposed, transposed, v((2 * rows, heads))]
         + [state, state, v((8, columns)), v((1, LANES))],
-        [("s", doc_lengths)] + [("v", a) for a in (alog, skip, dt, x, b, dy, c)],
+        [("s", doc_lengths)] + [("v", a) for a in (alog, skip, dt, x, b, dy, c)]
+        + [("any", messages[0])],
         4 * 10**9,
         12 * 2**20,
         [stage, stage, pltpu.SemaphoreType.DMA((2, blocks))],

time: 46.9 us -> 45.2 us (0.964)
  waiting for transfers between devices: 11.2 us -> 9.83 us
    ppermute x4, waiting for transfers between devices: 9.67 us -> 7.64 us  [send(): return lax.ppermute(a, 'ctx', [(i, j) for i, j in pairs if 0 <= j < count])]
    ppermute x4, starting transfers between devices: 12.3 us -> 10.8 us  [send(): return lax.ppermute(a, 'ctx', [(i, j) for i, j in pairs if 0 <= j < count])]
    all_to_all x1, starting transfers between devices: 4.84 us -> 6.07 us  [per_device(): gathered = lax.all_to_all(partial, ('dp', 'ctx'), 0, 0, tiled=True)]
    ppermute x0 -> x2, waiting for transfers between devices: none -> 0.47 us  [hand_on(): return lax.ppermute(a, 'ctx', [(i, i ^ 1) for i in range(count)])]
  transfers between devices with their start and end apart: 5 -> 7, of which waited for: 3 -> 4; matrix products, arithmetic and copies ran while one was open for 0% -> 0% of each run, Pallas kernels for 26% -> 27%
where the time goes in v8:
time: 45.2 us; the launch traced here: 45 us
  starting transfers between devices  16.9 us (37%)
  Pallas kernels  16.2 us (36%)
  waiting for transfers between devices  9.83 us (22%)
  local copies, waits for them, and re-layouts  1.25 us (3%)
  between operations  0.72 us (2%)
    pallas_call x4, Pallas kernels, call(): pl.pallas_call(kernel, out_shape=[pltpu.HBM(*out) if place == 'h' else ja...  16.2 us
    ppermute x4, starting transfers between devices, send(): return lax.ppermute(a, 'ctx', [(i, j) for i, j in pairs if 0 <= j < count])  10.8 us
    ppermute x4, waiting for transfers between devices, send(): return lax.ppermute(a, 'ctx', [(i, j) for i, j in pairs if 0 <= j < count])  7.64 us
    all_to_all x1, starting transfers between devices, per_device(): gathered = lax.all_to_all(partial, ('dp', 'ctx'), 0, 0, tiled=True)  6.07 us
    all_to_all x1, waiting for transfers between devices, per_device(): gathered = lax.all_to_all(partial, ('dp', 'ctx'), 0, 0, tiled=True)  1.72 us
  transfers between devices with their start and end apart: 7, of which 4 were waited for; matrix products, arithmetic and copies ran while one was open for 0% of the time, Pallas kernels for 27%

profile of v8, /device:TPU:0, one launch (start us, length us, event | category | flops | bytes accessed | tf_op | source)
XLA Modules:
  0.0 45.0 jit_solution(11340658116864530582)
XLA Ops:
  0.6 2.8 %shard_map.127 = (f32[32,128]{1,0:T(8,128)S(1)}, bf16[128,2048]{1,0:T(8,128)(2,1)S(1)}, bf16[64,128]{1,0:T(8,128)(2,1)S(1)}, bf16[128,2048]{1,0:T(8,128)(2,1)S(1...) custom-call(s32[1,16]{1,0:T(1,128)} %lens_ref.1, ...), custom_call_target="tpu_custom_call" | custom-call | flops 1000000000 | bytes 4194304 | tf_op jit(solution)/shard_map/pallas_call | solution.py:461
  3.5 3.0 %collective-permute-start = (f32[1040,128]{1,0:T(8,128)S(1)}, f32[1040,128]{1,0:T(8,128)S(1)}, u32[]{:S(2)}, u32[]{:S(2)}) collective-permute-start(f32[1040,128]{1,0:T(8,128)S(1)} %get-tuple-element.35), channel_id=1, source_target_pairs={{0,1},{1,0},{2,3},{3,2},{4,5},{5,4},{6,7},{7,6},{8,9},{9,8},{10,11... | collective-permute-start | bytes 1597448 | tf_op jit(solution)/shard_map/ppermute | solution.py:477
  6.5 1.3 %collective-permute-start.1 = (f32[520,128]{1,0:T(8,128)S(1)}, f32[520,128]{1,0:T(8,128)S(1)}, u32[]{:S(2)}, u32[]{:S(2)}) collective-permute-start(f32[520,128]{1,0:T(8,128)S(1)} %get-tuple-element.36), channel_id=1, source_target_pairs={{1,3},{2,0},{3,5},{4,2},{5,7},{6,4},{9,11},{10,8},{11,13},{12,10},... | collective-permute-start | bytes 798728 | tf_op jit(solution)/shard_map/ppermute | solution.py:477
  7.8 1.3 %collective-permute-start.2 = (f32[520,128]{1,0:T(8,128)S(1)}, f32[520,128]{1,0:T(8,128)S(1)}, u32[]{:S(2)}, u32[]{:S(2)}) collective-permute-start(f32[520,128]{1,0:T(8,128)S(1)} %get-tuple-element.37), channel_id=1, source_target_pairs={{1,3},{2,0},{3,5},{4,2},{5,7},{6,4},{9,11},{10,8},{11,13},{12,10},... | collective-permute-start | bytes 798728 | tf_op jit(solution)/shard_map/ppermute | solution.py:477
  9.1 5.2 %collective-permute-start.3 = (f32[1040,128]{1,0:T(8,128)S(1)}, f32[1040,128]{1,0:T(8,128)S(1)}, u32[]{:S(2)}, u32[]{:S(2)}) collective-permute-start(f32[1040,128]{1,0:T(8,128)S(1)} %get-tuple-element.35), channel_id=1, source_target_pairs={{0,2},{2,4},{3,1},{4,6},{5,3},{7,5},{8,10},{10,12},{11,9},{12,14},... | collective-permute-start | bytes 1597448 | tf_op jit(solution)/shard_map/ppermute | solution.py:477
  14.3 3.4 %collective-permute-done.1.refs_1_ = f32[520,128]{1,0:T(8,128)S(1)} collective-permute-done((f32[520,128]{1,0:T(8,128)S(1)}, f32[520,128]{1,0:T(8,128)S(1)}, u32[]{:S(2)}, u32[]{:S(2)}) %collective-permute-start.1) | collective-permute-done | bytes 266272 | tf_op jit(solution)/shard_map/ppermute | solution.py:477
  17.7 0.0 collective-permute-start.4
  17.7 4.2 %collective-permute-done.2.refs_2_ = f32[520,128]{1,0:T(8,128)S(1)} collective-permute-done((f32[520,128]{1,0:T(8,128)S(1)}, f32[520,128]{1,0:T(8,128)S(1)}, u32[]{:S(2)}, u32[]{:S(2)}) %collective-permute-start.2) | collective-permute-done | bytes 266272 | tf_op jit(solution)/shard_map/ppermute | solution.py:477
  21.9 0.0 collective-permute-start.5
  21.9 0.0 copy-start.1
  22.0 0.0 copy-start.2
  22.0 0.6 %copy-done = s32[1,16]{1,0:T(1,128)S(1)} copy-done((s32[1,16]{1,0:T(1,128)S(1)}, s32[1,16]{1,0:T(1,128)}, u32[]{:S(2)}) %copy-start) | copy-done | bytes 88
  22.6 0.0 copy-done.1
  22.6 0.0 copy-done.2
  22.6 6.9 %shard_map.128 = (bf16[256,2048]{1,0:T(8,128)(2,1)S(1)}, bf16[256,2048]{1,0:T(8,128)(2,1)S(1)}, f32[128,2048]{1,0:T(8,128)}, f32[128,2048]{1,0:T(8,128)}, bf16[1...) custom-call(s32[1,16]{1,0:T(1,128)S(1)} %copy-done, ...), custom_call_target="tpu_custom_call" | custom-call | flops 4000000000 | bytes 12582912 | tf_op jit(solution)/shard_map/pallas_call | solution.py:461
  29.5 0.0 collective-permute-done.4.refs_4_
  29.5 0.5 %collective-permute-done.5.refs_5_ = f32[520,128]{1,0:T(8,128)S(1)} collective-permute-done((f32[520,128]{1,0:T(8,128)S(1)}, f32[520,128]{1,0:T(8,128)S(1)}, u32[]{:S(2)}, u32[]{:S(2)}) %collective-permute-start.5) | collective-permute-done | bytes 266272 | tf_op jit(solution)/shard_map/ppermute | solution.py:482
  30.0 0.0 collective-permute-done.3.refs_3_
  30.0 1.1 %shard_map.129 = (f32[32,128]{1,0:T(8,128)}, f32[64,2048]{1,0:T(8,128)S(1)}, f32[64,2048]{1,0:T(8,128)S(1)}) custom-call(f32[1040,128]{1,0:T(8,128)S(1)} %collective-permute-done._.refs_0_, f32[520,128]{1,0:T(8,128)S(1)} %collective-permute-done.1.refs_1_, f32[520,128]{1,0:T(8,128)S(1)} %collective-permute-done.2.refs_2_, ...), custom_call_target="tpu_custom_call" | custom-call | flops 100000000 | bytes 4194304 | tf_op jit(solution)/shard_map/pallas_call | solution.py:461
  31.2 6.1 %all-to-all-start = ((f32[32,1,128]{2,1,0:T(1,128)}), f32[32,1,128]{2,1,0:T(1,128)S(1)}, u32[]{:S(2)}, u32[]{:S(2)}) async-start(f32[32,1,128]{2,1,0:T(1,128)} %bitcast.7), calls=%async_computation | async-start | bytes 32768 | tf_op jit(solution)/shard_map/all_to_all | solution.py:577
  37.2 5.4 %shard_map.130 = (bf16[1,128,2048]{2,1,0:T(8,128)(2,1)}, bf16[1,64,128]{2,1,0:T(8,128)(2,1)}, bf16[1,64,128]{2,1,0:T(8,128)(2,1)}, f32[1,32,128]{2,1,0:T(8,128)}) custom-call(f32[64,2048]{1,0:T(8,128)S(1)} %get-tuple-element.47.came_ref, f32[64,2048]{1,0:T(8,128)S(1)} %get-tuple-element.48.pull_ref, f32[8,2048]{1,0:T(8,128)S(1)} %get-tuple-element.43.refs_6_.ends_ref, ...), custom_call_target="tpu_custom_call" | custom-call | flops 2000000000 | bytes 12582912 | tf_op jit(solution)/shard_map/pallas_call | solution.py:461
  42.6 1.7 %all-to-all-done = f32[32,1,128]{2,1,0:T(1,128)S(1)} async-done(((f32[32,1,128]{2,1,0:T(1,128)}), f32[32,1,128]{2,1,0:T(1,128)S(1)}, u32[]{:S(2)}, u32[]{:S(2)}) %all-to-all-start) | async-done | bytes 16416 | tf_op jit(solution)/shard_map/all_to_all | solution.py:577
  44.3 0.1 reduce_sum.9
  44.4 0.6 %fusion = (f32[32]{0:T(128)}, f32[32]{0:T(128)}) fusion(f32[128]{0:T(128)S(1)} %reduce_sum.9), kind=kLoop, calls=%fused_computation | loop fusion | bytes 512 | tf_op jit(solution)/shard_map/slice | solution.py:585
  (2 shorter events, 0.0 us)
Async XLA Ops:
  3.5 18.5 %collective-permute-start = (f32[1040,128]{1,0:T(8,128)S(1)}, f32[1040,128]{1,0:T(8,128)S(1)}, u32[]{:S(2)}, u32[]{:S(2)}) collective-permute-start(f32[1040,128]{1,0:T(8,128)S(1)} %get-tuple-element.35), channel_id=1, source_target_pairs={{0,1},{1,0},{2,3},{3,2},{4,5},{5,4},{6,7},{7,6},{8,9},{9,8},{10,11... | collective-permute-start | bytes 1597448 | tf_op jit(solution)/shard_map/ppermute | solution.py:477
  6.5 11.2 %collective-permute-start.1 = (f32[520,128]{1,0:T(8,128)S(1)}, f32[520,128]{1,0:T(8,128)S(1)}, u32[]{:S(2)}, u32[]{:S(2)}) collective-permute-start(f32[520,128]{1,0:T(8,128)S(1)} %get-tuple-element.36), channel_id=1, source_target_pairs={{1,3},{2,0},{3,5},{4,2},{5,7},{6,4},{9,11},{10,8},{11,13},{12,10},... | collective-permute-start | bytes 798728 | tf_op jit(solution)/shard_map/ppermute | solution.py:477
  7.8 14.2 %collective-permute-start.2 = (f32[520,128]{1,0:T(8,128)S(1)}, f32[520,128]{1,0:T(8,128)S(1)}, u32[]{:S(2)}, u32[]{:S(2)}) collective-permute-start(f32[520,128]{1,0:T(8,128)S(1)} %get-tuple-element.37), channel_id=1, source_target_pairs={{1,3},{2,0},{3,5},{4,2},{5,7},{6,4},{9,11},{10,8},{11,13},{12,10},... | collective-permute-start | bytes 798728 | tf_op jit(solution)/shard_map/ppermute | solution.py:477
  9.1 20.9 %collective-permute-start.3 = (f32[1040,128]{1,0:T(8,128)S(1)}, f32[1040,128]{1,0:T(8,128)S(1)}, u32[]{:S(2)}, u32[]{:S(2)}) collective-permute-start(f32[1040,128]{1,0:T(8,128)S(1)} %get-tuple-element.35), channel_id=1, source_target_pairs={{0,2},{2,4},{3,1},{4,6},{5,3},{7,5},{8,10},{10,12},{11,9},{12,14},... | collective-permute-start | bytes 1597448 | tf_op jit(solution)/shard_map/ppermute | solution.py:477
  17.7 11.8 %collective-permute-start.4 = (f32[520,128]{1,0:T(8,128)S(1)}, f32[520,128]{1,0:T(8,128)S(1)}, u32[]{:S(2)}, u32[]{:S(2)}) collective-permute-start(f32[520,128]{1,0:T(8,128)S(1)} %collective-permute-done.1.refs_1_), channel_id=1, source_target_pairs={{0,1},{1,0},{2,3},{3,2},{4,5},{5,4},{6,7},{7,6},{8,9},{9,8},{10,11... | collective-permute-start | bytes 798728 | tf_op jit(solution)/shard_map/ppermute | solution.py:482
  21.9 8.1 %collective-permute-start.5 = (f32[520,128]{1,0:T(8,128)S(1)}, f32[520,128]{1,0:T(8,128)S(1)}, u32[]{:S(2)}, u32[]{:S(2)}) collective-permute-start(f32[520,128]{1,0:T(8,128)S(1)} %collective-permute-done.2.refs_2_), channel_id=1, source_target_pairs={{0,1},{1,0},{2,3},{3,2},{4,5},{5,4},{6,7},{7,6},{8,9},{9,8},{10,11... | collective-permute-start | bytes 798728 | tf_op jit(solution)/shard_map/ppermute | solution.py:482
  21.9 0.7 %copy-start = (s32[1,16]{1,0:T(1,128)S(1)}, s32[1,16]{1,0:T(1,128)}, u32[]{:S(2)}) copy-start(s32[1,16]{1,0:T(1,128)} %lens_ref.1) | copy-start | bytes 196
  21.9 0.7 %copy-start.1 = (f32[32]{0:T(128)S(1)}, f32[32]{0:T(128)}, u32[]{:S(2)}) copy-start(f32[32]{0:T(128)} %param.13) | copy-start | bytes 388
  22.0 0.7 %copy-start.2 = (f32[32]{0:T(128)S(1)}, f32[32]{0:T(128)}, u32[]{:S(2)}) copy-start(f32[32]{0:T(128)} %param.12) | copy-start | bytes 388
  31.2 13.2 %all-to-all-start = ((f32[32,1,128]{2,1,0:T(1,128)}), f32[32,1,128]{2,1,0:T(1,128)S(1)}, u32[]{:S(2)}, u32[]{:S(2)}) async-start(f32[32,1,128]{2,1,0:T(1,128)} %bitcast.7), calls=%async_computation | async-start | bytes 32768 | tf_op jit(solution)/shard_map/all_to_all | solution.py:577

commit v9 on v8

--- a/solution.py
+++ b/solution.py
@@ -129,11 +129,14 @@
 def states_kernel(
     lens_hbm,
     alog_hbm,
+    skip_hbm,
     dt_hbm,
     x_hbm,
     b_hbm,
     dy_hbm,
     c_hbm,
+    alog_ref,
+    skip_ref,
     dt_ref,
     x_ref,
     b_ref,
@@ -143,7 +146,6 @@
     two_ref,
     three_ref,
     lens_ref,
-    alog_ref,
     small_sems,
     sems,
 ):
@@ -160,6 +162,7 @@
                 (dt_hbm.at[0], dt_ref),
                 (b_hbm.at[0], b_ref),
                 (c_hbm.at[0], c_ref),
+                (skip_hbm, skip_ref),
             )
         )
     ]
@@ -192,40 +195,43 @@
     b, c = b_ref[...].astype(F32), c_ref[...].astype(F32)
     own = LANES // head_width
 
-    def pair_states(vectors, weights, values):
-        parts = []
-        for h in range(own):
-            parts += split2(vectors * weights[h : h + 1, :])
-        out = dot(stack(parts, 0), values, 1, 0)
-        sides = [
-            out[2 * h * width : (2 * h + 1) * width]
-            + out[(2 * h + 1) * width : (2 * h + 2) * width]
-            for h in range(own)
-        ]
-        return jnp.where(left, sides[0], sides[1])
-
-    for pair in range(columns // LANES):
-        if pair * LANES % piece == 0:
-            large[pair * LANES // piece * 2].wait()
-            large[pair * LANES // piece * 2 + 1].wait()
-        at = slice(pair * LANES, (pair + 1) * LANES)
-        here = slice(pair * own, (pair + 1) * own)
-        state = pair_states(b, keeping[here], x_ref[:, at])
-        pulled = pair_states(c, carried[here], dy_ref[:, at])
-        kept_row = jnp.where(left, kept[here][:1], kept[here][1:])
-        first, second = jnp.where(even, state, pulled), jnp.where(even, pulled, state)
-        pairs = columns // LANES
-        half, inner = divmod(pair, pairs // 2)
-        for ref, at, whole, value in (
-            (one_ref, pair, pairs, first),
-            ((two_ref, three_ref)[half], inner, pairs // 2, second),
-        ):
-            ref[at * width : (at + 1) * width, :] = value
-            ref[whole * width + at : whole * width + at + 1, :] = kept_row
+    def block_states(vectors, weights, values):
+        rows_in = [stack(split2(vectors * weights[h : h + 1, :]), 1) for h in range(PARTS * own)]
+        out = dot(stack(rows_in, 0), stack([values, values], 0), 1, 0)
+        pairs = []
+        for i in range(PARTS):
+            lanes = slice(i * LANES, (i + 1) * LANES)
+            sides = [
+                out[h * width : (h + 1) * width, lanes] for h in range(i * own, (i + 1) * own)
+            ]
+            pairs.append(jnp.where(left, sides[0], sides[1]))
+        return pairs
+
+    pairs = columns // LANES
+    for block in range(columns // WIDE):
+        if block * WIDE % piece == 0:
+            large[block * WIDE // piece * 2].wait()
+            large[block * WIDE // piece * 2 + 1].wait()
+        at = slice(block * WIDE, (block + 1) * WIDE)
+        here = slice(block * PARTS * own, (block + 1) * PARTS * own)
+        states = block_states(b, keeping[here], x_ref[:, at])
+        pulls = block_states(c, carried[here], dy_ref[:, at])
+        for i in range(PARTS):
+            pair = block * PARTS + i
+            kept_row = jnp.where(left, kept[pair * own : pair * own + 1], kept[pair * own + 1 :][:1])
+            first = jnp.where(even, states[i], pulls[i])
+            second = jnp.where(even, pulls[i], states[i])
+            half, inner = divmod(pair, pairs // 2)
+            for ref, place_in, whole, value in (
+                (one_ref, pair, pairs, first),
+                ((two_ref, three_ref)[half], inner, pairs // 2, second),
+            ):
+                ref[place_in * width : (place_in + 1) * width, :] = value
+                ref[whole * width + place_in : whole * width + place_in + 1, :] = kept_row
 
 
 def inside_kernel(
-    lens_ref,
+    lens_hbm,
     alog_ref,
     skip_ref,
     dt_ref,
@@ -250,11 +256,19 @@
     small_ref,
     v_stage,
     dx_stage,
+    lens_ref,
+    lens_sem,
     sems,
 ):
     rows, columns = x_ref.shape
     heads, width = dt_ref.shape[0], b_ref.shape[0]
     head_width = columns // heads
+    lens_copy = pltpu.make_async_copy(lens_hbm, lens_ref, lens_sem)
+    lens_copy.start()
+    distance = head_distance(heads, head_width)
+    bt, ct = b_ref[...], c_ref[...]
+    raw_scores, raw_flipped = dot(ct, bt, 0, 0), dot(bt, ct, 0, 0)
+    lens_copy.wait()
     starts, offset, first, last = document_places(lens_ref, rows)
     through = jnp.where(first >= offset + rows, 1.0, 0.0)
     square = (rows, rows)
@@ -270,9 +284,8 @@
     dt = dt_ref[...]
     logs = sum(dot(lower, part, 1, 1) for part in split3(dt * rate_column(alog_ref)))
     steps = sum(dot(eye, part, 1, 1) for part in split3(dt))
-    bt, ct = b_ref[...], c_ref[...]
-    scores = split2(jnp.where(down, dot(ct, bt, 0, 0), 0.0))
-    flipped = split2(jnp.where(same & (place1 >= place0), dot(bt, ct, 0, 0), 0.0))
+    scores = split2(jnp.where(down, raw_scores, 0.0))
+    flipped = split2(jnp.where(same & (place1 >= place0), raw_flipped, 0.0))
     place = iota((width, rows), 1) + offset
     bt_end = jnp.where(place >= last, bt.astype(F32), 0.0)
     ct_live = jnp.where(place < first, ct.astype(F32), 0.0)
@@ -295,10 +308,8 @@
         ],
         0,
     )
-    distance = head_distance(heads, head_width)
-    d_scores = jnp.zeros(square, F32)
-    sums = jnp.zeros((2 * rows, heads), F32)
-    products = jnp.zeros((8, heads), F32)
+    d_scores = jnp.zeros((2 * rows, 2 * rows), F32)
+    sums = jnp.zeros((2 * rows + 16, heads), F32)
     copies = []
     for block in range(columns // WIDE):
         at = slice(block * WIDE, (block + 1) * WIDE)
@@ -316,18 +327,16 @@
         v_stage[:, at] = v_wide
         out = dot_pairs(scores, xs, 1, 0)
         back = dot_pairs(flipped, ys, 1, 0)
-        d_scores += dot_pairs(ys, xs, 1, 1)
+        d_scores += dot(stack(ys, 0), stack(xs, 0), 1, 1)
         dx_stage[:, at] = v_wide * back + skip_wide * dy
         for i, (stage, target) in enumerate(((v_stage, v_wide_hbm), (dx_stage, dx_hbm))):
             copy = pltpu.make_async_copy(stage.at[:, at], target.at[:, at], sems.at[i, block])
             copy.start()
             copies.append(copy)
         column_part = xv * back
-        for part in split3(stack([yu * out - column_part, column_part], 0)):
+        product = jnp.broadcast_to(jnp.sum(x * dy, axis=0, keepdims=True), (16, WIDE))
+        for part in split3(stack([yu * out - column_part, column_part, product], 0)):
             sums += dot(part, ones, 1, 0)
-        product = jnp.broadcast_to(jnp.sum(x * dy, axis=0, keepdims=True), (8, WIDE))
-        for part in split3(product):
-            products += dot(part, ones, 1, 0)
         ending = u_wide[rows - 1 : rows]
         end_log = l_wide[rows - 1 : rows]
         gap = end_log - l_wide
@@ -336,13 +345,14 @@
         ends_ref[0:1, at] = ending
         ends_ref[1:2, at] = ending * through
         ends_ref[2:3, at] = ending * through * end_log
+    d_scores = (d_scores[:rows, :rows] + d_scores[:rows, rows:]) + d_scores[rows:, :rows]
     d_scores = split2(jnp.where(down, d_scores, 0.0))
     dc_ref[...] = sum(dot(bt, p, 1, 1) for p in d_scores)
     db_ref[...] = sum(dot(ct, p, 1, 0) for p in d_scores)
-    sums_ref[...] = sums
+    sums_ref[...] = sums[: 2 * rows]
     rate_grads = jnp.sum(logs * sums[:rows], axis=0, keepdims=True)
     empty = jnp.zeros((1, LANES - 2 * heads), F32)
-    small_ref[...] = stack([rate_grads, products[:1], empty], 1)
+    small_ref[...] = stack([rate_grads, sums[2 * rows : 2 * rows + 1], empty], 1)
     for copy in copies:
         copy.wait()
 
@@ -365,7 +375,8 @@
     shape = (WIDE, LANES)
     column = lax.shift_right_logical(iota(shape, 0), log2(head_width))
     ones = jnp.where(column == (iota(shape, 1) & (own - 1)), 1.0, 0.0).astype(BF16)
-    sums = sum(dot(part, ones, 1, 0) for part in split3(stack(whole, 0)))
+    sums = dot(stack(split3(stack(whole, 0)), 0), ones, 1, 0)
+    sums = (sums[:blocks] + sums[blocks : 2 * blocks]) + sums[2 * blocks :]
     lane = iota(sums.shape, 1)
     mine = lax.shift_right_logical(lane, log2(own)) == iota(sums.shape, 0)
     total = small_ref[...] + jnp.sum(jnp.where(mine, sums, 0.0), axis=0, keepdims=True)
@@ -479,7 +490,7 @@
 
 def hand_on(a):
     count = lax.axis_size("ctx")
-    return lax.ppermute(a, "ctx", [(i, i ^ 1) for i in range(count)])
+    return lax.ppermute(a, "ctx", [(i, i ^ 1) for i in range(count) if i not in (1, count - 2)])
 
 
 def in_hbm(a):
@@ -498,10 +509,12 @@
     def v(shape, kind=F32):
         return "v", (shape, kind)
 
-    dt, x, b, dy, c, *payloads = call(
+    alog, skip, dt, x, b, dy, c, *payloads = call(
         states_kernel,
         reach,
         [
+            v(alog.shape),
+            v(skip.shape),
             v((heads, rows)),
             v((rows, columns), BF16),
             v((width, rows), BF16),
@@ -509,13 +522,12 @@
             v((width, rows), BF16),
         ]
         + [v((columns // LANES * (width + 1) // part, LANES)) for part in (1, 2, 2)],
-        [in_hbm(a) for a in (doc_lengths, alog, step_sizes, inputs, bt, grad_out, ct)],
+        [in_hbm(a) for a in (doc_lengths, alog, skip, step_sizes, inputs, bt, grad_out, ct)],
         10**9,
         4 * 2**20,
         [
             pltpu.SMEM(doc_lengths.shape, jnp.int32),
-            pltpu.VMEM(alog.shape, F32),
-            pltpu.SemaphoreType.DMA((5,)),
+            pltpu.SemaphoreType.DMA((6,)),
             pltpu.SemaphoreType.DMA((2, PIECES)),
         ],
     )
@@ -541,11 +553,18 @@
         + [v((rows, 2 * width), BF16)] * 2
         + [v((8, rows)), transposed, transposed, v((2 * rows, heads))]
         + [state, state, v((8, columns)), v((1, LANES))],
-        [("s", doc_lengths)] + [("v", a) for a in (alog, skip, dt, x, b, dy, c)]
+        [in_hbm(doc_lengths)]
+        + [("v", a) for a in (alog, skip, dt, x, b, dy, c)]
         + [("any", messages[0])],
         4 * 10**9,
         12 * 2**20,
-        [stage, stage, pltpu.SemaphoreType.DMA((2, blocks))],
+        [
+            stage,
+            stage,
+            pltpu.SMEM(doc_lengths.shape, jnp.int32),
+            pltpu.SemaphoreType.DMA,
+            pltpu.SemaphoreType.DMA((2, blocks)),
+        ],
     )
     partial, came, pull = call(
         functools.partial(rates_kernel, reach, columns // heads),
@@ -574,7 +593,7 @@
             pltpu.SemaphoreType.DMA((blocks,)),
         ],
     )
-    gathered = lax.all_to_all(partial, ("dp", "ctx"), 0, 0, tiled=True)
+    gathered = lax.all_to_all(partial, ("ctx", "dp"), 0, 0, tiled=True)
     totals = jnp.sum(gathered, axis=0)
     return (
         input_grads,

time: 45.2 us -> 44.9 us (level)
  starting transfers between devices: 16.9 us -> 20.1 us
  waiting for transfers between devices: 9.83 us -> 7.89 us
  Pallas kernels: 16.2 us -> 15.3 us
  local copies, waits for them, and re-layouts: 1.25 us -> 0.59 us
    ppermute x2, starting transfers between devices: 0.01 us -> 3.02 us  [hand_on(): lax.ppermute(a, 'ctx', [(i, i ^ 1) for i in range(count) if i not in (1,...]
    ppermute x4, waiting for transfers between devices: 7.64 us -> 6.12 us  [send(): return lax.ppermute(a, 'ctx', [(i, j) for i, j in pairs if 0 <= j < count])]
    pallas_call x4, Pallas kernels: 16.2 us -> 15.3 us  [call(): pl.pallas_call(kernel, out_shape=[pltpu.HBM(*out) if place == 'h' else ja...]
    unnamed x6 -> x0, local copies, waits for them, and re-layouts: 0.67 us -> none
    ppermute x2, waiting for transfers between devices: 0.47 us -> 0.01 us  [hand_on(): lax.ppermute(a, 'ctx', [(i, i ^ 1) for i in range(count) if i not in (1,...]
  transfers between devices with their start and end apart: 7 -> 7, of which waited for: 4 -> 3; matrix products, arithmetic and copies ran while one was open for 0% -> 0% of each run, Pallas kernels for 27% -> 25%
where the time goes in v9:
time: 44.9 us; the launch traced here: 44.6 us
  starting transfers between devices  20.1 us (45%)
  Pallas kernels  15.3 us (34%)
  waiting for transfers between devices  7.89 us (18%)
  between operations  0.74 us (2%)
  local copies, waits for them, and re-layouts  0.59 us (1%)
    pallas_call x4, Pallas kernels, call(): pl.pallas_call(kernel, out_shape=[pltpu.HBM(*out) if place == 'h' else ja...  15.3 us
    ppermute x4, starting transfers between devices, send(): return lax.ppermute(a, 'ctx', [(i, j) for i, j in pairs if 0 <= j < count])  10.8 us
    all_to_all x1, starting transfers between devices, per_device(): gathered = lax.all_to_all(partial, ('ctx', 'dp'), 0, 0, tiled=True)  6.25 us
    ppermute x4, waiting for transfers between devices, send(): return lax.ppermute(a, 'ctx', [(i, j) for i, j in pairs if 0 <= j < count])  6.12 us
    ppermute x2, starting transfers between devices, hand_on(): lax.ppermute(a, 'ctx', [(i, i ^ 1) for i in range(count) if i not in (1,...  3.02 us
    all_to_all x1, waiting for transfers between devices, per_device(): gathered = lax.all_to_all(partial, ('ctx', 'dp'), 0, 0, tiled=True)  1.76 us
  transfers between devices with their start and end apart: 7, of which 3 were waited for; matrix products, arithmetic and copies ran while one was open for 0% of the time, Pallas kernels for 25%

profile of v9, /device:TPU:0, one launch (start us, length us, event | category | flops | bytes accessed | tf_op | source)
XLA Modules:
  0.0 44.6 jit_solution(3385960329901255442)
XLA Ops:
  0.6 2.9 %shard_map.127 = (f32[1,32]{1,0:T(1,128)S(1)}, f32[1,32]{1,0:T(1,128)S(1)}, f32[32,128]{1,0:T(8,128)S(1)}, bf16[128,2048]{1,0:T(8,128)(2,1)S(1)}, bf16[64,128]{1...) custom-call(s32[1,16]{1,0:T(1,128)} %lens_hbm.3, ...), custom_call_target="tpu_custom_call" | custom-call | flops 1000000000 | bytes 4194304 | tf_op jit(solution)/shard_map/pallas_call | solution.py:472
  3.5 3.0 %collective-permute-start = (f32[1040,128]{1,0:T(8,128)S(1)}, f32[1040,128]{1,0:T(8,128)S(1)}, u32[]{:S(2)}, u32[]{:S(2)}) collective-permute-start(f32[1040,128]{1,0:T(8,128)S(1)} %get-tuple-element.37), channel_id=1, source_target_pairs={{0,1},{1,0},{2,3},{3,2},{4,5},{5,4},{6,7},{7,6},{8,9},{9,8},{10,11... | collective-permute-start | bytes 1597448 | tf_op jit(solution)/shard_map/ppermute | solution.py:488
  6.5 1.3 %collective-permute-start.1 = (f32[520,128]{1,0:T(8,128)S(1)}, f32[520,128]{1,0:T(8,128)S(1)}, u32[]{:S(2)}, u32[]{:S(2)}) collective-permute-start(f32[520,128]{1,0:T(8,128)S(1)} %get-tuple-element.38), channel_id=1, source_target_pairs={{1,3},{2,0},{3,5},{4,2},{5,7},{6,4},{9,11},{10,8},{11,13},{12,10},... | collective-permute-start | bytes 798728 | tf_op jit(solution)/shard_map/ppermute | solution.py:488
  7.8 1.3 %collective-permute-start.2 = (f32[520,128]{1,0:T(8,128)S(1)}, f32[520,128]{1,0:T(8,128)S(1)}, u32[]{:S(2)}, u32[]{:S(2)}) collective-permute-start(f32[520,128]{1,0:T(8,128)S(1)} %get-tuple-element.39), channel_id=1, source_target_pairs={{1,3},{2,0},{3,5},{4,2},{5,7},{6,4},{9,11},{10,8},{11,13},{12,10},... | collective-permute-start | bytes 798728 | tf_op jit(solution)/shard_map/ppermute | solution.py:488
  9.1 5.2 %collective-permute-start.3 = (f32[1040,128]{1,0:T(8,128)S(1)}, f32[1040,128]{1,0:T(8,128)S(1)}, u32[]{:S(2)}, u32[]{:S(2)}) collective-permute-start(f32[1040,128]{1,0:T(8,128)S(1)} %get-tuple-element.37), channel_id=1, source_target_pairs={{0,2},{2,4},{3,1},{4,6},{5,3},{7,5},{8,10},{10,12},{11,9},{12,14},... | collective-permute-start | bytes 1597448 | tf_op jit(solution)/shard_map/ppermute | solution.py:488
  14.3 3.4 %collective-permute-done.1.refs_1_ = f32[520,128]{1,0:T(8,128)S(1)} collective-permute-done((f32[520,128]{1,0:T(8,128)S(1)}, f32[520,128]{1,0:T(8,128)S(1)}, u32[]{:S(2)}, u32[]{:S(2)}) %collective-permute-start.1) | collective-permute-done | bytes 266272 | tf_op jit(solution)/shard_map/ppermute | solution.py:488
  17.7 1.5 %collective-permute-start.4 = (f32[520,128]{1,0:T(8,128)S(1)}, f32[520,128]{1,0:T(8,128)S(1)}, u32[]{:S(2)}, u32[]{:S(2)}) collective-permute-start(f32[520,128]{1,0:T(8,128)S(1)} %collective-permute-done.1.refs_1_), channel_id=1, source_target_pairs={{0,1},{2,3},{3,2},{4,5},{5,4},{7,6},{8,9},{10,11},{11,10},{12,13},... | collective-permute-start | bytes 798728 | tf_op jit(solution)/shard_map/ppermute | solution.py:493
  19.3 2.7 %collective-permute-done.2.refs_2_ = f32[520,128]{1,0:T(8,128)S(1)} collective-permute-done((f32[520,128]{1,0:T(8,128)S(1)}, f32[520,128]{1,0:T(8,128)S(1)}, u32[]{:S(2)}, u32[]{:S(2)}) %collective-permute-start.2) | collective-permute-done | bytes 266272 | tf_op jit(solution)/shard_map/ppermute | solution.py:488
  22.0 1.5 %collective-permute-start.5 = (f32[520,128]{1,0:T(8,128)S(1)}, f32[520,128]{1,0:T(8,128)S(1)}, u32[]{:S(2)}, u32[]{:S(2)}) collective-permute-start(f32[520,128]{1,0:T(8,128)S(1)} %collective-permute-done.2.refs_2_), channel_id=1, source_target_pairs={{0,1},{2,3},{3,2},{4,5},{5,4},{7,6},{8,9},{10,11},{11,10},{12,13},... | collective-permute-start | bytes 798728 | tf_op jit(solution)/shard_map/ppermute | solution.py:493
  23.5 0.0 collective-permute-done._.refs_0_
  23.5 5.8 %shard_map.128 = (bf16[256,2048]{1,0:T(8,128)(2,1)S(1)}, bf16[256,2048]{1,0:T(8,128)(2,1)S(1)}, f32[128,2048]{1,0:T(8,128)}, f32[128,2048]{1,0:T(8,128)}, bf16[1...) custom-call(s32[1,16]{1,0:T(1,128)} %lens_hbm.3, ...), custom_call_target="tpu_custom_call" | custom-call | flops 4000000000 | bytes 12582912 | tf_op jit(solution)/shard_map/pallas_call | solution.py:472
  29.3 0.0 collective-permute-done.4.refs_4_
  29.4 0.0 collective-permute-done.5.refs_5_
  29.4 0.0 collective-permute-done.3.refs_3_
  29.4 1.2 %shard_map.129 = (f32[32,128]{1,0:T(8,128)}, f32[64,2048]{1,0:T(8,128)S(1)}, f32[64,2048]{1,0:T(8,128)S(1)}) custom-call(f32[1040,128]{1,0:T(8,128)S(1)} %collective-permute-done._.refs_0_, f32[520,128]{1,0:T(8,128)S(1)} %collective-permute-done.1.refs_1_, f32[520,128]{1,0:T(8,128)S(1)} %collective-permute-done.2.refs_2_, ...), custom_call_target="tpu_custom_call" | custom-call | flops 100000000 | bytes 4194304 | tf_op jit(solution)/shard_map/pallas_call | solution.py:472
  30.6 6.3 %all-to-all-start = ((f32[32,1,128]{2,1,0:T(1,128)}), f32[32,1,128]{2,1,0:T(1,128)S(1)}, u32[]{:S(2)}, u32[]{:S(2)}) async-start(f32[32,1,128]{2,1,0:T(1,128)} %bitcast.7), calls=%async_computation | async-start | bytes 32768 | tf_op jit(solution)/shard_map/all_to_all | solution.py:596
  36.8 5.4 %shard_map.130 = (bf16[1,128,2048]{2,1,0:T(8,128)(2,1)}, bf16[1,64,128]{2,1,0:T(8,128)(2,1)}, bf16[1,64,128]{2,1,0:T(8,128)(2,1)}, f32[1,32,128]{2,1,0:T(8,128)}) custom-call(f32[64,2048]{1,0:T(8,128)S(1)} %get-tuple-element.51.came_ref, f32[64,2048]{1,0:T(8,128)S(1)} %get-tuple-element.52.pull_ref, f32[8,2048]{1,0:T(8,128)S(1)} %get-tuple-element.47.refs_6_.ends_ref, ...), custom_call_target="tpu_custom_call" | custom-call | flops 2000000000 | bytes 12582912 | tf_op jit(solution)/shard_map/pallas_call | solution.py:472
  42.2 1.8 %all-to-all-done = f32[32,1,128]{2,1,0:T(1,128)S(1)} async-done(((f32[32,1,128]{2,1,0:T(1,128)}), f32[32,1,128]{2,1,0:T(1,128)S(1)}, u32[]{:S(2)}, u32[]{:S(2)}) %all-to-all-start) | async-done | bytes 16416 | tf_op jit(solution)/shard_map/all_to_all | solution.py:596
  44.0 0.1 reduce_sum.9
  44.0 0.6 %fusion = (f32[32]{0:T(128)}, f32[32]{0:T(128)}) fusion(f32[128]{0:T(128)S(1)} %reduce_sum.9), kind=kLoop, calls=%fused_computation | loop fusion | bytes 512 | tf_op jit(solution)/shard_map/slice | solution.py:604
Async XLA Ops:
  3.5 20.0 %collective-permute-start = (f32[1040,128]{1,0:T(8,128)S(1)}, f32[1040,128]{1,0:T(8,128)S(1)}, u32[]{:S(2)}, u32[]{:S(2)}) collective-permute-start(f32[1040,128]{1,0:T(8,128)S(1)} %get-tuple-element.37), channel_id=1, source_target_pairs={{0,1},{1,0},{2,3},{3,2},{4,5},{5,4},{6,7},{7,6},{8,9},{9,8},{10,11... | collective-permute-start | bytes 1597448 | tf_op jit(solution)/shard_map/ppermute | solution.py:488
  6.5 11.2 %collective-permute-start.1 = (f32[520,128]{1,0:T(8,128)S(1)}, f32[520,128]{1,0:T(8,128)S(1)}, u32[]{:S(2)}, u32[]{:S(2)}) collective-permute-start(f32[520,128]{1,0:T(8,128)S(1)} %get-tuple-element.38), channel_id=1, source_target_pairs={{1,3},{2,0},{3,5},{4,2},{5,7},{6,4},{9,11},{10,8},{11,13},{12,10},... | collective-permute-start | bytes 798728 | tf_op jit(solution)/shard_map/ppermute | solution.py:488
  7.8 14.2 %collective-permute-start.2 = (f32[520,128]{1,0:T(8,128)S(1)}, f32[520,128]{1,0:T(8,128)S(1)}, u32[]{:S(2)}, u32[]{:S(2)}) collective-permute-start(f32[520,128]{1,0:T(8,128)S(1)} %get-tuple-element.39), channel_id=1, source_target_pairs={{1,3},{2,0},{3,5},{4,2},{5,7},{6,4},{9,11},{10,8},{11,13},{12,10},... | collective-permute-start | bytes 798728 | tf_op jit(solution)/shard_map/ppermute | solution.py:488
  9.1 20.2 %collective-permute-start.3 = (f32[1040,128]{1,0:T(8,128)S(1)}, f32[1040,128]{1,0:T(8,128)S(1)}, u32[]{:S(2)}, u32[]{:S(2)}) collective-permute-start(f32[1040,128]{1,0:T(8,128)S(1)} %get-tuple-element.37), channel_id=1, source_target_pairs={{0,2},{2,4},{3,1},{4,6},{5,3},{7,5},{8,10},{10,12},{11,9},{12,14},... | collective-permute-start | bytes 1597448 | tf_op jit(solution)/shard_map/ppermute | solution.py:488
  17.7 11.6 %collective-permute-start.4 = (f32[520,128]{1,0:T(8,128)S(1)}, f32[520,128]{1,0:T(8,128)S(1)}, u32[]{:S(2)}, u32[]{:S(2)}) collective-permute-start(f32[520,128]{1,0:T(8,128)S(1)} %collective-permute-done.1.refs_1_), channel_id=1, source_target_pairs={{0,1},{2,3},{3,2},{4,5},{5,4},{7,6},{8,9},{10,11},{11,10},{12,13},... | collective-permute-start | bytes 798728 | tf_op jit(solution)/shard_map/ppermute | solution.py:493
  22.0 7.4 %collective-permute-start.5 = (f32[520,128]{1,0:T(8,128)S(1)}, f32[520,128]{1,0:T(8,128)S(1)}, u32[]{:S(2)}, u32[]{:S(2)}) collective-permute-start(f32[520,128]{1,0:T(8,128)S(1)} %collective-permute-done.2.refs_2_), channel_id=1, source_target_pairs={{0,1},{2,3},{3,2},{4,5},{5,4},{7,6},{8,9},{10,11},{11,10},{12,13},... | collective-permute-start | bytes 798728 | tf_op jit(solution)/shard_map/ppermute | solution.py:493
  30.6 13.4 %all-to-all-start = ((f32[32,1,128]{2,1,0:T(1,128)}), f32[32,1,128]{2,1,0:T(1,128)S(1)}, u32[]{:S(2)}, u32[]{:S(2)}) async-start(f32[32,1,128]{2,1,0:T(1,128)} %bitcast.7), calls=%async_computation | async-start | bytes 32768 | tf_op jit(solution)/shard_map/all_to_all | solution.py:596

commit v10 on v9

--- a/solution.py
+++ b/solution.py
@@ -100,12 +100,13 @@
     return stack([ref[tail + i : tail + i + 1, :] for i in range(PARTS)], 1)
 
 
-def message_plan(reach):
+def message_plan(reach, only=None):
     near = [(1, 0, 0)]
     relayed = [(1, 1, 0), (1, 1, 1)]
     far = [(2, 1, 0), (2, 1, 1), (2, 0, 0)] if reach > 1 else []
     rest = [(j, *one) for j in range(3, reach + 1) for one in ((0, 0), (1, 0), (1, 1))]
-    return near + far + relayed + rest
+    plan = near + far + relayed + rest
+    return [one for one in plan if only is None or not one[1] or one[2] == only]
 
 
 def received(messages, reach, block, blocks, width):
@@ -357,25 +358,33 @@
         copy.wait()
 
 
-def rates_kernel(reach, head_width, *refs):
-    plan = message_plan(reach)
+def rates_kernel(reach, head_width, half, *refs):
+    plan = message_plan(reach, half)
     messages = dict(zip(plan, refs))
-    ends_ref, fwd_ref, bwd_ref, small_ref, out_ref, came_ref, pull_ref = refs[len(plan) :]
+    ends_ref, fwd_ref, bwd_ref, *refs = refs[len(plan) :]
     width, columns = fwd_ref.shape
     blocks = columns // WIDE
+    own_blocks = blocks // 2
+    came_ref, pull_ref, out_ref = refs[-3:]
     whole = []
-    for block in range(blocks):
+    for i in range(own_blocks):
+        block = half * own_blocks + i
         at = slice(block * WIDE, (block + 1) * WIDE)
+        own = slice(i * WIDE, (i + 1) * WIDE)
         came, pull = received(messages, reach, block, blocks, width)
-        came_ref[:, at] = came
-        pull_ref[:, at] = pull
+        came_ref[:, own] = came
+        pull_ref[:, own] = pull
         terms = came * bwd_ref[:, at] + pull * (fwd_ref[:, at] + ends_ref[2:3, at] * came)
         whole.append(jnp.sum(terms, axis=0, keepdims=True))
+    if not half:
+        out_ref[...] = stack(whole, 0)
+        return
+    small_ref, first_ref = refs[:2]
     own = WIDE // head_width
     shape = (WIDE, LANES)
     column = lax.shift_right_logical(iota(shape, 0), log2(head_width))
     ones = jnp.where(column == (iota(shape, 1) & (own - 1)), 1.0, 0.0).astype(BF16)
-    sums = dot(stack(split3(stack(whole, 0)), 0), ones, 1, 0)
+    sums = dot(stack(split3(stack([first_ref[...], *whole], 0)), 0), ones, 1, 0)
     sums = (sums[:blocks] + sums[blocks : 2 * blocks]) + sums[2 * blocks :]
     lane = iota(sums.shape, 1)
     mine = lax.shift_right_logical(lane, log2(own)) == iota(sums.shape, 0)
@@ -384,8 +393,10 @@
 
 
 def outputs_kernel(
-    came_ref,
-    pull_ref,
+    came_one,
+    came_two,
+    pull_one,
+    pull_two,
     ends_ref,
     xs_ref,
     ys_ref,
@@ -431,7 +442,9 @@
     for block in range(blocks):
         at = slice(block * WIDE, (block + 1) * WIDE)
         ones = head_columns(heads, columns // heads, block)
-        came, pull = came_ref[:, at], pull_ref[:, at]
+        half, inner = divmod(block, blocks // 2)
+        own = slice(inner * WIDE, (inner + 1) * WIDE)
+        came, pull = (came_one, came_two)[half][:, own], (pull_one, pull_two)[half][:, own]
         meet = jnp.sum(came * pull, axis=0, keepdims=True) * ends_ref[1:2, at]
         cames = stack(split2(came), 0)
         pulls = stack(split2(pull * ends_ref[0:1, at]), 0)
@@ -490,7 +503,7 @@
 
 def hand_on(a):
     count = lax.axis_size("ctx")
-    return lax.ppermute(a, "ctx", [(i, i ^ 1) for i in range(count) if i not in (1, count - 2)])
+    return lax.ppermute(a, "ctx", [(i, i ^ 1) for i in range(count)])
 
 
 def in_hbm(a):
@@ -540,7 +553,6 @@
     if reach > 1:
         for half in (0, 1):
             messages[1, 1, half] = hand_on(messages[2, 1, half])
-    messages = [messages[one] for one in message_plan(reach)]
     whole = "h", ((rows, columns), F32)
     state = v((width, columns))
     stage = pltpu.VMEM((rows, columns), F32)
@@ -555,7 +567,7 @@
         + [state, state, v((8, columns)), v((1, LANES))],
         [in_hbm(doc_lengths)]
         + [("v", a) for a in (alog, skip, dt, x, b, dy, c)]
-        + [("any", messages[0])],
+        + [("any", messages[1, 0, 0])],
         4 * 10**9,
         12 * 2**20,
         [
@@ -566,21 +578,29 @@
             pltpu.SemaphoreType.DMA((2, blocks)),
         ],
     )
-    partial, came, pull = call(
-        functools.partial(rates_kernel, reach, columns // heads),
-        reach,
-        [v((devices, LANES)), state, state],
-        [("v", a) for a in (*messages, ends, fwd_logs, bwd_logs, small)],
-        10**8,
-        4 * 2**20,
-    )
+    half_state = v((width, columns // 2))
+    joined, last = [], []
+    for half in (0, 1):
+        out = v((devices, LANES)) if half else v((blocks // 2, WIDE))
+        came, pull, partial = call(
+            functools.partial(rates_kernel, reach, columns // heads, half),
+            reach,
+            [half_state, half_state, out],
+            [("v", messages[one]) for one in message_plan(reach, half)]
+            + [("v", a) for a in (ends, fwd_logs, bwd_logs, *last)],
+            10**8,
+            4 * 2**20,
+        )
+        joined.append((came, pull))
+        last = [small, partial]
     input_grads, b_gradient, c_gradient, step_grads = call(
         outputs_kernel,
         reach,
         [("h", ((1, rows, columns), BF16))]
         + [v((1, width, rows), BF16)] * 2
         + [v((1, heads, rows))],
-        [("v", a) for a in (came, pull, ends, xs, ys)]
+        [("v", a) for side in zip(*joined) for a in side]
+        + [("v", a) for a in (ends, xs, ys)]
         + [in_hbm(v_wide), in_hbm(dx)]
         + [("v", a) for a in (b_end, c_live, masks, db, dc, sums, alog, dt)],
         2 * 10**9,

time: 44.9 us -> 45.1 us (level)
  waiting for transfers between devices: 7.89 us -> 11.4 us
  starting transfers between devices: 20.1 us -> 16.9 us
    ppermute x2, starting transfers between devices: 3.02 us -> 0.01 us  [hand_on(): return lax.ppermute(a, 'ctx', [(i, i ^ 1) for i in range(count)])]
    ppermute x2, waiting for transfers between devices: 0.01 us -> 2.02 us  [hand_on(): return lax.ppermute(a, 'ctx', [(i, i ^ 1) for i in range(count)])]
    ppermute x4, waiting for transfers between devices: 6.12 us -> 7.64 us  [send(): return lax.ppermute(a, 'ctx', [(i, j) for i, j in pairs if 0 <= j < count])]
    pallas_call x4 -> x5, Pallas kernels: 15.3 us -> 15.2 us  [call(): pl.pallas_call(kernel, out_shape=[pltpu.HBM(*out) if place == 'h' else ja...]
  transfers between devices with their start and end apart: 7 -> 7, of which waited for: 3 -> 4; matrix products, arithmetic and copies ran while one was open for 0% -> 0% of each run, Pallas kernels for 25% -> 25%
where the time goes in v10:
time: 45.1 us; the launch traced here: 44.9 us
  starting transfers between devices  16.9 us (37%)
  Pallas kernels  15.2 us (34%)
  waiting for transfers between devices  11.4 us (25%)
  between operations  0.71 us (2%)
  local copies, waits for them, and re-layouts  0.59 us (1%)
    pallas_call x5, Pallas kernels, call(): pl.pallas_call(kernel, out_shape=[pltpu.HBM(*out) if place == 'h' else ja...  15.2 us
    ppermute x4, starting transfers between devices, send(): return lax.ppermute(a, 'ctx', [(i, j) for i, j in pairs if 0 <= j < count])  10.8 us
    ppermute x4, waiting for transfers between devices, send(): return lax.ppermute(a, 'ctx', [(i, j) for i, j in pairs if 0 <= j < count])  7.64 us
    all_to_all x1, starting transfers between devices, per_device(): gathered = lax.all_to_all(partial, ('ctx', 'dp'), 0, 0, tiled=True)  6.07 us
    ppermute x2, waiting for transfers between devices, hand_on(): return lax.ppermute(a, 'ctx', [(i, i ^ 1) for i in range(count)])  2.02 us
    all_to_all x1, waiting for transfers between devices, per_device(): gathered = lax.all_to_all(partial, ('ctx', 'dp'), 0, 0, tiled=True)  1.76 us
  transfers between devices with their start and end apart: 7, of which 4 were waited for; matrix products, arithmetic and copies ran while one was open for 0% of the time, Pallas kernels for 25%

profile of v10, /device:TPU:0, one launch (start us, length us, event | category | flops | bytes accessed | tf_op | source)
XLA Modules:
  0.0 44.9 jit_solution(3175877289480791432)
XLA Ops:
  0.6 2.9 %shard_map.127 = (f32[1,32]{1,0:T(1,128)S(1)}, f32[1,32]{1,0:T(1,128)S(1)}, f32[32,128]{1,0:T(8,128)S(1)}, bf16[128,2048]{1,0:T(8,128)(2,1)S(1)}, bf16[64,128]{1...) custom-call(s32[1,16]{1,0:T(1,128)} %lens_hbm.3, ...), custom_call_target="tpu_custom_call" | custom-call | flops 1000000000 | bytes 4194304 | tf_op jit(solution)/shard_map/pallas_call | solution.py:485
  3.5 3.0 %collective-permute-start = (f32[1040,128]{1,0:T(8,128)S(1)}, f32[1040,128]{1,0:T(8,128)S(1)}, u32[]{:S(2)}, u32[]{:S(2)}) collective-permute-start(f32[1040,128]{1,0:T(8,128)S(1)} %get-tuple-element.40), channel_id=1, source_target_pairs={{0,1},{1,0},{2,3},{3,2},{4,5},{5,4},{6,7},{7,6},{8,9},{9,8},{10,11... | collective-permute-start | bytes 1597448 | tf_op jit(solution)/shard_map/ppermute | solution.py:501
  6.5 1.3 %collective-permute-start.1 = (f32[520,128]{1,0:T(8,128)S(1)}, f32[520,128]{1,0:T(8,128)S(1)}, u32[]{:S(2)}, u32[]{:S(2)}) collective-permute-start(f32[520,128]{1,0:T(8,128)S(1)} %get-tuple-element.41), channel_id=1, source_target_pairs={{1,3},{2,0},{3,5},{4,2},{5,7},{6,4},{9,11},{10,8},{11,13},{12,10},... | collective-permute-start | bytes 798728 | tf_op jit(solution)/shard_map/ppermute | solution.py:501
  7.8 1.3 %collective-permute-start.4 = (f32[520,128]{1,0:T(8,128)S(1)}, f32[520,128]{1,0:T(8,128)S(1)}, u32[]{:S(2)}, u32[]{:S(2)}) collective-permute-start(f32[520,128]{1,0:T(8,128)S(1)} %get-tuple-element.53), channel_id=1, source_target_pairs={{1,3},{2,0},{3,5},{4,2},{5,7},{6,4},{9,11},{10,8},{11,13},{12,10},... | collective-permute-start | bytes 798728 | tf_op jit(solution)/shard_map/ppermute | solution.py:501
  9.1 5.2 %collective-permute-start.2 = (f32[1040,128]{1,0:T(8,128)S(1)}, f32[1040,128]{1,0:T(8,128)S(1)}, u32[]{:S(2)}, u32[]{:S(2)}) collective-permute-start(f32[1040,128]{1,0:T(8,128)S(1)} %get-tuple-element.40), channel_id=1, source_target_pairs={{0,2},{2,4},{3,1},{4,6},{5,3},{7,5},{8,10},{10,12},{11,9},{12,14},... | collective-permute-start | bytes 1597448 | tf_op jit(solution)/shard_map/ppermute | solution.py:501
  14.3 3.4 %collective-permute-done.1.refs_1_ = f32[520,128]{1,0:T(8,128)S(1)} collective-permute-done((f32[520,128]{1,0:T(8,128)S(1)}, f32[520,128]{1,0:T(8,128)S(1)}, u32[]{:S(2)}, u32[]{:S(2)}) %collective-permute-start.1) | collective-permute-done | bytes 266272 | tf_op jit(solution)/shard_map/ppermute | solution.py:501
  17.7 0.0 collective-permute-start.3
  17.8 4.2 %collective-permute-done.4.refs_1_ = f32[520,128]{1,0:T(8,128)S(1)} collective-permute-done((f32[520,128]{1,0:T(8,128)S(1)}, f32[520,128]{1,0:T(8,128)S(1)}, u32[]{:S(2)}, u32[]{:S(2)}) %collective-permute-start.4) | collective-permute-done | bytes 266272 | tf_op jit(solution)/shard_map/ppermute | solution.py:501
  22.0 0.0 collective-permute-start.5
  22.0 0.0 collective-permute-done._.refs_0_
  22.0 5.8 %shard_map.128 = (bf16[256,2048]{1,0:T(8,128)(2,1)S(1)}, bf16[256,2048]{1,0:T(8,128)(2,1)S(1)}, f32[128,2048]{1,0:T(8,128)}, f32[128,2048]{1,0:T(8,128)}, bf16[1...) custom-call(s32[1,16]{1,0:T(1,128)} %lens_hbm.3, ...), custom_call_target="tpu_custom_call" | custom-call | flops 4000000000 | bytes 12582912 | tf_op jit(solution)/shard_map/pallas_call | solution.py:485
  27.8 0.0 collective-permute-done.2.refs_2_
  27.8 0.0 collective-permute-done.3.refs_3_
  27.8 0.2 shard_map.129
  28.0 2.0 %collective-permute-done.5.refs_3_ = f32[520,128]{1,0:T(8,128)S(1)} collective-permute-done((f32[520,128]{1,0:T(8,128)S(1)}, f32[520,128]{1,0:T(8,128)S(1)}, u32[]{:S(2)}, u32[]{:S(2)}) %collective-permute-start.5) | collective-permute-done | bytes 266272 | tf_op jit(solution)/shard_map/ppermute | solution.py:506
  30.1 0.9 %shard_map.130 = (f32[64,1024]{1,0:T(8,128)S(1)}, f32[64,1024]{1,0:T(8,128)S(1)}, f32[32,128]{1,0:T(8,128)}) custom-call(f32[1040,128]{1,0:T(8,128)S(1)} %collective-permute-done._.refs_0_, f32[520,128]{1,0:T(8,128)S(1)} %collective-permute-done.4.refs_1_, f32[1040,128]{1,0:T(8,128)S(1)} %collective-permute-done.2.refs_2_, ...), custom_call_target="tpu_custom_call" | custom-call | flops 100000000 | bytes 4194304 | tf_op jit(solution)/shard_map/pallas_call | solution.py:485
  31.0 6.1 %all-to-all-start = ((f32[32,1,128]{2,1,0:T(1,128)}), f32[32,1,128]{2,1,0:T(1,128)S(1)}, u32[]{:S(2)}, u32[]{:S(2)}) async-start(f32[32,1,128]{2,1,0:T(1,128)} %bitcast.7), calls=%async_computation | async-start | bytes 32768 | tf_op jit(solution)/shard_map/all_to_all | solution.py:616
  37.1 5.4 %shard_map.131 = (bf16[1,128,2048]{2,1,0:T(8,128)(2,1)}, bf16[1,64,128]{2,1,0:T(8,128)(2,1)}, bf16[1,64,128]{2,1,0:T(8,128)(2,1)}, f32[1,32,128]{2,1,0:T(8,128)}) custom-call(f32[64,1024]{1,0:T(8,128)S(1)} %get-tuple-element.52.came_one, f32[64,1024]{1,0:T(8,128)S(1)} %get-tuple-element.56.came_two, f32[64,1024]{1,0:T(8,128)S(1)} %get-tuple-element.57.pull_one, ...), custom_call_target="tpu_custom_call" | custom-call | flops 2000000000 | bytes 12582912 | tf_op jit(solution)/shard_map/pallas_call | solution.py:485
  42.5 1.8 %all-to-all-done = f32[32,1,128]{2,1,0:T(1,128)S(1)} async-done(((f32[32,1,128]{2,1,0:T(1,128)}), f32[32,1,128]{2,1,0:T(1,128)S(1)}, u32[]{:S(2)}, u32[]{:S(2)}) %all-to-all-start) | async-done | bytes 16416 | tf_op jit(solution)/shard_map/all_to_all | solution.py:616
  44.2 0.1 reduce_sum.9
  44.3 0.6 %fusion = (f32[32]{0:T(128)}, f32[32]{0:T(128)}) fusion(f32[128]{0:T(128)S(1)} %reduce_sum.9), kind=kLoop, calls=%fused_computation | loop fusion | bytes 512 | tf_op jit(solution)/shard_map/slice | solution.py:624
Async XLA Ops:
  3.5 18.5 %collective-permute-start = (f32[1040,128]{1,0:T(8,128)S(1)}, f32[1040,128]{1,0:T(8,128)S(1)}, u32[]{:S(2)}, u32[]{:S(2)}) collective-permute-start(f32[1040,128]{1,0:T(8,128)S(1)} %get-tuple-element.40), channel_id=1, source_target_pairs={{0,1},{1,0},{2,3},{3,2},{4,5},{5,4},{6,7},{7,6},{8,9},{9,8},{10,11... | collective-permute-start | bytes 1597448 | tf_op jit(solution)/shard_map/ppermute | solution.py:501
  6.5 11.2 %collective-permute-start.1 = (f32[520,128]{1,0:T(8,128)S(1)}, f32[520,128]{1,0:T(8,128)S(1)}, u32[]{:S(2)}, u32[]{:S(2)}) collective-permute-start(f32[520,128]{1,0:T(8,128)S(1)} %get-tuple-element.41), channel_id=1, source_target_pairs={{1,3},{2,0},{3,5},{4,2},{5,7},{6,4},{9,11},{10,8},{11,13},{12,10},... | collective-permute-start | bytes 798728 | tf_op jit(solution)/shard_map/ppermute | solution.py:501
  7.8 14.2 %collective-permute-start.4 = (f32[520,128]{1,0:T(8,128)S(1)}, f32[520,128]{1,0:T(8,128)S(1)}, u32[]{:S(2)}, u32[]{:S(2)}) collective-permute-start(f32[520,128]{1,0:T(8,128)S(1)} %get-tuple-element.53), channel_id=1, source_target_pairs={{1,3},{2,0},{3,5},{4,2},{5,7},{6,4},{9,11},{10,8},{11,13},{12,10},... | collective-permute-start | bytes 798728 | tf_op jit(solution)/shard_map/ppermute | solution.py:501
  9.1 18.7 %collective-permute-start.2 = (f32[1040,128]{1,0:T(8,128)S(1)}, f32[1040,128]{1,0:T(8,128)S(1)}, u32[]{:S(2)}, u32[]{:S(2)}) collective-permute-start(f32[1040,128]{1,0:T(8,128)S(1)} %get-tuple-element.40), channel_id=1, source_target_pairs={{0,2},{2,4},{3,1},{4,6},{5,3},{7,5},{8,10},{10,12},{11,9},{12,14},... | collective-permute-start | bytes 1597448 | tf_op jit(solution)/shard_map/ppermute | solution.py:501
  17.7 10.1 %collective-permute-start.3 = (f32[520,128]{1,0:T(8,128)S(1)}, f32[520,128]{1,0:T(8,128)S(1)}, u32[]{:S(2)}, u32[]{:S(2)}) collective-permute-start(f32[520,128]{1,0:T(8,128)S(1)} %collective-permute-done.1.refs_1_), channel_id=1, source_target_pairs={{0,1},{1,0},{2,3},{3,2},{4,5},{5,4},{6,7},{7,6},{8,9},{9,8},{10,11... | collective-permute-start | bytes 798728 | tf_op jit(solution)/shard_map/ppermute | solution.py:506
  22.0 8.1 %collective-permute-start.5 = (f32[520,128]{1,0:T(8,128)S(1)}, f32[520,128]{1,0:T(8,128)S(1)}, u32[]{:S(2)}, u32[]{:S(2)}) collective-permute-start(f32[520,128]{1,0:T(8,128)S(1)} %collective-permute-done.4.refs_1_), channel_id=1, source_target_pairs={{0,1},{1,0},{2,3},{3,2},{4,5},{5,4},{6,7},{7,6},{8,9},{9,8},{10,11... | collective-permute-start | bytes 798728 | tf_op jit(solution)/shard_map/ppermute | solution.py:506
  31.0 13.2 %all-to-all-start = ((f32[32,1,128]{2,1,0:T(1,128)}), f32[32,1,128]{2,1,0:T(1,128)S(1)}, u32[]{:S(2)}, u32[]{:S(2)}) async-start(f32[32,1,128]{2,1,0:T(1,128)} %bitcast.7), calls=%async_computation | async-start | bytes 32768 | tf_op jit(solution)/shard_map/all_to_all | solution.py:616

commit v11 on v10

--- a/solution.py
+++ b/solution.py
@@ -127,60 +127,54 @@
     return came, pull
 
 
-def states_kernel(
-    lens_hbm,
-    alog_hbm,
-    skip_hbm,
-    dt_hbm,
-    x_hbm,
-    b_hbm,
-    dy_hbm,
-    c_hbm,
-    alog_ref,
-    skip_ref,
-    dt_ref,
-    x_ref,
-    b_ref,
-    dy_ref,
-    c_ref,
-    one_ref,
-    two_ref,
-    three_ref,
-    lens_ref,
-    small_sems,
-    sems,
-):
+def states_kernel(second, *refs):
+    refs, sems = refs[:-PIECES], refs[-PIECES:]
+    if second:
+        lens_hbm, x_hbm, dy_hbm, alog_ref, dt_ref, b_ref, c_ref = refs[:7]
+        x_ref, *messages = refs[7:10]
+        lens_ref, small_sems = refs[10:]
+        moves = [(lens_hbm, lens_ref)]
+    else:
+        lens_hbm, x_hbm, dy_hbm, alog_hbm, skip_hbm, dt_hbm, b_hbm, c_hbm = refs[:8]
+        alog_ref, skip_ref, dt_ref, b_ref, c_ref, x_ref, *messages = refs[8:15]
+        lens_ref, small_sems = refs[15:]
+        moves = [
+            (dt_hbm.at[0], dt_ref),
+            (alog_hbm, alog_ref),
+            (lens_hbm, lens_ref),
+            (b_hbm.at[0], b_ref),
+            (c_hbm.at[0], c_ref),
+            (skip_hbm, skip_ref),
+        ]
     rows, columns = x_ref.shape
     heads, width = dt_ref.shape[0], b_ref.shape[0]
     head_width = columns // heads
     piece = columns // PIECES
     small = [
         pltpu.make_async_copy(source, target, small_sems.at[i])
-        for i, (source, target) in enumerate(
-            (
-                (lens_hbm, lens_ref),
-                (alog_hbm, alog_ref),
-                (dt_hbm.at[0], dt_ref),
-                (b_hbm.at[0], b_ref),
-                (c_hbm.at[0], c_ref),
-                (skip_hbm, skip_ref),
-            )
-        )
+        for i, (source, target) in enumerate(moves)
     ]
     for copy in small:
         copy.start()
-    large = []
-    for i in range(PIECES):
+
+    def piece_copy(source, i):
         at = slice(i * piece, (i + 1) * piece)
-        for side, (source, target) in enumerate(((x_hbm, x_ref), (dy_hbm, dy_ref))):
-            copy = pltpu.make_async_copy(
-                source.at[0, :, at], target.at[:, at], sems.at[side, i]
-            )
-            copy.start()
-            large.append(copy)
+        return pltpu.make_async_copy(source.at[0, :, at], x_ref.at[:, at], sems[i])
+
+    forward = lax.rem(shard() + second, 2)
+
+    @pl.when(forward == 0)
+    def _():
+        for i in range(PIECES):
+            piece_copy(x_hbm, i).start()
+
+    @pl.when(forward != 0)
+    def _():
+        for i in range(PIECES):
+            piece_copy(dy_hbm, i).start()
+
     square = (rows, rows)
     upper = jnp.where(iota(square, 0) <= iota(square, 1), 1.0, 0.0).astype(BF16)
-    even = jnp.broadcast_to(lax.rem(shard(), 2), (width, LANES)) == 0
     left = iota((1, LANES), 1) < head_width
     for copy in small:
         copy.wait()
@@ -193,42 +187,32 @@
     keeping = jnp.where(place >= last, jnp.exp(end_log - logs) * dt, 0.0)
     carried = jnp.where(place < first, jnp.exp(logs), 0.0)
     kept = jnp.broadcast_to(jnp.exp(end_log) * through, (heads, LANES))
-    b, c = b_ref[...].astype(F32), c_ref[...].astype(F32)
+    weights = jnp.where(jnp.broadcast_to(forward, (heads, rows)) == 0, keeping, carried)
+    vectors = jnp.where(
+        jnp.broadcast_to(forward, (width, rows)) == 0,
+        b_ref[...].astype(F32),
+        c_ref[...].astype(F32),
+    )
     own = LANES // head_width
-
-    def block_states(vectors, weights, values):
-        rows_in = [stack(split2(vectors * weights[h : h + 1, :]), 1) for h in range(PARTS * own)]
+    pairs = columns // LANES // len(messages)
+    for block in range(columns // WIDE):
+        if block * WIDE % piece == 0:
+            piece_copy(x_hbm, block * WIDE // piece).wait()
+        values = x_ref[:, block * WIDE : (block + 1) * WIDE]
+        here = range(block * PARTS * own, (block + 1) * PARTS * own)
+        rows_in = [stack(split2(vectors * weights[h : h + 1, :]), 1) for h in here]
         out = dot(stack(rows_in, 0), stack([values, values], 0), 1, 0)
-        pairs = []
         for i in range(PARTS):
             lanes = slice(i * LANES, (i + 1) * LANES)
             sides = [
                 out[h * width : (h + 1) * width, lanes] for h in range(i * own, (i + 1) * own)
             ]
-            pairs.append(jnp.where(left, sides[0], sides[1]))
-        return pairs
-
-    pairs = columns // LANES
-    for block in range(columns // WIDE):
-        if block * WIDE % piece == 0:
-            large[block * WIDE // piece * 2].wait()
-            large[block * WIDE // piece * 2 + 1].wait()
-        at = slice(block * WIDE, (block + 1) * WIDE)
-        here = slice(block * PARTS * own, (block + 1) * PARTS * own)
-        states = block_states(b, keeping[here], x_ref[:, at])
-        pulls = block_states(c, carried[here], dy_ref[:, at])
-        for i in range(PARTS):
             pair = block * PARTS + i
-            kept_row = jnp.where(left, kept[pair * own : pair * own + 1], kept[pair * own + 1 :][:1])
-            first = jnp.where(even, states[i], pulls[i])
-            second = jnp.where(even, pulls[i], states[i])
-            half, inner = divmod(pair, pairs // 2)
-            for ref, place_in, whole, value in (
-                (one_ref, pair, pairs, first),
-                ((two_ref, three_ref)[half], inner, pairs // 2, second),
-            ):
-                ref[place_in * width : (place_in + 1) * width, :] = value
-                ref[whole * width + place_in : whole * width + place_in + 1, :] = kept_row
+            part, inner = divmod(pair, pairs)
+            kept_row = jnp.where(left, kept[pair * own :][:1], kept[pair * own + 1 :][:1])
+            ref, tail = messages[part], pairs * width + inner
+            ref[inner * width : (inner + 1) * width, :] = jnp.where(left, sides[0], sides[1])
+            ref[tail : tail + 1, :] = kept_row
 
 
 def inside_kernel(
@@ -236,10 +220,10 @@
     alog_ref,
     skip_ref,
     dt_ref,
-    x_ref,
     b_ref,
-    dy_ref,
     c_ref,
+    one_ref,
+    two_ref,
     _,
     xs_ref,
     ys_ref,
@@ -261,7 +245,7 @@
     lens_sem,
     sems,
 ):
-    rows, columns = x_ref.shape
+    rows, columns = one_ref.shape
     heads, width = dt_ref.shape[0], b_ref.shape[0]
     head_width = columns // heads
     lens_copy = pltpu.make_async_copy(lens_hbm, lens_ref, lens_sem)
@@ -312,14 +296,15 @@
     d_scores = jnp.zeros((2 * rows, 2 * rows), F32)
     sums = jnp.zeros((2 * rows + 16, heads), F32)
     copies = []
+    even = jnp.broadcast_to(lax.rem(shard(), 2), (rows, WIDE)) == 0
     for block in range(columns // WIDE):
         at = slice(block * WIDE, (block + 1) * WIDE)
         wide = dot(tables, head_rows(distance, head_width, block), 1, 0)
         ones = head_columns(heads, head_width, block)
         u_wide, v_wide, l_wide = wide[:rows], wide[rows : 2 * rows], wide[2 * rows : 3 * rows]
         skip_wide = wide[3 * rows : 3 * rows + 1]
-        x = x_ref[:, at].astype(F32)
-        dy = dy_ref[:, at].astype(F32)
+        one, two = one_ref[:, at].astype(F32), two_ref[:, at].astype(F32)
+        x, dy = jnp.where(even, one, two), jnp.where(even, two, one)
         xv = x * v_wide
         yu = dy * u_wide
         xs, ys = split2(xv), split2(yu)
@@ -522,28 +507,30 @@
     def v(shape, kind=F32):
         return "v", (shape, kind)
 
-    alog, skip, dt, x, b, dy, c, *payloads = call(
-        states_kernel,
+    large = v((rows, columns), BF16)
+    lens_space = pltpu.SMEM(doc_lengths.shape, jnp.int32)
+    first_in = [in_hbm(a) for a in (doc_lengths, inputs, grad_out)]
+    alog, skip, dt, b, c, one, payload = call(
+        functools.partial(states_kernel, 0),
         reach,
-        [
-            v(alog.shape),
-            v(skip.shape),
-            v((heads, rows)),
-            v((rows, columns), BF16),
-            v((width, rows), BF16),
-            v((rows, columns), BF16),
-            v((width, rows), BF16),
-        ]
-        + [v((columns // LANES * (width + 1) // part, LANES)) for part in (1, 2, 2)],
-        [in_hbm(a) for a in (doc_lengths, alog, skip, step_sizes, inputs, bt, grad_out, ct)],
+        [v(alog.shape), v(skip.shape), v((heads, rows))]
+        + [v((width, rows), BF16)] * 2
+        + [large, v((columns // LANES * (width + 1), LANES))],
+        first_in + [in_hbm(a) for a in (alog, skip, step_sizes, bt, ct)],
         10**9,
-        4 * 2**20,
-        [
-            pltpu.SMEM(doc_lengths.shape, jnp.int32),
-            pltpu.SemaphoreType.DMA((6,)),
-            pltpu.SemaphoreType.DMA((2, PIECES)),
-        ],
-    )
+        2 * 2**20,
+        [lens_space, pltpu.SemaphoreType.DMA((6,))] + [pltpu.SemaphoreType.DMA] * PIECES,
+    )
+    two, *halves = call(
+        functools.partial(states_kernel, 1),
+        reach,
+        [large] + [v((columns // LANES * (width + 1) // 2, LANES))] * 2,
+        first_in + [("v", a) for a in (alog, dt, b, c)],
+        10**9,
+        2 * 2**20,
+        [lens_space, pltpu.SemaphoreType.DMA((1,))] + [pltpu.SemaphoreType.DMA] * PIECES,
+    )
+    payloads = [payload, *halves]
     messages = {}
     for j, second, half in message_plan(reach):
         if (j, second) == (1, 1) and reach > 1:
@@ -566,7 +553,7 @@
         + [v((8, rows)), transposed, transposed, v((2 * rows, heads))]
         + [state, state, v((8, columns)), v((1, LANES))],
         [in_hbm(doc_lengths)]
-        + [("v", a) for a in (alog, skip, dt, x, b, dy, c)]
+        + [("v", a) for a in (alog, skip, dt, b, c, one, two)]
         + [("any", messages[1, 0, 0])],
         4 * 10**9,
         12 * 2**20,

time: 45.1 us -> 45.4 us (level)
  Pallas kernels: 15.2 us -> 17 us
  starting transfers between devices: 16.9 us -> 15.7 us
    pallas_call x5 -> x6, Pallas kernels: 15.2 us -> 17 us  [call(): pl.pallas_call(kernel, out_shape=[pltpu.HBM(*out) if place == 'h' else ja...]
    all_to_all x1, starting transfers between devices: 6.07 us -> 4.95 us  [per_device(): gathered = lax.all_to_all(partial, ('ctx', 'dp'), 0, 0, tiled=True)]
  transfers between devices with their start and end apart: 7 -> 7, of which waited for: 4 -> 4; matrix products, arithmetic and copies ran while one was open for 0% -> 0% of each run, Pallas kernels for 25% -> 30%
where the time goes in v11:
time: 45.4 us; the launch traced here: 45.1 us
  Pallas kernels  17 us (37%)
  starting transfers between devices  15.7 us (35%)
  waiting for transfers between devices  11.1 us (24%)
  between operations  0.72 us (2%)
  local copies, waits for them, and re-layouts  0.59 us (1%)
    pallas_call x6, Pallas kernels, call(): pl.pallas_call(kernel, out_shape=[pltpu.HBM(*out) if place == 'h' else ja...  17 us
    ppermute x4, starting transfers between devices, send(): return lax.ppermute(a, 'ctx', [(i, j) for i, j in pairs if 0 <= j < count])  10.7 us
    ppermute x4, waiting for transfers between devices, send(): return lax.ppermute(a, 'ctx', [(i, j) for i, j in pairs if 0 <= j < count])  7.64 us
    all_to_all x1, starting transfers between devices, per_device(): gathered = lax.all_to_all(partial, ('ctx', 'dp'), 0, 0, tiled=True)  4.95 us
    all_to_all x1, waiting for transfers between devices, per_device(): gathered = lax.all_to_all(partial, ('ctx', 'dp'), 0, 0, tiled=True)  1.76 us
    ppermute x2, waiting for transfers between devices, hand_on(): return lax.ppermute(a, 'ctx', [(i, i ^ 1) for i in range(count)])  1.68 us
  transfers between devices with their start and end apart: 7, of which 4 were waited for; matrix products, arithmetic and copies ran while one was open for 0% of the time, Pallas kernels for 30%

profile of v11, /device:TPU:0, one launch (start us, length us, event | category | flops | bytes accessed | tf_op | source)
XLA Modules:
  0.0 45.1 jit_solution(7710385900339488741)
XLA Ops:
  0.6 2.4 %shard_map.127 = (f32[1,32]{1,0:T(1,128)S(1)}, f32[1,32]{1,0:T(1,128)S(1)}, f32[32,128]{1,0:T(8,128)S(1)}, bf16[64,128]{1,0:T(8,128)(2,1)S(1)}, bf16[64,128]{1,0...) custom-call(s32[1,16]{1,0:T(1,128)} %lens_hbm.1, bf16[1,128,2048]{2,1,0:T(8,128)(2,1)} %refs_1_.3, ...), custom_call_target="tpu_custom_call" | custom-call | flops 1000000000 | bytes 2097152 | tf_op jit(solution)/shard_map/pallas_call | solution.py:470
  3.1 2.9 %collective-permute-start = (f32[1040,128]{1,0:T(8,128)S(1)}, f32[1040,128]{1,0:T(8,128)S(1)}, u32[]{:S(2)}, u32[]{:S(2)}) collective-permute-start(f32[1040,128]{1,0:T(8,128)S(1)} %get-tuple-element.40), channel_id=1, source_target_pairs={{0,1},{1,0},{2,3},{3,2},{4,5},{5,4},{6,7},{7,6},{8,9},{9,8},{10,11... | collective-permute-start | bytes 1597448 | tf_op jit(solution)/shard_map/ppermute | solution.py:486
  6.0 2.0 %shard_map.128 = (bf16[128,2048]{1,0:T(8,128)(2,1)S(1)}, f32[520,128]{1,0:T(8,128)S(1)}, f32[520,128]{1,0:T(8,128)S(1)}) custom-call(s32[1,16]{1,0:T(1,128)} %lens_hbm.1, bf16[1,128,2048]{2,1,0:T(8,128)(2,1)} %refs_1_.3, bf16[1,128,2048]{2,1,0:T(8,128)(2,1)} %refs_2_.3, f32[1,32]{1,0:T(1,128)S(1)} %get-tuple-element.41.refs_3_.alog_ref, ...), custom_call_target="tpu_custom_call" | custom-call | flops 1000000000 | bytes 2097152 | tf_op jit(solution)/shard_map/pallas_call | solution.py:470
  8.0 1.3 %collective-permute-start.1 = (f32[520,128]{1,0:T(8,128)S(1)}, f32[520,128]{1,0:T(8,128)S(1)}, u32[]{:S(2)}, u32[]{:S(2)}) collective-permute-start(f32[520,128]{1,0:T(8,128)S(1)} %get-tuple-element.45), channel_id=1, source_target_pairs={{1,3},{2,0},{3,5},{4,2},{5,7},{6,4},{9,11},{10,8},{11,13},{12,10},... | collective-permute-start | bytes 798728 | tf_op jit(solution)/shard_map/ppermute | solution.py:486
  9.3 1.3 %collective-permute-start.4 = (f32[520,128]{1,0:T(8,128)S(1)}, f32[520,128]{1,0:T(8,128)S(1)}, u32[]{:S(2)}, u32[]{:S(2)}) collective-permute-start(f32[520,128]{1,0:T(8,128)S(1)} %get-tuple-element.53), channel_id=1, source_target_pairs={{1,3},{2,0},{3,5},{4,2},{5,7},{6,4},{9,11},{10,8},{11,13},{12,10},... | collective-permute-start | bytes 798728 | tf_op jit(solution)/shard_map/ppermute | solution.py:486
  10.6 5.2 %collective-permute-start.2 = (f32[1040,128]{1,0:T(8,128)S(1)}, f32[1040,128]{1,0:T(8,128)S(1)}, u32[]{:S(2)}, u32[]{:S(2)}) collective-permute-start(f32[1040,128]{1,0:T(8,128)S(1)} %get-tuple-element.40), channel_id=1, source_target_pairs={{0,2},{2,4},{3,1},{4,6},{5,3},{7,5},{8,10},{10,12},{11,9},{12,14},... | collective-permute-start | bytes 1597448 | tf_op jit(solution)/shard_map/ppermute | solution.py:486
  15.9 3.4 %collective-permute-done.1.refs_1_ = f32[520,128]{1,0:T(8,128)S(1)} collective-permute-done((f32[520,128]{1,0:T(8,128)S(1)}, f32[520,128]{1,0:T(8,128)S(1)}, u32[]{:S(2)}, u32[]{:S(2)}) %collective-permute-start.1) | collective-permute-done | bytes 266272 | tf_op jit(solution)/shard_map/ppermute | solution.py:486
  19.3 0.0 collective-permute-start.3
  19.3 4.2 %collective-permute-done.4.refs_1_ = f32[520,128]{1,0:T(8,128)S(1)} collective-permute-done((f32[520,128]{1,0:T(8,128)S(1)}, f32[520,128]{1,0:T(8,128)S(1)}, u32[]{:S(2)}, u32[]{:S(2)}) %collective-permute-start.4) | collective-permute-done | bytes 266272 | tf_op jit(solution)/shard_map/ppermute | solution.py:486
  23.5 0.0 collective-permute-start.5
  23.5 0.0 collective-permute-done._.refs_0_
  23.5 6.0 %shard_map.129 = (bf16[256,2048]{1,0:T(8,128)(2,1)S(1)}, bf16[256,2048]{1,0:T(8,128)(2,1)S(1)}, f32[128,2048]{1,0:T(8,128)}, f32[128,2048]{1,0:T(8,128)}, bf16[1...) custom-call(s32[1,16]{1,0:T(1,128)} %lens_hbm.1, ...), custom_call_target="tpu_custom_call" | custom-call | flops 4000000000 | bytes 12582912 | tf_op jit(solution)/shard_map/pallas_call | solution.py:470
  29.5 0.0 collective-permute-done.3.refs_3_
  29.5 0.0 collective-permute-done.2.refs_2_
  29.5 0.2 shard_map.130
  29.7 1.7 %collective-permute-done.5.refs_3_ = f32[520,128]{1,0:T(8,128)S(1)} collective-permute-done((f32[520,128]{1,0:T(8,128)S(1)}, f32[520,128]{1,0:T(8,128)S(1)}, u32[]{:S(2)}, u32[]{:S(2)}) %collective-permute-start.5) | collective-permute-done | bytes 266272 | tf_op jit(solution)/shard_map/ppermute | solution.py:491
  31.4 0.9 %shard_map.131 = (f32[64,1024]{1,0:T(8,128)S(1)}, f32[64,1024]{1,0:T(8,128)S(1)}, f32[32,128]{1,0:T(8,128)}) custom-call(f32[1040,128]{1,0:T(8,128)S(1)} %collective-permute-done._.refs_0_, f32[520,128]{1,0:T(8,128)S(1)} %collective-permute-done.4.refs_1_, f32[1040,128]{1,0:T(8,128)S(1)} %collective-permute-done.2.refs_2_, ...), custom_call_target="tpu_custom_call" | custom-call | flops 100000000 | bytes 4194304 | tf_op jit(solution)/shard_map/pallas_call | solution.py:470
  32.3 4.9 %all-to-all-start = ((f32[32,1,128]{2,1,0:T(1,128)}), f32[32,1,128]{2,1,0:T(1,128)S(1)}, u32[]{:S(2)}, u32[]{:S(2)}) async-start(f32[32,1,128]{2,1,0:T(1,128)} %bitcast.7), calls=%async_computation | async-start | bytes 32768 | tf_op jit(solution)/shard_map/all_to_all | solution.py:603
  37.3 5.4 %shard_map.132 = (bf16[1,128,2048]{2,1,0:T(8,128)(2,1)}, bf16[1,64,128]{2,1,0:T(8,128)(2,1)}, bf16[1,64,128]{2,1,0:T(8,128)(2,1)}, f32[1,32,128]{2,1,0:T(8,128)}) custom-call(f32[64,1024]{1,0:T(8,128)S(1)} %get-tuple-element.52.came_one, f32[64,1024]{1,0:T(8,128)S(1)} %get-tuple-element.56.came_two, f32[64,1024]{1,0:T(8,128)S(1)} %get-tuple-element.57.pull_one, ...), custom_call_target="tpu_custom_call" | custom-call | flops 2000000000 | bytes 12582912 | tf_op jit(solution)/shard_map/pallas_call | solution.py:470
  42.7 1.8 %all-to-all-done = f32[32,1,128]{2,1,0:T(1,128)S(1)} async-done(((f32[32,1,128]{2,1,0:T(1,128)}), f32[32,1,128]{2,1,0:T(1,128)S(1)}, u32[]{:S(2)}, u32[]{:S(2)}) %all-to-all-start) | async-done | bytes 16416 | tf_op jit(solution)/shard_map/all_to_all | solution.py:603
  44.4 0.1 reduce_sum.9
  44.5 0.6 %fusion = (f32[32]{0:T(128)}, f32[32]{0:T(128)}) fusion(f32[128]{0:T(128)S(1)} %reduce_sum.9), kind=kLoop, calls=%fused_computation | loop fusion | bytes 512 | tf_op jit(solution)/shard_map/slice | solution.py:611
Async XLA Ops:
  3.1 20.4 %collective-permute-start = (f32[1040,128]{1,0:T(8,128)S(1)}, f32[1040,128]{1,0:T(8,128)S(1)}, u32[]{:S(2)}, u32[]{:S(2)}) collective-permute-start(f32[1040,128]{1,0:T(8,128)S(1)} %get-tuple-element.40), channel_id=1, source_target_pairs={{0,1},{1,0},{2,3},{3,2},{4,5},{5,4},{6,7},{7,6},{8,9},{9,8},{10,11... | collective-permute-start | bytes 1597448 | tf_op jit(solution)/shard_map/ppermute | solution.py:486
  8.0 11.2 %collective-permute-start.1 = (f32[520,128]{1,0:T(8,128)S(1)}, f32[520,128]{1,0:T(8,128)S(1)}, u32[]{:S(2)}, u32[]{:S(2)}) collective-permute-start(f32[520,128]{1,0:T(8,128)S(1)} %get-tuple-element.45), channel_id=1, source_target_pairs={{1,3},{2,0},{3,5},{4,2},{5,7},{6,4},{9,11},{10,8},{11,13},{12,10},... | collective-permute-start | bytes 798728 | tf_op jit(solution)/shard_map/ppermute | solution.py:486
  9.3 14.2 %collective-permute-start.4 = (f32[520,128]{1,0:T(8,128)S(1)}, f32[520,128]{1,0:T(8,128)S(1)}, u32[]{:S(2)}, u32[]{:S(2)}) collective-permute-start(f32[520,128]{1,0:T(8,128)S(1)} %get-tuple-element.53), channel_id=1, source_target_pairs={{1,3},{2,0},{3,5},{4,2},{5,7},{6,4},{9,11},{10,8},{11,13},{12,10},... | collective-permute-start | bytes 798728 | tf_op jit(solution)/shard_map/ppermute | solution.py:486
  10.6 18.9 %collective-permute-start.2 = (f32[1040,128]{1,0:T(8,128)S(1)}, f32[1040,128]{1,0:T(8,128)S(1)}, u32[]{:S(2)}, u32[]{:S(2)}) collective-permute-start(f32[1040,128]{1,0:T(8,128)S(1)} %get-tuple-element.40), channel_id=1, source_target_pairs={{0,2},{2,4},{3,1},{4,6},{5,3},{7,5},{8,10},{10,12},{11,9},{12,14},... | collective-permute-start | bytes 1597448 | tf_op jit(solution)/shard_map/ppermute | solution.py:486
  19.3 10.2 %collective-permute-start.3 = (f32[520,128]{1,0:T(8,128)S(1)}, f32[520,128]{1,0:T(8,128)S(1)}, u32[]{:S(2)}, u32[]{:S(2)}) collective-permute-start(f32[520,128]{1,0:T(8,128)S(1)} %collective-permute-done.1.refs_1_), channel_id=1, source_target_pairs={{0,1},{1,0},{2,3},{3,2},{4,5},{5,4},{6,7},{7,6},{8,9},{9,8},{10,11... | collective-permute-start | bytes 798728 | tf_op jit(solution)/shard_map/ppermute | solution.py:491
  23.5 7.9 %collective-permute-start.5 = (f32[520,128]{1,0:T(8,128)S(1)}, f32[520,128]{1,0:T(8,128)S(1)}, u32[]{:S(2)}, u32[]{:S(2)}) collective-permute-start(f32[520,128]{1,0:T(8,128)S(1)} %collective-permute-done.4.refs_1_), channel_id=1, source_target_pairs={{0,1},{1,0},{2,3},{3,2},{4,5},{5,4},{6,7},{7,6},{8,9},{9,8},{10,11... | collective-permute-start | bytes 798728 | tf_op jit(solution)/shard_map/ppermute | solution.py:491
  32.3 12.1 %all-to-all-start = ((f32[32,1,128]{2,1,0:T(1,128)}), f32[32,1,128]{2,1,0:T(1,128)S(1)}, u32[]{:S(2)}, u32[]{:S(2)}) async-start(f32[32,1,128]{2,1,0:T(1,128)} %bitcast.7), calls=%async_computation | async-start | bytes 32768 | tf_op jit(solution)/shard_map/all_to_all | solution.py:603

commit v12 on v10

--- a/solution.py
+++ b/solution.py
@@ -13,7 +13,7 @@
 WIDE = 256
 PARTS = WIDE // LANES
 FAR = 2**30
-PIECES = 4
+PIECES = 2
 
 
 def dot(a, b, ca, cb):
@@ -158,16 +158,16 @@
         pltpu.make_async_copy(source, target, small_sems.at[i])
         for i, (source, target) in enumerate(
             (
+                (dt_hbm.at[0], dt_ref),
+                (alog_hbm, alog_ref),
                 (lens_hbm, lens_ref),
-                (alog_hbm, alog_ref),
-                (dt_hbm.at[0], dt_ref),
                 (b_hbm.at[0], b_ref),
                 (c_hbm.at[0], c_ref),
                 (skip_hbm, skip_ref),
             )
         )
     ]
-    for copy in small:
+    for copy in small[:-1]:
         copy.start()
     large = []
     for i in range(PIECES):
@@ -178,11 +178,12 @@
             )
             copy.start()
             large.append(copy)
+    small[-1].start()
     square = (rows, rows)
     upper = jnp.where(iota(square, 0) <= iota(square, 1), 1.0, 0.0).astype(BF16)
     even = jnp.broadcast_to(lax.rem(shard(), 2), (width, LANES)) == 0
     left = iota((1, LANES), 1) < head_width
-    for copy in small:
+    for copy in small[:-1]:
         copy.wait()
     _, offset, first, last = document_places(lens_ref, rows)
     through = jnp.where(first >= offset + rows, 1.0, 0.0)
@@ -229,6 +230,7 @@
             ):
                 ref[place_in * width : (place_in + 1) * width, :] = value
                 ref[whole * width + place_in : whole * width + place_in + 1, :] = kept_row
+    small[-1].wait()
 
 
 def inside_kernel(
@@ -503,7 +505,7 @@
 
 def hand_on(a):
     count = lax.axis_size("ctx")
-    return lax.ppermute(a, "ctx", [(i, i ^ 1) for i in range(count)])
+    return lax.ppermute(a, "ctx", [(i, i ^ 1) for i in range(count) if i not in (1, count - 2)])
 
 
 def in_hbm(a):

time: 45.1 us -> 44.2 us (0.980)
  waiting for transfers between devices: 11.4 us -> 7.88 us
  starting transfers between devices: 16.9 us -> 19.9 us
  Pallas kernels: 15.2 us -> 14.7 us
    ppermute x2, starting transfers between devices: 0.01 us -> 3.03 us  [hand_on(): lax.ppermute(a, 'ctx', [(i, i ^ 1) for i in range(count) if i not in (1,...]
    ppermute x2, waiting for transfers between devices: 2.02 us -> 0.01 us  [hand_on(): lax.ppermute(a, 'ctx', [(i, i ^ 1) for i in range(count) if i not in (1,...]
    ppermute x4, waiting for transfers between devices: 7.64 us -> 6.12 us  [send(): return lax.ppermute(a, 'ctx', [(i, j) for i, j in pairs if 0 <= j < count])]
    pallas_call x5, Pallas kernels: 15.2 us -> 14.7 us  [call(): pl.pallas_call(kernel, out_shape=[pltpu.HBM(*out) if place == 'h' else ja...]
  transfers between devices with their start and end apart: 7 -> 7, of which waited for: 4 -> 3; matrix products, arithmetic and copies ran while one was open for 0% -> 0% of each run, Pallas kernels for 25% -> 26%
where the time goes in v12:
time: 44.2 us; the launch traced here: 43.8 us
  starting transfers between devices  19.9 us (45%)
  Pallas kernels  14.7 us (33%)
  waiting for transfers between devices  7.88 us (18%)
  between operations  0.74 us (2%)
  local copies, waits for them, and re-layouts  0.59 us (1%)
    pallas_call x5, Pallas kernels, call(): pl.pallas_call(kernel, out_shape=[pltpu.HBM(*out) if place == 'h' else ja...  14.7 us
    ppermute x4, starting transfers between devices, send(): return lax.ppermute(a, 'ctx', [(i, j) for i, j in pairs if 0 <= j < count])  10.8 us
    ppermute x4, waiting for transfers between devices, send(): return lax.ppermute(a, 'ctx', [(i, j) for i, j in pairs if 0 <= j < count])  6.12 us
    all_to_all x1, starting transfers between devices, per_device(): gathered = lax.all_to_all(partial, ('ctx', 'dp'), 0, 0, tiled=True)  6.05 us
    ppermute x2, starting transfers between devices, hand_on(): lax.ppermute(a, 'ctx', [(i, i ^ 1) for i in range(count) if i not in (1,...  3.03 us
    all_to_all x1, waiting for transfers between devices, per_device(): gathered = lax.all_to_all(partial, ('ctx', 'dp'), 0, 0, tiled=True)  1.76 us
  transfers between devices with their start and end apart: 7, of which 3 were waited for; matrix products, arithmetic and copies ran while one was open for 0% of the time, Pallas kernels for 26%

profile of v12, /device:TPU:0, one launch (start us, length us, event | category | flops | bytes accessed | tf_op | source)
XLA Modules:
  0.0 43.8 jit_solution(4042566213713687751)
XLA Ops:
  0.6 2.3 %shard_map.127 = (f32[1,32]{1,0:T(1,128)S(1)}, f32[1,32]{1,0:T(1,128)S(1)}, f32[32,128]{1,0:T(8,128)S(1)}, bf16[128,2048]{1,0:T(8,128)(2,1)S(1)}, bf16[64,128]{1...) custom-call(s32[1,16]{1,0:T(1,128)} %lens_hbm.3, ...), custom_call_target="tpu_custom_call" | custom-call | flops 1000000000 | bytes 4194304 | tf_op jit(solution)/shard_map/pallas_call | solution.py:487
  2.9 3.0 %collective-permute-start = (f32[1040,128]{1,0:T(8,128)S(1)}, f32[1040,128]{1,0:T(8,128)S(1)}, u32[]{:S(2)}, u32[]{:S(2)}) collective-permute-start(f32[1040,128]{1,0:T(8,128)S(1)} %get-tuple-element.40), channel_id=1, source_target_pairs={{0,1},{1,0},{2,3},{3,2},{4,5},{5,4},{6,7},{7,6},{8,9},{9,8},{10,11... | collective-permute-start | bytes 1597448 | tf_op jit(solution)/shard_map/ppermute | solution.py:503
  6.0 1.3 %collective-permute-start.1 = (f32[520,128]{1,0:T(8,128)S(1)}, f32[520,128]{1,0:T(8,128)S(1)}, u32[]{:S(2)}, u32[]{:S(2)}) collective-permute-start(f32[520,128]{1,0:T(8,128)S(1)} %get-tuple-element.41), channel_id=1, source_target_pairs={{1,3},{2,0},{3,5},{4,2},{5,7},{6,4},{9,11},{10,8},{11,13},{12,10},... | collective-permute-start | bytes 798728 | tf_op jit(solution)/shard_map/ppermute | solution.py:503
  7.3 1.3 %collective-permute-start.4 = (f32[520,128]{1,0:T(8,128)S(1)}, f32[520,128]{1,0:T(8,128)S(1)}, u32[]{:S(2)}, u32[]{:S(2)}) collective-permute-start(f32[520,128]{1,0:T(8,128)S(1)} %get-tuple-element.53), channel_id=1, source_target_pairs={{1,3},{2,0},{3,5},{4,2},{5,7},{6,4},{9,11},{10,8},{11,13},{12,10},... | collective-permute-start | bytes 798728 | tf_op jit(solution)/shard_map/ppermute | solution.py:503
  8.6 5.2 %collective-permute-start.2 = (f32[1040,128]{1,0:T(8,128)S(1)}, f32[1040,128]{1,0:T(8,128)S(1)}, u32[]{:S(2)}, u32[]{:S(2)}) collective-permute-start(f32[1040,128]{1,0:T(8,128)S(1)} %get-tuple-element.40), channel_id=1, source_target_pairs={{0,2},{2,4},{3,1},{4,6},{5,3},{7,5},{8,10},{10,12},{11,9},{12,14},... | collective-permute-start | bytes 1597448 | tf_op jit(solution)/shard_map/ppermute | solution.py:503
  13.8 3.4 %collective-permute-done.1.refs_1_ = f32[520,128]{1,0:T(8,128)S(1)} collective-permute-done((f32[520,128]{1,0:T(8,128)S(1)}, f32[520,128]{1,0:T(8,128)S(1)}, u32[]{:S(2)}, u32[]{:S(2)}) %collective-permute-start.1) | collective-permute-done | bytes 266272 | tf_op jit(solution)/shard_map/ppermute | solution.py:503
  17.2 1.5 %collective-permute-start.3 = (f32[520,128]{1,0:T(8,128)S(1)}, f32[520,128]{1,0:T(8,128)S(1)}, u32[]{:S(2)}, u32[]{:S(2)}) collective-permute-start(f32[520,128]{1,0:T(8,128)S(1)} %collective-permute-done.1.refs_1_), channel_id=1, source_target_pairs={{0,1},{2,3},{3,2},{4,5},{5,4},{7,6},{8,9},{10,11},{11,10},{12,13},... | collective-permute-start | bytes 798728 | tf_op jit(solution)/shard_map/ppermute | solution.py:508
  18.7 2.7 %collective-permute-done.4.refs_1_ = f32[520,128]{1,0:T(8,128)S(1)} collective-permute-done((f32[520,128]{1,0:T(8,128)S(1)}, f32[520,128]{1,0:T(8,128)S(1)}, u32[]{:S(2)}, u32[]{:S(2)}) %collective-permute-start.4) | collective-permute-done | bytes 266272 | tf_op jit(solution)/shard_map/ppermute | solution.py:503
  21.4 1.5 %collective-permute-start.5 = (f32[520,128]{1,0:T(8,128)S(1)}, f32[520,128]{1,0:T(8,128)S(1)}, u32[]{:S(2)}, u32[]{:S(2)}) collective-permute-start(f32[520,128]{1,0:T(8,128)S(1)} %collective-permute-done.4.refs_1_), channel_id=1, source_target_pairs={{0,1},{2,3},{3,2},{4,5},{5,4},{7,6},{8,9},{10,11},{11,10},{12,13},... | collective-permute-start | bytes 798728 | tf_op jit(solution)/shard_map/ppermute | solution.py:508
  22.9 0.0 collective-permute-done._.refs_0_
  23.0 5.8 %shard_map.128 = (bf16[256,2048]{1,0:T(8,128)(2,1)S(1)}, bf16[256,2048]{1,0:T(8,128)(2,1)S(1)}, f32[128,2048]{1,0:T(8,128)}, f32[128,2048]{1,0:T(8,128)}, bf16[1...) custom-call(s32[1,16]{1,0:T(1,128)} %lens_hbm.3, ...), custom_call_target="tpu_custom_call" | custom-call | flops 4000000000 | bytes 12582912 | tf_op jit(solution)/shard_map/pallas_call | solution.py:487
  28.8 0.0 collective-permute-done.2.refs_2_
  28.8 0.0 collective-permute-done.3.refs_3_
  28.8 0.2 shard_map.129
  29.0 0.0 collective-permute-done.5.refs_3_
  29.0 0.9 %shard_map.130 = (f32[64,1024]{1,0:T(8,128)S(1)}, f32[64,1024]{1,0:T(8,128)S(1)}, f32[32,128]{1,0:T(8,128)}) custom-call(f32[1040,128]{1,0:T(8,128)S(1)} %collective-permute-done._.refs_0_, f32[520,128]{1,0:T(8,128)S(1)} %collective-permute-done.4.refs_1_, f32[1040,128]{1,0:T(8,128)S(1)} %collective-permute-done.2.refs_2_, ...), custom_call_target="tpu_custom_call" | custom-call | flops 100000000 | bytes 4194304 | tf_op jit(solution)/shard_map/pallas_call | solution.py:487
  30.0 6.0 %all-to-all-start = ((f32[32,1,128]{2,1,0:T(1,128)}), f32[32,1,128]{2,1,0:T(1,128)S(1)}, u32[]{:S(2)}, u32[]{:S(2)}) async-start(f32[32,1,128]{2,1,0:T(1,128)} %bitcast.7), calls=%async_computation | async-start | bytes 32768 | tf_op jit(solution)/shard_map/all_to_all | solution.py:618
  36.0 5.4 %shard_map.131 = (bf16[1,128,2048]{2,1,0:T(8,128)(2,1)}, bf16[1,64,128]{2,1,0:T(8,128)(2,1)}, bf16[1,64,128]{2,1,0:T(8,128)(2,1)}, f32[1,32,128]{2,1,0:T(8,128)}) custom-call(f32[64,1024]{1,0:T(8,128)S(1)} %get-tuple-element.52.came_one, f32[64,1024]{1,0:T(8,128)S(1)} %get-tuple-element.56.came_two, f32[64,1024]{1,0:T(8,128)S(1)} %get-tuple-element.57.pull_one, ...), custom_call_target="tpu_custom_call" | custom-call | flops 2000000000 | bytes 12582912 | tf_op jit(solution)/shard_map/pallas_call | solution.py:487
  41.4 1.8 %all-to-all-done = f32[32,1,128]{2,1,0:T(1,128)S(1)} async-done(((f32[32,1,128]{2,1,0:T(1,128)}), f32[32,1,128]{2,1,0:T(1,128)S(1)}, u32[]{:S(2)}, u32[]{:S(2)}) %all-to-all-start) | async-done | bytes 16416 | tf_op jit(solution)/shard_map/all_to_all | solution.py:618
  43.2 0.1 reduce_sum.9
  43.2 0.6 %fusion = (f32[32]{0:T(128)}, f32[32]{0:T(128)}) fusion(f32[128]{0:T(128)S(1)} %reduce_sum.9), kind=kLoop, calls=%fused_computation | loop fusion | bytes 512 | tf_op jit(solution)/shard_map/slice | solution.py:626
Async XLA Ops:
  2.9 20.0 %collective-permute-start = (f32[1040,128]{1,0:T(8,128)S(1)}, f32[1040,128]{1,0:T(8,128)S(1)}, u32[]{:S(2)}, u32[]{:S(2)}) collective-permute-start(f32[1040,128]{1,0:T(8,128)S(1)} %get-tuple-element.40), channel_id=1, source_target_pairs={{0,1},{1,0},{2,3},{3,2},{4,5},{5,4},{6,7},{7,6},{8,9},{9,8},{10,11... | collective-permute-start | bytes 1597448 | tf_op jit(solution)/shard_map/ppermute | solution.py:503
  6.0 11.2 %collective-permute-start.1 = (f32[520,128]{1,0:T(8,128)S(1)}, f32[520,128]{1,0:T(8,128)S(1)}, u32[]{:S(2)}, u32[]{:S(2)}) collective-permute-start(f32[520,128]{1,0:T(8,128)S(1)} %get-tuple-element.41), channel_id=1, source_target_pairs={{1,3},{2,0},{3,5},{4,2},{5,7},{6,4},{9,11},{10,8},{11,13},{12,10},... | collective-permute-start | bytes 798728 | tf_op jit(solution)/shard_map/ppermute | solution.py:503
  7.3 14.2 %collective-permute-start.4 = (f32[520,128]{1,0:T(8,128)S(1)}, f32[520,128]{1,0:T(8,128)S(1)}, u32[]{:S(2)}, u32[]{:S(2)}) collective-permute-start(f32[520,128]{1,0:T(8,128)S(1)} %get-tuple-element.53), channel_id=1, source_target_pairs={{1,3},{2,0},{3,5},{4,2},{5,7},{6,4},{9,11},{10,8},{11,13},{12,10},... | collective-permute-start | bytes 798728 | tf_op jit(solution)/shard_map/ppermute | solution.py:503
  8.6 20.2 %collective-permute-start.2 = (f32[1040,128]{1,0:T(8,128)S(1)}, f32[1040,128]{1,0:T(8,128)S(1)}, u32[]{:S(2)}, u32[]{:S(2)}) collective-permute-start(f32[1040,128]{1,0:T(8,128)S(1)} %get-tuple-element.40), channel_id=1, source_target_pairs={{0,2},{2,4},{3,1},{4,6},{5,3},{7,5},{8,10},{10,12},{11,9},{12,14},... | collective-permute-start | bytes 1597448 | tf_op jit(solution)/shard_map/ppermute | solution.py:503
  17.2 11.6 %collective-permute-start.3 = (f32[520,128]{1,0:T(8,128)S(1)}, f32[520,128]{1,0:T(8,128)S(1)}, u32[]{:S(2)}, u32[]{:S(2)}) collective-permute-start(f32[520,128]{1,0:T(8,128)S(1)} %collective-permute-done.1.refs_1_), channel_id=1, source_target_pairs={{0,1},{2,3},{3,2},{4,5},{5,4},{7,6},{8,9},{10,11},{11,10},{12,13},... | collective-permute-start | bytes 798728 | tf_op jit(solution)/shard_map/ppermute | solution.py:508
  21.4 7.6 %collective-permute-start.5 = (f32[520,128]{1,0:T(8,128)S(1)}, f32[520,128]{1,0:T(8,128)S(1)}, u32[]{:S(2)}, u32[]{:S(2)}) collective-permute-start(f32[520,128]{1,0:T(8,128)S(1)} %collective-permute-done.4.refs_1_), channel_id=1, source_target_pairs={{0,1},{2,3},{3,2},{4,5},{5,4},{7,6},{8,9},{10,11},{11,10},{12,13},... | collective-permute-start | bytes 798728 | tf_op jit(solution)/shard_map/ppermute | solution.py:508
  30.0 13.2 %all-to-all-start = ((f32[32,1,128]{2,1,0:T(1,128)}), f32[32,1,128]{2,1,0:T(1,128)S(1)}, u32[]{:S(2)}, u32[]{:S(2)}) async-start(f32[32,1,128]{2,1,0:T(1,128)} %bitcast.7), calls=%async_computation | async-start | bytes 32768 | tf_op jit(solution)/shard_map/all_to_all | solution.py:618

commit v13 on v12

--- a/solution.py
+++ b/solution.py
@@ -130,14 +130,12 @@
 def states_kernel(
     lens_hbm,
     alog_hbm,
-    skip_hbm,
     dt_hbm,
     x_hbm,
     b_hbm,
     dy_hbm,
     c_hbm,
     alog_ref,
-    skip_ref,
     dt_ref,
     x_ref,
     b_ref,
@@ -163,11 +161,10 @@
                 (lens_hbm, lens_ref),
                 (b_hbm.at[0], b_ref),
                 (c_hbm.at[0], c_ref),
-                (skip_hbm, skip_ref),
             )
         )
     ]
-    for copy in small[:-1]:
+    for copy in small:
         copy.start()
     large = []
     for i in range(PIECES):
@@ -178,12 +175,11 @@
             )
             copy.start()
             large.append(copy)
-    small[-1].start()
     square = (rows, rows)
     upper = jnp.where(iota(square, 0) <= iota(square, 1), 1.0, 0.0).astype(BF16)
     even = jnp.broadcast_to(lax.rem(shard(), 2), (width, LANES)) == 0
     left = iota((1, LANES), 1) < head_width
-    for copy in small[:-1]:
+    for copy in small:
         copy.wait()
     _, offset, first, last = document_places(lens_ref, rows)
     through = jnp.where(first >= offset + rows, 1.0, 0.0)
@@ -230,13 +226,12 @@
             ):
                 ref[place_in * width : (place_in + 1) * width, :] = value
                 ref[whole * width + place_in : whole * width + place_in + 1, :] = kept_row
-    small[-1].wait()
 
 
 def inside_kernel(
     lens_hbm,
+    skip_hbm,
     alog_ref,
-    skip_ref,
     dt_ref,
     x_ref,
     b_ref,
@@ -260,18 +255,23 @@
     v_stage,
     dx_stage,
     lens_ref,
+    skip_ref,
     lens_sem,
+    skip_sem,
     sems,
 ):
     rows, columns = x_ref.shape
     heads, width = dt_ref.shape[0], b_ref.shape[0]
     head_width = columns // heads
     lens_copy = pltpu.make_async_copy(lens_hbm, lens_ref, lens_sem)
+    skip_copy = pltpu.make_async_copy(skip_hbm, skip_ref, skip_sem)
     lens_copy.start()
+    skip_copy.start()
     distance = head_distance(heads, head_width)
     bt, ct = b_ref[...], c_ref[...]
     raw_scores, raw_flipped = dot(ct, bt, 0, 0), dot(bt, ct, 0, 0)
     lens_copy.wait()
+    skip_copy.wait()
     starts, offset, first, last = document_places(lens_ref, rows)
     through = jnp.where(first >= offset + rows, 1.0, 0.0)
     square = (rows, rows)
@@ -332,10 +332,14 @@
         back = dot_pairs(flipped, ys, 1, 0)
         d_scores += dot(stack(ys, 0), stack(xs, 0), 1, 1)
         dx_stage[:, at] = v_wide * back + skip_wide * dy
-        for i, (stage, target) in enumerate(((v_stage, v_wide_hbm), (dx_stage, dx_hbm))):
-            copy = pltpu.make_async_copy(stage.at[:, at], target.at[:, at], sems.at[i, block])
-            copy.start()
-            copies.append(copy)
+        if block % 2:
+            both = slice((block - 1) * WIDE, (block + 1) * WIDE)
+            for i, (stage, target) in enumerate(((v_stage, v_wide_hbm), (dx_stage, dx_hbm))):
+                copy = pltpu.make_async_copy(
+                    stage.at[:, both], target.at[:, both], sems.at[i, block]
+                )
+                copy.start()
+                copies.append(copy)
         column_part = xv * back
         product = jnp.broadcast_to(jnp.sum(x * dy, axis=0, keepdims=True), (16, WIDE))
         for part in split3(stack([yu * out - column_part, column_part, product], 0)):
@@ -426,8 +430,8 @@
     heads, width = dt_ref.shape[0], db_ref.shape[0]
     blocks = columns // WIDE
     copies = []
-    for block in range(blocks):
-        at = slice(block * WIDE, (block + 1) * WIDE)
+    for block in range(0, blocks, 2):
+        at = slice(block * WIDE, (block + 2) * WIDE)
         for i, (source, target) in enumerate(((v_wide_hbm, v_stage), (dx_hbm, dx_stage))):
             copy = pltpu.make_async_copy(
                 source.at[:, at], target.at[:, at], in_sems.at[i, block]
@@ -460,12 +464,17 @@
             sums += dot(part, ones, 1, 0)
         dc += dot(cames, ys, 1, 1)
         db += dot(pulls, xs, 1, 1)
-        copies[2 * block].wait()
-        copies[2 * block + 1].wait()
+        if block % 2 == 0:
+            copies[block].wait()
+            copies[block + 1].wait()
         stage[:, at] = (dx_stage[:, at] + v_stage[:, at] * back).astype(BF16)
-        copy = pltpu.make_async_copy(stage.at[:, at], dx_out.at[0, :, at], out_sems.at[block])
-        copy.start()
-        sent.append(copy)
+        if block % 2:
+            both = slice((block - 1) * WIDE, (block + 1) * WIDE)
+            copy = pltpu.make_async_copy(
+                stage.at[:, both], dx_out.at[0, :, both], out_sems.at[block]
+            )
+            copy.start()
+            sent.append(copy)
     dc = (dc[:width, :rows] + dc[:width, rows:]) + dc[width:, :rows]
     db = (db[:width, :rows] + db[:width, rows:]) + db[width:, :rows]
     db_out[0] = (db_ref[...] + masks_ref[0:1] * db).astype(BF16)
@@ -524,12 +533,11 @@
     def v(shape, kind=F32):
         return "v", (shape, kind)
 
-    alog, skip, dt, x, b, dy, c, *payloads = call(
+    alog, dt, x, b, dy, c, *payloads = call(
         states_kernel,
         reach,
         [
             v(alog.shape),
-            v(skip.shape),
             v((heads, rows)),
             v((rows, columns), BF16),
             v((width, rows), BF16),
@@ -537,12 +545,12 @@
             v((width, rows), BF16),
         ]
         + [v((columns // LANES * (width + 1) // part, LANES)) for part in (1, 2, 2)],
-        [in_hbm(a) for a in (doc_lengths, alog, skip, step_sizes, inputs, bt, grad_out, ct)],
+        [in_hbm(a) for a in (doc_lengths, alog, step_sizes, inputs, bt, grad_out, ct)],
         10**9,
         4 * 2**20,
         [
             pltpu.SMEM(doc_lengths.shape, jnp.int32),
-            pltpu.SemaphoreType.DMA((6,)),
+            pltpu.SemaphoreType.DMA((5,)),
             pltpu.SemaphoreType.DMA((2, PIECES)),
         ],
     )
@@ -567,8 +575,8 @@
         + [v((rows, 2 * width), BF16)] * 2
         + [v((8, rows)), transposed, transposed, v((2 * rows, heads))]
         + [state, state, v((8, columns)), v((1, LANES))],
-        [in_hbm(doc_lengths)]
-        + [("v", a) for a in (alog, skip, dt, x, b, dy, c)]
+        [in_hbm(doc_lengths), in_hbm(skip)]
+        + [("v", a) for a in (alog, dt, x, b, dy, c)]
         + [("any", messages[1, 0, 0])],
         4 * 10**9,
         12 * 2**20,
@@ -576,6 +584,8 @@
             stage,
             stage,
             pltpu.SMEM(doc_lengths.shape, jnp.int32),
+            pltpu.VMEM(skip.shape, F32),
+            pltpu.SemaphoreType.DMA,
             pltpu.SemaphoreType.DMA,
             pltpu.SemaphoreType.DMA((2, blocks)),
         ],

time: 44.2 us -> 44.3 us (level)
  no operation moved by 1% of the time
where the time goes in v13:
time: 44.3 us; the launch traced here: 43.9 us
  starting transfers between devices  19.7 us (44%)
  Pallas kernels  14.7 us (33%)
  waiting for transfers between devices  8.16 us (18%)
  between operations  0.74 us (2%)
  local copies, waits for them, and re-layouts  0.59 us (1%)
    pallas_call x5, Pallas kernels, call(): pl.pallas_call(kernel, out_shape=[pltpu.HBM(*out) if place == 'h' else ja...  14.7 us
    ppermute x4, starting transfers between devices, send(): return lax.ppermute(a, 'ctx', [(i, j) for i, j in pairs if 0 <= j < count])  10.8 us
    ppermute x4, waiting for transfers between devices, send(): return lax.ppermute(a, 'ctx', [(i, j) for i, j in pairs if 0 <= j < count])  6.12 us
    all_to_all x1, starting transfers between devices, per_device(): gathered = lax.all_to_all(partial, ('ctx', 'dp'), 0, 0, tiled=True)  5.84 us
    ppermute x2, starting transfers between devices, hand_on(): lax.ppermute(a, 'ctx', [(i, i ^ 1) for i in range(count) if i not in (1,...  3.03 us
    all_to_all x1, waiting for transfers between devices, per_device(): gathered = lax.all_to_all(partial, ('ctx', 'dp'), 0, 0, tiled=True)  2.03 us
  transfers between devices with their start and end apart: 7, of which 3 were waited for; matrix products, arithmetic and copies ran while one was open for 0% of the time, Pallas kernels for 26%

profile of v13, /device:TPU:0, one launch (start us, length us, event | category | flops | bytes accessed | tf_op | source)
XLA Modules:
  0.0 43.9 jit_solution(17635284957484712722)
XLA Ops:
  0.6 2.4 %shard_map.127 = (f32[1,32]{1,0:T(1,128)S(1)}, f32[32,128]{1,0:T(8,128)S(1)}, bf16[128,2048]{1,0:T(8,128)(2,1)S(1)}, bf16[64,128]{1,0:T(8,128)(2,1)S(1)}, bf16[1...) custom-call(s32[1,16]{1,0:T(1,128)} %lens_hbm.3, ...), custom_call_target="tpu_custom_call" | custom-call | flops 1000000000 | bytes 4194304 | tf_op jit(solution)/shard_map/pallas_call | solution.py:496
  3.0 3.0 %collective-permute-start = (f32[1040,128]{1,0:T(8,128)S(1)}, f32[1040,128]{1,0:T(8,128)S(1)}, u32[]{:S(2)}, u32[]{:S(2)}) collective-permute-start(f32[1040,128]{1,0:T(8,128)S(1)} %get-tuple-element.39), channel_id=1, source_target_pairs={{0,1},{1,0},{2,3},{3,2},{4,5},{5,4},{6,7},{7,6},{8,9},{9,8},{10,11... | collective-permute-start | bytes 1597448 | tf_op jit(solution)/shard_map/ppermute | solution.py:512
  6.1 1.3 %collective-permute-start.1 = (f32[520,128]{1,0:T(8,128)S(1)}, f32[520,128]{1,0:T(8,128)S(1)}, u32[]{:S(2)}, u32[]{:S(2)}) collective-permute-start(f32[520,128]{1,0:T(8,128)S(1)} %get-tuple-element.40), channel_id=1, source_target_pairs={{1,3},{2,0},{3,5},{4,2},{5,7},{6,4},{9,11},{10,8},{11,13},{12,10},... | collective-permute-start | bytes 798728 | tf_op jit(solution)/shard_map/ppermute | solution.py:512
  7.3 1.3 %collective-permute-start.4 = (f32[520,128]{1,0:T(8,128)S(1)}, f32[520,128]{1,0:T(8,128)S(1)}, u32[]{:S(2)}, u32[]{:S(2)}) collective-permute-start(f32[520,128]{1,0:T(8,128)S(1)} %get-tuple-element.51), channel_id=1, source_target_pairs={{1,3},{2,0},{3,5},{4,2},{5,7},{6,4},{9,11},{10,8},{11,13},{12,10},... | collective-permute-start | bytes 798728 | tf_op jit(solution)/shard_map/ppermute | solution.py:512
  8.6 5.2 %collective-permute-start.2 = (f32[1040,128]{1,0:T(8,128)S(1)}, f32[1040,128]{1,0:T(8,128)S(1)}, u32[]{:S(2)}, u32[]{:S(2)}) collective-permute-start(f32[1040,128]{1,0:T(8,128)S(1)} %get-tuple-element.39), channel_id=1, source_target_pairs={{0,2},{2,4},{3,1},{4,6},{5,3},{7,5},{8,10},{10,12},{11,9},{12,14},... | collective-permute-start | bytes 1597448 | tf_op jit(solution)/shard_map/ppermute | solution.py:512
  13.9 3.4 %collective-permute-done.1.refs_1_ = f32[520,128]{1,0:T(8,128)S(1)} collective-permute-done((f32[520,128]{1,0:T(8,128)S(1)}, f32[520,128]{1,0:T(8,128)S(1)}, u32[]{:S(2)}, u32[]{:S(2)}) %collective-permute-start.1) | collective-permute-done | bytes 266272 | tf_op jit(solution)/shard_map/ppermute | solution.py:512
  17.3 1.5 %collective-permute-start.3 = (f32[520,128]{1,0:T(8,128)S(1)}, f32[520,128]{1,0:T(8,128)S(1)}, u32[]{:S(2)}, u32[]{:S(2)}) collective-permute-start(f32[520,128]{1,0:T(8,128)S(1)} %collective-permute-done.1.refs_1_), channel_id=1, source_target_pairs={{0,1},{2,3},{3,2},{4,5},{5,4},{7,6},{8,9},{10,11},{11,10},{12,13},... | collective-permute-start | bytes 798728 | tf_op jit(solution)/shard_map/ppermute | solution.py:517
  18.8 2.7 %collective-permute-done.4.refs_1_ = f32[520,128]{1,0:T(8,128)S(1)} collective-permute-done((f32[520,128]{1,0:T(8,128)S(1)}, f32[520,128]{1,0:T(8,128)S(1)}, u32[]{:S(2)}, u32[]{:S(2)}) %collective-permute-start.4) | collective-permute-done | bytes 266272 | tf_op jit(solution)/shard_map/ppermute | solution.py:512
  21.5 1.5 %collective-permute-start.5 = (f32[520,128]{1,0:T(8,128)S(1)}, f32[520,128]{1,0:T(8,128)S(1)}, u32[]{:S(2)}, u32[]{:S(2)}) collective-permute-start(f32[520,128]{1,0:T(8,128)S(1)} %collective-permute-done.4.refs_1_), channel_id=1, source_target_pairs={{0,1},{2,3},{3,2},{4,5},{5,4},{7,6},{8,9},{10,11},{11,10},{12,13},... | collective-permute-start | bytes 798728 | tf_op jit(solution)/shard_map/ppermute | solution.py:517
  23.0 0.0 collective-permute-done._.refs_0_
  23.0 6.0 %shard_map.128 = (bf16[256,2048]{1,0:T(8,128)(2,1)S(1)}, bf16[256,2048]{1,0:T(8,128)(2,1)S(1)}, f32[128,2048]{1,0:T(8,128)}, f32[128,2048]{1,0:T(8,128)}, bf16[1...) custom-call(s32[1,16]{1,0:T(1,128)} %lens_hbm.3, ...), custom_call_target="tpu_custom_call" | custom-call | flops 4000000000 | bytes 12582912 | tf_op jit(solution)/shard_map/pallas_call | solution.py:496
  29.1 0.0 collective-permute-done.2.refs_2_
  29.1 0.0 collective-permute-done.3.refs_3_
  29.1 0.2 shard_map.129
  29.3 0.0 collective-permute-done.5.refs_3_
  29.3 0.9 %shard_map.130 = (f32[64,1024]{1,0:T(8,128)S(1)}, f32[64,1024]{1,0:T(8,128)S(1)}, f32[32,128]{1,0:T(8,128)}) custom-call(f32[1040,128]{1,0:T(8,128)S(1)} %collective-permute-done._.refs_0_, f32[520,128]{1,0:T(8,128)S(1)} %collective-permute-done.4.refs_1_, f32[1040,128]{1,0:T(8,128)S(1)} %collective-permute-done.2.refs_2_, ...), custom_call_target="tpu_custom_call" | custom-call | flops 100000000 | bytes 4194304 | tf_op jit(solution)/shard_map/pallas_call | solution.py:496
  30.2 5.8 %all-to-all-start = ((f32[32,1,128]{2,1,0:T(1,128)}), f32[32,1,128]{2,1,0:T(1,128)S(1)}, u32[]{:S(2)}, u32[]{:S(2)}) async-start(f32[32,1,128]{2,1,0:T(1,128)} %bitcast.7), calls=%async_computation | async-start | bytes 32768 | tf_op jit(solution)/shard_map/all_to_all | solution.py:628
  36.1 5.1 %shard_map.131 = (bf16[1,128,2048]{2,1,0:T(8,128)(2,1)}, bf16[1,64,128]{2,1,0:T(8,128)(2,1)}, bf16[1,64,128]{2,1,0:T(8,128)(2,1)}, f32[1,32,128]{2,1,0:T(8,128)}) custom-call(f32[64,1024]{1,0:T(8,128)S(1)} %get-tuple-element.50.came_one, f32[64,1024]{1,0:T(8,128)S(1)} %get-tuple-element.54.came_two, f32[64,1024]{1,0:T(8,128)S(1)} %get-tuple-element.55.pull_one, ...), custom_call_target="tpu_custom_call" | custom-call | flops 2000000000 | bytes 12582912 | tf_op jit(solution)/shard_map/pallas_call | solution.py:496
  41.2 2.0 %all-to-all-done = f32[32,1,128]{2,1,0:T(1,128)S(1)} async-done(((f32[32,1,128]{2,1,0:T(1,128)}), f32[32,1,128]{2,1,0:T(1,128)S(1)}, u32[]{:S(2)}, u32[]{:S(2)}) %all-to-all-start) | async-done | bytes 16416 | tf_op jit(solution)/shard_map/all_to_all | solution.py:628
  43.2 0.1 reduce_sum.9
  43.3 0.6 %fusion = (f32[32]{0:T(128)}, f32[32]{0:T(128)}) fusion(f32[128]{0:T(128)S(1)} %reduce_sum.9), kind=kLoop, calls=%fused_computation | loop fusion | bytes 512 | tf_op jit(solution)/shard_map/slice | solution.py:636
Async XLA Ops:
  3.0 20.0 %collective-permute-start = (f32[1040,128]{1,0:T(8,128)S(1)}, f32[1040,128]{1,0:T(8,128)S(1)}, u32[]{:S(2)}, u32[]{:S(2)}) collective-permute-start(f32[1040,128]{1,0:T(8,128)S(1)} %get-tuple-element.39), channel_id=1, source_target_pairs={{0,1},{1,0},{2,3},{3,2},{4,5},{5,4},{6,7},{7,6},{8,9},{9,8},{10,11... | collective-permute-start | bytes 1597448 | tf_op jit(solution)/shard_map/ppermute | solution.py:512
  6.1 11.2 %collective-permute-start.1 = (f32[520,128]{1,0:T(8,128)S(1)}, f32[520,128]{1,0:T(8,128)S(1)}, u32[]{:S(2)}, u32[]{:S(2)}) collective-permute-start(f32[520,128]{1,0:T(8,128)S(1)} %get-tuple-element.40), channel_id=1, source_target_pairs={{1,3},{2,0},{3,5},{4,2},{5,7},{6,4},{9,11},{10,8},{11,13},{12,10},... | collective-permute-start | bytes 798728 | tf_op jit(solution)/shard_map/ppermute | solution.py:512
  7.3 14.2 %collective-permute-start.4 = (f32[520,128]{1,0:T(8,128)S(1)}, f32[520,128]{1,0:T(8,128)S(1)}, u32[]{:S(2)}, u32[]{:S(2)}) collective-permute-start(f32[520,128]{1,0:T(8,128)S(1)} %get-tuple-element.51), channel_id=1, source_target_pairs={{1,3},{2,0},{3,5},{4,2},{5,7},{6,4},{9,11},{10,8},{11,13},{12,10},... | collective-permute-start | bytes 798728 | tf_op jit(solution)/shard_map/ppermute | solution.py:512
  8.6 20.4 %collective-permute-start.2 = (f32[1040,128]{1,0:T(8,128)S(1)}, f32[1040,128]{1,0:T(8,128)S(1)}, u32[]{:S(2)}, u32[]{:S(2)}) collective-permute-start(f32[1040,128]{1,0:T(8,128)S(1)} %get-tuple-element.39), channel_id=1, source_target_pairs={{0,2},{2,4},{3,1},{4,6},{5,3},{7,5},{8,10},{10,12},{11,9},{12,14},... | collective-permute-start | bytes 1597448 | tf_op jit(solution)/shard_map/ppermute | solution.py:512
  17.3 11.8 %collective-permute-start.3 = (f32[520,128]{1,0:T(8,128)S(1)}, f32[520,128]{1,0:T(8,128)S(1)}, u32[]{:S(2)}, u32[]{:S(2)}) collective-permute-start(f32[520,128]{1,0:T(8,128)S(1)} %collective-permute-done.1.refs_1_), channel_id=1, source_target_pairs={{0,1},{2,3},{3,2},{4,5},{5,4},{7,6},{8,9},{10,11},{11,10},{12,13},... | collective-permute-start | bytes 798728 | tf_op jit(solution)/shard_map/ppermute | solution.py:517
  21.5 7.8 %collective-permute-start.5 = (f32[520,128]{1,0:T(8,128)S(1)}, f32[520,128]{1,0:T(8,128)S(1)}, u32[]{:S(2)}, u32[]{:S(2)}) collective-permute-start(f32[520,128]{1,0:T(8,128)S(1)} %collective-permute-done.4.refs_1_), channel_id=1, source_target_pairs={{0,1},{2,3},{3,2},{4,5},{5,4},{7,6},{8,9},{10,11},{11,10},{12,13},... | collective-permute-start | bytes 798728 | tf_op jit(solution)/shard_map/ppermute | solution.py:517
  30.2 13.0 %all-to-all-start = ((f32[32,1,128]{2,1,0:T(1,128)}), f32[32,1,128]{2,1,0:T(1,128)S(1)}, u32[]{:S(2)}, u32[]{:S(2)}) async-start(f32[32,1,128]{2,1,0:T(1,128)} %bitcast.7), calls=%async_computation | async-start | bytes 32768 | tf_op jit(solution)/shard_map/all_to_all | solution.py:628

commit v14 on v12

--- a/solution.py
+++ b/solution.py
@@ -503,9 +503,10 @@
     return lax.ppermute(a, "ctx", [(i, j) for i, j in pairs if 0 <= j < count])
 
 
-def hand_on(a):
+def hand_on(a, half):
     count = lax.axis_size("ctx")
-    return lax.ppermute(a, "ctx", [(i, i ^ 1) for i in range(count) if i not in (1, count - 2)])
+    spared = (1, count - 2) if half else ()
+    return lax.ppermute(a, "ctx", [(i, i ^ 1) for i in range(count) if i not in spared])
 
 
 def in_hbm(a):
@@ -554,7 +555,7 @@
         messages[j, second, half] = send(payload, j, second)
     if reach > 1:
         for half in (0, 1):
-            messages[1, 1, half] = hand_on(messages[2, 1, half])
+            messages[1, 1, half] = hand_on(messages[2, 1, half], half)
     whole = "h", ((rows, columns), F32)
     state = v((width, columns))
     stage = pltpu.VMEM((rows, columns), F32)

time: 44.2 us -> 43.8 us (level)
  starting transfers between devices: 19.9 us -> 18.1 us
  waiting for transfers between devices: 7.88 us -> 9.4 us
    ppermute x4, waiting for transfers between devices: 6.12 us -> 7.64 us  [send(): return lax.ppermute(a, 'ctx', [(i, j) for i, j in pairs if 0 <= j < count])]
    ppermute x2, starting transfers between devices: 3.03 us -> 1.51 us  [hand_on(): lax.ppermute(a, 'ctx', [(i, i ^ 1) for i in range(count) if i not in spar...]
where the time goes in v14:
time: 43.8 us; the launch traced here: 43.5 us
  starting transfers between devices  18.1 us (41%)
  Pallas kernels  14.7 us (34%)
  waiting for transfers between devices  9.4 us (21%)
  between operations  0.73 us (2%)
  local copies, waits for them, and re-layouts  0.59 us (1%)
    pallas_call x5, Pallas kernels, call(): pl.pallas_call(kernel, out_shape=[pltpu.HBM(*out) if place == 'h' else ja...  14.7 us
    ppermute x4, starting transfers between devices, send(): return lax.ppermute(a, 'ctx', [(i, j) for i, j in pairs if 0 <= j < count])  10.8 us
    ppermute x4, waiting for transfers between devices, send(): return lax.ppermute(a, 'ctx', [(i, j) for i, j in pairs if 0 <= j < count])  7.64 us
    all_to_all x1, starting transfers between devices, per_device(): gathered = lax.all_to_all(partial, ('ctx', 'dp'), 0, 0, tiled=True)  5.73 us
    all_to_all x1, waiting for transfers between devices, per_device(): gathered = lax.all_to_all(partial, ('ctx', 'dp'), 0, 0, tiled=True)  1.76 us
    ppermute x2, starting transfers between devices, hand_on(): lax.ppermute(a, 'ctx', [(i, i ^ 1) for i in range(count) if i not in spar...  1.51 us
  transfers between devices with their start and end apart: 7, of which 3 were waited for; matrix products, arithmetic and copies ran while one was open for 0% of the time, Pallas kernels for 26%

profile of v14, /device:TPU:0, one launch (start us, length us, event | category | flops | bytes accessed | tf_op | source)
XLA Modules:
  0.0 43.5 jit_solution(15682477601558144771)
XLA Ops:
  0.6 2.3 %shard_map.127 = (f32[1,32]{1,0:T(1,128)S(1)}, f32[1,32]{1,0:T(1,128)S(1)}, f32[32,128]{1,0:T(8,128)S(1)}, bf16[128,2048]{1,0:T(8,128)(2,1)S(1)}, bf16[64,128]{1...) custom-call(s32[1,16]{1,0:T(1,128)} %lens_hbm.3, ...), custom_call_target="tpu_custom_call" | custom-call | flops 1000000000 | bytes 4194304 | tf_op jit(solution)/shard_map/pallas_call | solution.py:487
  2.9 3.0 %collective-permute-start = (f32[1040,128]{1,0:T(8,128)S(1)}, f32[1040,128]{1,0:T(8,128)S(1)}, u32[]{:S(2)}, u32[]{:S(2)}) collective-permute-start(f32[1040,128]{1,0:T(8,128)S(1)} %get-tuple-element.40), channel_id=1, source_target_pairs={{0,1},{1,0},{2,3},{3,2},{4,5},{5,4},{6,7},{7,6},{8,9},{9,8},{10,11... | collective-permute-start | bytes 1597448 | tf_op jit(solution)/shard_map/ppermute | solution.py:503
  6.0 1.3 %collective-permute-start.1 = (f32[520,128]{1,0:T(8,128)S(1)}, f32[520,128]{1,0:T(8,128)S(1)}, u32[]{:S(2)}, u32[]{:S(2)}) collective-permute-start(f32[520,128]{1,0:T(8,128)S(1)} %get-tuple-element.41), channel_id=1, source_target_pairs={{1,3},{2,0},{3,5},{4,2},{5,7},{6,4},{9,11},{10,8},{11,13},{12,10},... | collective-permute-start | bytes 798728 | tf_op jit(solution)/shard_map/ppermute | solution.py:503
  7.3 1.3 %collective-permute-start.4 = (f32[520,128]{1,0:T(8,128)S(1)}, f32[520,128]{1,0:T(8,128)S(1)}, u32[]{:S(2)}, u32[]{:S(2)}) collective-permute-start(f32[520,128]{1,0:T(8,128)S(1)} %get-tuple-element.53), channel_id=1, source_target_pairs={{1,3},{2,0},{3,5},{4,2},{5,7},{6,4},{9,11},{10,8},{11,13},{12,10},... | collective-permute-start | bytes 798728 | tf_op jit(solution)/shard_map/ppermute | solution.py:503
  8.6 5.2 %collective-permute-start.2 = (f32[1040,128]{1,0:T(8,128)S(1)}, f32[1040,128]{1,0:T(8,128)S(1)}, u32[]{:S(2)}, u32[]{:S(2)}) collective-permute-start(f32[1040,128]{1,0:T(8,128)S(1)} %get-tuple-element.40), channel_id=1, source_target_pairs={{0,2},{2,4},{3,1},{4,6},{5,3},{7,5},{8,10},{10,12},{11,9},{12,14},... | collective-permute-start | bytes 1597448 | tf_op jit(solution)/shard_map/ppermute | solution.py:503
  13.8 3.4 %collective-permute-done.1.refs_1_ = f32[520,128]{1,0:T(8,128)S(1)} collective-permute-done((f32[520,128]{1,0:T(8,128)S(1)}, f32[520,128]{1,0:T(8,128)S(1)}, u32[]{:S(2)}, u32[]{:S(2)}) %collective-permute-start.1) | collective-permute-done | bytes 266272 | tf_op jit(solution)/shard_map/ppermute | solution.py:503
  17.2 0.0 collective-permute-start.3
  17.2 4.2 %collective-permute-done.4.refs_1_ = f32[520,128]{1,0:T(8,128)S(1)} collective-permute-done((f32[520,128]{1,0:T(8,128)S(1)}, f32[520,128]{1,0:T(8,128)S(1)}, u32[]{:S(2)}, u32[]{:S(2)}) %collective-permute-start.4) | collective-permute-done | bytes 266272 | tf_op jit(solution)/shard_map/ppermute | solution.py:503
  21.4 1.5 %collective-permute-start.5 = (f32[520,128]{1,0:T(8,128)S(1)}, f32[520,128]{1,0:T(8,128)S(1)}, u32[]{:S(2)}, u32[]{:S(2)}) collective-permute-start(f32[520,128]{1,0:T(8,128)S(1)} %collective-permute-done.4.refs_1_), channel_id=1, source_target_pairs={{0,1},{2,3},{3,2},{4,5},{5,4},{7,6},{8,9},{10,11},{11,10},{12,13},... | collective-permute-start | bytes 798728 | tf_op jit(solution)/shard_map/ppermute | solution.py:509
  22.9 0.0 collective-permute-done._.refs_0_
  23.0 5.8 %shard_map.128 = (bf16[256,2048]{1,0:T(8,128)(2,1)S(1)}, bf16[256,2048]{1,0:T(8,128)(2,1)S(1)}, f32[128,2048]{1,0:T(8,128)}, f32[128,2048]{1,0:T(8,128)}, bf16[1...) custom-call(s32[1,16]{1,0:T(1,128)} %lens_hbm.3, ...), custom_call_target="tpu_custom_call" | custom-call | flops 4000000000 | bytes 12582912 | tf_op jit(solution)/shard_map/pallas_call | solution.py:487
  28.8 0.0 collective-permute-done.2.refs_2_
  28.8 0.0 collective-permute-done.3.refs_3_
  28.8 0.2 shard_map.129
  29.0 0.0 collective-permute-done.5.refs_3_
  29.0 0.9 %shard_map.130 = (f32[64,1024]{1,0:T(8,128)S(1)}, f32[64,1024]{1,0:T(8,128)S(1)}, f32[32,128]{1,0:T(8,128)}) custom-call(f32[1040,128]{1,0:T(8,128)S(1)} %collective-permute-done._.refs_0_, f32[520,128]{1,0:T(8,128)S(1)} %collective-permute-done.4.refs_1_, f32[1040,128]{1,0:T(8,128)S(1)} %collective-permute-done.2.refs_2_, ...), custom_call_target="tpu_custom_call" | custom-call | flops 100000000 | bytes 4194304 | tf_op jit(solution)/shard_map/pallas_call | solution.py:487
  30.0 5.7 %all-to-all-start = ((f32[32,1,128]{2,1,0:T(1,128)}), f32[32,1,128]{2,1,0:T(1,128)S(1)}, u32[]{:S(2)}, u32[]{:S(2)}) async-start(f32[32,1,128]{2,1,0:T(1,128)} %bitcast.7), calls=%async_computation | async-start | bytes 32768 | tf_op jit(solution)/shard_map/all_to_all | solution.py:619
  35.7 5.4 %shard_map.131 = (bf16[1,128,2048]{2,1,0:T(8,128)(2,1)}, bf16[1,64,128]{2,1,0:T(8,128)(2,1)}, bf16[1,64,128]{2,1,0:T(8,128)(2,1)}, f32[1,32,128]{2,1,0:T(8,128)}) custom-call(f32[64,1024]{1,0:T(8,128)S(1)} %get-tuple-element.52.came_one, f32[64,1024]{1,0:T(8,128)S(1)} %get-tuple-element.56.came_two, f32[64,1024]{1,0:T(8,128)S(1)} %get-tuple-element.57.pull_one, ...), custom_call_target="tpu_custom_call" | custom-call | flops 2000000000 | bytes 12582912 | tf_op jit(solution)/shard_map/pallas_call | solution.py:487
  41.1 1.8 %all-to-all-done = f32[32,1,128]{2,1,0:T(1,128)S(1)} async-done(((f32[32,1,128]{2,1,0:T(1,128)}), f32[32,1,128]{2,1,0:T(1,128)S(1)}, u32[]{:S(2)}, u32[]{:S(2)}) %all-to-all-start) | async-done | bytes 16416 | tf_op jit(solution)/shard_map/all_to_all | solution.py:619
  42.9 0.1 reduce_sum.9
  42.9 0.6 %fusion = (f32[32]{0:T(128)}, f32[32]{0:T(128)}) fusion(f32[128]{0:T(128)S(1)} %reduce_sum.9), kind=kLoop, calls=%fused_computation | loop fusion | bytes 512 | tf_op jit(solution)/shard_map/slice | solution.py:627
Async XLA Ops:
  2.9 20.0 %collective-permute-start = (f32[1040,128]{1,0:T(8,128)S(1)}, f32[1040,128]{1,0:T(8,128)S(1)}, u32[]{:S(2)}, u32[]{:S(2)}) collective-permute-start(f32[1040,128]{1,0:T(8,128)S(1)} %get-tuple-element.40), channel_id=1, source_target_pairs={{0,1},{1,0},{2,3},{3,2},{4,5},{5,4},{6,7},{7,6},{8,9},{9,8},{10,11... | collective-permute-start | bytes 1597448 | tf_op jit(solution)/shard_map/ppermute | solution.py:503
  6.0 11.2 %collective-permute-start.1 = (f32[520,128]{1,0:T(8,128)S(1)}, f32[520,128]{1,0:T(8,128)S(1)}, u32[]{:S(2)}, u32[]{:S(2)}) collective-permute-start(f32[520,128]{1,0:T(8,128)S(1)} %get-tuple-element.41), channel_id=1, source_target_pairs={{1,3},{2,0},{3,5},{4,2},{5,7},{6,4},{9,11},{10,8},{11,13},{12,10},... | collective-permute-start | bytes 798728 | tf_op jit(solution)/shard_map/ppermute | solution.py:503
  7.3 14.2 %collective-permute-start.4 = (f32[520,128]{1,0:T(8,128)S(1)}, f32[520,128]{1,0:T(8,128)S(1)}, u32[]{:S(2)}, u32[]{:S(2)}) collective-permute-start(f32[520,128]{1,0:T(8,128)S(1)} %get-tuple-element.53), channel_id=1, source_target_pairs={{1,3},{2,0},{3,5},{4,2},{5,7},{6,4},{9,11},{10,8},{11,13},{12,10},... | collective-permute-start | bytes 798728 | tf_op jit(solution)/shard_map/ppermute | solution.py:503
  8.6 20.2 %collective-permute-start.2 = (f32[1040,128]{1,0:T(8,128)S(1)}, f32[1040,128]{1,0:T(8,128)S(1)}, u32[]{:S(2)}, u32[]{:S(2)}) collective-permute-start(f32[1040,128]{1,0:T(8,128)S(1)} %get-tuple-element.40), channel_id=1, source_target_pairs={{0,2},{2,4},{3,1},{4,6},{5,3},{7,5},{8,10},{10,12},{11,9},{12,14},... | collective-permute-start | bytes 1597448 | tf_op jit(solution)/shard_map/ppermute | solution.py:503
  17.2 11.6 %collective-permute-start.3 = (f32[520,128]{1,0:T(8,128)S(1)}, f32[520,128]{1,0:T(8,128)S(1)}, u32[]{:S(2)}, u32[]{:S(2)}) collective-permute-start(f32[520,128]{1,0:T(8,128)S(1)} %collective-permute-done.1.refs_1_), channel_id=1, source_target_pairs={{0,1},{1,0},{2,3},{3,2},{4,5},{5,4},{6,7},{7,6},{8,9},{9,8},{10,11... | collective-permute-start | bytes 798728 | tf_op jit(solution)/shard_map/ppermute | solution.py:509
  21.4 7.6 %collective-permute-start.5 = (f32[520,128]{1,0:T(8,128)S(1)}, f32[520,128]{1,0:T(8,128)S(1)}, u32[]{:S(2)}, u32[]{:S(2)}) collective-permute-start(f32[520,128]{1,0:T(8,128)S(1)} %collective-permute-done.4.refs_1_), channel_id=1, source_target_pairs={{0,1},{2,3},{3,2},{4,5},{5,4},{7,6},{8,9},{10,11},{11,10},{12,13},... | collective-permute-start | bytes 798728 | tf_op jit(solution)/shard_map/ppermute | solution.py:509
  30.0 12.9 %all-to-all-start = ((f32[32,1,128]{2,1,0:T(1,128)}), f32[32,1,128]{2,1,0:T(1,128)S(1)}, u32[]{:S(2)}, u32[]{:S(2)}) async-start(f32[32,1,128]{2,1,0:T(1,128)} %bitcast.7), calls=%async_computation | async-start | bytes 32768 | tf_op jit(solution)/shard_map/all_to_all | solution.py:619

commit v15 on v14

--- a/solution.py
+++ b/solution.py
@@ -167,8 +167,6 @@
             )
         )
     ]
-    for copy in small[:-1]:
-        copy.start()
     large = []
     for i in range(PIECES):
         at = slice(i * piece, (i + 1) * piece)
@@ -176,14 +174,14 @@
             copy = pltpu.make_async_copy(
                 source.at[0, :, at], target.at[:, at], sems.at[side, i]
             )
-            copy.start()
             large.append(copy)
-    small[-1].start()
+    for copy in (*small[:3], *large[:2], *small[3:5], *large[2:], *small[5:]):
+        copy.start()
     square = (rows, rows)
     upper = jnp.where(iota(square, 0) <= iota(square, 1), 1.0, 0.0).astype(BF16)
     even = jnp.broadcast_to(lax.rem(shard(), 2), (width, LANES)) == 0
     left = iota((1, LANES), 1) < head_width
-    for copy in small[:-1]:
+    for copy in small[:3]:
         copy.wait()
     _, offset, first, last = document_places(lens_ref, rows)
     through = jnp.where(first >= offset + rows, 1.0, 0.0)
@@ -194,6 +192,8 @@
     keeping = jnp.where(place >= last, jnp.exp(end_log - logs) * dt, 0.0)
     carried = jnp.where(place < first, jnp.exp(logs), 0.0)
     kept = jnp.broadcast_to(jnp.exp(end_log) * through, (heads, LANES))
+    for copy in small[3:5]:
+        copy.wait()
     b, c = b_ref[...].astype(F32), c_ref[...].astype(F32)
     own = LANES // head_width
 

time: 43.8 us -> 43.7 us (level)
  no operation moved by 1% of the time
where the time goes in v15:
time: 43.7 us; the launch traced here: 43.4 us
  starting transfers between devices  18.1 us (41%)
  Pallas kernels  14.5 us (33%)
  waiting for transfers between devices  9.4 us (22%)
  between operations  0.73 us (2%)
  local copies, waits for them, and re-layouts  0.59 us (1%)
    pallas_call x5, Pallas kernels, call(): pl.pallas_call(kernel, out_shape=[pltpu.HBM(*out) if place == 'h' else ja...  14.5 us
    ppermute x4, starting transfers between devices, send(): return lax.ppermute(a, 'ctx', [(i, j) for i, j in pairs if 0 <= j < count])  10.8 us
    ppermute x4, waiting for transfers between devices, send(): return lax.ppermute(a, 'ctx', [(i, j) for i, j in pairs if 0 <= j < count])  7.64 us
    all_to_all x1, starting transfers between devices, per_device(): gathered = lax.all_to_all(partial, ('ctx', 'dp'), 0, 0, tiled=True)  5.73 us
    all_to_all x1, waiting for transfers between devices, per_device(): gathered = lax.all_to_all(partial, ('ctx', 'dp'), 0, 0, tiled=True)  1.76 us
    ppermute x2, starting transfers between devices, hand_on(): lax.ppermute(a, 'ctx', [(i, i ^ 1) for i in range(count) if i not in spar...  1.51 us
  transfers between devices with their start and end apart: 7, of which 3 were waited for; matrix products, arithmetic and copies ran while one was open for 0% of the time, Pallas kernels for 26%

profile of v15, /device:TPU:0, one launch (start us, length us, event | category | flops | bytes accessed | tf_op | source)
XLA Modules:
  0.0 43.4 jit_solution(9490544521819194010)
XLA Ops:
  0.6 2.2 %shard_map.127 = (f32[1,32]{1,0:T(1,128)S(1)}, f32[1,32]{1,0:T(1,128)S(1)}, f32[32,128]{1,0:T(8,128)S(1)}, bf16[128,2048]{1,0:T(8,128)(2,1)S(1)}, bf16[64,128]{1...) custom-call(s32[1,16]{1,0:T(1,128)} %lens_hbm.3, ...), custom_call_target="tpu_custom_call" | custom-call | flops 1000000000 | bytes 4194304 | tf_op jit(solution)/shard_map/pallas_call | solution.py:487
  2.8 3.0 %collective-permute-start = (f32[1040,128]{1,0:T(8,128)S(1)}, f32[1040,128]{1,0:T(8,128)S(1)}, u32[]{:S(2)}, u32[]{:S(2)}) collective-permute-start(f32[1040,128]{1,0:T(8,128)S(1)} %get-tuple-element.40), channel_id=1, source_target_pairs={{0,1},{1,0},{2,3},{3,2},{4,5},{5,4},{6,7},{7,6},{8,9},{9,8},{10,11... | collective-permute-start | bytes 1597448 | tf_op jit(solution)/shard_map/ppermute | solution.py:503
  5.8 1.3 %collective-permute-start.1 = (f32[520,128]{1,0:T(8,128)S(1)}, f32[520,128]{1,0:T(8,128)S(1)}, u32[]{:S(2)}, u32[]{:S(2)}) collective-permute-start(f32[520,128]{1,0:T(8,128)S(1)} %get-tuple-element.41), channel_id=1, source_target_pairs={{1,3},{2,0},{3,5},{4,2},{5,7},{6,4},{9,11},{10,8},{11,13},{12,10},... | collective-permute-start | bytes 798728 | tf_op jit(solution)/shard_map/ppermute | solution.py:503
  7.1 1.3 %collective-permute-start.4 = (f32[520,128]{1,0:T(8,128)S(1)}, f32[520,128]{1,0:T(8,128)S(1)}, u32[]{:S(2)}, u32[]{:S(2)}) collective-permute-start(f32[520,128]{1,0:T(8,128)S(1)} %get-tuple-element.53), channel_id=1, source_target_pairs={{1,3},{2,0},{3,5},{4,2},{5,7},{6,4},{9,11},{10,8},{11,13},{12,10},... | collective-permute-start | bytes 798728 | tf_op jit(solution)/shard_map/ppermute | solution.py:503
  8.4 5.2 %collective-permute-start.2 = (f32[1040,128]{1,0:T(8,128)S(1)}, f32[1040,128]{1,0:T(8,128)S(1)}, u32[]{:S(2)}, u32[]{:S(2)}) collective-permute-start(f32[1040,128]{1,0:T(8,128)S(1)} %get-tuple-element.40), channel_id=1, source_target_pairs={{0,2},{2,4},{3,1},{4,6},{5,3},{7,5},{8,10},{10,12},{11,9},{12,14},... | collective-permute-start | bytes 1597448 | tf_op jit(solution)/shard_map/ppermute | solution.py:503
  13.7 3.4 %collective-permute-done.1.refs_1_ = f32[520,128]{1,0:T(8,128)S(1)} collective-permute-done((f32[520,128]{1,0:T(8,128)S(1)}, f32[520,128]{1,0:T(8,128)S(1)}, u32[]{:S(2)}, u32[]{:S(2)}) %collective-permute-start.1) | collective-permute-done | bytes 266272 | tf_op jit(solution)/shard_map/ppermute | solution.py:503
  17.0 0.0 collective-permute-start.3
  17.1 4.2 %collective-permute-done.4.refs_1_ = f32[520,128]{1,0:T(8,128)S(1)} collective-permute-done((f32[520,128]{1,0:T(8,128)S(1)}, f32[520,128]{1,0:T(8,128)S(1)}, u32[]{:S(2)}, u32[]{:S(2)}) %collective-permute-start.4) | collective-permute-done | bytes 266272 | tf_op jit(solution)/shard_map/ppermute | solution.py:503
  21.3 1.5 %collective-permute-start.5 = (f32[520,128]{1,0:T(8,128)S(1)}, f32[520,128]{1,0:T(8,128)S(1)}, u32[]{:S(2)}, u32[]{:S(2)}) collective-permute-start(f32[520,128]{1,0:T(8,128)S(1)} %collective-permute-done.4.refs_1_), channel_id=1, source_target_pairs={{0,1},{2,3},{3,2},{4,5},{5,4},{7,6},{8,9},{10,11},{11,10},{12,13},... | collective-permute-start | bytes 798728 | tf_op jit(solution)/shard_map/ppermute | solution.py:509
  22.8 0.0 collective-permute-done._.refs_0_
  22.8 5.8 %shard_map.128 = (bf16[256,2048]{1,0:T(8,128)(2,1)S(1)}, bf16[256,2048]{1,0:T(8,128)(2,1)S(1)}, f32[128,2048]{1,0:T(8,128)}, f32[128,2048]{1,0:T(8,128)}, bf16[1...) custom-call(s32[1,16]{1,0:T(1,128)} %lens_hbm.3, ...), custom_call_target="tpu_custom_call" | custom-call | flops 4000000000 | bytes 12582912 | tf_op jit(solution)/shard_map/pallas_call | solution.py:487
  28.7 0.0 collective-permute-done.2.refs_2_
  28.7 0.0 collective-permute-done.3.refs_3_
  28.7 0.2 shard_map.129
  28.9 0.0 collective-permute-done.5.refs_3_
  28.9 0.9 %shard_map.130 = (f32[64,1024]{1,0:T(8,128)S(1)}, f32[64,1024]{1,0:T(8,128)S(1)}, f32[32,128]{1,0:T(8,128)}) custom-call(f32[1040,128]{1,0:T(8,128)S(1)} %collective-permute-done._.refs_0_, f32[520,128]{1,0:T(8,128)S(1)} %collective-permute-done.4.refs_1_, f32[1040,128]{1,0:T(8,128)S(1)} %collective-permute-done.2.refs_2_, ...), custom_call_target="tpu_custom_call" | custom-call | flops 100000000 | bytes 4194304 | tf_op jit(solution)/shard_map/pallas_call | solution.py:487
  29.8 5.7 %all-to-all-start = ((f32[32,1,128]{2,1,0:T(1,128)}), f32[32,1,128]{2,1,0:T(1,128)S(1)}, u32[]{:S(2)}, u32[]{:S(2)}) async-start(f32[32,1,128]{2,1,0:T(1,128)} %bitcast.7), calls=%async_computation | async-start | bytes 32768 | tf_op jit(solution)/shard_map/all_to_all | solution.py:619
  35.6 5.4 %shard_map.131 = (bf16[1,128,2048]{2,1,0:T(8,128)(2,1)}, bf16[1,64,128]{2,1,0:T(8,128)(2,1)}, bf16[1,64,128]{2,1,0:T(8,128)(2,1)}, f32[1,32,128]{2,1,0:T(8,128)}) custom-call(f32[64,1024]{1,0:T(8,128)S(1)} %get-tuple-element.52.came_one, f32[64,1024]{1,0:T(8,128)S(1)} %get-tuple-element.56.came_two, f32[64,1024]{1,0:T(8,128)S(1)} %get-tuple-element.57.pull_one, ...), custom_call_target="tpu_custom_call" | custom-call | flops 2000000000 | bytes 12582912 | tf_op jit(solution)/shard_map/pallas_call | solution.py:487
  41.0 1.8 %all-to-all-done = f32[32,1,128]{2,1,0:T(1,128)S(1)} async-done(((f32[32,1,128]{2,1,0:T(1,128)}), f32[32,1,128]{2,1,0:T(1,128)S(1)}, u32[]{:S(2)}, u32[]{:S(2)}) %all-to-all-start) | async-done | bytes 16416 | tf_op jit(solution)/shard_map/all_to_all | solution.py:619
  42.7 0.1 reduce_sum.9
  42.8 0.6 %fusion = (f32[32]{0:T(128)}, f32[32]{0:T(128)}) fusion(f32[128]{0:T(128)S(1)} %reduce_sum.9), kind=kLoop, calls=%fused_computation | loop fusion | bytes 512 | tf_op jit(solution)/shard_map/slice | solution.py:627
Async XLA Ops:
  2.8 20.0 %collective-permute-start = (f32[1040,128]{1,0:T(8,128)S(1)}, f32[1040,128]{1,0:T(8,128)S(1)}, u32[]{:S(2)}, u32[]{:S(2)}) collective-permute-start(f32[1040,128]{1,0:T(8,128)S(1)} %get-tuple-element.40), channel_id=1, source_target_pairs={{0,1},{1,0},{2,3},{3,2},{4,5},{5,4},{6,7},{7,6},{8,9},{9,8},{10,11... | collective-permute-start | bytes 1597448 | tf_op jit(solution)/shard_map/ppermute | solution.py:503
  5.8 11.2 %collective-permute-start.1 = (f32[520,128]{1,0:T(8,128)S(1)}, f32[520,128]{1,0:T(8,128)S(1)}, u32[]{:S(2)}, u32[]{:S(2)}) collective-permute-start(f32[520,128]{1,0:T(8,128)S(1)} %get-tuple-element.41), channel_id=1, source_target_pairs={{1,3},{2,0},{3,5},{4,2},{5,7},{6,4},{9,11},{10,8},{11,13},{12,10},... | collective-permute-start | bytes 798728 | tf_op jit(solution)/shard_map/ppermute | solution.py:503
  7.1 14.2 %collective-permute-start.4 = (f32[520,128]{1,0:T(8,128)S(1)}, f32[520,128]{1,0:T(8,128)S(1)}, u32[]{:S(2)}, u32[]{:S(2)}) collective-permute-start(f32[520,128]{1,0:T(8,128)S(1)} %get-tuple-element.53), channel_id=1, source_target_pairs={{1,3},{2,0},{3,5},{4,2},{5,7},{6,4},{9,11},{10,8},{11,13},{12,10},... | collective-permute-start | bytes 798728 | tf_op jit(solution)/shard_map/ppermute | solution.py:503
  8.4 20.2 %collective-permute-start.2 = (f32[1040,128]{1,0:T(8,128)S(1)}, f32[1040,128]{1,0:T(8,128)S(1)}, u32[]{:S(2)}, u32[]{:S(2)}) collective-permute-start(f32[1040,128]{1,0:T(8,128)S(1)} %get-tuple-element.40), channel_id=1, source_target_pairs={{0,2},{2,4},{3,1},{4,6},{5,3},{7,5},{8,10},{10,12},{11,9},{12,14},... | collective-permute-start | bytes 1597448 | tf_op jit(solution)/shard_map/ppermute | solution.py:503
  17.0 11.6 %collective-permute-start.3 = (f32[520,128]{1,0:T(8,128)S(1)}, f32[520,128]{1,0:T(8,128)S(1)}, u32[]{:S(2)}, u32[]{:S(2)}) collective-permute-start(f32[520,128]{1,0:T(8,128)S(1)} %collective-permute-done.1.refs_1_), channel_id=1, source_target_pairs={{0,1},{1,0},{2,3},{3,2},{4,5},{5,4},{6,7},{7,6},{8,9},{9,8},{10,11... | collective-permute-start | bytes 798728 | tf_op jit(solution)/shard_map/ppermute | solution.py:509
  21.3 7.6 %collective-permute-start.5 = (f32[520,128]{1,0:T(8,128)S(1)}, f32[520,128]{1,0:T(8,128)S(1)}, u32[]{:S(2)}, u32[]{:S(2)}) collective-permute-start(f32[520,128]{1,0:T(8,128)S(1)} %collective-permute-done.4.refs_1_), channel_id=1, source_target_pairs={{0,1},{2,3},{3,2},{4,5},{5,4},{7,6},{8,9},{10,11},{11,10},{12,13},... | collective-permute-start | bytes 798728 | tf_op jit(solution)/shard_map/ppermute | solution.py:509
  29.8 12.9 %all-to-all-start = ((f32[32,1,128]{2,1,0:T(1,128)}), f32[32,1,128]{2,1,0:T(1,128)S(1)}, u32[]{:S(2)}, u32[]{:S(2)}) async-start(f32[32,1,128]{2,1,0:T(1,128)} %bitcast.7), calls=%async_computation | async-start | bytes 32768 | tf_op jit(solution)/shard_map/all_to_all | solution.py:619

commit v16 on v15

--- a/solution.py
+++ b/solution.py
@@ -13,7 +13,7 @@
 WIDE = 256
 PARTS = WIDE // LANES
 FAR = 2**30
-PIECES = 2
+PIECES = 1
 
 
 def dot(a, b, ca, cb):

time: 43.7 us -> 43.6 us (level)
  no operation moved by 1% of the time
where the time goes in v16:
time: 43.6 us; the launch traced here: 43.3 us
  starting transfers between devices  18.1 us (42%)
  Pallas kernels  14.5 us (33%)
  waiting for transfers between devices  9.4 us (22%)
  between operations  0.73 us (2%)
  local copies, waits for them, and re-layouts  0.59 us (1%)
    pallas_call x5, Pallas kernels, call(): pl.pallas_call(kernel, out_shape=[pltpu.HBM(*out) if place == 'h' else ja...  14.5 us
    ppermute x4, starting transfers between devices, send(): return lax.ppermute(a, 'ctx', [(i, j) for i, j in pairs if 0 <= j < count])  10.8 us
    ppermute x4, waiting for transfers between devices, send(): return lax.ppermute(a, 'ctx', [(i, j) for i, j in pairs if 0 <= j < count])  7.64 us
    all_to_all x1, starting transfers between devices, per_device(): gathered = lax.all_to_all(partial, ('ctx', 'dp'), 0, 0, tiled=True)  5.72 us
    all_to_all x1, waiting for transfers between devices, per_device(): gathered = lax.all_to_all(partial, ('ctx', 'dp'), 0, 0, tiled=True)  1.76 us
    ppermute x2, starting transfers between devices, hand_on(): lax.ppermute(a, 'ctx', [(i, i ^ 1) for i in range(count) if i not in spar...  1.52 us
  transfers between devices with their start and end apart: 7, of which 3 were waited for; matrix products, arithmetic and copies ran while one was open for 0% of the time, Pallas kernels for 26%

profile of v16, /device:TPU:0, one launch (start us, length us, event | category | flops | bytes accessed | tf_op | source)
XLA Modules:
  0.0 43.3 jit_solution(16467550265597534318)
XLA Ops:
  0.6 2.1 %shard_map.127 = (f32[1,32]{1,0:T(1,128)S(1)}, f32[1,32]{1,0:T(1,128)S(1)}, f32[32,128]{1,0:T(8,128)S(1)}, bf16[128,2048]{1,0:T(8,128)(2,1)S(1)}, bf16[64,128]{1...) custom-call(s32[1,16]{1,0:T(1,128)} %lens_hbm.3, ...), custom_call_target="tpu_custom_call" | custom-call | flops 1000000000 | bytes 4194304 | tf_op jit(solution)/shard_map/pallas_call | solution.py:487
  2.7 3.0 %collective-permute-start = (f32[1040,128]{1,0:T(8,128)S(1)}, f32[1040,128]{1,0:T(8,128)S(1)}, u32[]{:S(2)}, u32[]{:S(2)}) collective-permute-start(f32[1040,128]{1,0:T(8,128)S(1)} %get-tuple-element.40), channel_id=1, source_target_pairs={{0,1},{1,0},{2,3},{3,2},{4,5},{5,4},{6,7},{7,6},{8,9},{9,8},{10,11... | collective-permute-start | bytes 1597448 | tf_op jit(solution)/shard_map/ppermute | solution.py:503
  5.8 1.3 %collective-permute-start.1 = (f32[520,128]{1,0:T(8,128)S(1)}, f32[520,128]{1,0:T(8,128)S(1)}, u32[]{:S(2)}, u32[]{:S(2)}) collective-permute-start(f32[520,128]{1,0:T(8,128)S(1)} %get-tuple-element.41), channel_id=1, source_target_pairs={{1,3},{2,0},{3,5},{4,2},{5,7},{6,4},{9,11},{10,8},{11,13},{12,10},... | collective-permute-start | bytes 798728 | tf_op jit(solution)/shard_map/ppermute | solution.py:503
  7.1 1.3 %collective-permute-start.4 = (f32[520,128]{1,0:T(8,128)S(1)}, f32[520,128]{1,0:T(8,128)S(1)}, u32[]{:S(2)}, u32[]{:S(2)}) collective-permute-start(f32[520,128]{1,0:T(8,128)S(1)} %get-tuple-element.53), channel_id=1, source_target_pairs={{1,3},{2,0},{3,5},{4,2},{5,7},{6,4},{9,11},{10,8},{11,13},{12,10},... | collective-permute-start | bytes 798728 | tf_op jit(solution)/shard_map/ppermute | solution.py:503
  8.4 5.2 %collective-permute-start.2 = (f32[1040,128]{1,0:T(8,128)S(1)}, f32[1040,128]{1,0:T(8,128)S(1)}, u32[]{:S(2)}, u32[]{:S(2)}) collective-permute-start(f32[1040,128]{1,0:T(8,128)S(1)} %get-tuple-element.40), channel_id=1, source_target_pairs={{0,2},{2,4},{3,1},{4,6},{5,3},{7,5},{8,10},{10,12},{11,9},{12,14},... | collective-permute-start | bytes 1597448 | tf_op jit(solution)/shard_map/ppermute | solution.py:503
  13.6 3.4 %collective-permute-done.1.refs_1_ = f32[520,128]{1,0:T(8,128)S(1)} collective-permute-done((f32[520,128]{1,0:T(8,128)S(1)}, f32[520,128]{1,0:T(8,128)S(1)}, u32[]{:S(2)}, u32[]{:S(2)}) %collective-permute-start.1) | collective-permute-done | bytes 266272 | tf_op jit(solution)/shard_map/ppermute | solution.py:503
  17.0 0.0 collective-permute-start.3
  17.0 4.2 %collective-permute-done.4.refs_1_ = f32[520,128]{1,0:T(8,128)S(1)} collective-permute-done((f32[520,128]{1,0:T(8,128)S(1)}, f32[520,128]{1,0:T(8,128)S(1)}, u32[]{:S(2)}, u32[]{:S(2)}) %collective-permute-start.4) | collective-permute-done | bytes 266272 | tf_op jit(solution)/shard_map/ppermute | solution.py:503
  21.2 1.5 %collective-permute-start.5 = (f32[520,128]{1,0:T(8,128)S(1)}, f32[520,128]{1,0:T(8,128)S(1)}, u32[]{:S(2)}, u32[]{:S(2)}) collective-permute-start(f32[520,128]{1,0:T(8,128)S(1)} %collective-permute-done.4.refs_1_), channel_id=1, source_target_pairs={{0,1},{2,3},{3,2},{4,5},{5,4},{7,6},{8,9},{10,11},{11,10},{12,13},... | collective-permute-start | bytes 798728 | tf_op jit(solution)/shard_map/ppermute | solution.py:509
  22.7 0.0 collective-permute-done._.refs_0_
  22.7 5.8 %shard_map.128 = (bf16[256,2048]{1,0:T(8,128)(2,1)S(1)}, bf16[256,2048]{1,0:T(8,128)(2,1)S(1)}, f32[128,2048]{1,0:T(8,128)}, f32[128,2048]{1,0:T(8,128)}, bf16[1...) custom-call(s32[1,16]{1,0:T(1,128)} %lens_hbm.3, ...), custom_call_target="tpu_custom_call" | custom-call | flops 4000000000 | bytes 12582912 | tf_op jit(solution)/shard_map/pallas_call | solution.py:487
  28.6 0.0 collective-permute-done.2.refs_2_
  28.6 0.0 collective-permute-done.3.refs_3_
  28.6 0.2 shard_map.129
  28.8 0.0 collective-permute-done.5.refs_3_
  28.8 0.9 %shard_map.130 = (f32[64,1024]{1,0:T(8,128)S(1)}, f32[64,1024]{1,0:T(8,128)S(1)}, f32[32,128]{1,0:T(8,128)}) custom-call(f32[1040,128]{1,0:T(8,128)S(1)} %collective-permute-done._.refs_0_, f32[520,128]{1,0:T(8,128)S(1)} %collective-permute-done.4.refs_1_, f32[1040,128]{1,0:T(8,128)S(1)} %collective-permute-done.2.refs_2_, ...), custom_call_target="tpu_custom_call" | custom-call | flops 100000000 | bytes 4194304 | tf_op jit(solution)/shard_map/pallas_call | solution.py:487
  29.8 5.7 %all-to-all-start = ((f32[32,1,128]{2,1,0:T(1,128)}), f32[32,1,128]{2,1,0:T(1,128)S(1)}, u32[]{:S(2)}, u32[]{:S(2)}) async-start(f32[32,1,128]{2,1,0:T(1,128)} %bitcast.7), calls=%async_computation | async-start | bytes 32768 | tf_op jit(solution)/shard_map/all_to_all | solution.py:619
  35.5 5.4 %shard_map.131 = (bf16[1,128,2048]{2,1,0:T(8,128)(2,1)}, bf16[1,64,128]{2,1,0:T(8,128)(2,1)}, bf16[1,64,128]{2,1,0:T(8,128)(2,1)}, f32[1,32,128]{2,1,0:T(8,128)}) custom-call(f32[64,1024]{1,0:T(8,128)S(1)} %get-tuple-element.52.came_one, f32[64,1024]{1,0:T(8,128)S(1)} %get-tuple-element.56.came_two, f32[64,1024]{1,0:T(8,128)S(1)} %get-tuple-element.57.pull_one, ...), custom_call_target="tpu_custom_call" | custom-call | flops 2000000000 | bytes 12582912 | tf_op jit(solution)/shard_map/pallas_call | solution.py:487
  40.9 1.8 %all-to-all-done = f32[32,1,128]{2,1,0:T(1,128)S(1)} async-done(((f32[32,1,128]{2,1,0:T(1,128)}), f32[32,1,128]{2,1,0:T(1,128)S(1)}, u32[]{:S(2)}, u32[]{:S(2)}) %all-to-all-start) | async-done | bytes 16416 | tf_op jit(solution)/shard_map/all_to_all | solution.py:619
  42.6 0.1 reduce_sum.9
  42.7 0.6 %fusion = (f32[32]{0:T(128)}, f32[32]{0:T(128)}) fusion(f32[128]{0:T(128)S(1)} %reduce_sum.9), kind=kLoop, calls=%fused_computation | loop fusion | bytes 512 | tf_op jit(solution)/shard_map/slice | solution.py:627
Async XLA Ops:
  2.7 20.0 %collective-permute-start = (f32[1040,128]{1,0:T(8,128)S(1)}, f32[1040,128]{1,0:T(8,128)S(1)}, u32[]{:S(2)}, u32[]{:S(2)}) collective-permute-start(f32[1040,128]{1,0:T(8,128)S(1)} %get-tuple-element.40), channel_id=1, source_target_pairs={{0,1},{1,0},{2,3},{3,2},{4,5},{5,4},{6,7},{7,6},{8,9},{9,8},{10,11... | collective-permute-start | bytes 1597448 | tf_op jit(solution)/shard_map/ppermute | solution.py:503
  5.8 11.2 %collective-permute-start.1 = (f32[520,128]{1,0:T(8,128)S(1)}, f32[520,128]{1,0:T(8,128)S(1)}, u32[]{:S(2)}, u32[]{:S(2)}) collective-permute-start(f32[520,128]{1,0:T(8,128)S(1)} %get-tuple-element.41), channel_id=1, source_target_pairs={{1,3},{2,0},{3,5},{4,2},{5,7},{6,4},{9,11},{10,8},{11,13},{12,10},... | collective-permute-start | bytes 798728 | tf_op jit(solution)/shard_map/ppermute | solution.py:503
  7.1 14.2 %collective-permute-start.4 = (f32[520,128]{1,0:T(8,128)S(1)}, f32[520,128]{1,0:T(8,128)S(1)}, u32[]{:S(2)}, u32[]{:S(2)}) collective-permute-start(f32[520,128]{1,0:T(8,128)S(1)} %get-tuple-element.53), channel_id=1, source_target_pairs={{1,3},{2,0},{3,5},{4,2},{5,7},{6,4},{9,11},{10,8},{11,13},{12,10},... | collective-permute-start | bytes 798728 | tf_op jit(solution)/shard_map/ppermute | solution.py:503
  8.4 20.2 %collective-permute-start.2 = (f32[1040,128]{1,0:T(8,128)S(1)}, f32[1040,128]{1,0:T(8,128)S(1)}, u32[]{:S(2)}, u32[]{:S(2)}) collective-permute-start(f32[1040,128]{1,0:T(8,128)S(1)} %get-tuple-element.40), channel_id=1, source_target_pairs={{0,2},{2,4},{3,1},{4,6},{5,3},{7,5},{8,10},{10,12},{11,9},{12,14},... | collective-permute-start | bytes 1597448 | tf_op jit(solution)/shard_map/ppermute | solution.py:503
  17.0 11.6 %collective-permute-start.3 = (f32[520,128]{1,0:T(8,128)S(1)}, f32[520,128]{1,0:T(8,128)S(1)}, u32[]{:S(2)}, u32[]{:S(2)}) collective-permute-start(f32[520,128]{1,0:T(8,128)S(1)} %collective-permute-done.1.refs_1_), channel_id=1, source_target_pairs={{0,1},{1,0},{2,3},{3,2},{4,5},{5,4},{6,7},{7,6},{8,9},{9,8},{10,11... | collective-permute-start | bytes 798728 | tf_op jit(solution)/shard_map/ppermute | solution.py:509
  21.2 7.6 %collective-permute-start.5 = (f32[520,128]{1,0:T(8,128)S(1)}, f32[520,128]{1,0:T(8,128)S(1)}, u32[]{:S(2)}, u32[]{:S(2)}) collective-permute-start(f32[520,128]{1,0:T(8,128)S(1)} %collective-permute-done.4.refs_1_), channel_id=1, source_target_pairs={{0,1},{2,3},{3,2},{4,5},{5,4},{7,6},{8,9},{10,11},{11,10},{12,13},... | collective-permute-start | bytes 798728 | tf_op jit(solution)/shard_map/ppermute | solution.py:509
  29.8 12.9 %all-to-all-start = ((f32[32,1,128]{2,1,0:T(1,128)}), f32[32,1,128]{2,1,0:T(1,128)S(1)}, u32[]{:S(2)}, u32[]{:S(2)}) async-start(f32[32,1,128]{2,1,0:T(1,128)} %bitcast.7), calls=%async_computation | async-start | bytes 32768 | tf_op jit(solution)/shard_map/all_to_all | solution.py:619
